TPU v7x, 512 devices: a whole 4x4x16 slice. The times are simulated.
512 devices in a mesh: scan: 32 (over z, core), depth: 16 (over y, x).
Axes of the slice: x: 4, y: 4, z: 16, core: 2. Of those that a mesh axis runs over, the one named last changes fastest.
Arguments:
- object_slices: float32 [16, 2, 8192, 128], P('depth', None, 'scan'), may hold values from -4 to 4
- probe_wave: float32 [2, 128, 128], replicated, may hold values from -6 to 6
- intensities: float32 [64, 128, 128], P('scan'), may hold values from 0.1 to 4
- offsets: int32 [64], P('scan'), may hold values from 0 to 255, as said below
- owners: int32 [64], P('scan'), may hold values from 0 to 31, as said below
Outputs:
- object_next: float32 [16, 2, 8192, 128], P('depth', None, 'scan')
Inputs may be any that keep to these rules, and one draw needn't show every extreme that they name: Position p is held by scan index p // 2; its window ends at row owners[p] * 256 + offsets[p] + 127, which is below 8192. owners[p] is p // 2 or one less.
All inputs are finite; a program needn't handle non-finite values.
Results may differ from a plain program's by a relative error of at most 0.0003.
Values sent between devices are 32-bit elements; how exact they have to be, the bound alone decides.
No kernel may reach another device: no remote copies, remote signals or barrier semaphores. Data moves between devices by JAX's collectives and lax.ppermute only.
A program may use at most 64 MiB of HBM per device.

v0:
```python
import math

import jax
import jax.numpy as jnp
from jax import lax
from jax.sharding import PartitionSpec as P

exact_mode = lax.Precision.HIGHEST
step_size = 0.25


def with_halo(block, sides, width):
    for axis, dim in sides:
        count = lax.axis_size(axis)
        forward = [(i, i + 1) for i in range(count - 1)]
        backward = [(target, source) for source, target in forward]
        low = lax.ppermute(
            lax.slice_in_dim(block, block.shape[dim] - width, None, axis=dim), axis, forward
        )
        high = lax.ppermute(lax.slice_in_dim(block, 0, width, axis=dim), axis, backward)
        block = jnp.concatenate([low, block, high], axis=dim)
    return block


def shifted(shard, axis, by):
    devices = lax.axis_size(axis)
    pairs = [(i, i + by) for i in range(devices) if 0 <= i + by < devices]
    return lax.ppermute(shard, axis, pairs)


def tables(win_size):
    indices = jnp.arange(win_size, dtype=jnp.int32)
    product = indices[:, None] * indices[None, :] % win_size
    angles = product.astype(jnp.float32) * (2.0 * math.pi / win_size)
    norm_scale = 1.0 / math.sqrt(win_size)
    cos_table = jnp.cos(angles) * norm_scale
    sin_table = jnp.sin(angles) * norm_scale
    frequency = jnp.where(indices < win_size // 2, indices, indices - win_size).astype(jnp.float32)
    phases = -(math.pi / win_size) * (
        frequency[:, None] * frequency[:, None] + frequency[None, :] * frequency[None, :]
    )
    forward_table = jnp.stack(
        [jnp.stack([cos_table, sin_table]), jnp.stack([-sin_table, cos_table])]
    )
    backward_table = jnp.stack(
        [jnp.stack([cos_table, -sin_table]), jnp.stack([sin_table, cos_table])]
    )
    return (forward_table, backward_table, jnp.cos(phases), jnp.sin(phases))


def transform(stacked, table):
    left_done = jnp.einsum("abkn,...bnm->...akm", table, stacked, precision=exact_mode)
    return jnp.einsum("...bkn,abnm->...akm", left_done, table, precision=exact_mode)


def propagate(stacked, tables_set, conj_sign):
    spec = transform(stacked, tables_set[0])
    kernel_cos, kernel_sin = (tables_set[2], tables_set[3])
    spec_real, spec_imag = (spec[..., 0, :, :], spec[..., 1, :, :])
    phased_real = spec_real * kernel_cos - conj_sign * spec_imag * kernel_sin
    phased_imag = spec_imag * kernel_cos + conj_sign * spec_real * kernel_sin
    return transform(jnp.stack([phased_real, phased_imag], -3), tables_set[1])


def mix_wave(wave_now, window):
    mixed_real = (
        wave_now[..., 0, :, :] * window[..., 0, :, :]
        - wave_now[..., 1, :, :] * window[..., 1, :, :]
    )
    mixed_imag = (
        wave_now[..., 0, :, :] * window[..., 1, :, :]
        + wave_now[..., 1, :, :] * window[..., 0, :, :]
    )
    return jnp.stack([mixed_real, mixed_imag], -3)


def advance(wave_now, window, tables_set):
    return propagate(mix_wave(wave_now, window), tables_set, 1.0)


def retreat(adjoint, window, tables_set):
    back_real = (
        window[..., 0, :, :] * adjoint[..., 0, :, :] + window[..., 1, :, :] * adjoint[..., 1, :, :]
    )
    back_imag = (
        window[..., 0, :, :] * adjoint[..., 1, :, :] - window[..., 1, :, :] * adjoint[..., 0, :, :]
    )
    return propagate(jnp.stack([back_real, back_imag], -3), tables_set, -1.0)


def far_field(wave_now, window, measured, tables_set):
    far_wave = transform(mix_wave(wave_now, window), tables_set[0])
    far_real, far_imag = (far_wave[..., 0, :, :], far_wave[..., 1, :, :])
    residual = far_real * far_real + far_imag * far_imag - measured
    return transform(jnp.stack([residual * far_real, residual * far_imag], -3), tables_set[1])


def object_grad(wave_now, adjoint):
    grad_real = (
        wave_now[..., 0, :, :] * adjoint[..., 0, :, :]
        + wave_now[..., 1, :, :] * adjoint[..., 1, :, :]
    )
    grad_imag = (
        wave_now[..., 0, :, :] * adjoint[..., 1, :, :]
        - wave_now[..., 1, :, :] * adjoint[..., 0, :, :]
    )
    return jnp.stack([grad_real, grad_imag], -3)


def shards(object_slices, probe_wave, intensities, offsets, owners):
    tile_rows = object_slices.shape[2]
    win_size = probe_wave.shape[-1]
    position_count = offsets.shape[0]
    sections = lax.axis_size("depth")
    depth_index = lax.axis_index("depth")
    scan_index = lax.axis_index("scan")
    tables_set = tables(win_size)
    padded = with_halo(object_slices, (("scan", 2),), tile_rows)
    halo_slab = padded[0]
    row_starts = (owners - scan_index + 1) * tile_rows + offsets
    windows = jax.vmap(
        lambda row_begin: lax.dynamic_slice_in_dim(halo_slab, row_begin, win_size, 1)
    )(row_starts)
    probe_stack = jnp.broadcast_to(probe_wave, (position_count,) + probe_wave.shape)
    is_last = depth_index == sections - 1
    steps_total = sections + position_count - 2
    slot_ids = jnp.arange(position_count, dtype=jnp.int32)

    def down_step(step_index, entering):
        item_index = step_index - depth_index
        is_valid = (item_index >= 0) & (item_index < position_count) & (depth_index < sections - 1)
        safe_index = jnp.clip(item_index, 0, position_count - 1)
        wave_in = lax.dynamic_index_in_dim(entering, safe_index, 0, keepdims=False)
        window = lax.dynamic_index_in_dim(windows, safe_index, 0, keepdims=False)
        computed = lax.cond(
            is_valid,
            lambda carried, patch: advance(carried, patch, tables_set),
            lambda carried, patch: carried,
            wave_in,
            window,
        )
        received = shifted(computed, "depth", 1)
        arrived = step_index - depth_index + 1
        stored = (arrived >= 0) & (arrived < position_count) & (depth_index >= 1)
        slot_mask = (slot_ids == arrived) & stored
        return jnp.where(slot_mask[:, None, None, None], received[None], entering)

    entering = lax.fori_loop(0, steps_total, down_step, probe_stack)
    adjoint = lax.cond(
        is_last,
        lambda carried: far_field(carried, windows, intensities, tables_set),
        lambda carried: jnp.zeros_like(carried),
        entering,
    )

    def up_step(step_index, own_adjoint):
        item_index = step_index - (sections - 1 - depth_index)
        is_valid = (item_index >= 0) & (item_index < position_count) & (depth_index >= 1)
        safe_index = jnp.clip(item_index, 0, position_count - 1)
        adjoint_in = lax.dynamic_index_in_dim(own_adjoint, safe_index, 0, keepdims=False)
        window = lax.dynamic_index_in_dim(windows, safe_index, 0, keepdims=False)
        computed = lax.cond(
            is_valid,
            lambda carried, patch: retreat(carried, patch, tables_set),
            lambda carried, patch: carried,
            adjoint_in,
            window,
        )
        received = shifted(computed, "depth", -1)
        arrived = step_index - (sections - 2 - depth_index)
        stored = (arrived >= 0) & (arrived < position_count) & (depth_index <= sections - 2)
        slot_mask = (slot_ids == arrived) & stored
        return jnp.where(slot_mask[:, None, None, None], received[None], own_adjoint)

    own_adjoint = lax.fori_loop(0, steps_total, up_step, adjoint)
    update = object_grad(entering, own_adjoint)
    buffer = jnp.zeros(halo_slab.shape, jnp.float32)
    for position in range(position_count):
        row_begin = row_starts[position]
        current = lax.dynamic_slice_in_dim(buffer, row_begin, win_size, 1)
        buffer = lax.dynamic_update_slice_in_dim(buffer, current + update[position], row_begin, 1)
    upper_rim = buffer[:, :tile_rows]
    middle = buffer[:, tile_rows : 2 * tile_rows]
    bottom = buffer[:, 2 * tile_rows :]
    from_below = shifted(upper_rim, "scan", -1)
    from_above = shifted(bottom, "scan", 1)
    gradient = middle + from_below + from_above
    return object_slices - step_size * gradient[None]


def solution(mesh):
    return jax.shard_map(
        shards,
        mesh=mesh,
        in_specs=(P("depth", None, "scan", None), P(), P("scan", None, None), P("scan"), P("scan")),
        out_specs=P("depth", None, "scan", None),
        check_vma=False,
    )
```

profile of v0, /device:TPU:134, one launch (start us, length us, event | category | flops | bytes accessed | tf_op | source)
XLA Modules:
  0.0 337.1 jit_solution(6656567266316737487)
XLA Ops:
  1.2 1.9 collective-permute-start.3
  3.1 2.4 collective-permute-start.2
  14.1 152.2 %while.35 = (s32[]{:T(128)}, f32[2,2,128,128]{3,2,1,0:T(8,128)S(1)}, s32[]{:T(128)}, pred[]{:T(512)}, pred[]{:T(512)}, /*index=5*/f32[2,2,128,128]{3,2,1,0:T(8,1...) while((s32[]{:T(128)}, ...), condition=%wide.region_3.4_spmd.clone.clone.clone, body=%wide.region_0.3_spmd.clone.clone.clone.sunk | while | flops 403013632 | bytes 4391779 | solution.py:148
  14.3 3.4 %collective-permute-start = (f32[2,128,128]{2,1,0:T(8,128)S(1)}, f32[2,128,128]{2,1,0:T(8,128)S(1)}, u32[]{:S(2)}, u32[]{:S(2)}) collective-permute-start(f32[2,128,128]{2,1,0:T(8,128)S(1)} %get-tuple-element.1045), channel_id=1, source_target_pairs={{0,1},{1,2},{2,3},{3,4},{4,5},{5,6},{6,7},{7,8},{8,9},{9,10},{10,1... | collective-permute-start | bytes 393224 | tf_op jit(solution)/shard_map/while/body/eval_jaxpr/ppermute | solution.py:28
  17.7 4.7 %collective-permute-done = f32[2,128,128]{2,1,0:T(8,128)S(1)} collective-permute-done((f32[2,128,128]{2,1,0:T(8,128)S(1)}, f32[2,128,128]{2,1,0:T(8,128)S(1)}, u32[]{:S(2)}, u32[]{:S(2)}) %collective-permute-start) | collective-permute-done | bytes 131104 | tf_op jit(solution)/shard_map/while/body/eval_jaxpr/ppermute | solution.py:28
  22.7 5.5 %collective-permute-start = (f32[2,128,128]{2,1,0:T(8,128)S(1)}, f32[2,128,128]{2,1,0:T(8,128)S(1)}, u32[]{:S(2)}, u32[]{:S(2)}) collective-permute-start(f32[2,128,128]{2,1,0:T(8,128)S(1)} %get-tuple-element.1045), channel_id=1, source_target_pairs={{0,1},{1,2},{2,3},{3,4},{4,5},{5,6},{6,7},{7,8},{8,9},{9,10},{10,1... | collective-permute-start | bytes 393224 | tf_op jit(solution)/shard_map/while/body/eval_jaxpr/ppermute | solution.py:28
  28.3 3.0 collective-permute-done
  31.5 6.5 %collective-permute-start = (f32[2,128,128]{2,1,0:T(8,128)S(1)}, f32[2,128,128]{2,1,0:T(8,128)S(1)}, u32[]{:S(2)}, u32[]{:S(2)}) collective-permute-start(f32[2,128,128]{2,1,0:T(8,128)S(1)} %get-tuple-element.1045), channel_id=1, source_target_pairs={{0,1},{1,2},{2,3},{3,4},{4,5},{5,6},{6,7},{7,8},{8,9},{9,10},{10,1... | collective-permute-start | bytes 393224 | tf_op jit(solution)/shard_map/while/body/eval_jaxpr/ppermute | solution.py:28
  38.1 2.5 collective-permute-done
  42.7 4.6 %collective-permute-start = (f32[2,128,128]{2,1,0:T(8,128)S(1)}, f32[2,128,128]{2,1,0:T(8,128)S(1)}, u32[]{:S(2)}, u32[]{:S(2)}) collective-permute-start(f32[2,128,128]{2,1,0:T(8,128)S(1)} %get-tuple-element.1045), channel_id=1, source_target_pairs={{0,1},{1,2},{2,3},{3,4},{4,5},{5,6},{6,7},{7,8},{8,9},{9,10},{10,1... | collective-permute-start | bytes 393224 | tf_op jit(solution)/shard_map/while/body/eval_jaxpr/ppermute | solution.py:28
  47.3 2.5 collective-permute-done
  51.9 6.5 %collective-permute-start = (f32[2,128,128]{2,1,0:T(8,128)S(1)}, f32[2,128,128]{2,1,0:T(8,128)S(1)}, u32[]{:S(2)}, u32[]{:S(2)}) collective-permute-start(f32[2,128,128]{2,1,0:T(8,128)S(1)} %get-tuple-element.1045), channel_id=1, source_target_pairs={{0,1},{1,2},{2,3},{3,4},{4,5},{5,6},{6,7},{7,8},{8,9},{9,10},{10,1... | collective-permute-start | bytes 393224 | tf_op jit(solution)/shard_map/while/body/eval_jaxpr/ppermute | solution.py:28
  58.4 2.5 collective-permute-done
  61.1 8.3 %collective-permute-start = (f32[2,128,128]{2,1,0:T(8,128)S(1)}, f32[2,128,128]{2,1,0:T(8,128)S(1)}, u32[]{:S(2)}, u32[]{:S(2)}) collective-permute-start(f32[2,128,128]{2,1,0:T(8,128)S(1)} %get-tuple-element.1045), channel_id=1, source_target_pairs={{0,1},{1,2},{2,3},{3,4},{4,5},{5,6},{6,7},{7,8},{8,9},{9,10},{10,1... | collective-permute-start | bytes 393224 | tf_op jit(solution)/shard_map/while/body/eval_jaxpr/ppermute | solution.py:28
  69.5 2.5 collective-permute-done
  72.2 6.5 %collective-permute-start = (f32[2,128,128]{2,1,0:T(8,128)S(1)}, f32[2,128,128]{2,1,0:T(8,128)S(1)}, u32[]{:S(2)}, u32[]{:S(2)}) collective-permute-start(f32[2,128,128]{2,1,0:T(8,128)S(1)} %get-tuple-element.1045), channel_id=1, source_target_pairs={{0,1},{1,2},{2,3},{3,4},{4,5},{5,6},{6,7},{7,8},{8,9},{9,10},{10,1... | collective-permute-start | bytes 393224 | tf_op jit(solution)/shard_map/while/body/eval_jaxpr/ppermute | solution.py:28
  78.7 2.5 collective-permute-done
  81.5 6.5 %collective-permute-start = (f32[2,128,128]{2,1,0:T(8,128)S(1)}, f32[2,128,128]{2,1,0:T(8,128)S(1)}, u32[]{:S(2)}, u32[]{:S(2)}) collective-permute-start(f32[2,128,128]{2,1,0:T(8,128)S(1)} %get-tuple-element.1045), channel_id=1, source_target_pairs={{0,1},{1,2},{2,3},{3,4},{4,5},{5,6},{6,7},{7,8},{8,9},{9,10},{10,1... | collective-permute-start | bytes 393224 | tf_op jit(solution)/shard_map/while/body/eval_jaxpr/ppermute | solution.py:28
  88.0 3.2 collective-permute-done
  91.5 6.5 %collective-permute-start = (f32[2,128,128]{2,1,0:T(8,128)S(1)}, f32[2,128,128]{2,1,0:T(8,128)S(1)}, u32[]{:S(2)}, u32[]{:S(2)}) collective-permute-start(f32[2,128,128]{2,1,0:T(8,128)S(1)} %get-tuple-element.1045), channel_id=1, source_target_pairs={{0,1},{1,2},{2,3},{3,4},{4,5},{5,6},{6,7},{7,8},{8,9},{9,10},{10,1... | collective-permute-start | bytes 393224 | tf_op jit(solution)/shard_map/while/body/eval_jaxpr/ppermute | solution.py:28
  98.0 3.3 collective-permute-done
  101.6 6.5 %collective-permute-start = (f32[2,128,128]{2,1,0:T(8,128)S(1)}, f32[2,128,128]{2,1,0:T(8,128)S(1)}, u32[]{:S(2)}, u32[]{:S(2)}) collective-permute-start(f32[2,128,128]{2,1,0:T(8,128)S(1)} %get-tuple-element.1045), channel_id=1, source_target_pairs={{0,1},{1,2},{2,3},{3,4},{4,5},{5,6},{6,7},{7,8},{8,9},{9,10},{10,1... | collective-permute-start | bytes 393224 | tf_op jit(solution)/shard_map/while/body/eval_jaxpr/ppermute | solution.py:28
  108.1 2.5 collective-permute-done
  110.9 6.5 %collective-permute-start = (f32[2,128,128]{2,1,0:T(8,128)S(1)}, f32[2,128,128]{2,1,0:T(8,128)S(1)}, u32[]{:S(2)}, u32[]{:S(2)}) collective-permute-start(f32[2,128,128]{2,1,0:T(8,128)S(1)} %get-tuple-element.1045), channel_id=1, source_target_pairs={{0,1},{1,2},{2,3},{3,4},{4,5},{5,6},{6,7},{7,8},{8,9},{9,10},{10,1... | collective-permute-start | bytes 393224 | tf_op jit(solution)/shard_map/while/body/eval_jaxpr/ppermute | solution.py:28
  117.5 2.5 collective-permute-done
  120.2 6.5 %collective-permute-start = (f32[2,128,128]{2,1,0:T(8,128)S(1)}, f32[2,128,128]{2,1,0:T(8,128)S(1)}, u32[]{:S(2)}, u32[]{:S(2)}) collective-permute-start(f32[2,128,128]{2,1,0:T(8,128)S(1)} %get-tuple-element.1045), channel_id=1, source_target_pairs={{0,1},{1,2},{2,3},{3,4},{4,5},{5,6},{6,7},{7,8},{8,9},{9,10},{10,1... | collective-permute-start | bytes 393224 | tf_op jit(solution)/shard_map/while/body/eval_jaxpr/ppermute | solution.py:28
  126.7 2.5 collective-permute-done
  129.5 6.5 %collective-permute-start = (f32[2,128,128]{2,1,0:T(8,128)S(1)}, f32[2,128,128]{2,1,0:T(8,128)S(1)}, u32[]{:S(2)}, u32[]{:S(2)}) collective-permute-start(f32[2,128,128]{2,1,0:T(8,128)S(1)} %get-tuple-element.1045), channel_id=1, source_target_pairs={{0,1},{1,2},{2,3},{3,4},{4,5},{5,6},{6,7},{7,8},{8,9},{9,10},{10,1... | collective-permute-start | bytes 393224 | tf_op jit(solution)/shard_map/while/body/eval_jaxpr/ppermute | solution.py:28
  136.0 2.5 collective-permute-done
  138.7 6.5 %collective-permute-start = (f32[2,128,128]{2,1,0:T(8,128)S(1)}, f32[2,128,128]{2,1,0:T(8,128)S(1)}, u32[]{:S(2)}, u32[]{:S(2)}) collective-permute-start(f32[2,128,128]{2,1,0:T(8,128)S(1)} %get-tuple-element.1045), channel_id=1, source_target_pairs={{0,1},{1,2},{2,3},{3,4},{4,5},{5,6},{6,7},{7,8},{8,9},{9,10},{10,1... | collective-permute-start | bytes 393224 | tf_op jit(solution)/shard_map/while/body/eval_jaxpr/ppermute | solution.py:28
  145.2 2.5 collective-permute-done
  148.0 6.5 %collective-permute-start = (f32[2,128,128]{2,1,0:T(8,128)S(1)}, f32[2,128,128]{2,1,0:T(8,128)S(1)}, u32[]{:S(2)}, u32[]{:S(2)}) collective-permute-start(f32[2,128,128]{2,1,0:T(8,128)S(1)} %get-tuple-element.1045), channel_id=1, source_target_pairs={{0,1},{1,2},{2,3},{3,4},{4,5},{5,6},{6,7},{7,8},{8,9},{9,10},{10,1... | collective-permute-start | bytes 393224 | tf_op jit(solution)/shard_map/while/body/eval_jaxpr/ppermute | solution.py:28
  154.5 2.5 collective-permute-done
  157.2 6.5 %collective-permute-start = (f32[2,128,128]{2,1,0:T(8,128)S(1)}, f32[2,128,128]{2,1,0:T(8,128)S(1)}, u32[]{:S(2)}, u32[]{:S(2)}) collective-permute-start(f32[2,128,128]{2,1,0:T(8,128)S(1)} %get-tuple-element.1045), channel_id=1, source_target_pairs={{0,1},{1,2},{2,3},{3,4},{4,5},{5,6},{6,7},{7,8},{8,9},{9,10},{10,1... | collective-permute-start | bytes 393224 | tf_op jit(solution)/shard_map/while/body/eval_jaxpr/ppermute | solution.py:28
  163.7 2.5 collective-permute-done
  166.4 157.6 %while.36 = (s32[]{:T(128)}, f32[2,2,128,128]{3,2,1,0:T(8,128)S(1)}, s32[]{:T(128)}, pred[]{:T(512)}, s32[]{:T(128)}, /*index=5*/pred[]{:T(512)}, f32[2,2,128,12...) while((s32[]{:T(128)}, ...), condition=%wide.region_9.10_spmd.clone.clone.clone, body=%wide.region_6.9_spmd.clone.clone.clone.sunk | while | flops 403046400 | bytes 4391795 | solution.py:175
  166.5 1.9 collective-permute-start.1
  168.5 8.1 %collective-permute-done.1 = f32[2,128,128]{2,1,0:T(8,128)S(1)} collective-permute-done((f32[2,128,128]{2,1,0:T(8,128)S(1)}, f32[2,128,128]{2,1,0:T(8,128)S(1)}, u32[]{:S(2)}, u32[]{:S(2)}) %collective-permute-start.1) | collective-permute-done | bytes 131104 | tf_op jit(solution)/shard_map/while/body/eval_jaxpr/ppermute | solution.py:28
  176.9 1.9 collective-permute-start.1
  178.8 7.0 %collective-permute-done.1 = f32[2,128,128]{2,1,0:T(8,128)S(1)} collective-permute-done((f32[2,128,128]{2,1,0:T(8,128)S(1)}, f32[2,128,128]{2,1,0:T(8,128)S(1)}, u32[]{:S(2)}, u32[]{:S(2)}) %collective-permute-start.1) | collective-permute-done | bytes 131104 | tf_op jit(solution)/shard_map/while/body/eval_jaxpr/ppermute | solution.py:28
  186.1 1.9 collective-permute-start.1
  188.1 7.0 %collective-permute-done.1 = f32[2,128,128]{2,1,0:T(8,128)S(1)} collective-permute-done((f32[2,128,128]{2,1,0:T(8,128)S(1)}, f32[2,128,128]{2,1,0:T(8,128)S(1)}, u32[]{:S(2)}, u32[]{:S(2)}) %collective-permute-start.1) | collective-permute-done | bytes 131104 | tf_op jit(solution)/shard_map/while/body/eval_jaxpr/ppermute | solution.py:28
  195.4 1.9 collective-permute-start.1
  197.3 7.0 %collective-permute-done.1 = f32[2,128,128]{2,1,0:T(8,128)S(1)} collective-permute-done((f32[2,128,128]{2,1,0:T(8,128)S(1)}, f32[2,128,128]{2,1,0:T(8,128)S(1)}, u32[]{:S(2)}, u32[]{:S(2)}) %collective-permute-start.1) | collective-permute-done | bytes 131104 | tf_op jit(solution)/shard_map/while/body/eval_jaxpr/ppermute | solution.py:28
  204.6 1.9 collective-permute-start.1
  206.6 7.0 %collective-permute-done.1 = f32[2,128,128]{2,1,0:T(8,128)S(1)} collective-permute-done((f32[2,128,128]{2,1,0:T(8,128)S(1)}, f32[2,128,128]{2,1,0:T(8,128)S(1)}, u32[]{:S(2)}, u32[]{:S(2)}) %collective-permute-start.1) | collective-permute-done | bytes 131104 | tf_op jit(solution)/shard_map/while/body/eval_jaxpr/ppermute | solution.py:28
  213.9 1.9 collective-permute-start.1
  215.8 7.0 %collective-permute-done.1 = f32[2,128,128]{2,1,0:T(8,128)S(1)} collective-permute-done((f32[2,128,128]{2,1,0:T(8,128)S(1)}, f32[2,128,128]{2,1,0:T(8,128)S(1)}, u32[]{:S(2)}, u32[]{:S(2)}) %collective-permute-start.1) | collective-permute-done | bytes 131104 | tf_op jit(solution)/shard_map/while/body/eval_jaxpr/ppermute | solution.py:28
  223.1 1.9 collective-permute-start.1
  225.1 7.6 %collective-permute-done.1 = f32[2,128,128]{2,1,0:T(8,128)S(1)} collective-permute-done((f32[2,128,128]{2,1,0:T(8,128)S(1)}, f32[2,128,128]{2,1,0:T(8,128)S(1)}, u32[]{:S(2)}, u32[]{:S(2)}) %collective-permute-start.1) | collective-permute-done | bytes 131104 | tf_op jit(solution)/shard_map/while/body/eval_jaxpr/ppermute | solution.py:28
  233.0 1.9 collective-permute-start.1
  235.0 8.1 %collective-permute-done.1 = f32[2,128,128]{2,1,0:T(8,128)S(1)} collective-permute-done((f32[2,128,128]{2,1,0:T(8,128)S(1)}, f32[2,128,128]{2,1,0:T(8,128)S(1)}, u32[]{:S(2)}, u32[]{:S(2)}) %collective-permute-start.1) | collective-permute-done | bytes 131104 | tf_op jit(solution)/shard_map/while/body/eval_jaxpr/ppermute | solution.py:28
  245.2 7.3 %collective-permute-done.1 = f32[2,128,128]{2,1,0:T(8,128)S(1)} collective-permute-done((f32[2,128,128]{2,1,0:T(8,128)S(1)}, f32[2,128,128]{2,1,0:T(8,128)S(1)}, u32[]{:S(2)}, u32[]{:S(2)}) %collective-permute-start.1) | collective-permute-done | bytes 131104 | tf_op jit(solution)/shard_map/while/body/eval_jaxpr/ppermute | solution.py:28
  254.8 8.3 %collective-permute-done.1 = f32[2,128,128]{2,1,0:T(8,128)S(1)} collective-permute-done((f32[2,128,128]{2,1,0:T(8,128)S(1)}, f32[2,128,128]{2,1,0:T(8,128)S(1)}, u32[]{:S(2)}, u32[]{:S(2)}) %collective-permute-start.1) | collective-permute-done | bytes 131104 | tf_op jit(solution)/shard_map/while/body/eval_jaxpr/ppermute | solution.py:28
  265.2 7.6 %collective-permute-done.1 = f32[2,128,128]{2,1,0:T(8,128)S(1)} collective-permute-done((f32[2,128,128]{2,1,0:T(8,128)S(1)}, f32[2,128,128]{2,1,0:T(8,128)S(1)}, u32[]{:S(2)}, u32[]{:S(2)}) %collective-permute-start.1) | collective-permute-done | bytes 131104 | tf_op jit(solution)/shard_map/while/body/eval_jaxpr/ppermute | solution.py:28
  275.1 8.1 %collective-permute-done.1 = f32[2,128,128]{2,1,0:T(8,128)S(1)} collective-permute-done((f32[2,128,128]{2,1,0:T(8,128)S(1)}, f32[2,128,128]{2,1,0:T(8,128)S(1)}, u32[]{:S(2)}, u32[]{:S(2)}) %collective-permute-start.1) | collective-permute-done | bytes 131104 | tf_op jit(solution)/shard_map/while/body/eval_jaxpr/ppermute | solution.py:28
  287.2 7.0 %collective-permute-done.1 = f32[2,128,128]{2,1,0:T(8,128)S(1)} collective-permute-done((f32[2,128,128]{2,1,0:T(8,128)S(1)}, f32[2,128,128]{2,1,0:T(8,128)S(1)}, u32[]{:S(2)}, u32[]{:S(2)}) %collective-permute-start.1) | collective-permute-done | bytes 131104 | tf_op jit(solution)/shard_map/while/body/eval_jaxpr/ppermute | solution.py:28
  298.3 7.0 %collective-permute-done.1 = f32[2,128,128]{2,1,0:T(8,128)S(1)} collective-permute-done((f32[2,128,128]{2,1,0:T(8,128)S(1)}, f32[2,128,128]{2,1,0:T(8,128)S(1)}, u32[]{:S(2)}, u32[]{:S(2)}) %collective-permute-start.1) | collective-permute-done | bytes 131104 | tf_op jit(solution)/shard_map/while/body/eval_jaxpr/ppermute | solution.py:28
  305.6 1.9 collective-permute-start.1
  307.6 7.0 %collective-permute-done.1 = f32[2,128,128]{2,1,0:T(8,128)S(1)} collective-permute-done((f32[2,128,128]{2,1,0:T(8,128)S(1)}, f32[2,128,128]{2,1,0:T(8,128)S(1)}, u32[]{:S(2)}, u32[]{:S(2)}) %collective-permute-start.1) | collective-permute-done | bytes 131104 | tf_op jit(solution)/shard_map/while/body/eval_jaxpr/ppermute | solution.py:28
  316.8 7.0 %collective-permute-done.1 = f32[2,128,128]{2,1,0:T(8,128)S(1)} collective-permute-done((f32[2,128,128]{2,1,0:T(8,128)S(1)}, f32[2,128,128]{2,1,0:T(8,128)S(1)}, u32[]{:S(2)}, u32[]{:S(2)}) %collective-permute-start.1) | collective-permute-done | bytes 131104 | tf_op jit(solution)/shard_map/while/body/eval_jaxpr/ppermute | solution.py:28
  325.4 2.1 collective-permute-start.4
  327.4 2.4 collective-permute-start.5
  331.3 5.0 %collective-permute-done.5 = f32[2,256,128]{2,1,0:T(8,128)S(1)} collective-permute-done((f32[2,256,128]{2,1,0:T(8,128)S(1)}, f32[2,256,128]{2,1,0:T(8,128)S(1)}, u32[]{:S(2)}, u32[]{:S(2)}) %collective-permute-start.5) | collective-permute-done | bytes 262176 | tf_op jit(solution)/shard_map/ppermute | solution.py:28
  (227 shorter events, 44.5 us)
Async XLA Ops:
  1.2 10.3 %collective-permute-start.3 = (f32[1,2,256,128]{3,1,2,0:T(2,128)S(1)}, f32[1,2,256,128]{3,1,2,0:T(2,128)S(1)}, u32[]{:S(2)}, u32[]{:S(2)}) collective-permute-start(f32[1,2,256,128]{3,1,2,0:T(2,128)S(1)} %copy.8), channel_id=1, source_target_pairs={{16,0},{32,16},{48,32},{64,48},{80,64},{96,80},{112,96},{128,112},... | collective-permute-start | bytes 786440 | tf_op jit(solution)/shard_map/ppermute | solution.py:20
  3.1 8.9 %collective-permute-start.2 = (f32[1,2,256,128]{3,1,2,0:T(2,128)S(1)}, f32[1,2,256,128]{3,1,2,0:T(2,128)S(1)}, u32[]{:S(2)}, u32[]{:S(2)}) collective-permute-start(f32[1,2,256,128]{3,1,2,0:T(2,128)S(1)} %copy.8), channel_id=1, source_target_pairs={{0,16},{16,32},{32,48},{48,64},{64,80},{80,96},{96,112},{112,128},... | collective-permute-start | bytes 786440 | tf_op jit(solution)/shard_map/ppermute | solution.py:17
  6.3 0.7 copy-start.3
  6.3 0.7 copy-start.4
  13.2 0.9 copy-start.1
  14.1 152.2 %copy-start.2 = (f32[2,128,128]{2,1,0:T(8,128)S(1)}, f32[2,128,128]{2,1,0:T(8,128)}, u32[]{:S(2)}) copy-start(f32[2,128,128]{2,1,0:T(8,128)} %param.17) | copy-start | bytes 393220
  14.3 8.2 %collective-permute-start = (f32[2,128,128]{2,1,0:T(8,128)S(1)}, f32[2,128,128]{2,1,0:T(8,128)S(1)}, u32[]{:S(2)}, u32[]{:S(2)}) collective-permute-start(f32[2,128,128]{2,1,0:T(8,128)S(1)} %get-tuple-element.1045), channel_id=1, source_target_pairs={{0,1},{1,2},{2,3},{3,4},{4,5},{5,6},{6,7},{7,8},{8,9},{9,10},{10,1... | collective-permute-start | bytes 393224 | tf_op jit(solution)/shard_map/while/body/eval_jaxpr/ppermute | solution.py:28
  22.7 8.5 %collective-permute-start = (f32[2,128,128]{2,1,0:T(8,128)S(1)}, f32[2,128,128]{2,1,0:T(8,128)S(1)}, u32[]{:S(2)}, u32[]{:S(2)}) collective-permute-start(f32[2,128,128]{2,1,0:T(8,128)S(1)} %get-tuple-element.1045), channel_id=1, source_target_pairs={{0,1},{1,2},{2,3},{3,4},{4,5},{5,6},{6,7},{7,8},{8,9},{9,10},{10,1... | collective-permute-start | bytes 393224 | tf_op jit(solution)/shard_map/while/body/eval_jaxpr/ppermute | solution.py:28
  31.5 9.0 %collective-permute-start = (f32[2,128,128]{2,1,0:T(8,128)S(1)}, f32[2,128,128]{2,1,0:T(8,128)S(1)}, u32[]{:S(2)}, u32[]{:S(2)}) collective-permute-start(f32[2,128,128]{2,1,0:T(8,128)S(1)} %get-tuple-element.1045), channel_id=1, source_target_pairs={{0,1},{1,2},{2,3},{3,4},{4,5},{5,6},{6,7},{7,8},{8,9},{9,10},{10,1... | collective-permute-start | bytes 393224 | tf_op jit(solution)/shard_map/while/body/eval_jaxpr/ppermute | solution.py:28
  42.7 7.1 %collective-permute-start = (f32[2,128,128]{2,1,0:T(8,128)S(1)}, f32[2,128,128]{2,1,0:T(8,128)S(1)}, u32[]{:S(2)}, u32[]{:S(2)}) collective-permute-start(f32[2,128,128]{2,1,0:T(8,128)S(1)} %get-tuple-element.1045), channel_id=1, source_target_pairs={{0,1},{1,2},{2,3},{3,4},{4,5},{5,6},{6,7},{7,8},{8,9},{9,10},{10,1... | collective-permute-start | bytes 393224 | tf_op jit(solution)/shard_map/while/body/eval_jaxpr/ppermute | solution.py:28
  51.9 9.0 %collective-permute-start = (f32[2,128,128]{2,1,0:T(8,128)S(1)}, f32[2,128,128]{2,1,0:T(8,128)S(1)}, u32[]{:S(2)}, u32[]{:S(2)}) collective-permute-start(f32[2,128,128]{2,1,0:T(8,128)S(1)} %get-tuple-element.1045), channel_id=1, source_target_pairs={{0,1},{1,2},{2,3},{3,4},{4,5},{5,6},{6,7},{7,8},{8,9},{9,10},{10,1... | collective-permute-start | bytes 393224 | tf_op jit(solution)/shard_map/while/body/eval_jaxpr/ppermute | solution.py:28
  61.1 10.8 %collective-permute-start = (f32[2,128,128]{2,1,0:T(8,128)S(1)}, f32[2,128,128]{2,1,0:T(8,128)S(1)}, u32[]{:S(2)}, u32[]{:S(2)}) collective-permute-start(f32[2,128,128]{2,1,0:T(8,128)S(1)} %get-tuple-element.1045), channel_id=1, source_target_pairs={{0,1},{1,2},{2,3},{3,4},{4,5},{5,6},{6,7},{7,8},{8,9},{9,10},{10,1... | collective-permute-start | bytes 393224 | tf_op jit(solution)/shard_map/while/body/eval_jaxpr/ppermute | solution.py:28
  72.2 9.0 %collective-permute-start = (f32[2,128,128]{2,1,0:T(8,128)S(1)}, f32[2,128,128]{2,1,0:T(8,128)S(1)}, u32[]{:S(2)}, u32[]{:S(2)}) collective-permute-start(f32[2,128,128]{2,1,0:T(8,128)S(1)} %get-tuple-element.1045), channel_id=1, source_target_pairs={{0,1},{1,2},{2,3},{3,4},{4,5},{5,6},{6,7},{7,8},{8,9},{9,10},{10,1... | collective-permute-start | bytes 393224 | tf_op jit(solution)/shard_map/while/body/eval_jaxpr/ppermute | solution.py:28
  81.5 9.7 %collective-permute-start = (f32[2,128,128]{2,1,0:T(8,128)S(1)}, f32[2,128,128]{2,1,0:T(8,128)S(1)}, u32[]{:S(2)}, u32[]{:S(2)}) collective-permute-start(f32[2,128,128]{2,1,0:T(8,128)S(1)} %get-tuple-element.1045), channel_id=1, source_target_pairs={{0,1},{1,2},{2,3},{3,4},{4,5},{5,6},{6,7},{7,8},{8,9},{9,10},{10,1... | collective-permute-start | bytes 393224 | tf_op jit(solution)/shard_map/while/body/eval_jaxpr/ppermute | solution.py:28
  91.5 9.8 %collective-permute-start = (f32[2,128,128]{2,1,0:T(8,128)S(1)}, f32[2,128,128]{2,1,0:T(8,128)S(1)}, u32[]{:S(2)}, u32[]{:S(2)}) collective-permute-start(f32[2,128,128]{2,1,0:T(8,128)S(1)} %get-tuple-element.1045), channel_id=1, source_target_pairs={{0,1},{1,2},{2,3},{3,4},{4,5},{5,6},{6,7},{7,8},{8,9},{9,10},{10,1... | collective-permute-start | bytes 393224 | tf_op jit(solution)/shard_map/while/body/eval_jaxpr/ppermute | solution.py:28
  101.6 9.1 %collective-permute-start = (f32[2,128,128]{2,1,0:T(8,128)S(1)}, f32[2,128,128]{2,1,0:T(8,128)S(1)}, u32[]{:S(2)}, u32[]{:S(2)}) collective-permute-start(f32[2,128,128]{2,1,0:T(8,128)S(1)} %get-tuple-element.1045), channel_id=1, source_target_pairs={{0,1},{1,2},{2,3},{3,4},{4,5},{5,6},{6,7},{7,8},{8,9},{9,10},{10,1... | collective-permute-start | bytes 393224 | tf_op jit(solution)/shard_map/while/body/eval_jaxpr/ppermute | solution.py:28
  110.9 9.0 %collective-permute-start = (f32[2,128,128]{2,1,0:T(8,128)S(1)}, f32[2,128,128]{2,1,0:T(8,128)S(1)}, u32[]{:S(2)}, u32[]{:S(2)}) collective-permute-start(f32[2,128,128]{2,1,0:T(8,128)S(1)} %get-tuple-element.1045), channel_id=1, source_target_pairs={{0,1},{1,2},{2,3},{3,4},{4,5},{5,6},{6,7},{7,8},{8,9},{9,10},{10,1... | collective-permute-start | bytes 393224 | tf_op jit(solution)/shard_map/while/body/eval_jaxpr/ppermute | solution.py:28
  120.2 9.0 %collective-permute-start = (f32[2,128,128]{2,1,0:T(8,128)S(1)}, f32[2,128,128]{2,1,0:T(8,128)S(1)}, u32[]{:S(2)}, u32[]{:S(2)}) collective-permute-start(f32[2,128,128]{2,1,0:T(8,128)S(1)} %get-tuple-element.1045), channel_id=1, source_target_pairs={{0,1},{1,2},{2,3},{3,4},{4,5},{5,6},{6,7},{7,8},{8,9},{9,10},{10,1... | collective-permute-start | bytes 393224 | tf_op jit(solution)/shard_map/while/body/eval_jaxpr/ppermute | solution.py:28
  129.5 9.0 %collective-permute-start = (f32[2,128,128]{2,1,0:T(8,128)S(1)}, f32[2,128,128]{2,1,0:T(8,128)S(1)}, u32[]{:S(2)}, u32[]{:S(2)}) collective-permute-start(f32[2,128,128]{2,1,0:T(8,128)S(1)} %get-tuple-element.1045), channel_id=1, source_target_pairs={{0,1},{1,2},{2,3},{3,4},{4,5},{5,6},{6,7},{7,8},{8,9},{9,10},{10,1... | collective-permute-start | bytes 393224 | tf_op jit(solution)/shard_map/while/body/eval_jaxpr/ppermute | solution.py:28
  138.7 9.0 %collective-permute-start = (f32[2,128,128]{2,1,0:T(8,128)S(1)}, f32[2,128,128]{2,1,0:T(8,128)S(1)}, u32[]{:S(2)}, u32[]{:S(2)}) collective-permute-start(f32[2,128,128]{2,1,0:T(8,128)S(1)} %get-tuple-element.1045), channel_id=1, source_target_pairs={{0,1},{1,2},{2,3},{3,4},{4,5},{5,6},{6,7},{7,8},{8,9},{9,10},{10,1... | collective-permute-start | bytes 393224 | tf_op jit(solution)/shard_map/while/body/eval_jaxpr/ppermute | solution.py:28
  148.0 9.0 %collective-permute-start = (f32[2,128,128]{2,1,0:T(8,128)S(1)}, f32[2,128,128]{2,1,0:T(8,128)S(1)}, u32[]{:S(2)}, u32[]{:S(2)}) collective-permute-start(f32[2,128,128]{2,1,0:T(8,128)S(1)} %get-tuple-element.1045), channel_id=1, source_target_pairs={{0,1},{1,2},{2,3},{3,4},{4,5},{5,6},{6,7},{7,8},{8,9},{9,10},{10,1... | collective-permute-start | bytes 393224 | tf_op jit(solution)/shard_map/while/body/eval_jaxpr/ppermute | solution.py:28
  157.2 9.0 %collective-permute-start = (f32[2,128,128]{2,1,0:T(8,128)S(1)}, f32[2,128,128]{2,1,0:T(8,128)S(1)}, u32[]{:S(2)}, u32[]{:S(2)}) collective-permute-start(f32[2,128,128]{2,1,0:T(8,128)S(1)} %get-tuple-element.1045), channel_id=1, source_target_pairs={{0,1},{1,2},{2,3},{3,4},{4,5},{5,6},{6,7},{7,8},{8,9},{9,10},{10,1... | collective-permute-start | bytes 393224 | tf_op jit(solution)/shard_map/while/body/eval_jaxpr/ppermute | solution.py:28
  166.5 10.1 %collective-permute-start.1 = (f32[2,128,128]{2,1,0:T(8,128)S(1)}, f32[2,128,128]{2,1,0:T(8,128)S(1)}, u32[]{:S(2)}, u32[]{:S(2)}) collective-permute-start(f32[2,128,128]{2,1,0:T(8,128)S(1)} %get-tuple-element.1046), channel_id=1, source_target_pairs={{1,0},{2,1},{3,2},{4,3},{5,4},{6,5},{7,6},{8,7},{9,8},{10,9},{11,1... | collective-permute-start | bytes 393224 | tf_op jit(solution)/shard_map/while/body/eval_jaxpr/ppermute | solution.py:28
  176.9 9.0 %collective-permute-start.1 = (f32[2,128,128]{2,1,0:T(8,128)S(1)}, f32[2,128,128]{2,1,0:T(8,128)S(1)}, u32[]{:S(2)}, u32[]{:S(2)}) collective-permute-start(f32[2,128,128]{2,1,0:T(8,128)S(1)} %get-tuple-element.1046), channel_id=1, source_target_pairs={{1,0},{2,1},{3,2},{4,3},{5,4},{6,5},{7,6},{8,7},{9,8},{10,9},{11,1... | collective-permute-start | bytes 393224 | tf_op jit(solution)/shard_map/while/body/eval_jaxpr/ppermute | solution.py:28
  186.1 9.0 %collective-permute-start.1 = (f32[2,128,128]{2,1,0:T(8,128)S(1)}, f32[2,128,128]{2,1,0:T(8,128)S(1)}, u32[]{:S(2)}, u32[]{:S(2)}) collective-permute-start(f32[2,128,128]{2,1,0:T(8,128)S(1)} %get-tuple-element.1046), channel_id=1, source_target_pairs={{1,0},{2,1},{3,2},{4,3},{5,4},{6,5},{7,6},{8,7},{9,8},{10,9},{11,1... | collective-permute-start | bytes 393224 | tf_op jit(solution)/shard_map/while/body/eval_jaxpr/ppermute | solution.py:28
  195.4 9.0 %collective-permute-start.1 = (f32[2,128,128]{2,1,0:T(8,128)S(1)}, f32[2,128,128]{2,1,0:T(8,128)S(1)}, u32[]{:S(2)}, u32[]{:S(2)}) collective-permute-start(f32[2,128,128]{2,1,0:T(8,128)S(1)} %get-tuple-element.1046), channel_id=1, source_target_pairs={{1,0},{2,1},{3,2},{4,3},{5,4},{6,5},{7,6},{8,7},{9,8},{10,9},{11,1... | collective-permute-start | bytes 393224 | tf_op jit(solution)/shard_map/while/body/eval_jaxpr/ppermute | solution.py:28
  204.6 9.0 %collective-permute-start.1 = (f32[2,128,128]{2,1,0:T(8,128)S(1)}, f32[2,128,128]{2,1,0:T(8,128)S(1)}, u32[]{:S(2)}, u32[]{:S(2)}) collective-permute-start(f32[2,128,128]{2,1,0:T(8,128)S(1)} %get-tuple-element.1046), channel_id=1, source_target_pairs={{1,0},{2,1},{3,2},{4,3},{5,4},{6,5},{7,6},{8,7},{9,8},{10,9},{11,1... | collective-permute-start | bytes 393224 | tf_op jit(solution)/shard_map/while/body/eval_jaxpr/ppermute | solution.py:28
  213.9 9.0 %collective-permute-start.1 = (f32[2,128,128]{2,1,0:T(8,128)S(1)}, f32[2,128,128]{2,1,0:T(8,128)S(1)}, u32[]{:S(2)}, u32[]{:S(2)}) collective-permute-start(f32[2,128,128]{2,1,0:T(8,128)S(1)} %get-tuple-element.1046), channel_id=1, source_target_pairs={{1,0},{2,1},{3,2},{4,3},{5,4},{6,5},{7,6},{8,7},{9,8},{10,9},{11,1... | collective-permute-start | bytes 393224 | tf_op jit(solution)/shard_map/while/body/eval_jaxpr/ppermute | solution.py:28
  223.1 9.6 %collective-permute-start.1 = (f32[2,128,128]{2,1,0:T(8,128)S(1)}, f32[2,128,128]{2,1,0:T(8,128)S(1)}, u32[]{:S(2)}, u32[]{:S(2)}) collective-permute-start(f32[2,128,128]{2,1,0:T(8,128)S(1)} %get-tuple-element.1046), channel_id=1, source_target_pairs={{1,0},{2,1},{3,2},{4,3},{5,4},{6,5},{7,6},{8,7},{9,8},{10,9},{11,1... | collective-permute-start | bytes 393224 | tf_op jit(solution)/shard_map/while/body/eval_jaxpr/ppermute | solution.py:28
  233.0 10.0 %collective-permute-start.1 = (f32[2,128,128]{2,1,0:T(8,128)S(1)}, f32[2,128,128]{2,1,0:T(8,128)S(1)}, u32[]{:S(2)}, u32[]{:S(2)}) collective-permute-start(f32[2,128,128]{2,1,0:T(8,128)S(1)} %get-tuple-element.1046), channel_id=1, source_target_pairs={{1,0},{2,1},{3,2},{4,3},{5,4},{6,5},{7,6},{8,7},{9,8},{10,9},{11,1... | collective-permute-start | bytes 393224 | tf_op jit(solution)/shard_map/while/body/eval_jaxpr/ppermute | solution.py:28
  243.3 9.2 %collective-permute-start.1 = (f32[2,128,128]{2,1,0:T(8,128)S(1)}, f32[2,128,128]{2,1,0:T(8,128)S(1)}, u32[]{:S(2)}, u32[]{:S(2)}) collective-permute-start(f32[2,128,128]{2,1,0:T(8,128)S(1)} %get-tuple-element.1046), channel_id=1, source_target_pairs={{1,0},{2,1},{3,2},{4,3},{5,4},{6,5},{7,6},{8,7},{9,8},{10,9},{11,1... | collective-permute-start | bytes 393224 | tf_op jit(solution)/shard_map/while/body/eval_jaxpr/ppermute | solution.py:28
  252.8 10.2 %collective-permute-start.1 = (f32[2,128,128]{2,1,0:T(8,128)S(1)}, f32[2,128,128]{2,1,0:T(8,128)S(1)}, u32[]{:S(2)}, u32[]{:S(2)}) collective-permute-start(f32[2,128,128]{2,1,0:T(8,128)S(1)} %get-tuple-element.1046), channel_id=1, source_target_pairs={{1,0},{2,1},{3,2},{4,3},{5,4},{6,5},{7,6},{8,7},{9,8},{10,9},{11,1... | collective-permute-start | bytes 393224 | tf_op jit(solution)/shard_map/while/body/eval_jaxpr/ppermute | solution.py:28
  263.3 9.6 %collective-permute-start.1 = (f32[2,128,128]{2,1,0:T(8,128)S(1)}, f32[2,128,128]{2,1,0:T(8,128)S(1)}, u32[]{:S(2)}, u32[]{:S(2)}) collective-permute-start(f32[2,128,128]{2,1,0:T(8,128)S(1)} %get-tuple-element.1046), channel_id=1, source_target_pairs={{1,0},{2,1},{3,2},{4,3},{5,4},{6,5},{7,6},{8,7},{9,8},{10,9},{11,1... | collective-permute-start | bytes 393224 | tf_op jit(solution)/shard_map/while/body/eval_jaxpr/ppermute | solution.py:28
  273.2 10.0 %collective-permute-start.1 = (f32[2,128,128]{2,1,0:T(8,128)S(1)}, f32[2,128,128]{2,1,0:T(8,128)S(1)}, u32[]{:S(2)}, u32[]{:S(2)}) collective-permute-start(f32[2,128,128]{2,1,0:T(8,128)S(1)} %get-tuple-element.1046), channel_id=1, source_target_pairs={{1,0},{2,1},{3,2},{4,3},{5,4},{6,5},{7,6},{8,7},{9,8},{10,9},{11,1... | collective-permute-start | bytes 393224 | tf_op jit(solution)/shard_map/while/body/eval_jaxpr/ppermute | solution.py:28
  285.3 9.0 %collective-permute-start.1 = (f32[2,128,128]{2,1,0:T(8,128)S(1)}, f32[2,128,128]{2,1,0:T(8,128)S(1)}, u32[]{:S(2)}, u32[]{:S(2)}) collective-permute-start(f32[2,128,128]{2,1,0:T(8,128)S(1)} %get-tuple-element.1046), channel_id=1, source_target_pairs={{1,0},{2,1},{3,2},{4,3},{5,4},{6,5},{7,6},{8,7},{9,8},{10,9},{11,1... | collective-permute-start | bytes 393224 | tf_op jit(solution)/shard_map/while/body/eval_jaxpr/ppermute | solution.py:28
  296.4 9.0 %collective-permute-start.1 = (f32[2,128,128]{2,1,0:T(8,128)S(1)}, f32[2,128,128]{2,1,0:T(8,128)S(1)}, u32[]{:S(2)}, u32[]{:S(2)}) collective-permute-start(f32[2,128,128]{2,1,0:T(8,128)S(1)} %get-tuple-element.1046), channel_id=1, source_target_pairs={{1,0},{2,1},{3,2},{4,3},{5,4},{6,5},{7,6},{8,7},{9,8},{10,9},{11,1... | collective-permute-start | bytes 393224 | tf_op jit(solution)/shard_map/while/body/eval_jaxpr/ppermute | solution.py:28
  305.6 9.0 %collective-permute-start.1 = (f32[2,128,128]{2,1,0:T(8,128)S(1)}, f32[2,128,128]{2,1,0:T(8,128)S(1)}, u32[]{:S(2)}, u32[]{:S(2)}) collective-permute-start(f32[2,128,128]{2,1,0:T(8,128)S(1)} %get-tuple-element.1046), channel_id=1, source_target_pairs={{1,0},{2,1},{3,2},{4,3},{5,4},{6,5},{7,6},{8,7},{9,8},{10,9},{11,1... | collective-permute-start | bytes 393224 | tf_op jit(solution)/shard_map/while/body/eval_jaxpr/ppermute | solution.py:28
  314.9 9.0 %collective-permute-start.1 = (f32[2,128,128]{2,1,0:T(8,128)S(1)}, f32[2,128,128]{2,1,0:T(8,128)S(1)}, u32[]{:S(2)}, u32[]{:S(2)}) collective-permute-start(f32[2,128,128]{2,1,0:T(8,128)S(1)} %get-tuple-element.1046), channel_id=1, source_target_pairs={{1,0},{2,1},{3,2},{4,3},{5,4},{6,5},{7,6},{8,7},{9,8},{10,9},{11,1... | collective-permute-start | bytes 393224 | tf_op jit(solution)/shard_map/while/body/eval_jaxpr/ppermute | solution.py:28
  325.3 11.0 %copy-start = (f32[1,2,256,128]{3,2,1,0:T(8,128)S(1)}, f32[1,2,256,128]{3,2,1,0:T(8,128)}, u32[]{:S(2)}) copy-start(f32[1,2,256,128]{3,2,1,0:T(8,128)} %param.15) | copy-start | bytes 786436
  325.4 5.9 %collective-permute-start.4 = (f32[2,256,128]{2,1,0:T(8,128)S(1)}, f32[2,256,128]{2,1,0:T(8,128)S(1)}, u32[]{:S(2)}, u32[]{:S(2)}) collective-permute-start(f32[2,256,128]{2,1,0:T(8,128)S(1)} %get-tuple-element.839), channel_id=1, source_target_pairs={{16,0},{32,16},{48,32},{64,48},{80,64},{96,80},{112,96},{128,112},... | collective-permute-start | bytes 786440 | tf_op jit(solution)/shard_map/ppermute | solution.py:28
  327.4 8.9 %collective-permute-start.5 = (f32[2,256,128]{2,1,0:T(8,128)S(1)}, f32[2,256,128]{2,1,0:T(8,128)S(1)}, u32[]{:S(2)}, u32[]{:S(2)}) collective-permute-start(f32[2,256,128]{2,1,0:T(8,128)S(1)} %get-tuple-element.840), channel_id=1, source_target_pairs={{0,16},{16,32},{32,48},{48,64},{64,80},{80,96},{96,112},{112,128},... | collective-permute-start | bytes 786440 | tf_op jit(solution)/shard_map/ppermute | solution.py:28
where the time goes:
time: 338 us; the launch traced here: 337 us
  waiting for transfers between devices  169 us (50%)
  starting transfers between devices  139 us (41%)
  other arithmetic  10.1 us (3%)
  local copies, waits for them, and re-layouts  6.02 us (2%)
  matrix products  5.29 us (2%)
  between operations  3.97 us (1%)
  loops' own time  3.53 us (1%)
    ppermute x34, waiting for transfers between devices, shifted(): return lax.ppermute(shard, axis, pairs)  169 us
    ppermute x34, starting transfers between devices, shifted(): return lax.ppermute(shard, axis, pairs)  135 us
  transfers between devices with their start and end apart: 36, of which 35 were waited for; matrix products, arithmetic and copies ran while one was open for 1% of the time, Pallas kernels for 0%

commit v1 on v0

v1 whole, which is shorter than its diff:
```python
import functools

import jax
import jax.numpy as jnp
import ml_dtypes
import numpy as np
from jax import lax
from jax.experimental import pallas as pl
from jax.experimental.pallas import tpu as pltpu
from jax.sharding import PartitionSpec as P

step_size = 0.25
side = 128
tile = 256
slab_rows = 2 * tile + side
group = 8
swap = 5
params = pltpu.CompilerParams(vmem_limit_bytes=48 * 2**20)
in_vmem = pl.BlockSpec(memory_space=pltpu.VMEM)
in_smem = pl.BlockSpec(memory_space=pltpu.SMEM)
window_type = jax.ShapeDtypeStruct((2, side, side), jnp.float32)
stack_type = jax.ShapeDtypeStruct((group, 2, side, side), jnp.float32)


def two_parts(table):
    table = table.astype(np.float32)
    high = table.astype(ml_dtypes.bfloat16)
    low = (table - high.astype(np.float32)).astype(ml_dtypes.bfloat16)
    return high, low


def both_sides(matrix):
    left = np.block([[matrix.real, -matrix.imag], [matrix.imag, matrix.real]])
    right = np.block([[matrix.real, matrix.imag], [-matrix.imag, matrix.real]])
    return two_parts(left) + two_parts(right)


def tables():
    index = np.arange(side)
    angles = 2.0 * np.pi * (index[:, None] * index[None, :] % side) / side
    fourier = (np.cos(angles) - 1j * np.sin(angles)) / np.sqrt(side)
    frequency = np.where(index < side // 2, index, index - side).astype(np.float64)
    phase = np.exp(-1j * np.pi / side * frequency * frequency)
    step = np.conj(fourier) @ (phase[:, None] * fourier)
    return both_sides(step), both_sides(fourier)


def split(x):
    high = x.astype(jnp.bfloat16)
    return high, (x - high.astype(jnp.float32)).astype(jnp.bfloat16)


def dot(a, b):
    return jnp.dot(a, b, preferred_element_type=jnp.float32)


def two_sided(real, imag, table):
    left_high, left_low, right_high, right_low = table
    high, low = split(jnp.concatenate([real, imag], 0))
    both = dot(left_high[...], jnp.concatenate([high, low], 1))
    left = both[:, :side] + both[:, side:] + dot(left_low[...], high)
    high, low = split(jnp.concatenate([left[:side], left[side:]], 1))
    done = dot(high, right_high[...]) + (dot(low, right_high[...]) + dot(high, right_low[...]))
    return done[:, :side], done[:, side:]


def times(a, b):
    return a[0] * b[0] - a[1] * b[1], a[0] * b[1] + a[1] * b[0]


def pair(ref, *at):
    return ref[(*at, 0)], ref[(*at, 1)]


def put(ref, value, *at):
    ref[(*at, 0)] = value[0]
    ref[(*at, 1)] = value[1]


def cut_kernel(starts, low, block, high, odd_out, even_out, slab):
    slab[:, :tile] = low[...]
    slab[:, tile : 2 * tile] = block[...]
    slab[:, 2 * tile :] = high[...]
    for at, out in ((0, odd_out), (1, even_out)):
        out[...] = slab[:, pl.ds(starts[at], side), :]


def upper_kernel(*refs):
    probe, arrived, table = refs[0], refs[1 : 1 + group], refs[1 + group : 5 + group]
    wave_out, waves, windows = refs[5 + group :]
    me = lax.axis_index("depth") & (group - 1)
    for turn in range(group):
        windows[turn ^ me] = arrived[turn][...]
    wave = pair(probe)
    for layer in range(group):
        put(waves, wave, layer)
        wave = two_sided(*times(wave, pair(windows, layer)), table)
    put(wave_out, wave)


def middle_kernel(*refs):
    entering, windows, late, measured = refs[:4]
    table, fourier = refs[4:8], refs[8:12]
    adjoint_out, parts = refs[12], refs[13 : 13 + group]
    held, waves, updates = refs[13 + group :]
    depth = lax.axis_index("depth")
    me = depth & (group - 1)
    first = 2 * (1 - (lax.axis_index("scan") & 1))
    which = jnp.where((me ^ first) == 0, 0, 1)
    held[...] = windows[...]
    held[me] = late[...]
    wave = pair(entering)
    for layer in range(group):
        put(waves, wave, layer)
        last = layer == group - 1
        wave = two_sided(*times(wave, pair(held, layer)), fourier if last else table)
    far_real, far_imag = wave
    residual = far_real * far_real + far_imag * far_imag - measured[which]
    adjoint = two_sided(residual * far_real, -(residual * far_imag), fourier)
    for layer in reversed(range(group)):
        real, imag = times(pair(waves, layer), adjoint)
        put(updates, (real, -imag), layer)
        adjoint = two_sided(*times(pair(held, layer), adjoint), table)
    put(adjoint_out, adjoint)
    for turn in range(group):
        parts[turn][...] = updates[turn ^ me]


def lower_kernel(*refs):
    returned, waves, windows = refs[:3]
    theirs, table = refs[3 : 3 + group], refs[3 + group : 7 + group]
    parts, updates = refs[7 + group : 7 + 2 * group], refs[-1]
    depth = lax.axis_index("depth")
    me = depth & (group - 1)
    mine = (me ^ (2 * (lax.axis_index("scan") & 1)))
    is_upper = (mine == 0) | (mine == swap)
    adjoint = pair(returned)
    for layer in reversed(range(group)):
        real, imag = times(pair(waves, layer), adjoint)
        put(updates, (real, -imag), layer)
        if layer:
            adjoint = two_sided(*times(pair(windows, layer), adjoint), table)

    @pl.when(is_upper)
    def _():
        for turn in range(group):
            parts[turn][...] = updates[turn ^ me]

    @pl.when(jnp.logical_not(is_upper))
    def _():
        for turn in range(group):
            parts[turn][...] = theirs[turn][...]


def place_kernel(*refs):
    starts, own, arrived = refs[0], refs[1], refs[2 : 2 + group]
    up, middle, down, slab = refs[2 + group :]
    depth = lax.axis_index("depth")
    mine = depth ^ (2 * (lax.axis_index("scan") & 1))
    is_upper = (mine == 0) | (mine == swap)
    slab[...] = jnp.zeros_like(slab)
    odd = (arrived[1][...] + arrived[3][...]) + (arrived[5][...] + arrived[7][...])
    even = (arrived[2][...] + arrived[4][...]) + arrived[6][...]
    even = even + jnp.where(is_upper, own[...], arrived[0][...])
    for at, update in ((0, odd), (1, even)):
        rows = pl.ds(starts[at], side)
        slab[:, rows, :] = slab[:, rows, :] + update
    up[...] = slab[:, :tile]
    middle[...] = slab[:, tile : 2 * tile]
    down[...] = slab[:, 2 * tile :]


def last_kernel(block, middle, below, above, out):
    head = middle[:, :side] + below[:, :side] + above[...]
    tail = middle[:, side:] + below[:, side:]
    out[0, :, :side] = block[:, :side] - step_size * head
    out[0, :, side:] = block[:, side:] - step_size * tail


def shards(object_slices, probe_wave, intensities, offsets, owners):
    scans = lax.axis_size("scan")
    depths = lax.axis_size("depth")
    scan_index = lax.axis_index("scan")
    depth_index = lax.axis_index("depth")
    axes = ("scan", "depth")
    step_tables, fourier_tables = tables()
    vmem = functools.partial(pl.pallas_call, compiler_params=params)

    def at(scan, depth):
        return scan * depths + depth

    targets = [(i, (2 * (i & 1)) ^ (swap * q)) for i in range(scans) for q in range(2)]
    gathers = []
    for turn in range(group):
        pairs = []
        for i, target in targets:
            if turn:
                pairs.append((at(i, target ^ turn), at(i, target)))
            pairs.append((at(i, group + (target ^ turn)), at(i ^ 1, target)))
        gathers.append(pairs)
    scatters = [[(b, a) for a, b in pairs] for pairs in gathers]
    across = [(at(i, target), at(i ^ 1, target)) for i, target in targets]
    back = [(b, a) for a, b in across]
    onward = [(i, i + 1) for i in range(scans - 1)]
    rearward = [(i + 1, i) for i in range(scans - 1)]

    block = object_slices[0]
    low = lax.ppermute(block, "scan", onward)
    high = lax.ppermute(block[:, :side], "scan", rearward)
    measured = lax.ppermute(intensities, axes, across)

    starts = jnp.clip((owners - scan_index + 1) * tile + offsets, 0, 2 * tile)
    is_odd = ((depth_index ^ (2 * (scan_index & 1))) & 1) == 1
    starts = jnp.where(is_odd, starts, starts[::-1])
    odd_window, even_window = vmem(
        cut_kernel,
        out_shape=[window_type] * 2,
        in_specs=[in_smem] + [in_vmem] * 3,
        out_specs=[in_vmem] * 2,
        scratch_shapes=[pltpu.VMEM((2, slab_rows, side), jnp.float32)],
        name="cut",
    )(starts, low, block, high)

    arrived = [even_window]
    for turn in range(1, group):
        arrived.append(
            lax.ppermute(odd_window if turn & 1 else even_window, axes, gathers[turn])
        )
    wave, waves, windows = vmem(
        upper_kernel,
        out_shape=[window_type, stack_type, stack_type],
        in_specs=[in_vmem] * (5 + group),
        out_specs=[in_vmem] * 3,
        name="upper",
    )(probe_wave, *arrived, *step_tables)
    entering = lax.ppermute(wave, axes, across)
    late = lax.ppermute(even_window, axes, gathers[0])

    adjoint, *lower_parts = vmem(
        middle_kernel,
        out_shape=[window_type] * (1 + group),
        in_specs=[in_vmem] * 12,
        out_specs=[in_vmem] * (1 + group),
        scratch_shapes=[pltpu.VMEM(stack_type.shape, jnp.float32)] * 3,
        name="middle",
    )(entering, windows, late, measured, *step_tables, *fourier_tables)
    returned = lax.ppermute(adjoint, axes, back)
    first_back = lax.ppermute(lower_parts[0], axes, scatters[0])

    parts = vmem(
        lower_kernel,
        out_shape=[window_type] * group,
        in_specs=[in_vmem] * (7 + group),
        out_specs=[in_vmem] * group,
        scratch_shapes=[pltpu.VMEM(stack_type.shape, jnp.float32)],
        name="lower",
    )(returned, waves, windows, *lower_parts, *step_tables)
    landed = [first_back] + [
        lax.ppermute(parts[turn], axes, scatters[turn]) for turn in range(1, group)
    ]

    up, middle, down = vmem(
        place_kernel,
        out_shape=[
            jax.ShapeDtypeStruct((2, tile, side), jnp.float32),
            jax.ShapeDtypeStruct((2, tile, side), jnp.float32),
            jax.ShapeDtypeStruct((2, side, side), jnp.float32),
        ],
        in_specs=[in_smem] + [in_vmem] * (1 + group),
        out_specs=[in_vmem] * 3,
        scratch_shapes=[pltpu.VMEM((2, slab_rows, side), jnp.float32)],
        name="place",
    )(starts, parts[0], *landed)
    below = lax.ppermute(up, "scan", rearward)
    above = lax.ppermute(down, "scan", onward)
    return vmem(
        last_kernel,
        out_shape=jax.ShapeDtypeStruct(object_slices.shape, jnp.float32),
        in_specs=[in_vmem] * 4,
        out_specs=in_vmem,
        name="last",
    )(block, middle, below, above)


def solution(mesh):
    return jax.shard_map(
        shards,
        mesh=mesh,
        in_specs=(P("depth", None, "scan", None), P(), P("scan", None, None), P("scan"), P("scan")),
        out_specs=P("depth", None, "scan", None),
        check_vma=False,
    )
```

time: 338 us -> 87.9 us (0.26)
  the two profiles are of different devices: /device:TPU:134 before, /device:TPU:384 now
where the time goes in v1:
time: 87.9 us; the launch traced here: 87.3 us
  starting transfers between devices  54.9 us (62%)
  Pallas kernels  15.7 us (18%)
  waiting for transfers between devices  14.5 us (16%)
  local copies, waits for them, and re-layouts  1.73 us (2%)
    ppermute x7, starting transfers between devices, shards(): lax.ppermute(odd_window if turn & 1 else even_window, axes, gathers[turn])  12.3 us
    ppermute x7, starting transfers between devices, shards(): lax.ppermute(parts[turn], axes, scatters[turn])  12 us
    ppermute x1, starting transfers between devices, shards(): below = lax.ppermute(up, 'scan', rearward)  7.75 us
    pallas_call x1, Pallas kernels, shards(): vmem(middle_kernel, out_shape=[window_type] * (1 + group), in_specs=[in_v...  7.17 us
    ppermute x1, starting transfers between devices, shards(): entering = lax.ppermute(wave, axes, across)  5.94 us
    ppermute x1, waiting for transfers between devices, shards(): above = lax.ppermute(down, 'scan', onward)  5.57 us
    ppermute x1, starting transfers between devices, shards(): measured = lax.ppermute(intensities, axes, across)  5.46 us
    ppermute x1, starting transfers between devices, shards(): high = lax.ppermute(block[:, :side], 'scan', rearward)  4.86 us
  transfers between devices with their start and end apart: 23, of which 8 were waited for; matrix products, arithmetic and copies ran while one was open for 1% of the time, Pallas kernels for 7%

profile of v1, /device:TPU:384, one launch (start us, length us, event | category | flops | bytes accessed | tf_op | source)
XLA Modules:
  0.0 87.3 jit_solution(5326319287824963105)
XLA Ops:
  0.0 2.0 %collective-permute-start = (f32[2,256,128]{2,1,0:T(8,128)}, f32[2,256,128]{2,1,0:T(8,128)S(1)}, u32[]{:S(2)}, u32[]{:S(2)}) collective-permute-start(f32[2,256,128]{2,1,0:T(8,128)} %bitcast.1), channel_id=1, source_target_pairs={{0,16},{16,32},{32,48},{48,64},{64,80},{80,96},{96,112},{112,128},... | collective-permute-start | bytes 786440 | tf_op jit(solution)/shard_map/ppermute | solution.py:208
  2.0 0.9 %slice.4 = f32[2,128,128]{2,1,0:T(8,128)S(1)} slice(f32[2,256,128]{2,1,0:T(8,128)} %bitcast.2), slice={[0:2], [0:128], [0:128]} | slice | bytes 262144 | tf_op jit(solution)/shard_map/slice | solution.py:209
  3.0 4.9 %collective-permute-start.1 = (f32[2,128,128]{2,1,0:T(8,128)S(1)}, f32[2,128,128]{2,1,0:T(8,128)S(1)}, u32[]{:S(2)}, u32[]{:S(2)}) collective-permute-start(f32[2,128,128]{2,1,0:T(8,128)S(1)} %slice.4), channel_id=1, source_target_pairs={{16,0},{32,16},{48,32},{64,48},{80,64},{96,80},{112,96},{128,112},... | collective-permute-start | bytes 393224 | tf_op jit(solution)/shard_map/ppermute | solution.py:209
  7.8 0.0 copy-start.10
  7.9 0.0 copy-start.11
  7.9 0.6 copy-done.10
  8.5 0.0 copy-done.11
  8.5 0.1 rev.3
  8.6 0.0 copy-start.4
  8.7 0.0 copy-start.9
  8.7 1.7 %collective-permute-done.1.high = f32[2,128,128]{2,1,0:T(8,128)S(1)} collective-permute-done((f32[2,128,128]{2,1,0:T(8,128)S(1)}, f32[2,128,128]{2,1,0:T(8,128)S(1)}, u32[]{:S(2)}, u32[]{:S(2)}) %collective-permute-start.1) | collective-permute-done | bytes 131104 | tf_op jit(solution)/shard_map/ppermute | solution.py:209
  10.3 0.0 collective-permute-done.low
  10.3 0.6 cut.1
  11.0 1.3 %collective-permute-start.8 = (f32[2,128,128]{2,1,0:T(8,128)S(1)}, f32[2,128,128]{2,1,0:T(8,128)S(1)}, u32[]{:S(2)}, u32[]{:S(2)}) collective-permute-start(f32[2,128,128]{2,1,0:T(8,128)S(1)} %get-tuple-element.31), channel_id=1, source_target_pairs={{7,0},{15,16},{2,5},{10,21},{21,18},{29,2},{16,23},{24,7},{39,32},... | collective-permute-start | bytes 393224 | tf_op jit(solution)/shard_map/ppermute | solution.py:227
  12.3 4.4 %collective-permute-start.6 = (f32[2,128,128]{2,1,0:T(8,128)S(1)}, f32[2,128,128]{2,1,0:T(8,128)S(1)}, u32[]{:S(2)}, u32[]{:S(2)}) collective-permute-start(f32[2,128,128]{2,1,0:T(8,128)S(1)} %get-tuple-element.31), channel_id=1, source_target_pairs={{5,0},{13,16},{0,5},{8,21},{23,18},{31,2},{18,23},{26,7},{37,32},{... | collective-permute-start | bytes 393224 | tf_op jit(solution)/shard_map/ppermute | solution.py:227
  16.7 1.3 %collective-permute-start.4 = (f32[2,128,128]{2,1,0:T(8,128)S(1)}, f32[2,128,128]{2,1,0:T(8,128)S(1)}, u32[]{:S(2)}, u32[]{:S(2)}) collective-permute-start(f32[2,128,128]{2,1,0:T(8,128)S(1)} %get-tuple-element.31), channel_id=1, source_target_pairs={{3,0},{11,16},{6,5},{14,21},{17,18},{25,2},{20,23},{28,7},{35,32},... | collective-permute-start | bytes 393224 | tf_op jit(solution)/shard_map/ppermute | solution.py:227
  18.0 1.3 %collective-permute-start.2 = (f32[2,128,128]{2,1,0:T(8,128)S(1)}, f32[2,128,128]{2,1,0:T(8,128)S(1)}, u32[]{:S(2)}, u32[]{:S(2)}) collective-permute-start(f32[2,128,128]{2,1,0:T(8,128)S(1)} %get-tuple-element.31), channel_id=1, source_target_pairs={{1,0},{9,16},{4,5},{12,21},{19,18},{27,2},{22,23},{30,7},{33,32},{... | collective-permute-start | bytes 393224 | tf_op jit(solution)/shard_map/ppermute | solution.py:227
  19.3 0.0 copy-start.5
  19.3 0.0 copy-start.6
  19.3 0.0 copy-start.7
  19.3 0.0 copy-start.8
  19.3 1.4 %collective-permute-start.7 = (f32[2,128,128]{2,1,0:T(8,128)S(1)}, f32[2,128,128]{2,1,0:T(8,128)S(1)}, u32[]{:S(2)}, u32[]{:S(2)}) collective-permute-start(f32[2,128,128]{2,1,0:T(8,128)S(1)} %get-tuple-element.30.refs_1_), channel_id=1, source_target_pairs={{6,0},{14,16},{3,5},{11,21},{20,18},{28,2},{17,23},{25,7},{38,32},... | collective-permute-start | bytes 393224 | tf_op jit(solution)/shard_map/ppermute | solution.py:227
  20.8 0.3 collective-permute-done.8.refs_8_
  21.1 1.3 %collective-permute-start.5 = (f32[2,128,128]{2,1,0:T(8,128)S(1)}, f32[2,128,128]{2,1,0:T(8,128)S(1)}, u32[]{:S(2)}, u32[]{:S(2)}) collective-permute-start(f32[2,128,128]{2,1,0:T(8,128)S(1)} %get-tuple-element.30.refs_1_), channel_id=1, source_target_pairs={{4,0},{12,16},{1,5},{9,21},{22,18},{30,2},{19,23},{27,7},{36,32},{... | collective-permute-start | bytes 393224 | tf_op jit(solution)/shard_map/ppermute | solution.py:227
  22.4 0.0 collective-permute-done.6.refs_6_
  22.4 1.3 %collective-permute-start.3 = (f32[2,128,128]{2,1,0:T(8,128)S(1)}, f32[2,128,128]{2,1,0:T(8,128)S(1)}, u32[]{:S(2)}, u32[]{:S(2)}) collective-permute-start(f32[2,128,128]{2,1,0:T(8,128)S(1)} %get-tuple-element.30.refs_1_), channel_id=1, source_target_pairs={{2,0},{10,16},{7,5},{15,21},{16,18},{24,2},{21,23},{29,7},{34,32},... | collective-permute-start | bytes 393224 | tf_op jit(solution)/shard_map/ppermute | solution.py:227
  23.7 1.1 %collective-permute-done.4.refs_4_ = f32[2,128,128]{2,1,0:T(8,128)S(1)} collective-permute-done((f32[2,128,128]{2,1,0:T(8,128)S(1)}, f32[2,128,128]{2,1,0:T(8,128)S(1)}, u32[]{:S(2)}, u32[]{:S(2)}) %collective-permute-start.4) | collective-permute-done | bytes 131104 | tf_op jit(solution)/shard_map/ppermute | solution.py:227
  24.7 5.5 %collective-permute-start.11 = (f32[2,128,128]{2,1,0:T(8,128)}, f32[2,128,128]{2,1,0:T(8,128)S(1)}, u32[]{:S(2)}, u32[]{:S(2)}) collective-permute-start(f32[2,128,128]{2,1,0:T(8,128)} %param.15), channel_id=1, source_target_pairs={{0,16},{5,21},{18,2},{23,7},{32,48},{37,53},{50,34},{55,39},{64,80... | collective-permute-start | bytes 393224 | tf_op jit(solution)/shard_map/ppermute | solution.py:210
  30.2 0.0 collective-permute-done.2.refs_2_
  30.2 0.7 collective-permute-start.10
  30.9 0.0 collective-permute-done.7.refs_7_
  30.9 0.0 collective-permute-done.5.refs_5_
  30.9 0.0 collective-permute-done.3.refs_3_
  31.0 3.4 %upper.1 = (f32[2,128,128]{2,1,0:T(8,128)S(1)}, f32[8,2,128,128]{3,2,1,0:T(8,128)S(1)}, f32[8,2,128,128]{3,2,1,0:T(8,128)S(1)}) custom-call(f32[2,128,128]{2,1,0:T(8,128)S(1)} %copy-done.9, f32[2,128,128]{2,1,0:T(8,128)S(1)} %get-tuple-element.30.refs_1_, f32[2,128,128]{2,1,0:T(8,128)S(1)} %collective-permute-done.2.refs_2_, ...), custom_call_target="tpu_custom_call" | custom-call | tf_op jit(solution)/shard_map/upper/pallas_call | solution.py:229
  34.4 5.9 %collective-permute-start.9 = (f32[2,128,128]{2,1,0:T(8,128)S(1)}, f32[2,128,128]{2,1,0:T(8,128)S(1)}, u32[]{:S(2)}, u32[]{:S(2)}) collective-permute-start(f32[2,128,128]{2,1,0:T(8,128)S(1)} %get-tuple-element.32), channel_id=1, source_target_pairs={{0,16},{5,21},{18,2},{23,7},{32,48},{37,53},{50,34},{55,39},{64,80... | collective-permute-start | bytes 393224 | tf_op jit(solution)/shard_map/ppermute | solution.py:236
  40.4 0.0 collective-permute-done.11.refs_3_
  40.4 0.0 collective-permute-done.10.refs_2_
  40.4 0.9 %collective-permute-done.9.refs_0_ = f32[2,128,128]{2,1,0:T(8,128)S(1)} collective-permute-done((f32[2,128,128]{2,1,0:T(8,128)S(1)}, f32[2,128,128]{2,1,0:T(8,128)S(1)}, u32[]{:S(2)}, u32[]{:S(2)}) %collective-permute-start.9) | collective-permute-done | bytes 131104 | tf_op jit(solution)/shard_map/ppermute | solution.py:236
  41.3 7.2 %middle.1 = (f32[2,128,128]{2,1,0:T(8,128)S(1)}, f32[2,128,128]{2,1,0:T(8,128)S(1)}, f32[2,128,128]{2,1,0:T(8,128)S(1)}, f32[2,128,128]{2,1,0:T(8,128)S(1)}, f32...) custom-call(f32[2,128,128]{2,1,0:T(8,128)S(1)} %collective-permute-d, ...), custom_call_target="tpu_custom_call" | custom-call | tf_op jit(solution)/shard_map/middle/pallas_call | solution.py:239
  48.5 1.3 %collective-permute-start.12 = (f32[2,128,128]{2,1,0:T(8,128)S(1)}, f32[2,128,128]{2,1,0:T(8,128)S(1)}, u32[]{:S(2)}, u32[]{:S(2)}) collective-permute-start(f32[2,128,128]{2,1,0:T(8,128)S(1)} %get-tuple-element.34), channel_id=1, source_target_pairs={{16,0},{21,5},{2,18},{7,23},{48,32},{53,37},{34,50},{39,55},{80,64... | collective-permute-start | bytes 393224 | tf_op jit(solution)/shard_map/ppermute | solution.py:247
  49.8 0.7 collective-permute-start.13
  50.5 1.3 %collective-permute-done.12.refs_0_ = f32[2,128,128]{2,1,0:T(8,128)S(1)} collective-permute-done((f32[2,128,128]{2,1,0:T(8,128)S(1)}, f32[2,128,128]{2,1,0:T(8,128)S(1)}, u32[]{:S(2)}, u32[]{:S(2)}) %collective-permute-start.12) | collective-permute-done | bytes 131104 | tf_op jit(solution)/shard_map/ppermute | solution.py:247
  51.8 3.0 %lower.1 = (f32[2,128,128]{2,1,0:T(8,128)S(1)}, f32[2,128,128]{2,1,0:T(8,128)S(1)}, f32[2,128,128]{2,1,0:T(8,128)S(1)}, f32[2,128,128]{2,1,0:T(8,128)S(1)}, f32[...) custom-call(f32[2,128,128]{2,1,0:T(8,128)S(1)} %collective-permute-d, ...), custom_call_target="tpu_custom_call" | custom-call | tf_op jit(solution)/shard_map/lower/pallas_call | solution.py:250
  54.8 1.3 %collective-permute-start.14 = (f32[2,128,128]{2,1,0:T(8,128)S(1)}, f32[2,128,128]{2,1,0:T(8,128)S(1)}, u32[]{:S(2)}, u32[]{:S(2)}) collective-permute-start(f32[2,128,128]{2,1,0:T(8,128)S(1)} %get-tuple-element.45), channel_id=1, source_target_pairs={{0,1},{16,9},{5,4},{21,12},{18,19},{2,27},{23,22},{7,30},{32,33},{... | collective-permute-start | bytes 393224 | tf_op jit(solution)/shard_map/ppermute | solution.py:259
  56.1 3.5 %collective-permute-start.15 = (f32[2,128,128]{2,1,0:T(8,128)S(1)}, f32[2,128,128]{2,1,0:T(8,128)S(1)}, u32[]{:S(2)}, u32[]{:S(2)}) collective-permute-start(f32[2,128,128]{2,1,0:T(8,128)S(1)} %get-tuple-element.46), channel_id=1, source_target_pairs={{0,2},{16,10},{5,7},{21,15},{18,16},{2,24},{23,21},{7,29},{32,34},... | collective-permute-start | bytes 393224 | tf_op jit(solution)/shard_map/ppermute | solution.py:259
  59.6 1.3 %collective-permute-start.16 = (f32[2,128,128]{2,1,0:T(8,128)S(1)}, f32[2,128,128]{2,1,0:T(8,128)S(1)}, u32[]{:S(2)}, u32[]{:S(2)}) collective-permute-start(f32[2,128,128]{2,1,0:T(8,128)S(1)} %get-tuple-element.47), channel_id=1, source_target_pairs={{0,3},{16,11},{5,6},{21,14},{18,17},{2,25},{23,20},{7,28},{32,35},... | collective-permute-start | bytes 393224 | tf_op jit(solution)/shard_map/ppermute | solution.py:259
  60.9 1.3 %collective-permute-start.17 = (f32[2,128,128]{2,1,0:T(8,128)S(1)}, f32[2,128,128]{2,1,0:T(8,128)S(1)}, u32[]{:S(2)}, u32[]{:S(2)}) collective-permute-start(f32[2,128,128]{2,1,0:T(8,128)S(1)} %get-tuple-element.48), channel_id=1, source_target_pairs={{0,4},{16,12},{5,1},{21,9},{18,22},{2,30},{23,19},{7,27},{32,36},{... | collective-permute-start | bytes 393224 | tf_op jit(solution)/shard_map/ppermute | solution.py:259
  62.2 0.0 collective-permute-done.13.refs_2_
  62.2 1.9 %collective-permute-start.18 = (f32[2,128,128]{2,1,0:T(8,128)S(1)}, f32[2,128,128]{2,1,0:T(8,128)S(1)}, u32[]{:S(2)}, u32[]{:S(2)}) collective-permute-start(f32[2,128,128]{2,1,0:T(8,128)S(1)} %get-tuple-element.49), channel_id=1, source_target_pairs={{0,5},{16,13},{5,0},{21,8},{18,23},{2,31},{23,18},{7,26},{32,37},{... | collective-permute-start | bytes 393224 | tf_op jit(solution)/shard_map/ppermute | solution.py:259
  64.2 0.0 collective-permute-done.14.refs_3_
  64.2 1.3 %collective-permute-start.19 = (f32[2,128,128]{2,1,0:T(8,128)S(1)}, f32[2,128,128]{2,1,0:T(8,128)S(1)}, u32[]{:S(2)}, u32[]{:S(2)}) collective-permute-start(f32[2,128,128]{2,1,0:T(8,128)S(1)} %get-tuple-element.50), channel_id=1, source_target_pairs={{0,6},{16,14},{5,3},{21,11},{18,20},{2,28},{23,17},{7,25},{32,38},... | collective-permute-start | bytes 393224 | tf_op jit(solution)/shard_map/ppermute | solution.py:259
  65.5 0.0 collective-permute-done.15.refs_4_
  65.5 1.4 %collective-permute-start.20 = (f32[2,128,128]{2,1,0:T(8,128)S(1)}, f32[2,128,128]{2,1,0:T(8,128)S(1)}, u32[]{:S(2)}, u32[]{:S(2)}) collective-permute-start(f32[2,128,128]{2,1,0:T(8,128)S(1)} %get-tuple-element.51), channel_id=1, source_target_pairs={{0,7},{16,15},{5,2},{21,10},{18,21},{2,29},{23,16},{7,24},{32,39},... | collective-permute-start | bytes 393224 | tf_op jit(solution)/shard_map/ppermute | solution.py:259
  66.9 0.0 collective-permute-done.16.refs_5_
  66.9 0.0 collective-permute-done.17.refs_6_
  66.9 3.1 %collective-permute-done.18.refs_7_ = f32[2,128,128]{2,1,0:T(8,128)S(1)} collective-permute-done((f32[2,128,128]{2,1,0:T(8,128)S(1)}, f32[2,128,128]{2,1,0:T(8,128)S(1)}, u32[]{:S(2)}, u32[]{:S(2)}) %collective-permute-start.18) | collective-permute-done | bytes 131104 | tf_op jit(solution)/shard_map/ppermute | solution.py:259
  70.0 0.0 collective-permute-done.19.refs_8_
  70.0 0.5 collective-permute-done.20.refs_9_
  70.5 0.7 place.1
  71.2 7.8 %collective-permute-start.21 = (f32[2,256,128]{2,1,0:T(8,128)S(1)}, f32[2,256,128]{2,1,0:T(8,128)S(1)}, u32[]{:S(2)}, u32[]{:S(2)}) collective-permute-start(f32[2,256,128]{2,1,0:T(8,128)S(1)} %get-tuple-element.53), channel_id=1, source_target_pairs={{16,0},{32,16},{48,32},{64,48},{80,64},{96,80},{112,96},{128,112},... | collective-permute-start | bytes 786440 | tf_op jit(solution)/shard_map/ppermute | solution.py:274
  79.0 1.9 %collective-permute-start.22 = (f32[2,128,128]{2,1,0:T(8,128)S(1)}, f32[2,128,128]{2,1,0:T(8,128)S(1)}, u32[]{:S(2)}, u32[]{:S(2)}) collective-permute-start(f32[2,128,128]{2,1,0:T(8,128)S(1)} %get-tuple-element.54), channel_id=1, source_target_pairs={{0,16},{16,32},{32,48},{48,64},{64,80},{80,96},{96,112},{112,128},... | collective-permute-start | bytes 393224 | tf_op jit(solution)/shard_map/ppermute | solution.py:275
  80.9 5.6 %collective-permute-done.22.above = f32[2,128,128]{2,1,0:T(8,128)S(1)} collective-permute-done((f32[2,128,128]{2,1,0:T(8,128)S(1)}, f32[2,128,128]{2,1,0:T(8,128)S(1)}, u32[]{:S(2)}, u32[]{:S(2)}) %collective-permute-start.22) | collective-permute-done | bytes 131104 | tf_op jit(solution)/shard_map/ppermute | solution.py:275
  86.5 0.0 collective-permute-done.21.below
  86.5 0.8 last.1
  (16 shorter events, 0.0 us)
Async XLA Ops:
  0.0 10.3 %copy-start = (f32[1,2,256,128]{3,2,1,0:T(8,128)S(1)}, f32[1,2,256,128]{3,2,1,0:T(8,128)}, u32[]{:S(2)}) copy-start(f32[1,2,256,128]{3,2,1,0:T(8,128)} %param.13) | copy-start | bytes 786436
  0.0 10.3 %collective-permute-start = (f32[2,256,128]{2,1,0:T(8,128)}, f32[2,256,128]{2,1,0:T(8,128)S(1)}, u32[]{:S(2)}, u32[]{:S(2)}) collective-permute-start(f32[2,256,128]{2,1,0:T(8,128)} %bitcast.1), channel_id=1, source_target_pairs={{0,16},{16,32},{32,48},{48,64},{64,80},{80,96},{96,112},{112,128},... | collective-permute-start | bytes 786440 | tf_op jit(solution)/shard_map/ppermute | solution.py:208
  3.0 7.4 %collective-permute-start.1 = (f32[2,128,128]{2,1,0:T(8,128)S(1)}, f32[2,128,128]{2,1,0:T(8,128)S(1)}, u32[]{:S(2)}, u32[]{:S(2)}) collective-permute-start(f32[2,128,128]{2,1,0:T(8,128)S(1)} %slice.4), channel_id=1, source_target_pairs={{16,0},{32,16},{48,32},{64,48},{80,64},{96,80},{112,96},{128,112},... | collective-permute-start | bytes 393224 | tf_op jit(solution)/shard_map/ppermute | solution.py:209
  7.8 0.7 copy-start.10
  7.9 0.7 copy-start.11
  8.6 22.3 %copy-start.1 = (bf16[256,256]{1,0:T(8,128)(2,1)S(1)}, bf16[256,256]{1,0:T(8,128)(2,1)}, u32[]{:S(2)}) copy-start(bf16[256,256]{1,0:T(8,128)(2,1)} %constant.39.clone.refs_12_.refs_7_.refs_14_) | copy-start | bytes 393220
  8.6 22.3 %copy-start.2 = (bf16[256,256]{1,0:T(8,128)(2,1)S(1)}, bf16[256,256]{1,0:T(8,128)(2,1)}, u32[]{:S(2)}) copy-start(bf16[256,256]{1,0:T(8,128)(2,1)} %constant.38.clone.refs_11_.refs_6_.refs_13_) | copy-start | bytes 393220
  8.6 22.3 %copy-start.3 = (bf16[256,256]{1,0:T(8,128)(2,1)S(1)}, bf16[256,256]{1,0:T(8,128)(2,1)}, u32[]{:S(2)}) copy-start(bf16[256,256]{1,0:T(8,128)(2,1)} %constant.37.clone.refs_10_.refs_5_.refs_12_) | copy-start | bytes 393220
  8.6 22.3 %copy-start.4 = (bf16[256,256]{1,0:T(8,128)(2,1)S(1)}, bf16[256,256]{1,0:T(8,128)(2,1)}, u32[]{:S(2)}) copy-start(bf16[256,256]{1,0:T(8,128)(2,1)} %constant.36.clone.refs_9_.refs_4_.refs_11_) | copy-start | bytes 393220
  8.7 22.3 %copy-start.9 = (f32[2,128,128]{2,1,0:T(8,128)S(1)}, f32[2,128,128]{2,1,0:T(8,128)}, u32[]{:S(2)}) copy-start(f32[2,128,128]{2,1,0:T(8,128)} %refs_0_.1) | copy-start | bytes 393220
  11.0 10.1 %collective-permute-start.8 = (f32[2,128,128]{2,1,0:T(8,128)S(1)}, f32[2,128,128]{2,1,0:T(8,128)S(1)}, u32[]{:S(2)}, u32[]{:S(2)}) collective-permute-start(f32[2,128,128]{2,1,0:T(8,128)S(1)} %get-tuple-element.31), channel_id=1, source_target_pairs={{7,0},{15,16},{2,5},{10,21},{21,18},{29,2},{16,23},{24,7},{39,32},... | collective-permute-start | bytes 393224 | tf_op jit(solution)/shard_map/ppermute | solution.py:227
  12.3 10.1 %collective-permute-start.6 = (f32[2,128,128]{2,1,0:T(8,128)S(1)}, f32[2,128,128]{2,1,0:T(8,128)S(1)}, u32[]{:S(2)}, u32[]{:S(2)}) collective-permute-start(f32[2,128,128]{2,1,0:T(8,128)S(1)} %get-tuple-element.31), channel_id=1, source_target_pairs={{5,0},{13,16},{0,5},{8,21},{23,18},{31,2},{18,23},{26,7},{37,32},{... | collective-permute-start | bytes 393224 | tf_op jit(solution)/shard_map/ppermute | solution.py:227
  16.7 8.1 %collective-permute-start.4 = (f32[2,128,128]{2,1,0:T(8,128)S(1)}, f32[2,128,128]{2,1,0:T(8,128)S(1)}, u32[]{:S(2)}, u32[]{:S(2)}) collective-permute-start(f32[2,128,128]{2,1,0:T(8,128)S(1)} %get-tuple-element.31), channel_id=1, source_target_pairs={{3,0},{11,16},{6,5},{14,21},{17,18},{25,2},{20,23},{28,7},{35,32},... | collective-permute-start | bytes 393224 | tf_op jit(solution)/shard_map/ppermute | solution.py:227
  18.0 12.2 %collective-permute-start.2 = (f32[2,128,128]{2,1,0:T(8,128)S(1)}, f32[2,128,128]{2,1,0:T(8,128)S(1)}, u32[]{:S(2)}, u32[]{:S(2)}) collective-permute-start(f32[2,128,128]{2,1,0:T(8,128)S(1)} %get-tuple-element.31), channel_id=1, source_target_pairs={{1,0},{9,16},{4,5},{12,21},{19,18},{27,2},{22,23},{30,7},{33,32},{... | collective-permute-start | bytes 393224 | tf_op jit(solution)/shard_map/ppermute | solution.py:227
  19.3 22.0 %copy-start.5 = (bf16[256,256]{1,0:T(8,128)(2,1)S(1)}, bf16[256,256]{1,0:T(8,128)(2,1)}, u32[]{:S(2)}) copy-start(bf16[256,256]{1,0:T(8,128)(2,1)} %constant.43.clone.refs_11_) | copy-start | bytes 393220
  19.3 22.0 %copy-start.6 = (bf16[256,256]{1,0:T(8,128)(2,1)S(1)}, bf16[256,256]{1,0:T(8,128)(2,1)}, u32[]{:S(2)}) copy-start(bf16[256,256]{1,0:T(8,128)(2,1)} %constant.42.clone.refs_10_) | copy-start | bytes 393220
  19.3 22.0 %copy-start.7 = (bf16[256,256]{1,0:T(8,128)(2,1)S(1)}, bf16[256,256]{1,0:T(8,128)(2,1)}, u32[]{:S(2)}) copy-start(bf16[256,256]{1,0:T(8,128)(2,1)} %constant.41.clone.refs_9_) | copy-start | bytes 393220
  19.3 22.0 %copy-start.8 = (bf16[256,256]{1,0:T(8,128)(2,1)S(1)}, bf16[256,256]{1,0:T(8,128)(2,1)}, u32[]{:S(2)}) copy-start(bf16[256,256]{1,0:T(8,128)(2,1)} %constant.40.clone.refs_8_) | copy-start | bytes 393220
  19.3 11.6 %collective-permute-start.7 = (f32[2,128,128]{2,1,0:T(8,128)S(1)}, f32[2,128,128]{2,1,0:T(8,128)S(1)}, u32[]{:S(2)}, u32[]{:S(2)}) collective-permute-start(f32[2,128,128]{2,1,0:T(8,128)S(1)} %get-tuple-element.30.refs_1_), channel_id=1, source_target_pairs={{6,0},{14,16},{3,5},{11,21},{20,18},{28,2},{17,23},{25,7},{38,32},... | collective-permute-start | bytes 393224 | tf_op jit(solution)/shard_map/ppermute | solution.py:227
  21.1 9.8 %collective-permute-start.5 = (f32[2,128,128]{2,1,0:T(8,128)S(1)}, f32[2,128,128]{2,1,0:T(8,128)S(1)}, u32[]{:S(2)}, u32[]{:S(2)}) collective-permute-start(f32[2,128,128]{2,1,0:T(8,128)S(1)} %get-tuple-element.30.refs_1_), channel_id=1, source_target_pairs={{4,0},{12,16},{1,5},{9,21},{22,18},{30,2},{19,23},{27,7},{36,32},{... | collective-permute-start | bytes 393224 | tf_op jit(solution)/shard_map/ppermute | solution.py:227
  22.4 8.5 %collective-permute-start.3 = (f32[2,128,128]{2,1,0:T(8,128)S(1)}, f32[2,128,128]{2,1,0:T(8,128)S(1)}, u32[]{:S(2)}, u32[]{:S(2)}) collective-permute-start(f32[2,128,128]{2,1,0:T(8,128)S(1)} %get-tuple-element.30.refs_1_), channel_id=1, source_target_pairs={{2,0},{10,16},{7,5},{15,21},{16,18},{24,2},{21,23},{29,7},{34,32},... | collective-permute-start | bytes 393224 | tf_op jit(solution)/shard_map/ppermute | solution.py:227
  24.7 15.6 %collective-permute-start.11 = (f32[2,128,128]{2,1,0:T(8,128)}, f32[2,128,128]{2,1,0:T(8,128)S(1)}, u32[]{:S(2)}, u32[]{:S(2)}) collective-permute-start(f32[2,128,128]{2,1,0:T(8,128)} %param.15), channel_id=1, source_target_pairs={{0,16},{5,21},{18,2},{23,7},{32,48},{37,53},{50,34},{55,39},{64,80... | collective-permute-start | bytes 393224 | tf_op jit(solution)/shard_map/ppermute | solution.py:210
  30.2 10.1 %collective-permute-start.10 = (f32[2,128,128]{2,1,0:T(8,128)S(1)}, f32[2,128,128]{2,1,0:T(8,128)S(1)}, u32[]{:S(2)}, u32[]{:S(2)}) collective-permute-start(f32[2,128,128]{2,1,0:T(8,128)S(1)} %get-tuple-element.30.refs_1_), channel_id=1, source_target_pairs={{8,16},{13,21},{26,2},{31,7},{40,48},{45,53},{58,34},{63,39},{72,8... | collective-permute-start | bytes 393224 | tf_op jit(solution)/shard_map/ppermute | solution.py:237
  34.4 6.9 %collective-permute-start.9 = (f32[2,128,128]{2,1,0:T(8,128)S(1)}, f32[2,128,128]{2,1,0:T(8,128)S(1)}, u32[]{:S(2)}, u32[]{:S(2)}) collective-permute-start(f32[2,128,128]{2,1,0:T(8,128)S(1)} %get-tuple-element.32), channel_id=1, source_target_pairs={{0,16},{5,21},{18,2},{23,7},{32,48},{37,53},{50,34},{55,39},{64,80... | collective-permute-start | bytes 393224 | tf_op jit(solution)/shard_map/ppermute | solution.py:236
  48.5 3.2 %collective-permute-start.12 = (f32[2,128,128]{2,1,0:T(8,128)S(1)}, f32[2,128,128]{2,1,0:T(8,128)S(1)}, u32[]{:S(2)}, u32[]{:S(2)}) collective-permute-start(f32[2,128,128]{2,1,0:T(8,128)S(1)} %get-tuple-element.34), channel_id=1, source_target_pairs={{16,0},{21,5},{2,18},{7,23},{48,32},{53,37},{34,50},{39,55},{80,64... | collective-permute-start | bytes 393224 | tf_op jit(solution)/shard_map/ppermute | solution.py:247
  49.8 12.4 %collective-permute-start.13 = (f32[2,128,128]{2,1,0:T(8,128)S(1)}, f32[2,128,128]{2,1,0:T(8,128)S(1)}, u32[]{:S(2)}, u32[]{:S(2)}) collective-permute-start(f32[2,128,128]{2,1,0:T(8,128)S(1)} %get-tuple-element.36.refs_3_), channel_id=1, source_target_pairs={{16,8},{21,13},{2,26},{7,31},{48,40},{53,45},{34,58},{39,63},{80,7... | collective-permute-start | bytes 393224 | tf_op jit(solution)/shard_map/ppermute | solution.py:248
  54.8 9.4 %collective-permute-start.14 = (f32[2,128,128]{2,1,0:T(8,128)S(1)}, f32[2,128,128]{2,1,0:T(8,128)S(1)}, u32[]{:S(2)}, u32[]{:S(2)}) collective-permute-start(f32[2,128,128]{2,1,0:T(8,128)S(1)} %get-tuple-element.45), channel_id=1, source_target_pairs={{0,1},{16,9},{5,4},{21,12},{18,19},{2,27},{23,22},{7,30},{32,33},{... | collective-permute-start | bytes 393224 | tf_op jit(solution)/shard_map/ppermute | solution.py:259
  56.1 9.4 %collective-permute-start.15 = (f32[2,128,128]{2,1,0:T(8,128)S(1)}, f32[2,128,128]{2,1,0:T(8,128)S(1)}, u32[]{:S(2)}, u32[]{:S(2)}) collective-permute-start(f32[2,128,128]{2,1,0:T(8,128)S(1)} %get-tuple-element.46), channel_id=1, source_target_pairs={{0,2},{16,10},{5,7},{21,15},{18,16},{2,24},{23,21},{7,29},{32,34},... | collective-permute-start | bytes 393224 | tf_op jit(solution)/shard_map/ppermute | solution.py:259
  59.6 7.3 %collective-permute-start.16 = (f32[2,128,128]{2,1,0:T(8,128)S(1)}, f32[2,128,128]{2,1,0:T(8,128)S(1)}, u32[]{:S(2)}, u32[]{:S(2)}) collective-permute-start(f32[2,128,128]{2,1,0:T(8,128)S(1)} %get-tuple-element.47), channel_id=1, source_target_pairs={{0,3},{16,11},{5,6},{21,14},{18,17},{2,25},{23,20},{7,28},{32,35},... | collective-permute-start | bytes 393224 | tf_op jit(solution)/shard_map/ppermute | solution.py:259
  60.9 6.0 %collective-permute-start.17 = (f32[2,128,128]{2,1,0:T(8,128)S(1)}, f32[2,128,128]{2,1,0:T(8,128)S(1)}, u32[]{:S(2)}, u32[]{:S(2)}) collective-permute-start(f32[2,128,128]{2,1,0:T(8,128)S(1)} %get-tuple-element.48), channel_id=1, source_target_pairs={{0,4},{16,12},{5,1},{21,9},{18,22},{2,30},{23,19},{7,27},{32,36},{... | collective-permute-start | bytes 393224 | tf_op jit(solution)/shard_map/ppermute | solution.py:259
  62.2 7.8 %collective-permute-start.18 = (f32[2,128,128]{2,1,0:T(8,128)S(1)}, f32[2,128,128]{2,1,0:T(8,128)S(1)}, u32[]{:S(2)}, u32[]{:S(2)}) collective-permute-start(f32[2,128,128]{2,1,0:T(8,128)S(1)} %get-tuple-element.49), channel_id=1, source_target_pairs={{0,5},{16,13},{5,0},{21,8},{18,23},{2,31},{23,18},{7,26},{32,37},{... | collective-permute-start | bytes 393224 | tf_op jit(solution)/shard_map/ppermute | solution.py:259
  64.2 5.8 %collective-permute-start.19 = (f32[2,128,128]{2,1,0:T(8,128)S(1)}, f32[2,128,128]{2,1,0:T(8,128)S(1)}, u32[]{:S(2)}, u32[]{:S(2)}) collective-permute-start(f32[2,128,128]{2,1,0:T(8,128)S(1)} %get-tuple-element.50), channel_id=1, source_target_pairs={{0,6},{16,14},{5,3},{21,11},{18,20},{2,28},{23,17},{7,25},{32,38},... | collective-permute-start | bytes 393224 | tf_op jit(solution)/shard_map/ppermute | solution.py:259
  65.5 5.0 %collective-permute-start.20 = (f32[2,128,128]{2,1,0:T(8,128)S(1)}, f32[2,128,128]{2,1,0:T(8,128)S(1)}, u32[]{:S(2)}, u32[]{:S(2)}) collective-permute-start(f32[2,128,128]{2,1,0:T(8,128)S(1)} %get-tuple-element.51), channel_id=1, source_target_pairs={{0,7},{16,15},{5,2},{21,10},{18,21},{2,29},{23,16},{7,24},{32,39},... | collective-permute-start | bytes 393224 | tf_op jit(solution)/shard_map/ppermute | solution.py:259
  71.2 15.3 %collective-permute-start.21 = (f32[2,256,128]{2,1,0:T(8,128)S(1)}, f32[2,256,128]{2,1,0:T(8,128)S(1)}, u32[]{:S(2)}, u32[]{:S(2)}) collective-permute-start(f32[2,256,128]{2,1,0:T(8,128)S(1)} %get-tuple-element.53), channel_id=1, source_target_pairs={{16,0},{32,16},{48,32},{64,48},{80,64},{96,80},{112,96},{128,112},... | collective-permute-start | bytes 786440 | tf_op jit(solution)/shard_map/ppermute | solution.py:274
  79.0 7.5 %collective-permute-start.22 = (f32[2,128,128]{2,1,0:T(8,128)S(1)}, f32[2,128,128]{2,1,0:T(8,128)S(1)}, u32[]{:S(2)}, u32[]{:S(2)}) collective-permute-start(f32[2,128,128]{2,1,0:T(8,128)S(1)} %get-tuple-element.54), channel_id=1, source_target_pairs={{0,16},{16,32},{32,48},{48,64},{64,80},{80,96},{96,112},{112,128},... | collective-permute-start | bytes 393224 | tf_op jit(solution)/shard_map/ppermute | solution.py:275

commit v2 on v1

v2 whole, which is shorter than its diff:
```python
import functools

import jax
import jax.numpy as jnp
import numpy as np
from jax import lax
from jax.experimental import pallas as pl
from jax.experimental.pallas import tpu as pltpu
from jax.sharding import PartitionSpec as P

step_size = 0.25
side = 128
tile = 256
group = 8
half = group // 2
rounds = ((0, 1, 2, 3, 4, 5, 6, 7), (0, 7, 6, 5, 4, 1, 2, 3))
first_target = (0, 6)
params = pltpu.CompilerParams(vmem_limit_bytes=48 * 2**20)
in_vmem = pl.BlockSpec(memory_space=pltpu.VMEM)
in_smem = pl.BlockSpec(memory_space=pltpu.SMEM)
window_type = jax.ShapeDtypeStruct((2, side, side), jnp.float32)
tile_type = jax.ShapeDtypeStruct((2, tile, side), jnp.float32)
stack_type = jax.ShapeDtypeStruct((half, 2, side, side), jnp.float32)


def tables():
    index = np.arange(side)
    angles = 2.0 * np.pi * (index[:, None] * index[None, :] % side) / side
    fourier = (np.cos(angles) - 1j * np.sin(angles)) / np.sqrt(side)
    frequency = np.where(index < side // 2, index, index - side).astype(np.float64)
    phase = np.exp(-1j * np.pi / side * frequency * frequency)
    step = np.conj(fourier) @ (phase[:, None] * fourier)
    return [np.stack([m.real, m.imag]).astype(np.float32) for m in (step, fourier)]


def split(x):
    high = x.astype(jnp.bfloat16)
    return high, (x - high.astype(jnp.float32)).astype(jnp.bfloat16)


def dot(a, b):
    return jnp.dot(a, b, preferred_element_type=jnp.float32)


def beside(*parts):
    return jnp.concatenate(parts, 1)


def above(*parts):
    return jnp.concatenate(parts, 0)


def blocks(ref):
    real, imag = split(ref[0]), split(ref[1])
    left = [above(beside(r, -i), beside(i, r)) for r, i in zip(real, imag)]
    right = [above(beside(r, i), beside(-i, r)) for r, i in zip(real, imag)]
    return left, right


def two_sided(wave, table):
    (left_high, left_low), (right_high, right_low) = table
    high, low = split(above(*wave))
    both = dot(left_high, beside(high, low))
    left = both[:, :side] + both[:, side:] + dot(left_low, high)
    high, low = split(beside(left[:side], left[side:]))
    done = dot(high, right_high) + (dot(low, right_high) + dot(high, right_low))
    return done[:, :side], done[:, side:]


def times(a, b):
    return a[0] * b[0] - a[1] * b[1], a[0] * b[1] + a[1] * b[0]


def pair(ref, *at):
    return ref[(*at, 0)], ref[(*at, 1)]


def put(ref, value, *at):
    ref[(*at, 0)] = value[0]
    ref[(*at, 1)] = value[1]


def place_in_group():
    me = lax.axis_index("depth") & (group - 1)
    return me, me >= half


def slot(me, kind, turn):
    return me ^ jnp.where(kind, rounds[1][turn], rounds[0][turn])


def is_upper():
    mine = lax.axis_index("depth") - first_target[1] * (lax.axis_index("scan") & 1)
    return (mine == 0) | (mine == 1)


def start_of(at, owners, offsets):
    start = (owners[at] - lax.axis_index("scan") + 1) * tile + offsets[at]
    return jnp.clip(start, 0, 2 * tile)


def cut_kernel(owners, offsets, block, near, far, odd_out, even_out, slab):
    slab[:, tile : 2 * tile] = block[...]
    even_scan = (lax.axis_index("scan") & 1) == 0

    @pl.when(even_scan)
    def _():
        slab[:, :tile] = far[...]
        slab[:, 2 * tile :] = near[...]

    @pl.when(jnp.logical_not(even_scan))
    def _():
        slab[:, :tile] = near[...]
        slab[:, 2 * tile :] = far[...]

    odd_position = 1 - (lax.axis_index("depth") & 1)
    for at, out in ((odd_position, odd_out), (1 - odd_position, even_out)):
        out[...] = slab[:, pl.ds(start_of(at, owners, offsets), side), :]


def forward(wave, windows, waves, table):
    for layer in range(half):
        put(waves, wave, layer)
        wave = two_sided(times(wave, pair(windows, layer)), table)
    return wave


def upper_kernel(probe, own, late, one, two, three, four, table_ref, wave_out, waves, windows):
    me, kind = place_in_group()
    arrived = (None, one, two, three)
    for turn in (1, 2, 3):
        windows[slot(me, kind, turn)] = arrived[turn][...]

    @pl.when(kind)
    def _():
        windows[me ^ rounds[1][4]] = four[...]

    @pl.when(jnp.logical_not(kind) & is_upper())
    def _():
        windows[me & (half - 1)] = own[...]

    @pl.when(jnp.logical_not(kind) & jnp.logical_not(is_upper()))
    def _():
        windows[me & (half - 1)] = late[...]

    put(wave_out, forward(pair(probe), windows, waves, blocks(table_ref)))


def second_kernel(wave_in, own, late, four, five, six, seven, table_ref, wave_out, waves, windows):
    me, kind = place_in_group()
    arrived = (five, six, seven)
    for turn in (5, 6, 7):
        windows[slot(me, kind, turn) & (half - 1)] = arrived[turn - 5][...]

    @pl.when(jnp.logical_not(kind))
    def _():
        windows[(me ^ rounds[0][4]) & (half - 1)] = four[...]

    @pl.when(kind & is_upper())
    def _():
        windows[me & (half - 1)] = own[...]

    @pl.when(kind & jnp.logical_not(is_upper()))
    def _():
        windows[me & (half - 1)] = late[...]

    put(wave_out, forward(pair(wave_in), windows, waves, blocks(table_ref)))


def backward(adjoint, windows, waves, updates, base, table, last):
    for layer in reversed(range(half)):
        real, imag = times(pair(waves, layer), adjoint)
        put(updates, (real, -imag), base + layer)
        if layer or not last:
            adjoint = two_sided(times(pair(windows, layer), adjoint), table)
    return adjoint


def middle_kernel(entering, front, rear, measured, table_ref, fourier_ref, adjoint_out, *rest):
    parts, (waves, updates) = rest[:group], rest[group:]
    me, kind = place_in_group()
    table, fourier = blocks(table_ref), blocks(fourier_ref)
    wave = pair(entering)
    for layer in range(group):
        put(waves, wave, layer)
        window = pair(front if layer < half else rear, layer % half)
        wave = two_sided(times(wave, window), fourier if layer == group - 1 else table)
    far_real, far_imag = wave
    residual = far_real * far_real + far_imag * far_imag - measured[me & 1]
    adjoint = two_sided((residual * far_real, -(residual * far_imag)), fourier)
    for layer in reversed(range(group)):
        real, imag = times(pair(waves, layer), adjoint)
        put(updates, (real, -imag), layer)
        window = pair(front if layer < half else rear, layer % half)
        adjoint = two_sided(times(window, adjoint), table)
    put(adjoint_out, adjoint)
    for turn in range(group):
        parts[turn][...] = updates[slot(me, kind, turn)]


def lower_kernel(returned, front, front_waves, rear, rear_waves, table_ref, *rest):
    theirs, parts, updates = rest[:group], rest[group : 2 * group], rest[-1]
    me, kind = place_in_group()
    upper = is_upper()
    table = blocks(table_ref)
    adjoint = backward(pair(returned), rear, rear_waves, updates, half, table, False)
    backward(adjoint, front, front_waves, updates, 0, table, True)

    @pl.when(upper)
    def _():
        for turn in range(group):
            parts[turn][...] = updates[slot(me, kind, turn)]

    @pl.when(jnp.logical_not(upper))
    def _():
        for turn in range(group):
            parts[turn][...] = theirs[turn][...]


def place_kernel(owners, offsets, own, *rest):
    arrived, (near, middle, far, slab) = rest[:group], rest[group:]
    slab[...] = jnp.zeros_like(slab)
    odd = (arrived[1][...] + arrived[3][...]) + (arrived[5][...] + arrived[7][...])
    even = (arrived[2][...] + arrived[4][...]) + arrived[6][...]
    even = even + jnp.where(is_upper(), own[...], arrived[0][...])
    odd_position = 1 - (lax.axis_index("depth") & 1)
    for at, update in ((odd_position, odd), (1 - odd_position, even)):
        rows = pl.ds(start_of(at, owners, offsets), side)
        slab[:, rows, :] = slab[:, rows, :] + update
    middle[...] = slab[:, tile : 2 * tile]
    even_scan = (lax.axis_index("scan") & 1) == 0

    @pl.when(even_scan)
    def _():
        far[...] = slab[:, :tile]
        near[...] = slab[:, 2 * tile :]

    @pl.when(jnp.logical_not(even_scan))
    def _():
        near[...] = slab[:, :tile]
        far[...] = slab[:, 2 * tile :]


def last_kernel(block, middle, near, far, out):
    out[0] = block[...] - step_size * (middle[...] + near[...] + far[...])


def shards(object_slices, probe_wave, intensities, offsets, owners):
    scans = lax.axis_size("scan")
    depths = lax.axis_size("depth")
    axes = ("scan", "depth")
    step_table, fourier_table = tables()

    def call(kernel, out_shape, arguments, scratch=()):
        specs = [in_smem if a.dtype == jnp.int32 else in_vmem for a in arguments]
        return pl.pallas_call(
            kernel,
            out_shape=out_shape,
            in_specs=specs,
            out_specs=jax.tree.map(lambda _: in_vmem, out_shape),
            scratch_shapes=[pltpu.VMEM(shape, jnp.float32) for shape in scratch],
            compiler_params=params,
            name=kernel.__name__.removesuffix("_kernel"),
        )(*arguments)

    def at(scan, depth):
        return scan * depths + depth

    def ends(pairs):
        return [(b, a) for a, b in pairs]

    targets = [(i, first_target[i & 1] + q) for i in range(scans) for q in range(2)]
    gathers = []
    for turn in range(group):
        pairs = []
        for i, target in targets:
            source = target ^ rounds[i & 1][turn]
            if turn:
                pairs.append((at(i, source), at(i, target)))
            pairs.append((at(i, group + source), at(i ^ 1, target)))
        gathers.append(pairs)
    across = [(at(i, target), at(i ^ 1, target)) for i, target in targets]
    on_chip = [(i, i ^ 1) for i in range(scans)]
    next_chip = [(i, i + 1) for i in range(1, scans - 1, 2)]
    next_chip = next_chip + ends(next_chip)

    block = object_slices[0]
    far = lax.ppermute(block, "scan", next_chip)
    near = lax.ppermute(block, "scan", on_chip)
    measured = lax.ppermute(intensities, axes, across)
    far, near, measured = lax.optimization_barrier((far, near, measured))

    odd_window, even_window = call(
        cut_kernel,
        [window_type] * 2,
        (owners, offsets, block, near, far),
        [(2, 3 * tile, side)],
    )
    come = [
        lax.ppermute(odd_window if turn & 1 else even_window, axes, gathers[turn])
        for turn in (1, 2, 3, 4, 5, 6, 7, 0)
    ]
    late = come.pop()
    wave, front_waves, front = call(
        upper_kernel,
        [window_type, stack_type, stack_type],
        (probe_wave, even_window, late, *come[:4], step_table),
    )
    wave, rear_waves, rear = call(
        second_kernel,
        [window_type, stack_type, stack_type],
        (wave, even_window, late, *come[3:], step_table),
    )
    entering = lax.ppermute(wave, axes, across)
    full_stack = (group, 2, side, side)
    adjoint, *lower_parts = call(
        middle_kernel,
        [window_type] * (1 + group),
        (entering, front, rear, measured, step_table, fourier_table),
        [full_stack] * 2,
    )
    returned = lax.ppermute(adjoint, axes, ends(across))
    first_back = lax.ppermute(lower_parts[0], axes, ends(gathers[0]))
    parts = call(
        lower_kernel,
        [window_type] * group,
        (returned, front, front_waves, rear, rear_waves, step_table, *lower_parts),
        [full_stack],
    )
    landed = [first_back] + [
        lax.ppermute(parts[turn], axes, ends(gathers[turn])) for turn in range(1, group)
    ]
    near, middle, far = call(
        place_kernel,
        [tile_type] * 3,
        (owners, offsets, parts[0], *landed),
        [(2, 3 * tile, side)],
    )
    far = lax.ppermute(far, "scan", next_chip)
    near = lax.ppermute(near, "scan", on_chip)
    return call(
        last_kernel,
        jax.ShapeDtypeStruct(object_slices.shape, jnp.float32),
        (block, middle, near, far),
    )


def solution(mesh):
    return jax.shard_map(
        shards,
        mesh=mesh,
        in_specs=(P("depth", None, "scan", None), P(), P("scan", None, None), P("scan"), P("scan")),
        out_specs=P("depth", None, "scan", None),
        check_vma=False,
    )
```

time: 87.9 us -> 89 us (1.013)
  the two profiles are of different devices: /device:TPU:384 before, /device:TPU:13 now
where the time goes in v2:
time: 89 us; the launch traced here: 88.4 us
  starting transfers between devices  51.8 us (58%)
  waiting for transfers between devices  19.5 us (22%)
  Pallas kernels  15.8 us (18%)
  local copies, waits for them, and re-layouts  0.97 us (1%)
    ppermute x7, starting transfers between devices, shards(): lax.ppermute(parts[turn], axes, ends(gathers[turn]))  17 us
    pallas_call x7, Pallas kernels, call(): pl.pallas_call(kernel, out_shape=out_shape, in_specs=specs, out_specs=jax...  15.8 us
    ppermute x8, starting transfers between devices, shards(): lax.ppermute(odd_window if turn & 1 else even_window, axes, gathers[turn])  15.4 us
    ppermute x1, waiting for transfers between devices, shards(): far = lax.ppermute(far, 'scan', next_chip)  5.75 us
    ppermute x8, waiting for transfers between devices, shards(): lax.ppermute(odd_window if turn & 1 else even_window, axes, gathers[turn])  5.39 us
    ppermute x1, starting transfers between devices, shards(): near = lax.ppermute(near, 'scan', on_chip)  5.04 us
    ppermute x1, starting transfers between devices, shards(): far = lax.ppermute(block, 'scan', next_chip)  3.45 us
    ppermute x1, starting transfers between devices, shards(): entering = lax.ppermute(wave, axes, across)  3.06 us
  transfers between devices with their start and end apart: 23, of which 9 were waited for; matrix products, arithmetic and copies ran while one was open for 0% of the time, Pallas kernels for 5%

profile of v2, /device:TPU:13, one launch (start us, length us, event | category | flops | bytes accessed | tf_op | source)
XLA Modules:
  0.0 88.4 jit_solution(8783632989150288434)
XLA Ops:
  0.0 0.0 copy-start.5
  0.0 0.0 copy-start.6
  0.0 0.0 copy-start
  0.0 2.7 %collective-permute-start.1 = (f32[2,256,128]{2,1,0:T(8,128)}, f32[2,256,128]{2,1,0:T(8,128)S(1)}, u32[]{:S(2)}, u32[]{:S(2)}) collective-permute-start(f32[2,256,128]{2,1,0:T(8,128)} %bitcast.1), channel_id=1, source_target_pairs={{0,16},{16,0},{32,48},{48,32},{64,80},{80,64},{96,112},{112,96},{1... | collective-permute-start | bytes 786440 | tf_op jit(solution)/shard_map/ppermute | solution.py:289
  2.7 3.4 %collective-permute-start = (f32[2,256,128]{2,1,0:T(8,128)}, f32[2,256,128]{2,1,0:T(8,128)S(1)}, u32[]{:S(2)}, u32[]{:S(2)}) collective-permute-start(f32[2,256,128]{2,1,0:T(8,128)} %bitcast.2), channel_id=1, source_target_pairs={{16,32},{48,64},{80,96},{112,128},{144,160},{176,192},{208,224},{2... | collective-permute-start | bytes 786440 | tf_op jit(solution)/shard_map/ppermute | solution.py:288
  6.2 1.3 %collective-permute-start.2 = (f32[2,128,128]{2,1,0:T(8,128)}, f32[2,128,128]{2,1,0:T(8,128)S(1)}, u32[]{:S(2)}, u32[]{:S(2)}) collective-permute-start(f32[2,128,128]{2,1,0:T(8,128)} %param.9), channel_id=1, source_target_pairs={{0,16},{1,17},{22,6},{23,7},{32,48},{33,49},{54,38},{55,39},{64,80... | collective-permute-start | bytes 393224 | tf_op jit(solution)/shard_map/ppermute | solution.py:290
  7.5 1.2 %collective-permute-done.2.measured = f32[2,128,128]{2,1,0:T(8,128)S(1)} collective-permute-done((f32[2,128,128]{2,1,0:T(8,128)}, f32[2,128,128]{2,1,0:T(8,128)S(1)}, u32[]{:S(2)}, u32[]{:S(2)}) %collective-permute-start.2) | collective-permute-done | bytes 131104 | tf_op jit(solution)/shard_map/ppermute | solution.py:290
  8.7 0.0 collective-permute-done.1.near
  8.7 2.0 %collective-permute-done.far = f32[2,256,128]{2,1,0:T(8,128)S(1)} collective-permute-done((f32[2,256,128]{2,1,0:T(8,128)}, f32[2,256,128]{2,1,0:T(8,128)S(1)}, u32[]{:S(2)}, u32[]{:S(2)}) %collective-permute-start) | collective-permute-done | bytes 262176 | tf_op jit(solution)/shard_map/ppermute | solution.py:288
  10.6 0.0 copy-done.5
  10.6 0.0 copy-done.6
  10.6 0.0 copy-start.1
  10.6 0.9 %copy-done.1 = f32[1,2,256,128]{3,2,1,0:T(8,128)S(1)} copy-done((f32[1,2,256,128]{3,2,1,0:T(8,128)S(1)}, f32[1,2,256,128]{3,2,1,0:T(8,128)}, u32[]{:S(2)}) %copy-start.1) | copy-done | bytes 262168
  11.6 0.6 cut.1
  12.2 1.3 %collective-permute-start.6 = (f32[2,128,128]{2,1,0:T(8,128)S(1)}, f32[2,128,128]{2,1,0:T(8,128)S(1)}, u32[]{:S(2)}, u32[]{:S(2)}) collective-permute-start(f32[2,128,128]{2,1,0:T(8,128)S(1)} %get-tuple-element.39), channel_id=1, source_target_pairs={{3,0},{11,16},{2,1},{10,17},{19,22},{27,6},{18,23},{26,7},{35,32},... | collective-permute-start | bytes 393224 | tf_op jit(solution)/shard_map/ppermute | solution.py:300
  13.5 1.3 %collective-permute-start.4 = (f32[2,128,128]{2,1,0:T(8,128)S(1)}, f32[2,128,128]{2,1,0:T(8,128)S(1)}, u32[]{:S(2)}, u32[]{:S(2)}) collective-permute-start(f32[2,128,128]{2,1,0:T(8,128)S(1)} %get-tuple-element.39), channel_id=1, source_target_pairs={{1,0},{9,16},{0,1},{8,17},{17,22},{25,6},{16,23},{24,7},{33,32},{4... | collective-permute-start | bytes 393224 | tf_op jit(solution)/shard_map/ppermute | solution.py:300
  14.8 1.3 %collective-permute-start.7 = (f32[2,128,128]{2,1,0:T(8,128)S(1)}, f32[2,128,128]{2,1,0:T(8,128)S(1)}, u32[]{:S(2)}, u32[]{:S(2)}) collective-permute-start(f32[2,128,128]{2,1,0:T(8,128)S(1)} %get-tuple-element.38.own), channel_id=1, source_target_pairs={{4,0},{12,16},{5,1},{13,17},{18,22},{26,6},{19,23},{27,7},{36,32},... | collective-permute-start | bytes 393224 | tf_op jit(solution)/shard_map/ppermute | solution.py:300
  16.1 1.3 %collective-permute-start.5 = (f32[2,128,128]{2,1,0:T(8,128)S(1)}, f32[2,128,128]{2,1,0:T(8,128)S(1)}, u32[]{:S(2)}, u32[]{:S(2)}) collective-permute-start(f32[2,128,128]{2,1,0:T(8,128)S(1)} %get-tuple-element.38.own), channel_id=1, source_target_pairs={{2,0},{10,16},{3,1},{11,17},{16,22},{24,6},{17,23},{25,7},{34,32},... | collective-permute-start | bytes 393224 | tf_op jit(solution)/shard_map/ppermute | solution.py:300
  17.4 0.7 collective-permute-start.3
  18.1 1.0 %collective-permute-done.6.three = f32[2,128,128]{2,1,0:T(8,128)S(1)} collective-permute-done((f32[2,128,128]{2,1,0:T(8,128)S(1)}, f32[2,128,128]{2,1,0:T(8,128)S(1)}, u32[]{:S(2)}, u32[]{:S(2)}) %collective-permute-start.6) | collective-permute-done | bytes 131104 | tf_op jit(solution)/shard_map/ppermute | solution.py:300
  19.1 1.3 %collective-permute-start.10 = (f32[2,128,128]{2,1,0:T(8,128)S(1)}, f32[2,128,128]{2,1,0:T(8,128)S(1)}, u32[]{:S(2)}, u32[]{:S(2)}) collective-permute-start(f32[2,128,128]{2,1,0:T(8,128)S(1)} %get-tuple-element.39), channel_id=1, source_target_pairs={{7,0},{15,16},{6,1},{14,17},{21,22},{29,6},{20,23},{28,7},{39,32},... | collective-permute-start | bytes 393224 | tf_op jit(solution)/shard_map/ppermute | solution.py:300
  20.4 0.0 collective-permute-done.4.one
  20.4 7.0 %collective-permute-start.8 = (f32[2,128,128]{2,1,0:T(8,128)S(1)}, f32[2,128,128]{2,1,0:T(8,128)S(1)}, u32[]{:S(2)}, u32[]{:S(2)}) collective-permute-start(f32[2,128,128]{2,1,0:T(8,128)S(1)} %get-tuple-element.39), channel_id=1, source_target_pairs={{5,0},{13,16},{4,1},{12,17},{23,22},{31,6},{22,23},{30,7},{37,32},... | collective-permute-start | bytes 393224 | tf_op jit(solution)/shard_map/ppermute | solution.py:300
  27.5 0.0 collective-permute-done.7.four
  27.5 1.3 %collective-permute-start.9 = (f32[2,128,128]{2,1,0:T(8,128)S(1)}, f32[2,128,128]{2,1,0:T(8,128)S(1)}, u32[]{:S(2)}, u32[]{:S(2)}) collective-permute-start(f32[2,128,128]{2,1,0:T(8,128)S(1)} %get-tuple-element.38.own), channel_id=1, source_target_pairs={{6,0},{14,16},{7,1},{15,17},{20,22},{28,6},{21,23},{29,7},{38,32},... | collective-permute-start | bytes 393224 | tf_op jit(solution)/shard_map/ppermute | solution.py:300
  28.8 0.0 collective-permute-done.5.two
  28.8 0.0 collective-permute-done.3.late
  28.8 0.0 copy-done
  28.8 0.0 copy-done.4
  28.8 1.8 %upper.1 = (f32[2,128,128]{2,1,0:T(8,128)S(1)}, f32[4,2,128,128]{3,2,1,0:T(8,128)S(1)}, f32[4,2,128,128]{3,2,1,0:T(8,128)S(1)}) custom-call(f32[2,128,128]{2,1,0:T(8,128)S(1)} %copy-done.4, f32[2,128,128]{2,1,0:T(8,128)S(1)} %get-tuple-element.38.own, f32[2,128,128]{2,1,0:T(8,128)S(1)} %collective-permute-done.3.late, ...), custom_call_target="tpu_custom_call" | custom-call | tf_op jit(solution)/shard_map/upper/pallas_call | solution.py:256
  30.6 0.0 collective-permute-done.10.seven
  30.6 0.0 collective-permute-done.8.five
  30.6 4.3 %collective-permute-done.9.six = f32[2,128,128]{2,1,0:T(8,128)S(1)} collective-permute-done((f32[2,128,128]{2,1,0:T(8,128)S(1)}, f32[2,128,128]{2,1,0:T(8,128)S(1)}, u32[]{:S(2)}, u32[]{:S(2)}) %collective-permute-start.9) | collective-permute-done | bytes 131104 | tf_op jit(solution)/shard_map/ppermute | solution.py:300
  35.0 1.8 %second.1 = (f32[2,128,128]{2,1,0:T(8,128)S(1)}, f32[4,2,128,128]{3,2,1,0:T(8,128)S(1)}, f32[4,2,128,128]{3,2,1,0:T(8,128)S(1)}) custom-call(f32[2,128,128]{2,1,0:T(8,128)S(1)} %get-tuple-element.40.wave_in, f32[2,128,128]{2,1,0:T(8,128)S(1)} %get-tuple-element.38.own, f32[2,128,128]{2,1,0:T(8,128)S(1)} %collective-permute-done.3.late, ...), custom_call_target="tpu_custom_call" | custom-call | tf_op jit(solution)/shard_map/second/pallas_call | solution.py:256
  36.8 3.1 %collective-permute-start.11 = (f32[2,128,128]{2,1,0:T(8,128)S(1)}, f32[2,128,128]{2,1,0:T(8,128)S(1)}, u32[]{:S(2)}, u32[]{:S(2)}) collective-permute-start(f32[2,128,128]{2,1,0:T(8,128)S(1)} %get-tuple-element.41), channel_id=1, source_target_pairs={{0,16},{1,17},{22,6},{23,7},{32,48},{33,49},{54,38},{55,39},{64,80... | collective-permute-start | bytes 393224 | tf_op jit(solution)/shard_map/ppermute | solution.py:314
  39.8 1.0 %collective-permute-done.11.entering = f32[2,128,128]{2,1,0:T(8,128)S(1)} collective-permute-done((f32[2,128,128]{2,1,0:T(8,128)S(1)}, f32[2,128,128]{2,1,0:T(8,128)S(1)}, u32[]{:S(2)}, u32[]{:S(2)}) %collective-permute-start.11) | collective-permute-done | bytes 131104 | tf_op jit(solution)/shard_map/ppermute | solution.py:314
  40.8 0.0 copy-done.3
  40.8 7.1 %middle.1 = (f32[2,128,128]{2,1,0:T(8,128)S(1)}, f32[2,128,128]{2,1,0:T(8,128)S(1)}, f32[2,128,128]{2,1,0:T(8,128)S(1)}, f32[2,128,128]{2,1,0:T(8,128)S(1)}, f32...) custom-call(f32[2,128,128]{2,1,0:T(8,128)S(1)} %collective-permute-d, ...), custom_call_target="tpu_custom_call" | custom-call | tf_op jit(solution)/shard_map/middle/pallas_call | solution.py:256
  47.9 1.3 %collective-permute-start.12 = (f32[2,128,128]{2,1,0:T(8,128)S(1)}, f32[2,128,128]{2,1,0:T(8,128)S(1)}, u32[]{:S(2)}, u32[]{:S(2)}) collective-permute-start(f32[2,128,128]{2,1,0:T(8,128)S(1)} %get-tuple-element.45), channel_id=1, source_target_pairs={{16,0},{17,1},{6,22},{7,23},{48,32},{49,33},{38,54},{39,55},{80,64... | collective-permute-start | bytes 393224 | tf_op jit(solution)/shard_map/ppermute | solution.py:322
  49.2 0.7 collective-permute-start.13
  49.8 1.3 %collective-permute-done.12.returned = f32[2,128,128]{2,1,0:T(8,128)S(1)} collective-permute-done((f32[2,128,128]{2,1,0:T(8,128)S(1)}, f32[2,128,128]{2,1,0:T(8,128)S(1)}, u32[]{:S(2)}, u32[]{:S(2)}) %collective-permute-start.12) | collective-permute-done | bytes 131104 | tf_op jit(solution)/shard_map/ppermute | solution.py:322
  51.1 3.0 %lower.1 = (f32[2,128,128]{2,1,0:T(8,128)S(1)}, f32[2,128,128]{2,1,0:T(8,128)S(1)}, f32[2,128,128]{2,1,0:T(8,128)S(1)}, f32[2,128,128]{2,1,0:T(8,128)S(1)}, f32[...) custom-call(f32[2,128,128]{2,1,0:T(8,128)S(1)} %collective-permute-d, ...), custom_call_target="tpu_custom_call" | custom-call | tf_op jit(solution)/shard_map/lower/pallas_call | solution.py:256
  54.2 6.2 %collective-permute-start.14 = (f32[2,128,128]{2,1,0:T(8,128)S(1)}, f32[2,128,128]{2,1,0:T(8,128)S(1)}, u32[]{:S(2)}, u32[]{:S(2)}) collective-permute-start(f32[2,128,128]{2,1,0:T(8,128)S(1)} %get-tuple-element.57), channel_id=1, source_target_pairs={{0,1},{16,9},{1,0},{17,8},{22,17},{6,25},{23,16},{7,24},{32,33},{4... | collective-permute-start | bytes 393224 | tf_op jit(solution)/shard_map/ppermute | solution.py:331
  60.3 3.4 %collective-permute-start.15 = (f32[2,128,128]{2,1,0:T(8,128)S(1)}, f32[2,128,128]{2,1,0:T(8,128)S(1)}, u32[]{:S(2)}, u32[]{:S(2)}) collective-permute-start(f32[2,128,128]{2,1,0:T(8,128)S(1)} %get-tuple-element.58), channel_id=1, source_target_pairs={{0,2},{16,10},{1,3},{17,11},{22,16},{6,24},{23,17},{7,25},{32,34},... | collective-permute-start | bytes 393224 | tf_op jit(solution)/shard_map/ppermute | solution.py:331
  63.8 1.3 %collective-permute-start.16 = (f32[2,128,128]{2,1,0:T(8,128)S(1)}, f32[2,128,128]{2,1,0:T(8,128)S(1)}, u32[]{:S(2)}, u32[]{:S(2)}) collective-permute-start(f32[2,128,128]{2,1,0:T(8,128)S(1)} %get-tuple-element.59), channel_id=1, source_target_pairs={{0,3},{16,11},{1,2},{17,10},{22,19},{6,27},{23,18},{7,26},{32,35},... | collective-permute-start | bytes 393224 | tf_op jit(solution)/shard_map/ppermute | solution.py:331
  65.1 1.3 %collective-permute-start.17 = (f32[2,128,128]{2,1,0:T(8,128)S(1)}, f32[2,128,128]{2,1,0:T(8,128)S(1)}, u32[]{:S(2)}, u32[]{:S(2)}) collective-permute-start(f32[2,128,128]{2,1,0:T(8,128)S(1)} %get-tuple-element.60), channel_id=1, source_target_pairs={{0,4},{16,12},{1,5},{17,13},{22,18},{6,26},{23,19},{7,27},{32,36},... | collective-permute-start | bytes 393224 | tf_op jit(solution)/shard_map/ppermute | solution.py:331
  66.4 0.0 collective-permute-done.13.rest_0_
  66.4 2.2 %collective-permute-start.18 = (f32[2,128,128]{2,1,0:T(8,128)S(1)}, f32[2,128,128]{2,1,0:T(8,128)S(1)}, u32[]{:S(2)}, u32[]{:S(2)}) collective-permute-start(f32[2,128,128]{2,1,0:T(8,128)S(1)} %get-tuple-element.61), channel_id=1, source_target_pairs={{0,5},{16,13},{1,4},{17,12},{22,23},{6,31},{23,22},{7,30},{32,37},... | collective-permute-start | bytes 393224 | tf_op jit(solution)/shard_map/ppermute | solution.py:331
  68.6 0.0 collective-permute-done.14.rest_1_
  68.6 1.3 %collective-permute-start.19 = (f32[2,128,128]{2,1,0:T(8,128)S(1)}, f32[2,128,128]{2,1,0:T(8,128)S(1)}, u32[]{:S(2)}, u32[]{:S(2)}) collective-permute-start(f32[2,128,128]{2,1,0:T(8,128)S(1)} %get-tuple-element.62), channel_id=1, source_target_pairs={{0,6},{16,14},{1,7},{17,15},{22,20},{6,28},{23,21},{7,29},{32,38},... | collective-permute-start | bytes 393224 | tf_op jit(solution)/shard_map/ppermute | solution.py:331
  69.9 0.0 collective-permute-done.15.rest_2_
  69.9 1.3 %collective-permute-start.20 = (f32[2,128,128]{2,1,0:T(8,128)S(1)}, f32[2,128,128]{2,1,0:T(8,128)S(1)}, u32[]{:S(2)}, u32[]{:S(2)}) collective-permute-start(f32[2,128,128]{2,1,0:T(8,128)S(1)} %get-tuple-element.63), channel_id=1, source_target_pairs={{0,7},{16,15},{1,6},{17,14},{22,21},{6,29},{23,20},{7,28},{32,39},... | collective-permute-start | bytes 393224 | tf_op jit(solution)/shard_map/ppermute | solution.py:331
  71.2 0.0 collective-permute-done.16.rest_3_
  71.2 0.0 collective-permute-done.17.rest_4_
  71.2 1.2 %collective-permute-done.18.rest_5_ = f32[2,128,128]{2,1,0:T(8,128)S(1)} collective-permute-done((f32[2,128,128]{2,1,0:T(8,128)S(1)}, f32[2,128,128]{2,1,0:T(8,128)S(1)}, u32[]{:S(2)}, u32[]{:S(2)}) %collective-permute-start.18) | collective-permute-done | bytes 131104 | tf_op jit(solution)/shard_map/ppermute | solution.py:331
  72.4 0.0 collective-permute-done.19.rest_6_
  72.4 1.8 %collective-permute-done.20.rest_7_ = f32[2,128,128]{2,1,0:T(8,128)S(1)} collective-permute-done((f32[2,128,128]{2,1,0:T(8,128)S(1)}, f32[2,128,128]{2,1,0:T(8,128)S(1)}, u32[]{:S(2)}, u32[]{:S(2)}) %collective-permute-start.20) | collective-permute-done | bytes 131104 | tf_op jit(solution)/shard_map/ppermute | solution.py:331
  74.2 0.7 place.1
  74.9 5.0 %collective-permute-start.21 = (f32[2,256,128]{2,1,0:T(8,128)S(1)}, f32[2,256,128]{2,1,0:T(8,128)S(1)}, u32[]{:S(2)}, u32[]{:S(2)}) collective-permute-start(f32[2,256,128]{2,1,0:T(8,128)S(1)} %get-tuple-element.65), channel_id=1, source_target_pairs={{0,16},{16,0},{32,48},{48,32},{64,80},{80,64},{96,112},{112,96},{1... | collective-permute-start | bytes 786440 | tf_op jit(solution)/shard_map/ppermute | solution.py:340
  80.0 1.9 %collective-permute-start.22 = (f32[2,256,128]{2,1,0:T(8,128)S(1)}, f32[2,256,128]{2,1,0:T(8,128)S(1)}, u32[]{:S(2)}, u32[]{:S(2)}) collective-permute-start(f32[2,256,128]{2,1,0:T(8,128)S(1)} %get-tuple-element.66), channel_id=1, source_target_pairs={{16,32},{48,64},{80,96},{112,128},{144,160},{176,192},{208,224},{2... | collective-permute-start | bytes 786440 | tf_op jit(solution)/shard_map/ppermute | solution.py:339
  81.9 0.0 collective-permute-done.21.near
  81.9 5.8 %collective-permute-done.22.far = f32[2,256,128]{2,1,0:T(8,128)S(1)} collective-permute-done((f32[2,256,128]{2,1,0:T(8,128)S(1)}, f32[2,256,128]{2,1,0:T(8,128)S(1)}, u32[]{:S(2)}, u32[]{:S(2)}) %collective-permute-start.22) | collective-permute-done | bytes 262176 | tf_op jit(solution)/shard_map/ppermute | solution.py:339
  87.7 0.0 copy-done.2
  87.7 0.8 last.1
  (3 shorter events, 0.0 us)
Async XLA Ops:
  0.0 10.6 %copy-start.5 = (s32[2]{0:T(128)S(1)}, s32[2]{0:T(128)}, u32[]{:S(2)}) copy-start(s32[2]{0:T(128)} %owners.3) | copy-start | bytes 28
  0.0 10.6 %copy-start.6 = (s32[2]{0:T(128)S(1)}, s32[2]{0:T(128)}, u32[]{:S(2)}) copy-start(s32[2]{0:T(128)} %offsets.3) | copy-start | bytes 28
  0.0 28.8 %copy-start = (f32[2,128,128]{2,1,0:T(8,128)S(1)}, f32[2,128,128]{2,1,0:T(8,128)}, u32[]{:S(2)}) copy-start(f32[2,128,128]{2,1,0:T(8,128)} %constant.4.clone.table_ref) | copy-start | bytes 393220
  0.0 8.7 %collective-permute-start.1 = (f32[2,256,128]{2,1,0:T(8,128)}, f32[2,256,128]{2,1,0:T(8,128)S(1)}, u32[]{:S(2)}, u32[]{:S(2)}) collective-permute-start(f32[2,256,128]{2,1,0:T(8,128)} %bitcast.1), channel_id=1, source_target_pairs={{0,16},{16,0},{32,48},{48,32},{64,80},{80,64},{96,112},{112,96},{1... | collective-permute-start | bytes 786440 | tf_op jit(solution)/shard_map/ppermute | solution.py:289
  2.7 7.9 %collective-permute-start = (f32[2,256,128]{2,1,0:T(8,128)}, f32[2,256,128]{2,1,0:T(8,128)S(1)}, u32[]{:S(2)}, u32[]{:S(2)}) collective-permute-start(f32[2,256,128]{2,1,0:T(8,128)} %bitcast.2), channel_id=1, source_target_pairs={{16,32},{48,64},{80,96},{112,128},{144,160},{176,192},{208,224},{2... | collective-permute-start | bytes 786440 | tf_op jit(solution)/shard_map/ppermute | solution.py:288
  6.2 2.5 %collective-permute-start.2 = (f32[2,128,128]{2,1,0:T(8,128)}, f32[2,128,128]{2,1,0:T(8,128)S(1)}, u32[]{:S(2)}, u32[]{:S(2)}) collective-permute-start(f32[2,128,128]{2,1,0:T(8,128)} %param.9), channel_id=1, source_target_pairs={{0,16},{1,17},{22,6},{23,7},{32,48},{33,49},{54,38},{55,39},{64,80... | collective-permute-start | bytes 393224 | tf_op jit(solution)/shard_map/ppermute | solution.py:290
  10.6 1.0 %copy-start.1 = (f32[1,2,256,128]{3,2,1,0:T(8,128)S(1)}, f32[1,2,256,128]{3,2,1,0:T(8,128)}, u32[]{:S(2)}) copy-start(f32[1,2,256,128]{3,2,1,0:T(8,128)} %param.7) | copy-start | bytes 786436
  11.6 17.2 %copy-start.4 = (f32[2,128,128]{2,1,0:T(8,128)S(1)}, f32[2,128,128]{2,1,0:T(8,128)}, u32[]{:S(2)}) copy-start(f32[2,128,128]{2,1,0:T(8,128)} %probe.1) | copy-start | bytes 393220
  12.2 6.9 %collective-permute-start.6 = (f32[2,128,128]{2,1,0:T(8,128)S(1)}, f32[2,128,128]{2,1,0:T(8,128)S(1)}, u32[]{:S(2)}, u32[]{:S(2)}) collective-permute-start(f32[2,128,128]{2,1,0:T(8,128)S(1)} %get-tuple-element.39), channel_id=1, source_target_pairs={{3,0},{11,16},{2,1},{10,17},{19,22},{27,6},{18,23},{26,7},{35,32},... | collective-permute-start | bytes 393224 | tf_op jit(solution)/shard_map/ppermute | solution.py:300
  13.5 6.9 %collective-permute-start.4 = (f32[2,128,128]{2,1,0:T(8,128)S(1)}, f32[2,128,128]{2,1,0:T(8,128)S(1)}, u32[]{:S(2)}, u32[]{:S(2)}) collective-permute-start(f32[2,128,128]{2,1,0:T(8,128)S(1)} %get-tuple-element.39), channel_id=1, source_target_pairs={{1,0},{9,16},{0,1},{8,17},{17,22},{25,6},{16,23},{24,7},{33,32},{4... | collective-permute-start | bytes 393224 | tf_op jit(solution)/shard_map/ppermute | solution.py:300
  14.8 12.6 %collective-permute-start.7 = (f32[2,128,128]{2,1,0:T(8,128)S(1)}, f32[2,128,128]{2,1,0:T(8,128)S(1)}, u32[]{:S(2)}, u32[]{:S(2)}) collective-permute-start(f32[2,128,128]{2,1,0:T(8,128)S(1)} %get-tuple-element.38.own), channel_id=1, source_target_pairs={{4,0},{12,16},{5,1},{13,17},{18,22},{26,6},{19,23},{27,7},{36,32},... | collective-permute-start | bytes 393224 | tf_op jit(solution)/shard_map/ppermute | solution.py:300
  16.1 12.6 %collective-permute-start.5 = (f32[2,128,128]{2,1,0:T(8,128)S(1)}, f32[2,128,128]{2,1,0:T(8,128)S(1)}, u32[]{:S(2)}, u32[]{:S(2)}) collective-permute-start(f32[2,128,128]{2,1,0:T(8,128)S(1)} %get-tuple-element.38.own), channel_id=1, source_target_pairs={{2,0},{10,16},{3,1},{11,17},{16,22},{24,6},{17,23},{25,7},{34,32},... | collective-permute-start | bytes 393224 | tf_op jit(solution)/shard_map/ppermute | solution.py:300
  17.4 11.4 %collective-permute-start.3 = (f32[2,128,128]{2,1,0:T(8,128)S(1)}, f32[2,128,128]{2,1,0:T(8,128)S(1)}, u32[]{:S(2)}, u32[]{:S(2)}) collective-permute-start(f32[2,128,128]{2,1,0:T(8,128)S(1)} %get-tuple-element.38.own), channel_id=1, source_target_pairs={{8,16},{9,17},{30,6},{31,7},{40,48},{41,49},{62,38},{63,39},{72,80... | collective-permute-start | bytes 393224 | tf_op jit(solution)/shard_map/ppermute | solution.py:300
  19.1 11.5 %collective-permute-start.10 = (f32[2,128,128]{2,1,0:T(8,128)S(1)}, f32[2,128,128]{2,1,0:T(8,128)S(1)}, u32[]{:S(2)}, u32[]{:S(2)}) collective-permute-start(f32[2,128,128]{2,1,0:T(8,128)S(1)} %get-tuple-element.39), channel_id=1, source_target_pairs={{7,0},{15,16},{6,1},{14,17},{21,22},{29,6},{20,23},{28,7},{39,32},... | collective-permute-start | bytes 393224 | tf_op jit(solution)/shard_map/ppermute | solution.py:300
  20.4 10.2 %collective-permute-start.8 = (f32[2,128,128]{2,1,0:T(8,128)S(1)}, f32[2,128,128]{2,1,0:T(8,128)S(1)}, u32[]{:S(2)}, u32[]{:S(2)}) collective-permute-start(f32[2,128,128]{2,1,0:T(8,128)S(1)} %get-tuple-element.39), channel_id=1, source_target_pairs={{5,0},{13,16},{4,1},{12,17},{23,22},{31,6},{22,23},{30,7},{37,32},... | collective-permute-start | bytes 393224 | tf_op jit(solution)/shard_map/ppermute | solution.py:300
  27.5 7.5 %collective-permute-start.9 = (f32[2,128,128]{2,1,0:T(8,128)S(1)}, f32[2,128,128]{2,1,0:T(8,128)S(1)}, u32[]{:S(2)}, u32[]{:S(2)}) collective-permute-start(f32[2,128,128]{2,1,0:T(8,128)S(1)} %get-tuple-element.38.own), channel_id=1, source_target_pairs={{6,0},{14,16},{7,1},{15,17},{20,22},{28,6},{21,23},{29,7},{38,32},... | collective-permute-start | bytes 393224 | tf_op jit(solution)/shard_map/ppermute | solution.py:300
  35.0 5.8 %copy-start.3 = (f32[2,128,128]{2,1,0:T(8,128)S(1)}, f32[2,128,128]{2,1,0:T(8,128)}, u32[]{:S(2)}) copy-start(f32[2,128,128]{2,1,0:T(8,128)} %constant.5.clone.fourier_ref) | copy-start | bytes 393220
  36.8 4.0 %collective-permute-start.11 = (f32[2,128,128]{2,1,0:T(8,128)S(1)}, f32[2,128,128]{2,1,0:T(8,128)S(1)}, u32[]{:S(2)}, u32[]{:S(2)}) collective-permute-start(f32[2,128,128]{2,1,0:T(8,128)S(1)} %get-tuple-element.41), channel_id=1, source_target_pairs={{0,16},{1,17},{22,6},{23,7},{32,48},{33,49},{54,38},{55,39},{64,80... | collective-permute-start | bytes 393224 | tf_op jit(solution)/shard_map/ppermute | solution.py:314
  47.9 3.2 %collective-permute-start.12 = (f32[2,128,128]{2,1,0:T(8,128)S(1)}, f32[2,128,128]{2,1,0:T(8,128)S(1)}, u32[]{:S(2)}, u32[]{:S(2)}) collective-permute-start(f32[2,128,128]{2,1,0:T(8,128)S(1)} %get-tuple-element.45), channel_id=1, source_target_pairs={{16,0},{17,1},{6,22},{7,23},{48,32},{49,33},{38,54},{39,55},{80,64... | collective-permute-start | bytes 393224 | tf_op jit(solution)/shard_map/ppermute | solution.py:322
  49.2 17.2 %collective-permute-start.13 = (f32[2,128,128]{2,1,0:T(8,128)S(1)}, f32[2,128,128]{2,1,0:T(8,128)S(1)}, u32[]{:S(2)}, u32[]{:S(2)}) collective-permute-start(f32[2,128,128]{2,1,0:T(8,128)S(1)} %get-tuple-element.48.rest_0_), channel_id=1, source_target_pairs={{16,8},{17,9},{6,30},{7,31},{48,40},{49,41},{38,62},{39,63},{80,72... | collective-permute-start | bytes 393224 | tf_op jit(solution)/shard_map/ppermute | solution.py:323
  54.2 14.4 %collective-permute-start.14 = (f32[2,128,128]{2,1,0:T(8,128)S(1)}, f32[2,128,128]{2,1,0:T(8,128)S(1)}, u32[]{:S(2)}, u32[]{:S(2)}) collective-permute-start(f32[2,128,128]{2,1,0:T(8,128)S(1)} %get-tuple-element.57), channel_id=1, source_target_pairs={{0,1},{16,9},{1,0},{17,8},{22,17},{6,25},{23,16},{7,24},{32,33},{4... | collective-permute-start | bytes 393224 | tf_op jit(solution)/shard_map/ppermute | solution.py:331
  60.3 9.6 %collective-permute-start.15 = (f32[2,128,128]{2,1,0:T(8,128)S(1)}, f32[2,128,128]{2,1,0:T(8,128)S(1)}, u32[]{:S(2)}, u32[]{:S(2)}) collective-permute-start(f32[2,128,128]{2,1,0:T(8,128)S(1)} %get-tuple-element.58), channel_id=1, source_target_pairs={{0,2},{16,10},{1,3},{17,11},{22,16},{6,24},{23,17},{7,25},{32,34},... | collective-permute-start | bytes 393224 | tf_op jit(solution)/shard_map/ppermute | solution.py:331
  63.8 7.4 %collective-permute-start.16 = (f32[2,128,128]{2,1,0:T(8,128)S(1)}, f32[2,128,128]{2,1,0:T(8,128)S(1)}, u32[]{:S(2)}, u32[]{:S(2)}) collective-permute-start(f32[2,128,128]{2,1,0:T(8,128)S(1)} %get-tuple-element.59), channel_id=1, source_target_pairs={{0,3},{16,11},{1,2},{17,10},{22,19},{6,27},{23,18},{7,26},{32,35},... | collective-permute-start | bytes 393224 | tf_op jit(solution)/shard_map/ppermute | solution.py:331
  65.1 6.1 %collective-permute-start.17 = (f32[2,128,128]{2,1,0:T(8,128)S(1)}, f32[2,128,128]{2,1,0:T(8,128)S(1)}, u32[]{:S(2)}, u32[]{:S(2)}) collective-permute-start(f32[2,128,128]{2,1,0:T(8,128)S(1)} %get-tuple-element.60), channel_id=1, source_target_pairs={{0,4},{16,12},{1,5},{17,13},{22,18},{6,26},{23,19},{7,27},{32,36},... | collective-permute-start | bytes 393224 | tf_op jit(solution)/shard_map/ppermute | solution.py:331
  66.4 6.0 %collective-permute-start.18 = (f32[2,128,128]{2,1,0:T(8,128)S(1)}, f32[2,128,128]{2,1,0:T(8,128)S(1)}, u32[]{:S(2)}, u32[]{:S(2)}) collective-permute-start(f32[2,128,128]{2,1,0:T(8,128)S(1)} %get-tuple-element.61), channel_id=1, source_target_pairs={{0,5},{16,13},{1,4},{17,12},{22,23},{6,31},{23,22},{7,30},{32,37},... | collective-permute-start | bytes 393224 | tf_op jit(solution)/shard_map/ppermute | solution.py:331
  68.6 3.8 %collective-permute-start.19 = (f32[2,128,128]{2,1,0:T(8,128)S(1)}, f32[2,128,128]{2,1,0:T(8,128)S(1)}, u32[]{:S(2)}, u32[]{:S(2)}) collective-permute-start(f32[2,128,128]{2,1,0:T(8,128)S(1)} %get-tuple-element.62), channel_id=1, source_target_pairs={{0,6},{16,14},{1,7},{17,15},{22,20},{6,28},{23,21},{7,29},{32,38},... | collective-permute-start | bytes 393224 | tf_op jit(solution)/shard_map/ppermute | solution.py:331
  69.9 4.3 %collective-permute-start.20 = (f32[2,128,128]{2,1,0:T(8,128)S(1)}, f32[2,128,128]{2,1,0:T(8,128)S(1)}, u32[]{:S(2)}, u32[]{:S(2)}) collective-permute-start(f32[2,128,128]{2,1,0:T(8,128)S(1)} %get-tuple-element.63), channel_id=1, source_target_pairs={{0,7},{16,15},{1,6},{17,14},{22,21},{6,29},{23,20},{7,28},{32,39},... | collective-permute-start | bytes 393224 | tf_op jit(solution)/shard_map/ppermute | solution.py:331
  74.2 13.5 %copy-start.2 = (f32[1,2,256,128]{3,2,1,0:T(8,128)S(1)}, f32[1,2,256,128]{3,2,1,0:T(8,128)}, u32[]{:S(2)}) copy-start(f32[1,2,256,128]{3,2,1,0:T(8,128)} %param.7) | copy-start | bytes 786436
  74.9 7.0 %collective-permute-start.21 = (f32[2,256,128]{2,1,0:T(8,128)S(1)}, f32[2,256,128]{2,1,0:T(8,128)S(1)}, u32[]{:S(2)}, u32[]{:S(2)}) collective-permute-start(f32[2,256,128]{2,1,0:T(8,128)S(1)} %get-tuple-element.65), channel_id=1, source_target_pairs={{0,16},{16,0},{32,48},{48,32},{64,80},{80,64},{96,112},{112,96},{1... | collective-permute-start | bytes 786440 | tf_op jit(solution)/shard_map/ppermute | solution.py:340
  80.0 7.7 %collective-permute-start.22 = (f32[2,256,128]{2,1,0:T(8,128)S(1)}, f32[2,256,128]{2,1,0:T(8,128)S(1)}, u32[]{:S(2)}, u32[]{:S(2)}) collective-permute-start(f32[2,256,128]{2,1,0:T(8,128)S(1)} %get-tuple-element.66), channel_id=1, source_target_pairs={{16,32},{48,64},{80,96},{112,128},{144,160},{176,192},{208,224},{2... | collective-permute-start | bytes 786440 | tf_op jit(solution)/shard_map/ppermute | solution.py:339

commit v3 on v2

v3 whole, which is shorter than its diff:
```python
import functools

import jax
import jax.numpy as jnp
import numpy as np
from jax import lax
from jax.experimental import pallas as pl
from jax.experimental.pallas import tpu as pltpu
from jax.sharding import PartitionSpec as P

step_size = 0.25
side = 128
tile = 256
group = 4
long_cost = pl.CostEstimate(flops=2 * 10**10, bytes_accessed=2**25, transcendentals=0)
params = pltpu.CompilerParams(vmem_limit_bytes=48 * 2**20)
in_vmem = pl.BlockSpec(memory_space=pltpu.VMEM)
in_smem = pl.BlockSpec(memory_space=pltpu.SMEM)
window_type = jax.ShapeDtypeStruct((2, side, side), jnp.float32)
tile_type = jax.ShapeDtypeStruct((2, tile, side), jnp.float32)
slab_type = jax.ShapeDtypeStruct((2, 3 * tile, side), jnp.float32)
stack_type = jax.ShapeDtypeStruct((group, 2, side, side), jnp.float32)


def tables():
    index = np.arange(side)
    angles = 2.0 * np.pi * (index[:, None] * index[None, :] % side) / side
    fourier = (np.cos(angles) - 1j * np.sin(angles)) / np.sqrt(side)
    frequency = np.where(index < side // 2, index, index - side).astype(np.float64)
    phase = np.exp(-1j * np.pi / side * frequency * frequency)
    step = np.conj(fourier) @ (phase[:, None] * fourier)
    return [np.stack([m.real, m.imag]).astype(np.float32) for m in (step, fourier)]


def split(x):
    high = x.astype(jnp.bfloat16)
    return high, (x - high.astype(jnp.float32)).astype(jnp.bfloat16)


def dot(a, b):
    return jnp.dot(a, b, preferred_element_type=jnp.float32)


def beside(*parts):
    return jnp.concatenate(parts, 1)


def above(*parts):
    return jnp.concatenate(parts, 0)


def blocks(ref):
    real, imag = split(ref[0]), split(ref[1])
    left = [above(beside(r, -i), beside(i, r)) for r, i in zip(real, imag)]
    right = [above(beside(r, i), beside(-i, r)) for r, i in zip(real, imag)]
    return left, right


def two_sided(wave, table):
    (left_high, left_low), (right_high, right_low) = table
    high, low = split(above(*wave))
    both = dot(left_high, beside(high, low))
    left = both[:, :side] + both[:, side:] + dot(left_low, high)
    high, low = split(beside(left[:side], left[side:]))
    done = dot(high, right_high) + (dot(low, right_high) + dot(high, right_low))
    return done[:, :side], done[:, side:]


def times(a, b):
    return a[0] * b[0] - a[1] * b[1], a[0] * b[1] + a[1] * b[0]


def pair(ref, *at):
    return ref[(*at, 0)], ref[(*at, 1)]


def put(ref, value, *at):
    ref[(*at, 0)] = value[0]
    ref[(*at, 1)] = value[1]


def role():
    depth, scan = lax.axis_index("depth"), lax.axis_index("scan")
    row, column = depth // group, depth % group
    home = (column // 2) == (scan & 1)
    first, last = row == 0, row == group - 1
    return jnp.where(first, jnp.where(home, 0, 1), jnp.where(last, jnp.where(home, 3, 2), -1))


def column():
    return lax.axis_index("depth") % group


def start_of(at, owners, offsets):
    start = (owners[at] - lax.axis_index("scan") + 1) * tile + offsets[at]
    return jnp.clip(start, 0, 2 * tile)


def stage_kernel(block, top, bottom):
    top[...] = block[:, :side]
    bottom[...] = block[:, side:]


def by_scan_parity(even, odd):
    even_scan = (lax.axis_index("scan") & 1) == 0
    pl.when(even_scan)(even)
    pl.when(jnp.logical_not(even_scan))(odd)


def cut_kernel(owners, offsets, block, near_top, near_bottom, far, odd_out, even_out, slab):
    slab[:, tile : 2 * tile] = block[0]

    def even():
        slab[:, :tile] = far[...]
        slab[:, 2 * tile : 2 * tile + side] = near_top[...]

    def odd():
        slab[:, :side] = near_top[...]
        slab[:, side:tile] = near_bottom[...]
        slab[:, 2 * tile :] = far[...]

    by_scan_parity(even, odd)
    odd_position = 1 - (lax.axis_index("depth") & 1)
    for at, out in ((odd_position, odd_out), (1 - odd_position, even_out)):
        out[...] = slab[:, pl.ds(start_of(at, owners, offsets), side), :]


def collect(arrived, windows):
    me = column()
    for turn in range(group):
        windows[me ^ turn] = arrived[turn][...]


def forward_kernel(mine, wave_in, zero, one, two, three, table_ref, *rest):
    wave_out, waves, windows = rest[-3:]

    @pl.when(role() == mine)
    def _():
        collect((zero, one, two, three), windows)
        table = blocks(table_ref)
        wave = pair(wave_in)
        for layer in range(group):
            put(waves, wave, layer)
            wave = two_sided(times(wave, pair(windows, layer)), table)
        put(wave_out, wave)


def backward(adjoint, waves, windows, updates, table, last):
    for layer in reversed(range(group)):
        real, imag = times(pair(waves, layer), adjoint)
        put(updates, (real, -imag), layer)
        if layer or not last:
            adjoint = two_sided(times(pair(windows, layer), adjoint), table)
    return adjoint


def share(updates, parts):
    me = column()
    for turn in range(group):
        parts[turn][...] = updates[me ^ turn]


def far_kernel(wave_in, zero, one, two, three, measured, table_ref, fourier_ref, *rest):
    adjoint_out, parts, (waves, windows, updates) = rest[0], rest[1 : 1 + group], rest[1 + group :]

    @pl.when(role() == group - 1)
    def _():
        collect((zero, one, two, three), windows)
        table, fourier = blocks(table_ref), blocks(fourier_ref)
        wave = pair(wave_in)
        for layer in range(group):
            put(waves, wave, layer)
            last = layer == group - 1
            wave = two_sided(times(wave, pair(windows, layer)), fourier if last else table)
        far_real, far_imag = wave
        residual = far_real * far_real + far_imag * far_imag - measured[column() & 1]
        adjoint = two_sided((residual * far_real, -(residual * far_imag)), fourier)
        put(adjoint_out, backward(adjoint, waves, windows, updates, table, False))
        share(updates, parts)


def backward_kernel(mine, adjoint_in, waves, windows, table_ref, *rest):
    adjoint_out, parts, updates = rest[group], rest[group + 1 : -1], rest[-1]

    @pl.when(role() == mine)
    def _():
        adjoint = backward(
            pair(adjoint_in), waves, windows, updates, blocks(table_ref), mine == 0
        )
        if mine:
            put(adjoint_out, adjoint)
        share(updates, parts)


def place_kernel(owners, offsets, own, zero, one, two, three, slab, far):
    slab[...] = jnp.zeros_like(slab)
    local = (role() == 0) | (role() == group - 1)
    odd = one[...] + three[...]
    even = two[...] + jnp.where(local, own[...], zero[...])
    odd_position = 1 - (lax.axis_index("depth") & 1)
    for at, update in ((odd_position, odd), (1 - odd_position, even)):
        rows = pl.ds(start_of(at, owners, offsets), side)
        slab[:, rows, :] = slab[:, rows, :] + update

    def even_scan():
        far[...] = slab[:, :tile]

    def odd_scan():
        far[...] = slab[:, 2 * tile :]

    by_scan_parity(even_scan, odd_scan)


def near_kernel(slab, near_top, near_bottom):
    def even_scan():
        near_top[...] = slab[:, 2 * tile : 2 * tile + side]

    def odd_scan():
        near_top[...] = slab[:, :side]
        near_bottom[...] = slab[:, side:tile]

    by_scan_parity(even_scan, odd_scan)


def last_kernel(block, slab, near_top, near_bottom, far, out):
    for half, near in enumerate((near_top, near_bottom)):
        rows = slice(half * side, (half + 1) * side)
        mine = slab[:, tile + half * side : tile + (half + 1) * side]
        out[0, :, rows] = block[0, :, rows] - step_size * (mine + near[...] + far[:, rows])


def shards(object_slices, probe_wave, intensities, offsets, owners):
    scans = lax.axis_size("scan")
    depths = lax.axis_size("depth")
    axes = ("scan", "depth")
    step_table, fourier_table = tables()
    bottom = depths - group

    def call(kernel, name, out_shape, arguments, scratch=(), aliases=(), cost=None):
        specs = [in_smem if a.dtype == jnp.int32 else in_vmem for a in arguments]
        return pl.pallas_call(
            kernel,
            out_shape=out_shape,
            in_specs=specs,
            out_specs=jax.tree.map(lambda _: in_vmem, out_shape),
            scratch_shapes=[pltpu.VMEM(kind.shape, jnp.float32) for kind in scratch],
            input_output_aliases=dict(aliases),
            compiler_params=params,
            cost_estimate=cost,
            name=name,
        )(*arguments)

    def at(scan, depth):
        return scan * depths + depth

    def ends(pairs):
        return [(b, a) for a, b in pairs]

    targets = [(i, 2 * (i & 1) + q) for i in range(scans) for q in range(2)]
    gathers = []
    for turn in range(group):
        pairs = []
        for i, x in targets:
            source = x ^ turn
            if turn:
                pairs.append((at(i, source), at(i, x)))
                pairs.append((at(i, bottom + source), at(i, bottom + x)))
            pairs.append((at(i, group + source), at(i ^ 1, x)))
            pairs.append((at(i, 2 * group + source), at(i ^ 1, bottom + x)))
        gathers.append(pairs)
    hops = [
        [(at(i, x), at(i ^ 1, x)) for i, x in targets],
        [(at(i ^ 1, x), at(i ^ 1, bottom + x)) for i, x in targets],
        [(at(i ^ 1, bottom + x), at(i, bottom + x)) for i, x in targets],
    ]
    on_chip = [(i, i ^ 1) for i in range(scans)]
    downward = [(i, i + 1) for i in range(0, scans, 2)]
    next_chip = [(i, i + 1) for i in range(1, scans - 1, 2)]
    next_chip = next_chip + ends(next_chip)

    far = lax.ppermute(object_slices[0], "scan", next_chip)
    near_top, near_bottom = call(
        stage_kernel, "stage", [window_type] * 2, (object_slices[0],), cost=long_cost
    )
    near_top = lax.ppermute(near_top, "scan", on_chip)
    near_bottom = lax.ppermute(near_bottom, "scan", downward)
    odd_window, even_window = call(
        cut_kernel,
        "cut",
        [window_type] * 2,
        (owners, offsets, object_slices, near_top, near_bottom, far),
        [slab_type],
    )
    come = [
        lax.ppermute(odd_window if turn & 1 else even_window, axes, gathers[turn])
        for turn in (1, 2, 3, 0)
    ]
    late = come.pop()

    wave, waves, windows = call(
        functools.partial(forward_kernel, 0),
        "first",
        [window_type, stack_type, stack_type],
        (probe_wave, even_window, *come, step_table),
    )
    for mine, name in ((1, "second"), (2, "third")):
        wave = lax.ppermute(wave, axes, hops[mine - 1])
        wave, waves, windows = call(
            functools.partial(forward_kernel, mine),
            name,
            [window_type, stack_type, stack_type],
            (wave, late, *come, step_table, waves, windows),
            aliases=((6, 1), (7, 2)),
        )
    wave = lax.ppermute(wave, axes, hops[2])
    adjoint, *parts = call(
        far_kernel,
        "far",
        [window_type] * (1 + group),
        (wave, even_window, *come, intensities, step_table, fourier_table),
        [stack_type] * 3,
    )
    first_back = None
    for mine, name in ((2, "back_third"), (1, "back_second"), (0, "back_first")):
        adjoint = lax.ppermute(adjoint, axes, ends(hops[mine]))
        if mine == 0:
            first_back = lax.ppermute(parts[0], axes, ends(gathers[0]))
        adjoint, *parts = call(
            functools.partial(backward_kernel, mine),
            name,
            [window_type] * (1 + group),
            (adjoint, waves, windows, step_table, *parts),
            [stack_type],
            aliases=[(4 + turn, 1 + turn) for turn in range(group)],
        )
    landed = [
        lax.ppermute(parts[turn], axes, ends(gathers[turn])) for turn in range(1, group)
    ]
    slab, far = call(
        place_kernel,
        "place",
        [slab_type, tile_type],
        (owners, offsets, parts[0], first_back, *landed),
    )
    far = lax.ppermute(far, "scan", next_chip)
    near_top, near_bottom = call(
        near_kernel, "near", [window_type] * 2, (slab,), cost=long_cost
    )
    near_top = lax.ppermute(near_top, "scan", on_chip)
    near_bottom = lax.ppermute(near_bottom, "scan", ends(downward))
    return call(
        last_kernel,
        "last",
        jax.ShapeDtypeStruct(object_slices.shape, jnp.float32),
        (object_slices, slab, near_top, near_bottom, far),
    )


def solution(mesh):
    return jax.shard_map(
        shards,
        mesh=mesh,
        in_specs=(P("depth", None, "scan", None), P(), P("scan", None, None), P("scan"), P("scan")),
        out_specs=P("depth", None, "scan", None),
        check_vma=False,
    )
```

time: 89 us -> 88.1 us (0.990)
  the two profiles are of different devices: /device:TPU:13 before, /device:TPU:97 now
where the time goes in v3:
time: 88.1 us; the launch traced here: 87.6 us
  starting transfers between devices  40.9 us (46%)
  waiting for transfers between devices  39 us (44%)
  Pallas kernels  6.28 us (7%)
  local copies, waits for them, and re-layouts  1.14 us (1%)
    ppermute x3, waiting for transfers between devices, shards(): adjoint = lax.ppermute(adjoint, axes, ends(hops[mine]))  15.8 us
    ppermute x4, starting transfers between devices, shards(): lax.ppermute(odd_window if turn & 1 else even_window, axes, gathers[turn])  10.1 us
    ppermute x3, waiting for transfers between devices, shards(): lax.ppermute(parts[turn], axes, ends(gathers[turn]))  8.65 us
    ppermute x3, starting transfers between devices, shards(): lax.ppermute(parts[turn], axes, ends(gathers[turn]))  7.85 us
    pallas_call x12, Pallas kernels, call(): pl.pallas_call(kernel, out_shape=out_shape, in_specs=specs, out_specs=jax...  6.28 us
    ppermute x1, starting transfers between devices, shards(): far = lax.ppermute(object_slices[0], 'scan', next_chip)  5.31 us
    ppermute x4, waiting for transfers between devices, shards(): lax.ppermute(odd_window if turn & 1 else even_window, axes, gathers[turn])  4.39 us
    ppermute x2, starting transfers between devices, shards(): near_top = lax.ppermute(near_top, 'scan', on_chip)  3.97 us
  transfers between devices with their start and end apart: 20, of which 11 were waited for; matrix products, arithmetic and copies ran while one was open for 0% of the time, Pallas kernels for 0%

profile of v3, /device:TPU:97, one launch (start us, length us, event | category | flops | bytes accessed | tf_op | source)
XLA Modules:
  0.0 87.6 jit_solution(2689244278757057944)
XLA Ops:
  0.0 5.3 %collective-permute-start.2 = (f32[2,256,128]{2,1,0:T(8,128)}, f32[2,256,128]{2,1,0:T(8,128)S(1)}, u32[]{:S(2)}, u32[]{:S(2)}) collective-permute-start(f32[2,256,128]{2,1,0:T(8,128)} %bitcast.1), channel_id=1, source_target_pairs={{16,32},{48,64},{80,96},{112,128},{144,160},{176,192},{208,224},{2... | collective-permute-start | bytes 786440 | tf_op jit(solution)/shard_map/ppermute | solution.py:281
  5.3 0.0 copy-start.1
  5.3 0.9 %copy-done.1 = f32[1,2,256,128]{3,2,1,0:T(8,128)S(1)} copy-done((f32[1,2,256,128]{3,2,1,0:T(8,128)S(1)}, f32[1,2,256,128]{3,2,1,0:T(8,128)}, u32[]{:S(2)}) %copy-start.1) | copy-done | bytes 262168
  6.3 0.0 copy-start.6
  6.3 0.0 copy-start.7
  6.3 1.9 %collective-permute-start = (f32[2,128,128]{2,1,0:T(8,128)S(1)}, f32[2,128,128]{2,1,0:T(8,128)S(1)}, u32[]{:S(2)}, u32[]{:S(2)}) collective-permute-start(f32[2,128,128]{2,1,0:T(8,128)S(1)} %get-tuple-element.41), channel_id=1, source_target_pairs={{0,16},{16,0},{32,48},{48,32},{64,80},{80,64},{96,112},{112,96},{1... | collective-permute-start | bytes 393224 | tf_op jit(solution)/shard_map/ppermute | solution.py:285
  8.3 0.0 copy-start
  8.3 0.0 copy-start.3
  8.3 1.4 %collective-permute-start.1 = (f32[2,128,128]{2,1,0:T(8,128)S(1)}, f32[2,128,128]{2,1,0:T(8,128)S(1)}, u32[]{:S(2)}, u32[]{:S(2)}) collective-permute-start(f32[2,128,128]{2,1,0:T(8,128)S(1)} %get-tuple-element.42), channel_id=1, source_target_pairs={{0,16},{32,48},{64,80},{96,112},{128,144},{160,176},{192,208},{224... | collective-permute-start | bytes 393224 | tf_op jit(solution)/shard_map/ppermute | solution.py:286
  9.7 0.0 collective-permute-done.near_top
  9.7 1.9 %collective-permute-done.1.near_bottom = f32[2,128,128]{2,1,0:T(8,128)S(1)} collective-permute-done((f32[2,128,128]{2,1,0:T(8,128)S(1)}, f32[2,128,128]{2,1,0:T(8,128)S(1)}, u32[]{:S(2)}, u32[]{:S(2)}) %collective-permute-start.1) | collective-permute-done | bytes 131104 | tf_op jit(solution)/shard_map/ppermute | solution.py:286
  11.7 0.0 collective-permute-done.2.far
  11.7 0.0 copy-done.6
  11.7 0.0 copy-done.7
  11.7 0.6 cut.1
  12.3 4.4 %collective-permute-start.5 = (f32[2,128,128]{2,1,0:T(8,128)S(1)}, f32[2,128,128]{2,1,0:T(8,128)S(1)}, u32[]{:S(2)}, u32[]{:S(2)}) collective-permute-start(f32[2,128,128]{2,1,0:T(8,128)S(1)} %get-tuple-element.44), channel_id=1, source_target_pairs={{3,0},{15,12},{7,16},{11,28},{2,1},{14,13},{6,17},{10,29},{17,18},... | collective-permute-start | bytes 393224 | tf_op jit(solution)/shard_map/ppermute | solution.py:295
  16.7 1.3 %collective-permute-start.3 = (f32[2,128,128]{2,1,0:T(8,128)S(1)}, f32[2,128,128]{2,1,0:T(8,128)S(1)}, u32[]{:S(2)}, u32[]{:S(2)}) collective-permute-start(f32[2,128,128]{2,1,0:T(8,128)S(1)} %get-tuple-element.44), channel_id=1, source_target_pairs={{1,0},{13,12},{5,16},{9,28},{0,1},{12,13},{4,17},{8,29},{19,18},{3... | collective-permute-start | bytes 393224 | tf_op jit(solution)/shard_map/ppermute | solution.py:295
  18.0 3.1 %collective-permute-start.4 = (f32[2,128,128]{2,1,0:T(8,128)S(1)}, f32[2,128,128]{2,1,0:T(8,128)S(1)}, u32[]{:S(2)}, u32[]{:S(2)}) collective-permute-start(f32[2,128,128]{2,1,0:T(8,128)S(1)} %get-tuple-element.43.zero), channel_id=1, source_target_pairs={{2,0},{14,12},{6,16},{10,28},{3,1},{15,13},{7,17},{11,29},{16,18},... | collective-permute-start | bytes 393224 | tf_op jit(solution)/shard_map/ppermute | solution.py:295
  21.1 1.3 %collective-permute-start.7 = (f32[2,128,128]{2,1,0:T(8,128)S(1)}, f32[2,128,128]{2,1,0:T(8,128)S(1)}, u32[]{:S(2)}, u32[]{:S(2)}) collective-permute-start(f32[2,128,128]{2,1,0:T(8,128)S(1)} %get-tuple-element.43.zero), channel_id=1, source_target_pairs={{4,16},{8,28},{5,17},{9,29},{22,2},{26,14},{23,3},{27,15},{36,48},... | collective-permute-start | bytes 393224 | tf_op jit(solution)/shard_map/ppermute | solution.py:295
  22.4 0.0 collective-permute-done.5.three
  22.4 2.7 %collective-permute-done.3.one = f32[2,128,128]{2,1,0:T(8,128)S(1)} collective-permute-done((f32[2,128,128]{2,1,0:T(8,128)S(1)}, f32[2,128,128]{2,1,0:T(8,128)S(1)}, u32[]{:S(2)}, u32[]{:S(2)}) %collective-permute-start.3) | collective-permute-done | bytes 131104 | tf_op jit(solution)/shard_map/ppermute | solution.py:295
  25.1 1.6 %collective-permute-done.4.two = f32[2,128,128]{2,1,0:T(8,128)S(1)} collective-permute-done((f32[2,128,128]{2,1,0:T(8,128)S(1)}, f32[2,128,128]{2,1,0:T(8,128)S(1)}, u32[]{:S(2)}, u32[]{:S(2)}) %collective-permute-start.4) | collective-permute-done | bytes 131104 | tf_op jit(solution)/shard_map/ppermute | solution.py:295
  26.8 0.0 copy-done
  26.8 0.0 copy-done.3
  26.8 1.3 %collective-permute-start.6 = (f32[2,128,128]{2,1,0:T(8,128)S(1)}, f32[2,128,128]{2,1,0:T(8,128)S(1)}, u32[]{:S(2)}, u32[]{:S(2)}) collective-permute-start(f32[2,128,128]{2,1,0:T(8,128)S(1)} %get-tuple-element.45), channel_id=1, source_target_pairs={{0,16},{1,17},{18,2},{19,3},{32,48},{33,49},{50,34},{51,35},{64,80... | collective-permute-start | bytes 393224 | tf_op jit(solution)/shard_map/ppermute | solution.py:307
  28.1 0.0 collective-permute-done.7.zero
  28.1 1.9 %collective-permute-done.6.wave_in = f32[2,128,128]{2,1,0:T(8,128)S(1)} collective-permute-done((f32[2,128,128]{2,1,0:T(8,128)S(1)}, f32[2,128,128]{2,1,0:T(8,128)S(1)}, u32[]{:S(2)}, u32[]{:S(2)}) %collective-permute-start.6) | collective-permute-done | bytes 131104 | tf_op jit(solution)/shard_map/ppermute | solution.py:307
  30.0 1.8 %second.1 = (f32[2,128,128]{2,1,0:T(8,128)S(1)}, f32[4,2,128,128]{3,2,1,0:T(8,128)S(1)}, f32[4,2,128,128]{3,2,1,0:T(8,128)S(1)}) custom-call(f32[2,128,128]{2,1,0:T(8,128)S(1)} %collective-permute-done.6.wave_in, f32[2,128,128]{2,1,0:T(8,128)S(1)} %collective-permute-done.7.zero, ...), custom_call_target="tpu_custom_call", output_to_operand_aliasing={{1}: (6, {}), {2}: (7, {})} | custom-call | tf_op jit(solution)/shard_map/second/pallas_call | solution.py:241
  31.8 1.3 %collective-permute-start.8 = (f32[2,128,128]{2,1,0:T(8,128)S(1)}, f32[2,128,128]{2,1,0:T(8,128)S(1)}, u32[]{:S(2)}, u32[]{:S(2)}) collective-permute-start(f32[2,128,128]{2,1,0:T(8,128)S(1)} %get-tuple-element.48), channel_id=1, source_target_pairs={{16,28},{17,29},{2,14},{3,15},{48,60},{49,61},{34,46},{35,47},{80,... | collective-permute-start | bytes 393224 | tf_op jit(solution)/shard_map/ppermute | solution.py:307
  33.1 1.9 %collective-permute-done.8.wave_in = f32[2,128,128]{2,1,0:T(8,128)S(1)} collective-permute-done((f32[2,128,128]{2,1,0:T(8,128)S(1)}, f32[2,128,128]{2,1,0:T(8,128)S(1)}, u32[]{:S(2)}, u32[]{:S(2)}) %collective-permute-start.8) | collective-permute-done | bytes 131104 | tf_op jit(solution)/shard_map/ppermute | solution.py:307
  35.0 0.0 copy-start.4
  35.0 0.0 copy-start.5
  35.0 0.8 collective-permute-start.9
  35.8 0.0 collective-permute-done.9.wave_in
  35.8 0.1 copy-done.4
  35.9 0.1 copy-done.5
  36.0 0.7 collective-permute-start.10
  36.6 0.0 collective-permute-done.10.adjoint_in
  36.7 1.3 %collective-permute-start.11 = (f32[2,128,128]{2,1,0:T(8,128)S(1)}, f32[2,128,128]{2,1,0:T(8,128)S(1)}, u32[]{:S(2)}, u32[]{:S(2)}) collective-permute-start(f32[2,128,128]{2,1,0:T(8,128)S(1)} %get-tuple-element.59), channel_id=1, source_target_pairs={{28,16},{29,17},{14,2},{15,3},{60,48},{61,49},{46,34},{47,35},{92,... | collective-permute-start | bytes 393224 | tf_op jit(solution)/shard_map/ppermute | solution.py:325
  38.0 15.8 %collective-permute-done.11.adjoint_in = f32[2,128,128]{2,1,0:T(8,128)S(1)} collective-permute-done((f32[2,128,128]{2,1,0:T(8,128)S(1)}, f32[2,128,128]{2,1,0:T(8,128)S(1)}, u32[]{:S(2)}, u32[]{:S(2)}) %collective-permute-start.11) | collective-permute-done | bytes 131104 | tf_op jit(solution)/shard_map/ppermute | solution.py:325
  53.8 1.7 %back_second.1 = (f32[2,128,128]{2,1,0:T(8,128)S(1)}, f32[2,128,128]{2,1,0:T(8,128)S(1)}, f32[2,128,128]{2,1,0:T(8,128)S(1)}, f32[2,128,128]{2,1,0:T(8,128)S(1)}, f32[2,128,128]{2,1,0:T(8,128)S(1)}) custom-call(f32[2,128,128]{2,1,0:T(8,128)S(1)} %collective-permute-done.11.adjoint_in, ...), custom_call_target="tpu_custom_call", output_to_operand_aliasing={{1}: (4, {}), {2}: (5, {}), {3}: (6, {}), {4}: (7, {})} | custom-call | tf_op jit(solution)/shard_map/back_second/pallas_call | solution.py:241
  55.5 1.3 %collective-permute-start.12 = (f32[2,128,128]{2,1,0:T(8,128)S(1)}, f32[2,128,128]{2,1,0:T(8,128)S(1)}, u32[]{:S(2)}, u32[]{:S(2)}) collective-permute-start(f32[2,128,128]{2,1,0:T(8,128)S(1)} %get-tuple-element.64), channel_id=1, source_target_pairs={{16,0},{17,1},{2,18},{3,19},{48,32},{49,33},{34,50},{35,51},{80,64... | collective-permute-start | bytes 393224 | tf_op jit(solution)/shard_map/ppermute | solution.py:325
  56.8 1.3 %collective-permute-start.13 = (f32[2,128,128]{2,1,0:T(8,128)S(1)}, f32[2,128,128]{2,1,0:T(8,128)S(1)}, u32[]{:S(2)}, u32[]{:S(2)}) collective-permute-start(f32[2,128,128]{2,1,0:T(8,128)S(1)} %get-tuple-element.65.rest_0_), channel_id=1, source_target_pairs={{16,4},{28,8},{17,5},{29,9},{2,22},{14,26},{3,23},{15,27},{48,36},... | collective-permute-start | bytes 393224 | tf_op jit(solution)/shard_map/ppermute | solution.py:327
  58.2 0.0 collective-permute-done.12.adjoint_in
  58.2 1.9 %collective-permute-done.13.zero = f32[2,128,128]{2,1,0:T(8,128)S(1)} collective-permute-done((f32[2,128,128]{2,1,0:T(8,128)S(1)}, f32[2,128,128]{2,1,0:T(8,128)S(1)}, u32[]{:S(2)}, u32[]{:S(2)}) %collective-permute-start.13) | collective-permute-done | bytes 131104 | tf_op jit(solution)/shard_map/ppermute | solution.py:327
  60.1 0.7 back_first.1
  60.7 4.0 %collective-permute-start.14 = (f32[2,128,128]{2,1,0:T(8,128)S(1)}, f32[2,128,128]{2,1,0:T(8,128)S(1)}, u32[]{:S(2)}, u32[]{:S(2)}) collective-permute-start(f32[2,128,128]{2,1,0:T(8,128)S(1)} %get-tuple-element.70), channel_id=1, source_target_pairs={{0,1},{12,13},{16,5},{28,9},{1,0},{13,12},{17,4},{29,8},{18,19},{3... | collective-permute-start | bytes 393224 | tf_op jit(solution)/shard_map/ppermute | solution.py:337
  64.7 1.9 %collective-permute-start.15 = (f32[2,128,128]{2,1,0:T(8,128)S(1)}, f32[2,128,128]{2,1,0:T(8,128)S(1)}, u32[]{:S(2)}, u32[]{:S(2)}) collective-permute-start(f32[2,128,128]{2,1,0:T(8,128)S(1)} %get-tuple-element.71), channel_id=1, source_target_pairs={{0,2},{12,14},{16,6},{28,10},{1,3},{13,15},{17,7},{29,11},{18,16},... | collective-permute-start | bytes 393224 | tf_op jit(solution)/shard_map/ppermute | solution.py:337
  66.7 1.9 %collective-permute-start.16 = (f32[2,128,128]{2,1,0:T(8,128)S(1)}, f32[2,128,128]{2,1,0:T(8,128)S(1)}, u32[]{:S(2)}, u32[]{:S(2)}) collective-permute-start(f32[2,128,128]{2,1,0:T(8,128)S(1)} %get-tuple-element.72), channel_id=1, source_target_pairs={{0,3},{12,15},{16,7},{28,11},{1,2},{13,14},{17,6},{29,10},{18,17},... | collective-permute-start | bytes 393224 | tf_op jit(solution)/shard_map/ppermute | solution.py:337
  68.6 0.0 collective-permute-done.14.one
  68.6 4.9 %collective-permute-done.15.two = f32[2,128,128]{2,1,0:T(8,128)S(1)} collective-permute-done((f32[2,128,128]{2,1,0:T(8,128)S(1)}, f32[2,128,128]{2,1,0:T(8,128)S(1)}, u32[]{:S(2)}, u32[]{:S(2)}) %collective-permute-start.15) | collective-permute-done | bytes 131104 | tf_op jit(solution)/shard_map/ppermute | solution.py:337
  73.5 3.8 %collective-permute-done.16.three = f32[2,128,128]{2,1,0:T(8,128)S(1)} collective-permute-done((f32[2,128,128]{2,1,0:T(8,128)S(1)}, f32[2,128,128]{2,1,0:T(8,128)S(1)}, u32[]{:S(2)}, u32[]{:S(2)}) %collective-permute-start.16) | collective-permute-done | bytes 131104 | tf_op jit(solution)/shard_map/ppermute | solution.py:337
  77.3 0.7 place.1
  77.9 1.9 %collective-permute-start.19 = (f32[2,256,128]{2,1,0:T(8,128)S(1)}, f32[2,256,128]{2,1,0:T(8,128)S(1)}, u32[]{:S(2)}, u32[]{:S(2)}) collective-permute-start(f32[2,256,128]{2,1,0:T(8,128)S(1)} %get-tuple-element.76), channel_id=1, source_target_pairs={{16,32},{48,64},{80,96},{112,128},{144,160},{176,192},{208,224},{2... | collective-permute-start | bytes 786440 | tf_op jit(solution)/shard_map/ppermute | solution.py:345
  79.9 0.0 copy-start.2
  79.9 2.1 %collective-permute-start.17 = (f32[2,128,128]{2,1,0:T(8,128)S(1)}, f32[2,128,128]{2,1,0:T(8,128)S(1)}, u32[]{:S(2)}, u32[]{:S(2)}) collective-permute-start(f32[2,128,128]{2,1,0:T(8,128)S(1)} %get-tuple-element.74), channel_id=1, source_target_pairs={{0,16},{16,0},{32,48},{48,32},{64,80},{80,64},{96,112},{112,96},{1... | collective-permute-start | bytes 393224 | tf_op jit(solution)/shard_map/ppermute | solution.py:349
  82.0 2.4 %collective-permute-start.18 = (f32[2,128,128]{2,1,0:T(8,128)S(1)}, f32[2,128,128]{2,1,0:T(8,128)S(1)}, u32[]{:S(2)}, u32[]{:S(2)}) collective-permute-start(f32[2,128,128]{2,1,0:T(8,128)S(1)} %get-tuple-element.75), channel_id=1, source_target_pairs={{16,0},{48,32},{80,64},{112,96},{144,128},{176,160},{208,192},{240... | collective-permute-start | bytes 393224 | tf_op jit(solution)/shard_map/ppermute | solution.py:350
  84.4 0.0 collective-permute-done.17.near_top
  84.4 1.0 %collective-permute-done.18.near_bottom = f32[2,128,128]{2,1,0:T(8,128)S(1)} collective-permute-done((f32[2,128,128]{2,1,0:T(8,128)S(1)}, f32[2,128,128]{2,1,0:T(8,128)S(1)}, u32[]{:S(2)}, u32[]{:S(2)}) %collective-permute-start.18) | collective-permute-done | bytes 131104 | tf_op jit(solution)/shard_map/ppermute | solution.py:350
  85.3 1.5 %collective-permute-done.19.far = f32[2,256,128]{2,1,0:T(8,128)S(1)} collective-permute-done((f32[2,256,128]{2,1,0:T(8,128)S(1)}, f32[2,256,128]{2,1,0:T(8,128)S(1)}, u32[]{:S(2)}, u32[]{:S(2)}) %collective-permute-start.19) | collective-permute-done | bytes 262176 | tf_op jit(solution)/shard_map/ppermute | solution.py:345
  86.8 0.0 copy-done.2
  86.8 0.8 last.1
  (6 shorter events, 0.1 us)
Async XLA Ops:
  0.0 11.7 %collective-permute-start.2 = (f32[2,256,128]{2,1,0:T(8,128)}, f32[2,256,128]{2,1,0:T(8,128)S(1)}, u32[]{:S(2)}, u32[]{:S(2)}) collective-permute-start(f32[2,256,128]{2,1,0:T(8,128)} %bitcast.1), channel_id=1, source_target_pairs={{16,32},{48,64},{80,96},{112,128},{144,160},{176,192},{208,224},{2... | collective-permute-start | bytes 786440 | tf_op jit(solution)/shard_map/ppermute | solution.py:281
  5.3 1.0 %copy-start.1 = (f32[1,2,256,128]{3,2,1,0:T(8,128)S(1)}, f32[1,2,256,128]{3,2,1,0:T(8,128)}, u32[]{:S(2)}) copy-start(f32[1,2,256,128]{3,2,1,0:T(8,128)} %block.3) | copy-start | bytes 786436
  6.3 5.4 %copy-start.6 = (s32[2]{0:T(128)S(1)}, s32[2]{0:T(128)}, u32[]{:S(2)}) copy-start(s32[2]{0:T(128)} %owners.3) | copy-start | bytes 28
  6.3 5.3 %copy-start.7 = (s32[2]{0:T(128)S(1)}, s32[2]{0:T(128)}, u32[]{:S(2)}) copy-start(s32[2]{0:T(128)} %offsets.3) | copy-start | bytes 28
  6.3 3.4 %collective-permute-start = (f32[2,128,128]{2,1,0:T(8,128)S(1)}, f32[2,128,128]{2,1,0:T(8,128)S(1)}, u32[]{:S(2)}, u32[]{:S(2)}) collective-permute-start(f32[2,128,128]{2,1,0:T(8,128)S(1)} %get-tuple-element.41), channel_id=1, source_target_pairs={{0,16},{16,0},{32,48},{48,32},{64,80},{80,64},{96,112},{112,96},{1... | collective-permute-start | bytes 393224 | tf_op jit(solution)/shard_map/ppermute | solution.py:285
  8.3 18.5 %copy-start = (f32[2,128,128]{2,1,0:T(8,128)S(1)}, f32[2,128,128]{2,1,0:T(8,128)}, u32[]{:S(2)}) copy-start(f32[2,128,128]{2,1,0:T(8,128)} %constant.4.clone.table_ref) | copy-start | bytes 393220
  8.3 18.5 %copy-start.3 = (f32[2,128,128]{2,1,0:T(8,128)S(1)}, f32[2,128,128]{2,1,0:T(8,128)}, u32[]{:S(2)}) copy-start(f32[2,128,128]{2,1,0:T(8,128)} %wave_in.1) | copy-start | bytes 393220
  8.3 3.4 %collective-permute-start.1 = (f32[2,128,128]{2,1,0:T(8,128)S(1)}, f32[2,128,128]{2,1,0:T(8,128)S(1)}, u32[]{:S(2)}, u32[]{:S(2)}) collective-permute-start(f32[2,128,128]{2,1,0:T(8,128)S(1)} %get-tuple-element.42), channel_id=1, source_target_pairs={{0,16},{32,48},{64,80},{96,112},{128,144},{160,176},{192,208},{224... | collective-permute-start | bytes 393224 | tf_op jit(solution)/shard_map/ppermute | solution.py:286
  12.3 10.1 %collective-permute-start.5 = (f32[2,128,128]{2,1,0:T(8,128)S(1)}, f32[2,128,128]{2,1,0:T(8,128)S(1)}, u32[]{:S(2)}, u32[]{:S(2)}) collective-permute-start(f32[2,128,128]{2,1,0:T(8,128)S(1)} %get-tuple-element.44), channel_id=1, source_target_pairs={{3,0},{15,12},{7,16},{11,28},{2,1},{14,13},{6,17},{10,29},{17,18},... | collective-permute-start | bytes 393224 | tf_op jit(solution)/shard_map/ppermute | solution.py:295
  16.7 8.4 %collective-permute-start.3 = (f32[2,128,128]{2,1,0:T(8,128)S(1)}, f32[2,128,128]{2,1,0:T(8,128)S(1)}, u32[]{:S(2)}, u32[]{:S(2)}) collective-permute-start(f32[2,128,128]{2,1,0:T(8,128)S(1)} %get-tuple-element.44), channel_id=1, source_target_pairs={{1,0},{13,12},{5,16},{9,28},{0,1},{12,13},{4,17},{8,29},{19,18},{3... | collective-permute-start | bytes 393224 | tf_op jit(solution)/shard_map/ppermute | solution.py:295
  18.0 8.8 %collective-permute-start.4 = (f32[2,128,128]{2,1,0:T(8,128)S(1)}, f32[2,128,128]{2,1,0:T(8,128)S(1)}, u32[]{:S(2)}, u32[]{:S(2)}) collective-permute-start(f32[2,128,128]{2,1,0:T(8,128)S(1)} %get-tuple-element.43.zero), channel_id=1, source_target_pairs={{2,0},{14,12},{6,16},{10,28},{3,1},{15,13},{7,17},{11,29},{16,18},... | collective-permute-start | bytes 393224 | tf_op jit(solution)/shard_map/ppermute | solution.py:295
  21.1 7.0 %collective-permute-start.7 = (f32[2,128,128]{2,1,0:T(8,128)S(1)}, f32[2,128,128]{2,1,0:T(8,128)S(1)}, u32[]{:S(2)}, u32[]{:S(2)}) collective-permute-start(f32[2,128,128]{2,1,0:T(8,128)S(1)} %get-tuple-element.43.zero), channel_id=1, source_target_pairs={{4,16},{8,28},{5,17},{9,29},{22,2},{26,14},{23,3},{27,15},{36,48},... | collective-permute-start | bytes 393224 | tf_op jit(solution)/shard_map/ppermute | solution.py:295
  26.8 3.2 %collective-permute-start.6 = (f32[2,128,128]{2,1,0:T(8,128)S(1)}, f32[2,128,128]{2,1,0:T(8,128)S(1)}, u32[]{:S(2)}, u32[]{:S(2)}) collective-permute-start(f32[2,128,128]{2,1,0:T(8,128)S(1)} %get-tuple-element.45), channel_id=1, source_target_pairs={{0,16},{1,17},{18,2},{19,3},{32,48},{33,49},{50,34},{51,35},{64,80... | collective-permute-start | bytes 393224 | tf_op jit(solution)/shard_map/ppermute | solution.py:307
  31.8 3.2 %collective-permute-start.8 = (f32[2,128,128]{2,1,0:T(8,128)S(1)}, f32[2,128,128]{2,1,0:T(8,128)S(1)}, u32[]{:S(2)}, u32[]{:S(2)}) collective-permute-start(f32[2,128,128]{2,1,0:T(8,128)S(1)} %get-tuple-element.48), channel_id=1, source_target_pairs={{16,28},{17,29},{2,14},{3,15},{48,60},{49,61},{34,46},{35,47},{80,... | collective-permute-start | bytes 393224 | tf_op jit(solution)/shard_map/ppermute | solution.py:307
  35.0 0.9 %copy-start.4 = (f32[2,128,128]{2,1,0:T(8,128)S(1)}, f32[2,128,128]{2,1,0:T(8,128)}, u32[]{:S(2)}) copy-start(f32[2,128,128]{2,1,0:T(8,128)} %measured.1) | copy-start | bytes 393220
  35.0 1.0 %copy-start.5 = (f32[2,128,128]{2,1,0:T(8,128)S(1)}, f32[2,128,128]{2,1,0:T(8,128)}, u32[]{:S(2)}) copy-start(f32[2,128,128]{2,1,0:T(8,128)} %constant.5.clone.fourier_ref) | copy-start | bytes 393220
  35.0 0.8 collective-permute-start.9
  36.0 0.7 collective-permute-start.10
  36.7 17.1 %collective-permute-start.11 = (f32[2,128,128]{2,1,0:T(8,128)S(1)}, f32[2,128,128]{2,1,0:T(8,128)S(1)}, u32[]{:S(2)}, u32[]{:S(2)}) collective-permute-start(f32[2,128,128]{2,1,0:T(8,128)S(1)} %get-tuple-element.59), channel_id=1, source_target_pairs={{28,16},{29,17},{14,2},{15,3},{60,48},{61,49},{46,34},{47,35},{92,... | collective-permute-start | bytes 393224 | tf_op jit(solution)/shard_map/ppermute | solution.py:325
  55.5 2.6 %collective-permute-start.12 = (f32[2,128,128]{2,1,0:T(8,128)S(1)}, f32[2,128,128]{2,1,0:T(8,128)S(1)}, u32[]{:S(2)}, u32[]{:S(2)}) collective-permute-start(f32[2,128,128]{2,1,0:T(8,128)S(1)} %get-tuple-element.64), channel_id=1, source_target_pairs={{16,0},{17,1},{2,18},{3,19},{48,32},{49,33},{34,50},{35,51},{80,64... | collective-permute-start | bytes 393224 | tf_op jit(solution)/shard_map/ppermute | solution.py:325
  56.8 3.2 %collective-permute-start.13 = (f32[2,128,128]{2,1,0:T(8,128)S(1)}, f32[2,128,128]{2,1,0:T(8,128)S(1)}, u32[]{:S(2)}, u32[]{:S(2)}) collective-permute-start(f32[2,128,128]{2,1,0:T(8,128)S(1)} %get-tuple-element.65.rest_0_), channel_id=1, source_target_pairs={{16,4},{28,8},{17,5},{29,9},{2,22},{14,26},{3,23},{15,27},{48,36},... | collective-permute-start | bytes 393224 | tf_op jit(solution)/shard_map/ppermute | solution.py:327
  60.7 7.9 %collective-permute-start.14 = (f32[2,128,128]{2,1,0:T(8,128)S(1)}, f32[2,128,128]{2,1,0:T(8,128)S(1)}, u32[]{:S(2)}, u32[]{:S(2)}) collective-permute-start(f32[2,128,128]{2,1,0:T(8,128)S(1)} %get-tuple-element.70), channel_id=1, source_target_pairs={{0,1},{12,13},{16,5},{28,9},{1,0},{13,12},{17,4},{29,8},{18,19},{3... | collective-permute-start | bytes 393224 | tf_op jit(solution)/shard_map/ppermute | solution.py:337
  64.7 8.7 %collective-permute-start.15 = (f32[2,128,128]{2,1,0:T(8,128)S(1)}, f32[2,128,128]{2,1,0:T(8,128)S(1)}, u32[]{:S(2)}, u32[]{:S(2)}) collective-permute-start(f32[2,128,128]{2,1,0:T(8,128)S(1)} %get-tuple-element.71), channel_id=1, source_target_pairs={{0,2},{12,14},{16,6},{28,10},{1,3},{13,15},{17,7},{29,11},{18,16},... | collective-permute-start | bytes 393224 | tf_op jit(solution)/shard_map/ppermute | solution.py:337
  66.7 10.6 %collective-permute-start.16 = (f32[2,128,128]{2,1,0:T(8,128)S(1)}, f32[2,128,128]{2,1,0:T(8,128)S(1)}, u32[]{:S(2)}, u32[]{:S(2)}) collective-permute-start(f32[2,128,128]{2,1,0:T(8,128)S(1)} %get-tuple-element.72), channel_id=1, source_target_pairs={{0,3},{12,15},{16,7},{28,11},{1,2},{13,14},{17,6},{29,10},{18,17},... | collective-permute-start | bytes 393224 | tf_op jit(solution)/shard_map/ppermute | solution.py:337
  77.9 8.9 %collective-permute-start.19 = (f32[2,256,128]{2,1,0:T(8,128)S(1)}, f32[2,256,128]{2,1,0:T(8,128)S(1)}, u32[]{:S(2)}, u32[]{:S(2)}) collective-permute-start(f32[2,256,128]{2,1,0:T(8,128)S(1)} %get-tuple-element.76), channel_id=1, source_target_pairs={{16,32},{48,64},{80,96},{112,128},{144,160},{176,192},{208,224},{2... | collective-permute-start | bytes 786440 | tf_op jit(solution)/shard_map/ppermute | solution.py:345
  79.9 7.0 %copy-start.2 = (f32[1,2,256,128]{3,2,1,0:T(8,128)S(1)}, f32[1,2,256,128]{3,2,1,0:T(8,128)}, u32[]{:S(2)}) copy-start(f32[1,2,256,128]{3,2,1,0:T(8,128)} %block.3) | copy-start | bytes 786436
  79.9 4.5 %collective-permute-start.17 = (f32[2,128,128]{2,1,0:T(8,128)S(1)}, f32[2,128,128]{2,1,0:T(8,128)S(1)}, u32[]{:S(2)}, u32[]{:S(2)}) collective-permute-start(f32[2,128,128]{2,1,0:T(8,128)S(1)} %get-tuple-element.74), channel_id=1, source_target_pairs={{0,16},{16,0},{32,48},{48,32},{64,80},{80,64},{96,112},{112,96},{1... | collective-permute-start | bytes 393224 | tf_op jit(solution)/shard_map/ppermute | solution.py:349
  82.0 3.4 %collective-permute-start.18 = (f32[2,128,128]{2,1,0:T(8,128)S(1)}, f32[2,128,128]{2,1,0:T(8,128)S(1)}, u32[]{:S(2)}, u32[]{:S(2)}) collective-permute-start(f32[2,128,128]{2,1,0:T(8,128)S(1)} %get-tuple-element.75), channel_id=1, source_target_pairs={{16,0},{48,32},{80,64},{112,96},{144,128},{176,160},{208,192},{240... | collective-permute-start | bytes 393224 | tf_op jit(solution)/shard_map/ppermute | solution.py:350

commit v4 on v3

--- a/solution.py
+++ b/solution.py
@@ -12,6 +12,7 @@
 side = 128
 tile = 256
 group = 4
+masks = (0, 1, 3, 2)
 long_cost = pl.CostEstimate(flops=2 * 10**10, bytes_accessed=2**25, transcendentals=0)
 params = pltpu.CompilerParams(vmem_limit_bytes=48 * 2**20)
 in_vmem = pl.BlockSpec(memory_space=pltpu.VMEM)
@@ -82,13 +83,17 @@
 def role():
     depth, scan = lax.axis_index("depth"), lax.axis_index("scan")
     row, column = depth // group, depth % group
-    home = (column // 2) == (scan & 1)
+    home = (column & 1) == (scan & 1)
     first, last = row == 0, row == group - 1
     return jnp.where(first, jnp.where(home, 0, 1), jnp.where(last, jnp.where(home, 3, 2), -1))
 
 
 def column():
     return lax.axis_index("depth") % group
+
+
+def upper_position():
+    return 1 - column() // 2
 
 
 def start_of(at, owners, offsets):
@@ -107,7 +112,7 @@
     pl.when(jnp.logical_not(even_scan))(odd)
 
 
-def cut_kernel(owners, offsets, block, near_top, near_bottom, far, odd_out, even_out, slab):
+def cut_kernel(owners, offsets, block, near_top, near_bottom, far, lower_out, upper_out, slab):
     slab[:, tile : 2 * tile] = block[0]
 
     def even():
@@ -120,15 +125,15 @@
         slab[:, 2 * tile :] = far[...]
 
     by_scan_parity(even, odd)
-    odd_position = 1 - (lax.axis_index("depth") & 1)
-    for at, out in ((odd_position, odd_out), (1 - odd_position, even_out)):
+    upper = upper_position()
+    for at, out in ((upper, upper_out), (1 - upper, lower_out)):
         out[...] = slab[:, pl.ds(start_of(at, owners, offsets), side), :]
 
 
 def collect(arrived, windows):
     me = column()
     for turn in range(group):
-        windows[me ^ turn] = arrived[turn][...]
+        windows[me ^ masks[turn]] = arrived[turn][...]
 
 
 def forward_kernel(mine, wave_in, zero, one, two, three, table_ref, *rest):
@@ -157,7 +162,7 @@
 def share(updates, parts):
     me = column()
     for turn in range(group):
-        parts[turn][...] = updates[me ^ turn]
+        parts[turn][...] = updates[me ^ masks[turn]]
 
 
 def far_kernel(wave_in, zero, one, two, three, measured, table_ref, fourier_ref, *rest):
@@ -173,14 +178,14 @@
             last = layer == group - 1
             wave = two_sided(times(wave, pair(windows, layer)), fourier if last else table)
         far_real, far_imag = wave
-        residual = far_real * far_real + far_imag * far_imag - measured[column() & 1]
+        residual = far_real * far_real + far_imag * far_imag - measured[column() // 2]
         adjoint = two_sided((residual * far_real, -(residual * far_imag)), fourier)
         put(adjoint_out, backward(adjoint, waves, windows, updates, table, False))
         share(updates, parts)
 
 
 def backward_kernel(mine, adjoint_in, waves, windows, table_ref, *rest):
-    adjoint_out, parts, updates = rest[group], rest[group + 1 : -1], rest[-1]
+    parts, updates = rest[group : 2 * group], rest[-1]
 
     @pl.when(role() == mine)
     def _():
@@ -188,17 +193,17 @@
             pair(adjoint_in), waves, windows, updates, blocks(table_ref), mine == 0
         )
         if mine:
-            put(adjoint_out, adjoint)
+            put(rest[2 * group], adjoint)
         share(updates, parts)
 
 
 def place_kernel(owners, offsets, own, zero, one, two, three, slab, far):
     slab[...] = jnp.zeros_like(slab)
     local = (role() == 0) | (role() == group - 1)
-    odd = one[...] + three[...]
-    even = two[...] + jnp.where(local, own[...], zero[...])
-    odd_position = 1 - (lax.axis_index("depth") & 1)
-    for at, update in ((odd_position, odd), (1 - odd_position, even)):
+    late = two[...] + three[...]
+    early = one[...] + jnp.where(local, own[...], zero[...])
+    upper = upper_position()
+    for at, update in ((upper, late), (1 - upper, early)):
         rows = pl.ds(start_of(at, owners, offsets), side)
         slab[:, rows, :] = slab[:, rows, :] + update
 
@@ -256,12 +261,12 @@
     def ends(pairs):
         return [(b, a) for a, b in pairs]
 
-    targets = [(i, 2 * (i & 1) + q) for i in range(scans) for q in range(2)]
+    targets = [(i, (i & 1) + 2 * q) for i in range(scans) for q in range(2)]
     gathers = []
     for turn in range(group):
         pairs = []
         for i, x in targets:
-            source = x ^ turn
+            source = x ^ masks[turn]
             if turn:
                 pairs.append((at(i, source), at(i, x)))
                 pairs.append((at(i, bottom + source), at(i, bottom + x)))
@@ -284,7 +289,7 @@
     )
     near_top = lax.ppermute(near_top, "scan", on_chip)
     near_bottom = lax.ppermute(near_bottom, "scan", downward)
-    odd_window, even_window = call(
+    lower_window, upper_window = call(
         cut_kernel,
         "cut",
         [window_type] * 2,
@@ -292,16 +297,16 @@
         [slab_type],
     )
     come = [
-        lax.ppermute(odd_window if turn & 1 else even_window, axes, gathers[turn])
-        for turn in (1, 2, 3, 0)
+        lax.ppermute(upper_window if turn & 2 else lower_window, axes, gathers[turn])
+        for turn in range(group)
     ]
-    late = come.pop()
+    late, *come = come
 
     wave, waves, windows = call(
         functools.partial(forward_kernel, 0),
         "first",
         [window_type, stack_type, stack_type],
-        (probe_wave, even_window, *come, step_table),
+        (probe_wave, lower_window, *come, step_table),
     )
     for mine, name in ((1, "second"), (2, "third")):
         wave = lax.ppermute(wave, axes, hops[mine - 1])
@@ -317,30 +322,26 @@
         far_kernel,
         "far",
         [window_type] * (1 + group),
-        (wave, even_window, *come, intensities, step_table, fourier_table),
+        (wave, lower_window, *come, intensities, step_table, fourier_table),
         [stack_type] * 3,
     )
-    first_back = None
     for mine, name in ((2, "back_third"), (1, "back_second"), (0, "back_first")):
         adjoint = lax.ppermute(adjoint, axes, ends(hops[mine]))
-        if mine == 0:
-            first_back = lax.ppermute(parts[0], axes, ends(gathers[0]))
-        adjoint, *parts = call(
+        returned = call(
             functools.partial(backward_kernel, mine),
             name,
-            [window_type] * (1 + group),
+            [window_type] * (group + min(mine, 1)),
             (adjoint, waves, windows, step_table, *parts),
             [stack_type],
-            aliases=[(4 + turn, 1 + turn) for turn in range(group)],
+            aliases=[(4 + turn, turn) for turn in range(group)],
         )
-    landed = [
-        lax.ppermute(parts[turn], axes, ends(gathers[turn])) for turn in range(1, group)
-    ]
+        parts, adjoint = returned[:group], returned[-1]
+    landed = [lax.ppermute(parts[turn], axes, ends(gathers[turn])) for turn in range(group)]
     slab, far = call(
         place_kernel,
         "place",
         [slab_type, tile_type],
-        (owners, offsets, parts[0], first_back, *landed),
+        (owners, offsets, parts[0], *landed),
     )
     far = lax.ppermute(far, "scan", next_chip)
     near_top, near_bottom = call(

time: 88.1 us -> 85.7 us (0.973)
  waiting for transfers between devices: 39 us -> 33.7 us
  starting transfers between devices: 40.9 us -> 44.3 us
    ppermute x1, starting transfers between devices: 1.92 us -> 7.53 us  [shards(): far = lax.ppermute(far, 'scan', next_chip)]
    ppermute x3 -> x4, waiting for transfers between devices: 8.65 us -> 6.19 us  [shards(): lax.ppermute(parts[turn], axes, ends(gathers[turn]))]
    ppermute x5 -> x4, waiting for transfers between devices: 6.3 us -> 4.05 us  [shards(): lax.ppermute(upper_window if turn & 2 else lower_window, axes, gathers[tu...]
    ppermute x1, waiting for transfers between devices: 1.48 us -> 0.01 us  [shards(): far = lax.ppermute(far, 'scan', next_chip)]
    ppermute x3 -> x4, starting transfers between devices: 7.85 us -> 6.42 us  [shards(): lax.ppermute(parts[turn], axes, ends(gathers[turn]))]
    ppermute x3, waiting for transfers between devices: 15.8 us -> 16.8 us  [shards(): adjoint = lax.ppermute(adjoint, axes, ends(hops[mine]))]
    ppermute x5 -> x4, starting transfers between devices: 11.4 us -> 10.6 us  [shards(): lax.ppermute(upper_window if turn & 2 else lower_window, axes, gathers[tu...]
  transfers between devices with their start and end apart: 20 -> 20, of which waited for: 11 -> 10; matrix products, arithmetic and copies ran while one was open for 0% -> 0% of each run, Pallas kernels for 0% -> 0%
where the time goes in v4:
time: 85.7 us; the launch traced here: 85.1 us
  starting transfers between devices  44.3 us (52%)
  waiting for transfers between devices  33.7 us (39%)
  Pallas kernels  5.63 us (7%)
  local copies, waits for them, and re-layouts  1.14 us (1%)
    ppermute x3, waiting for transfers between devices, shards(): adjoint = lax.ppermute(adjoint, axes, ends(hops[mine]))  16.8 us
    ppermute x4, starting transfers between devices, shards(): lax.ppermute(upper_window if turn & 2 else lower_window, axes, gathers[tu...  10.6 us
    ppermute x1, starting transfers between devices, shards(): far = lax.ppermute(far, 'scan', next_chip)  7.53 us
    ppermute x4, starting transfers between devices, shards(): lax.ppermute(parts[turn], axes, ends(gathers[turn]))  6.42 us
    ppermute x4, waiting for transfers between devices, shards(): lax.ppermute(parts[turn], axes, ends(gathers[turn]))  6.19 us
    pallas_call x12, Pallas kernels, call(): pl.pallas_call(kernel, out_shape=out_shape, in_specs=specs, out_specs=jax...  5.63 us
    ppermute x1, starting transfers between devices, shards(): far = lax.ppermute(object_slices[0], 'scan', next_chip)  5.31 us
    ppermute x4, waiting for transfers between devices, shards(): lax.ppermute(upper_window if turn & 2 else lower_window, axes, gathers[tu...  4.05 us
  transfers between devices with their start and end apart: 20, of which 10 were waited for; matrix products, arithmetic and copies ran while one was open for 0% of the time, Pallas kernels for 0%

profile of v4, /device:TPU:97, one launch (start us, length us, event | category | flops | bytes accessed | tf_op | source)
XLA Modules:
  0.0 85.1 jit_solution(8925614492623910617)
XLA Ops:
  0.0 5.3 %collective-permute-start.2 = (f32[2,256,128]{2,1,0:T(8,128)}, f32[2,256,128]{2,1,0:T(8,128)S(1)}, u32[]{:S(2)}, u32[]{:S(2)}) collective-permute-start(f32[2,256,128]{2,1,0:T(8,128)} %bitcast.1), channel_id=1, source_target_pairs={{16,32},{48,64},{80,96},{112,128},{144,160},{176,192},{208,224},{2... | collective-permute-start | bytes 786440 | tf_op jit(solution)/shard_map/ppermute | solution.py:286
  5.3 0.0 copy-start.1
  5.3 0.9 %copy-done.1 = f32[1,2,256,128]{3,2,1,0:T(8,128)S(1)} copy-done((f32[1,2,256,128]{3,2,1,0:T(8,128)S(1)}, f32[1,2,256,128]{3,2,1,0:T(8,128)}, u32[]{:S(2)}) %copy-start.1) | copy-done | bytes 262168
  6.3 0.0 copy-start.6
  6.3 0.0 copy-start.7
  6.3 1.9 %collective-permute-start = (f32[2,128,128]{2,1,0:T(8,128)S(1)}, f32[2,128,128]{2,1,0:T(8,128)S(1)}, u32[]{:S(2)}, u32[]{:S(2)}) collective-permute-start(f32[2,128,128]{2,1,0:T(8,128)S(1)} %get-tuple-element.41), channel_id=1, source_target_pairs={{0,16},{16,0},{32,48},{48,32},{64,80},{80,64},{96,112},{112,96},{1... | collective-permute-start | bytes 393224 | tf_op jit(solution)/shard_map/ppermute | solution.py:290
  8.3 0.0 copy-start
  8.3 0.0 copy-start.3
  8.3 1.4 %collective-permute-start.1 = (f32[2,128,128]{2,1,0:T(8,128)S(1)}, f32[2,128,128]{2,1,0:T(8,128)S(1)}, u32[]{:S(2)}, u32[]{:S(2)}) collective-permute-start(f32[2,128,128]{2,1,0:T(8,128)S(1)} %get-tuple-element.42), channel_id=1, source_target_pairs={{0,16},{32,48},{64,80},{96,112},{128,144},{160,176},{192,208},{224... | collective-permute-start | bytes 393224 | tf_op jit(solution)/shard_map/ppermute | solution.py:291
  9.7 0.0 collective-permute-done.near_top
  9.7 1.9 %collective-permute-done.1.near_bottom = f32[2,128,128]{2,1,0:T(8,128)S(1)} collective-permute-done((f32[2,128,128]{2,1,0:T(8,128)S(1)}, f32[2,128,128]{2,1,0:T(8,128)S(1)}, u32[]{:S(2)}, u32[]{:S(2)}) %collective-permute-start.1) | collective-permute-done | bytes 131104 | tf_op jit(solution)/shard_map/ppermute | solution.py:291
  11.7 0.0 collective-permute-done.2.far
  11.7 0.0 copy-done.6
  11.7 0.0 copy-done.7
  11.7 0.6 cut.1
  12.3 1.3 %collective-permute-start.5 = (f32[2,128,128]{2,1,0:T(8,128)S(1)}, f32[2,128,128]{2,1,0:T(8,128)S(1)}, u32[]{:S(2)}, u32[]{:S(2)}) collective-permute-start(f32[2,128,128]{2,1,0:T(8,128)S(1)} %get-tuple-element.44), channel_id=1, source_target_pairs={{2,0},{14,12},{6,16},{10,28},{0,2},{12,14},{4,18},{8,30},{19,17},{... | collective-permute-start | bytes 393224 | tf_op jit(solution)/shard_map/ppermute | solution.py:300
  13.6 6.1 %collective-permute-start.4 = (f32[2,128,128]{2,1,0:T(8,128)S(1)}, f32[2,128,128]{2,1,0:T(8,128)S(1)}, u32[]{:S(2)}, u32[]{:S(2)}) collective-permute-start(f32[2,128,128]{2,1,0:T(8,128)S(1)} %get-tuple-element.44), channel_id=1, source_target_pairs={{3,0},{15,12},{7,16},{11,28},{1,2},{13,14},{5,18},{9,30},{18,17},{... | collective-permute-start | bytes 393224 | tf_op jit(solution)/shard_map/ppermute | solution.py:300
  19.7 1.9 %collective-permute-start.3 = (f32[2,128,128]{2,1,0:T(8,128)S(1)}, f32[2,128,128]{2,1,0:T(8,128)S(1)}, u32[]{:S(2)}, u32[]{:S(2)}) collective-permute-start(f32[2,128,128]{2,1,0:T(8,128)S(1)} %get-tuple-element.43.zero), channel_id=1, source_target_pairs={{1,0},{13,12},{5,16},{9,28},{3,2},{15,14},{7,18},{11,30},{16,17},{... | collective-permute-start | bytes 393224 | tf_op jit(solution)/shard_map/ppermute | solution.py:300
  21.7 1.3 %collective-permute-start.7 = (f32[2,128,128]{2,1,0:T(8,128)S(1)}, f32[2,128,128]{2,1,0:T(8,128)S(1)}, u32[]{:S(2)}, u32[]{:S(2)}) collective-permute-start(f32[2,128,128]{2,1,0:T(8,128)S(1)} %get-tuple-element.43.zero), channel_id=1, source_target_pairs={{4,16},{8,28},{6,18},{10,30},{21,1},{25,13},{23,3},{27,15},{36,48}... | collective-permute-start | bytes 393224 | tf_op jit(solution)/shard_map/ppermute | solution.py:300
  23.0 0.0 collective-permute-done.5.three
  23.0 0.0 collective-permute-done.4.two
  23.0 4.0 %collective-permute-done.3.one = f32[2,128,128]{2,1,0:T(8,128)S(1)} collective-permute-done((f32[2,128,128]{2,1,0:T(8,128)S(1)}, f32[2,128,128]{2,1,0:T(8,128)S(1)}, u32[]{:S(2)}, u32[]{:S(2)}) %collective-permute-start.3) | collective-permute-done | bytes 131104 | tf_op jit(solution)/shard_map/ppermute | solution.py:300
  27.0 0.0 copy-done
  27.0 0.0 copy-done.3
  27.0 1.3 %collective-permute-start.6 = (f32[2,128,128]{2,1,0:T(8,128)S(1)}, f32[2,128,128]{2,1,0:T(8,128)S(1)}, u32[]{:S(2)}, u32[]{:S(2)}) collective-permute-start(f32[2,128,128]{2,1,0:T(8,128)S(1)} %get-tuple-element.45), channel_id=1, source_target_pairs={{0,16},{2,18},{17,1},{19,3},{32,48},{34,50},{49,33},{51,35},{64,80... | collective-permute-start | bytes 393224 | tf_op jit(solution)/shard_map/ppermute | solution.py:312
  28.3 0.1 collective-permute-done.7.zero
  28.3 1.9 %collective-permute-done.6.wave_in = f32[2,128,128]{2,1,0:T(8,128)S(1)} collective-permute-done((f32[2,128,128]{2,1,0:T(8,128)S(1)}, f32[2,128,128]{2,1,0:T(8,128)S(1)}, u32[]{:S(2)}, u32[]{:S(2)}) %collective-permute-start.6) | collective-permute-done | bytes 131104 | tf_op jit(solution)/shard_map/ppermute | solution.py:312
  30.2 1.8 %second.1 = (f32[2,128,128]{2,1,0:T(8,128)S(1)}, f32[4,2,128,128]{3,2,1,0:T(8,128)S(1)}, f32[4,2,128,128]{3,2,1,0:T(8,128)S(1)}) custom-call(f32[2,128,128]{2,1,0:T(8,128)S(1)} %collective-permute-done.6.wave_in, f32[2,128,128]{2,1,0:T(8,128)S(1)} %collective-permute-done.7.zero, ...), custom_call_target="tpu_custom_call", output_to_operand_aliasing={{1}: (6, {}), {2}: (7, {})} | custom-call | tf_op jit(solution)/shard_map/second/pallas_call | solution.py:246
  32.0 1.3 %collective-permute-start.8 = (f32[2,128,128]{2,1,0:T(8,128)S(1)}, f32[2,128,128]{2,1,0:T(8,128)S(1)}, u32[]{:S(2)}, u32[]{:S(2)}) collective-permute-start(f32[2,128,128]{2,1,0:T(8,128)S(1)} %get-tuple-element.48), channel_id=1, source_target_pairs={{16,28},{18,30},{1,13},{3,15},{48,60},{50,62},{33,45},{35,47},{80,... | collective-permute-start | bytes 393224 | tf_op jit(solution)/shard_map/ppermute | solution.py:312
  33.3 1.9 %collective-permute-done.8.wave_in = f32[2,128,128]{2,1,0:T(8,128)S(1)} collective-permute-done((f32[2,128,128]{2,1,0:T(8,128)S(1)}, f32[2,128,128]{2,1,0:T(8,128)S(1)}, u32[]{:S(2)}, u32[]{:S(2)}) %collective-permute-start.8) | collective-permute-done | bytes 131104 | tf_op jit(solution)/shard_map/ppermute | solution.py:312
  35.2 0.0 copy-start.4
  35.2 0.0 copy-start.5
  35.2 0.8 collective-permute-start.9
  36.0 0.0 collective-permute-done.9.wave_in
  36.0 0.1 copy-done.4
  36.1 0.1 copy-done.5
  36.2 0.7 collective-permute-start.10
  36.8 0.0 collective-permute-done.10.adjoint_in
  36.9 1.3 %collective-permute-start.11 = (f32[2,128,128]{2,1,0:T(8,128)S(1)}, f32[2,128,128]{2,1,0:T(8,128)S(1)}, u32[]{:S(2)}, u32[]{:S(2)}) collective-permute-start(f32[2,128,128]{2,1,0:T(8,128)S(1)} %get-tuple-element.59), channel_id=1, source_target_pairs={{28,16},{30,18},{13,1},{15,3},{60,48},{62,50},{45,33},{47,35},{92,... | collective-permute-start | bytes 393224 | tf_op jit(solution)/shard_map/ppermute | solution.py:329
  38.2 15.8 %collective-permute-done.11.adjoint_in = f32[2,128,128]{2,1,0:T(8,128)S(1)} collective-permute-done((f32[2,128,128]{2,1,0:T(8,128)S(1)}, f32[2,128,128]{2,1,0:T(8,128)S(1)}, u32[]{:S(2)}, u32[]{:S(2)}) %collective-permute-start.11) | collective-permute-done | bytes 131104 | tf_op jit(solution)/shard_map/ppermute | solution.py:329
  54.0 1.7 %back_second.1 = (f32[2,128,128]{2,1,0:T(8,128)S(1)}, f32[2,128,128]{2,1,0:T(8,128)S(1)}, f32[2,128,128]{2,1,0:T(8,128)S(1)}, f32[2,128,128]{2,1,0:T(8,128)S(1)}, f32[2,128,128]{2,1,0:T(8,128)S(1)}) custom-call(f32[2,128,128]{2,1,0:T(8,128)S(1)} %collective-permute-done.11.adjoint_in, ...), custom_call_target="tpu_custom_call", output_to_operand_aliasing={{0}: (4, {}), {1}: (5, {}), {2}: (6, {}), {3}: (7, {})} | custom-call | tf_op jit(solution)/shard_map/back_second/pallas_call | solution.py:246
  55.8 1.3 %collective-permute-start.12 = (f32[2,128,128]{2,1,0:T(8,128)S(1)}, f32[2,128,128]{2,1,0:T(8,128)S(1)}, u32[]{:S(2)}, u32[]{:S(2)}) collective-permute-start(f32[2,128,128]{2,1,0:T(8,128)S(1)} %get-tuple-element.64), channel_id=1, source_target_pairs={{16,0},{18,2},{1,17},{3,19},{48,32},{50,34},{33,49},{35,51},{80,64... | collective-permute-start | bytes 393224 | tf_op jit(solution)/shard_map/ppermute | solution.py:329
  57.1 1.0 %collective-permute-done.12.adjoint_in = f32[2,128,128]{2,1,0:T(8,128)S(1)} collective-permute-done((f32[2,128,128]{2,1,0:T(8,128)S(1)}, f32[2,128,128]{2,1,0:T(8,128)S(1)}, u32[]{:S(2)}, u32[]{:S(2)}) %collective-permute-start.12) | collective-permute-done | bytes 131104 | tf_op jit(solution)/shard_map/ppermute | solution.py:329
  58.0 1.9 %collective-permute-start.14 = (f32[2,128,128]{2,1,0:T(8,128)S(1)}, f32[2,128,128]{2,1,0:T(8,128)S(1)}, u32[]{:S(2)}, u32[]{:S(2)}) collective-permute-start(f32[2,128,128]{2,1,0:T(8,128)S(1)} %get-tuple-element.70), channel_id=1, source_target_pairs={{0,1},{12,13},{16,5},{28,9},{2,3},{14,15},{18,7},{30,11},{17,16},{... | collective-permute-start | bytes 393224 | tf_op jit(solution)/shard_map/ppermute | solution.py:339
  59.9 1.9 %collective-permute-start.15 = (f32[2,128,128]{2,1,0:T(8,128)S(1)}, f32[2,128,128]{2,1,0:T(8,128)S(1)}, u32[]{:S(2)}, u32[]{:S(2)}) collective-permute-start(f32[2,128,128]{2,1,0:T(8,128)S(1)} %get-tuple-element.71), channel_id=1, source_target_pairs={{0,3},{12,15},{16,7},{28,11},{2,1},{14,13},{18,5},{30,9},{17,18},{... | collective-permute-start | bytes 393224 | tf_op jit(solution)/shard_map/ppermute | solution.py:339
  61.9 1.3 %collective-permute-start.16 = (f32[2,128,128]{2,1,0:T(8,128)S(1)}, f32[2,128,128]{2,1,0:T(8,128)S(1)}, u32[]{:S(2)}, u32[]{:S(2)}) collective-permute-start(f32[2,128,128]{2,1,0:T(8,128)S(1)} %get-tuple-element.72), channel_id=1, source_target_pairs={{0,2},{12,14},{16,6},{28,10},{2,0},{14,12},{18,4},{30,8},{17,19},{... | collective-permute-start | bytes 393224 | tf_op jit(solution)/shard_map/ppermute | solution.py:339
  63.2 1.3 %collective-permute-start.13 = (f32[2,128,128]{2,1,0:T(8,128)S(1)}, f32[2,128,128]{2,1,0:T(8,128)S(1)}, u32[]{:S(2)}, u32[]{:S(2)}) collective-permute-start(f32[2,128,128]{2,1,0:T(8,128)S(1)} %get-tuple-element.69.own), channel_id=1, source_target_pairs={{16,4},{28,8},{18,6},{30,10},{1,21},{13,25},{3,23},{15,27},{48,36}... | collective-permute-start | bytes 393224 | tf_op jit(solution)/shard_map/ppermute | solution.py:339
  64.5 1.4 %collective-permute-done.14.one = f32[2,128,128]{2,1,0:T(8,128)S(1)} collective-permute-done((f32[2,128,128]{2,1,0:T(8,128)S(1)}, f32[2,128,128]{2,1,0:T(8,128)S(1)}, u32[]{:S(2)}, u32[]{:S(2)}) %collective-permute-start.14) | collective-permute-done | bytes 131104 | tf_op jit(solution)/shard_map/ppermute | solution.py:339
  65.9 4.8 %collective-permute-done.15.two = f32[2,128,128]{2,1,0:T(8,128)S(1)} collective-permute-done((f32[2,128,128]{2,1,0:T(8,128)S(1)}, f32[2,128,128]{2,1,0:T(8,128)S(1)}, u32[]{:S(2)}, u32[]{:S(2)}) %collective-permute-start.15) | collective-permute-done | bytes 131104 | tf_op jit(solution)/shard_map/ppermute | solution.py:339
  70.7 0.0 collective-permute-done.16.three
  70.7 0.0 collective-permute-done.13.zero
  70.7 0.7 place.1
  71.3 7.5 %collective-permute-start.19 = (f32[2,256,128]{2,1,0:T(8,128)S(1)}, f32[2,256,128]{2,1,0:T(8,128)S(1)}, u32[]{:S(2)}, u32[]{:S(2)}) collective-permute-start(f32[2,256,128]{2,1,0:T(8,128)S(1)} %get-tuple-element.76), channel_id=1, source_target_pairs={{16,32},{48,64},{80,96},{112,128},{144,160},{176,192},{208,224},{2... | collective-permute-start | bytes 786440 | tf_op jit(solution)/shard_map/ppermute | solution.py:346
  78.9 0.0 copy-start.2
  78.9 2.1 %collective-permute-start.17 = (f32[2,128,128]{2,1,0:T(8,128)S(1)}, f32[2,128,128]{2,1,0:T(8,128)S(1)}, u32[]{:S(2)}, u32[]{:S(2)}) collective-permute-start(f32[2,128,128]{2,1,0:T(8,128)S(1)} %get-tuple-element.74), channel_id=1, source_target_pairs={{0,16},{16,0},{32,48},{48,32},{64,80},{80,64},{96,112},{112,96},{1... | collective-permute-start | bytes 393224 | tf_op jit(solution)/shard_map/ppermute | solution.py:350
  81.0 2.4 %collective-permute-start.18 = (f32[2,128,128]{2,1,0:T(8,128)S(1)}, f32[2,128,128]{2,1,0:T(8,128)S(1)}, u32[]{:S(2)}, u32[]{:S(2)}) collective-permute-start(f32[2,128,128]{2,1,0:T(8,128)S(1)} %get-tuple-element.75), channel_id=1, source_target_pairs={{16,0},{48,32},{80,64},{112,96},{144,128},{176,160},{208,192},{240... | collective-permute-start | bytes 393224 | tf_op jit(solution)/shard_map/ppermute | solution.py:351
  83.4 0.0 collective-permute-done.17.near_top
  83.4 1.0 %collective-permute-done.18.near_bottom = f32[2,128,128]{2,1,0:T(8,128)S(1)} collective-permute-done((f32[2,128,128]{2,1,0:T(8,128)S(1)}, f32[2,128,128]{2,1,0:T(8,128)S(1)}, u32[]{:S(2)}, u32[]{:S(2)}) %collective-permute-start.18) | collective-permute-done | bytes 131104 | tf_op jit(solution)/shard_map/ppermute | solution.py:351
  84.4 0.0 collective-permute-done.19.far
  84.4 0.0 copy-done.2
  84.4 0.8 last.1
  (7 shorter events, 0.1 us)
Async XLA Ops:
  0.0 11.7 %collective-permute-start.2 = (f32[2,256,128]{2,1,0:T(8,128)}, f32[2,256,128]{2,1,0:T(8,128)S(1)}, u32[]{:S(2)}, u32[]{:S(2)}) collective-permute-start(f32[2,256,128]{2,1,0:T(8,128)} %bitcast.1), channel_id=1, source_target_pairs={{16,32},{48,64},{80,96},{112,128},{144,160},{176,192},{208,224},{2... | collective-permute-start | bytes 786440 | tf_op jit(solution)/shard_map/ppermute | solution.py:286
  5.3 1.0 %copy-start.1 = (f32[1,2,256,128]{3,2,1,0:T(8,128)S(1)}, f32[1,2,256,128]{3,2,1,0:T(8,128)}, u32[]{:S(2)}) copy-start(f32[1,2,256,128]{3,2,1,0:T(8,128)} %block.3) | copy-start | bytes 786436
  6.3 5.4 %copy-start.6 = (s32[2]{0:T(128)S(1)}, s32[2]{0:T(128)}, u32[]{:S(2)}) copy-start(s32[2]{0:T(128)} %owners.3) | copy-start | bytes 28
  6.3 5.3 %copy-start.7 = (s32[2]{0:T(128)S(1)}, s32[2]{0:T(128)}, u32[]{:S(2)}) copy-start(s32[2]{0:T(128)} %offsets.3) | copy-start | bytes 28
  6.3 3.4 %collective-permute-start = (f32[2,128,128]{2,1,0:T(8,128)S(1)}, f32[2,128,128]{2,1,0:T(8,128)S(1)}, u32[]{:S(2)}, u32[]{:S(2)}) collective-permute-start(f32[2,128,128]{2,1,0:T(8,128)S(1)} %get-tuple-element.41), channel_id=1, source_target_pairs={{0,16},{16,0},{32,48},{48,32},{64,80},{80,64},{96,112},{112,96},{1... | collective-permute-start | bytes 393224 | tf_op jit(solution)/shard_map/ppermute | solution.py:290
  8.3 18.7 %copy-start = (f32[2,128,128]{2,1,0:T(8,128)S(1)}, f32[2,128,128]{2,1,0:T(8,128)}, u32[]{:S(2)}) copy-start(f32[2,128,128]{2,1,0:T(8,128)} %constant.4.clone.table_ref) | copy-start | bytes 393220
  8.3 18.7 %copy-start.3 = (f32[2,128,128]{2,1,0:T(8,128)S(1)}, f32[2,128,128]{2,1,0:T(8,128)}, u32[]{:S(2)}) copy-start(f32[2,128,128]{2,1,0:T(8,128)} %wave_in.1) | copy-start | bytes 393220
  8.3 3.4 %collective-permute-start.1 = (f32[2,128,128]{2,1,0:T(8,128)S(1)}, f32[2,128,128]{2,1,0:T(8,128)S(1)}, u32[]{:S(2)}, u32[]{:S(2)}) collective-permute-start(f32[2,128,128]{2,1,0:T(8,128)S(1)} %get-tuple-element.42), channel_id=1, source_target_pairs={{0,16},{32,48},{64,80},{96,112},{128,144},{160,176},{192,208},{224... | collective-permute-start | bytes 393224 | tf_op jit(solution)/shard_map/ppermute | solution.py:291
  12.3 10.7 %collective-permute-start.5 = (f32[2,128,128]{2,1,0:T(8,128)S(1)}, f32[2,128,128]{2,1,0:T(8,128)S(1)}, u32[]{:S(2)}, u32[]{:S(2)}) collective-permute-start(f32[2,128,128]{2,1,0:T(8,128)S(1)} %get-tuple-element.44), channel_id=1, source_target_pairs={{2,0},{14,12},{6,16},{10,28},{0,2},{12,14},{4,18},{8,30},{19,17},{... | collective-permute-start | bytes 393224 | tf_op jit(solution)/shard_map/ppermute | solution.py:300
  13.6 9.4 %collective-permute-start.4 = (f32[2,128,128]{2,1,0:T(8,128)S(1)}, f32[2,128,128]{2,1,0:T(8,128)S(1)}, u32[]{:S(2)}, u32[]{:S(2)}) collective-permute-start(f32[2,128,128]{2,1,0:T(8,128)S(1)} %get-tuple-element.44), channel_id=1, source_target_pairs={{3,0},{15,12},{7,16},{11,28},{1,2},{13,14},{5,18},{9,30},{18,17},{... | collective-permute-start | bytes 393224 | tf_op jit(solution)/shard_map/ppermute | solution.py:300
  19.7 7.2 %collective-permute-start.3 = (f32[2,128,128]{2,1,0:T(8,128)S(1)}, f32[2,128,128]{2,1,0:T(8,128)S(1)}, u32[]{:S(2)}, u32[]{:S(2)}) collective-permute-start(f32[2,128,128]{2,1,0:T(8,128)S(1)} %get-tuple-element.43.zero), channel_id=1, source_target_pairs={{1,0},{13,12},{5,16},{9,28},{3,2},{15,14},{7,18},{11,30},{16,17},{... | collective-permute-start | bytes 393224 | tf_op jit(solution)/shard_map/ppermute | solution.py:300
  21.7 6.7 %collective-permute-start.7 = (f32[2,128,128]{2,1,0:T(8,128)S(1)}, f32[2,128,128]{2,1,0:T(8,128)S(1)}, u32[]{:S(2)}, u32[]{:S(2)}) collective-permute-start(f32[2,128,128]{2,1,0:T(8,128)S(1)} %get-tuple-element.43.zero), channel_id=1, source_target_pairs={{4,16},{8,28},{6,18},{10,30},{21,1},{25,13},{23,3},{27,15},{36,48}... | collective-permute-start | bytes 393224 | tf_op jit(solution)/shard_map/ppermute | solution.py:300
  27.0 3.2 %collective-permute-start.6 = (f32[2,128,128]{2,1,0:T(8,128)S(1)}, f32[2,128,128]{2,1,0:T(8,128)S(1)}, u32[]{:S(2)}, u32[]{:S(2)}) collective-permute-start(f32[2,128,128]{2,1,0:T(8,128)S(1)} %get-tuple-element.45), channel_id=1, source_target_pairs={{0,16},{2,18},{17,1},{19,3},{32,48},{34,50},{49,33},{51,35},{64,80... | collective-permute-start | bytes 393224 | tf_op jit(solution)/shard_map/ppermute | solution.py:312
  32.0 3.2 %collective-permute-start.8 = (f32[2,128,128]{2,1,0:T(8,128)S(1)}, f32[2,128,128]{2,1,0:T(8,128)S(1)}, u32[]{:S(2)}, u32[]{:S(2)}) collective-permute-start(f32[2,128,128]{2,1,0:T(8,128)S(1)} %get-tuple-element.48), channel_id=1, source_target_pairs={{16,28},{18,30},{1,13},{3,15},{48,60},{50,62},{33,45},{35,47},{80,... | collective-permute-start | bytes 393224 | tf_op jit(solution)/shard_map/ppermute | solution.py:312
  35.2 0.9 %copy-start.4 = (f32[2,128,128]{2,1,0:T(8,128)S(1)}, f32[2,128,128]{2,1,0:T(8,128)}, u32[]{:S(2)}) copy-start(f32[2,128,128]{2,1,0:T(8,128)} %measured.1) | copy-start | bytes 393220
  35.2 1.0 %copy-start.5 = (f32[2,128,128]{2,1,0:T(8,128)S(1)}, f32[2,128,128]{2,1,0:T(8,128)}, u32[]{:S(2)}) copy-start(f32[2,128,128]{2,1,0:T(8,128)} %constant.5.clone.fourier_ref) | copy-start | bytes 393220
  35.2 0.8 collective-permute-start.9
  36.2 0.7 collective-permute-start.10
  36.9 17.1 %collective-permute-start.11 = (f32[2,128,128]{2,1,0:T(8,128)S(1)}, f32[2,128,128]{2,1,0:T(8,128)S(1)}, u32[]{:S(2)}, u32[]{:S(2)}) collective-permute-start(f32[2,128,128]{2,1,0:T(8,128)S(1)} %get-tuple-element.59), channel_id=1, source_target_pairs={{28,16},{30,18},{13,1},{15,3},{60,48},{62,50},{45,33},{47,35},{92,... | collective-permute-start | bytes 393224 | tf_op jit(solution)/shard_map/ppermute | solution.py:329
  55.8 2.3 %collective-permute-start.12 = (f32[2,128,128]{2,1,0:T(8,128)S(1)}, f32[2,128,128]{2,1,0:T(8,128)S(1)}, u32[]{:S(2)}, u32[]{:S(2)}) collective-permute-start(f32[2,128,128]{2,1,0:T(8,128)S(1)} %get-tuple-element.64), channel_id=1, source_target_pairs={{16,0},{18,2},{1,17},{3,19},{48,32},{50,34},{33,49},{35,51},{80,64... | collective-permute-start | bytes 393224 | tf_op jit(solution)/shard_map/ppermute | solution.py:329
  58.0 7.8 %collective-permute-start.14 = (f32[2,128,128]{2,1,0:T(8,128)S(1)}, f32[2,128,128]{2,1,0:T(8,128)S(1)}, u32[]{:S(2)}, u32[]{:S(2)}) collective-permute-start(f32[2,128,128]{2,1,0:T(8,128)S(1)} %get-tuple-element.70), channel_id=1, source_target_pairs={{0,1},{12,13},{16,5},{28,9},{2,3},{14,15},{18,7},{30,11},{17,16},{... | collective-permute-start | bytes 393224 | tf_op jit(solution)/shard_map/ppermute | solution.py:339
  59.9 10.7 %collective-permute-start.15 = (f32[2,128,128]{2,1,0:T(8,128)S(1)}, f32[2,128,128]{2,1,0:T(8,128)S(1)}, u32[]{:S(2)}, u32[]{:S(2)}) collective-permute-start(f32[2,128,128]{2,1,0:T(8,128)S(1)} %get-tuple-element.71), channel_id=1, source_target_pairs={{0,3},{12,15},{16,7},{28,11},{2,1},{14,13},{18,5},{30,9},{17,18},{... | collective-permute-start | bytes 393224 | tf_op jit(solution)/shard_map/ppermute | solution.py:339
  61.9 8.8 %collective-permute-start.16 = (f32[2,128,128]{2,1,0:T(8,128)S(1)}, f32[2,128,128]{2,1,0:T(8,128)S(1)}, u32[]{:S(2)}, u32[]{:S(2)}) collective-permute-start(f32[2,128,128]{2,1,0:T(8,128)S(1)} %get-tuple-element.72), channel_id=1, source_target_pairs={{0,2},{12,14},{16,6},{28,10},{2,0},{14,12},{18,4},{30,8},{17,19},{... | collective-permute-start | bytes 393224 | tf_op jit(solution)/shard_map/ppermute | solution.py:339
  63.2 7.5 %collective-permute-start.13 = (f32[2,128,128]{2,1,0:T(8,128)S(1)}, f32[2,128,128]{2,1,0:T(8,128)S(1)}, u32[]{:S(2)}, u32[]{:S(2)}) collective-permute-start(f32[2,128,128]{2,1,0:T(8,128)S(1)} %get-tuple-element.69.own), channel_id=1, source_target_pairs={{16,4},{28,8},{18,6},{30,10},{1,21},{13,25},{3,23},{15,27},{48,36}... | collective-permute-start | bytes 393224 | tf_op jit(solution)/shard_map/ppermute | solution.py:339
  71.3 13.0 %collective-permute-start.19 = (f32[2,256,128]{2,1,0:T(8,128)S(1)}, f32[2,256,128]{2,1,0:T(8,128)S(1)}, u32[]{:S(2)}, u32[]{:S(2)}) collective-permute-start(f32[2,256,128]{2,1,0:T(8,128)S(1)} %get-tuple-element.76), channel_id=1, source_target_pairs={{16,32},{48,64},{80,96},{112,128},{144,160},{176,192},{208,224},{2... | collective-permute-start | bytes 786440 | tf_op jit(solution)/shard_map/ppermute | solution.py:346
  78.9 5.5 %copy-start.2 = (f32[1,2,256,128]{3,2,1,0:T(8,128)S(1)}, f32[1,2,256,128]{3,2,1,0:T(8,128)}, u32[]{:S(2)}) copy-start(f32[1,2,256,128]{3,2,1,0:T(8,128)} %block.3) | copy-start | bytes 786436
  78.9 4.5 %collective-permute-start.17 = (f32[2,128,128]{2,1,0:T(8,128)S(1)}, f32[2,128,128]{2,1,0:T(8,128)S(1)}, u32[]{:S(2)}, u32[]{:S(2)}) collective-permute-start(f32[2,128,128]{2,1,0:T(8,128)S(1)} %get-tuple-element.74), channel_id=1, source_target_pairs={{0,16},{16,0},{32,48},{48,32},{64,80},{80,64},{96,112},{112,96},{1... | collective-permute-start | bytes 393224 | tf_op jit(solution)/shard_map/ppermute | solution.py:350
  81.0 3.4 %collective-permute-start.18 = (f32[2,128,128]{2,1,0:T(8,128)S(1)}, f32[2,128,128]{2,1,0:T(8,128)S(1)}, u32[]{:S(2)}, u32[]{:S(2)}) collective-permute-start(f32[2,128,128]{2,1,0:T(8,128)S(1)} %get-tuple-element.75), channel_id=1, source_target_pairs={{16,0},{48,32},{80,64},{112,96},{144,128},{176,160},{208,192},{240... | collective-permute-start | bytes 393224 | tf_op jit(solution)/shard_map/ppermute | solution.py:351

commit v5 on v4

--- a/solution.py
+++ b/solution.py
@@ -12,8 +12,7 @@
 side = 128
 tile = 256
 group = 4
-masks = (0, 1, 3, 2)
-long_cost = pl.CostEstimate(flops=2 * 10**10, bytes_accessed=2**25, transcendentals=0)
+masks = (0, 2, 1, 3)
 params = pltpu.CompilerParams(vmem_limit_bytes=48 * 2**20)
 in_vmem = pl.BlockSpec(memory_space=pltpu.VMEM)
 in_smem = pl.BlockSpec(memory_space=pltpu.SMEM)
@@ -82,10 +81,9 @@
 
 def role():
     depth, scan = lax.axis_index("depth"), lax.axis_index("scan")
-    row, column = depth // group, depth % group
-    home = (column & 1) == (scan & 1)
-    first, last = row == 0, row == group - 1
-    return jnp.where(first, jnp.where(home, 0, 1), jnp.where(last, jnp.where(home, 3, 2), -1))
+    row, home = depth // group, (depth % group) // 2 == (scan & 1)
+    second, third = row == 1, row == 2
+    return jnp.where(second, jnp.where(home, 0, 1), jnp.where(third, jnp.where(home, 3, 2), -1))
 
 
 def column():
@@ -93,17 +91,12 @@
 
 
 def upper_position():
-    return 1 - column() // 2
+    return 1 - (column() & 1)
 
 
 def start_of(at, owners, offsets):
     start = (owners[at] - lax.axis_index("scan") + 1) * tile + offsets[at]
     return jnp.clip(start, 0, 2 * tile)
-
-
-def stage_kernel(block, top, bottom):
-    top[...] = block[:, :side]
-    bottom[...] = block[:, side:]
 
 
 def by_scan_parity(even, odd):
@@ -112,17 +105,24 @@
     pl.when(jnp.logical_not(even_scan))(odd)
 
 
-def cut_kernel(owners, offsets, block, near_top, near_bottom, far, lower_out, upper_out, slab):
+def lay_kernel(far, block, slab):
     slab[:, tile : 2 * tile] = block[0]
 
     def even():
         slab[:, :tile] = far[...]
-        slab[:, 2 * tile : 2 * tile + side] = near_top[...]
 
     def odd():
-        slab[:, :side] = near_top[...]
-        slab[:, side:tile] = near_bottom[...]
         slab[:, 2 * tile :] = far[...]
+
+    by_scan_parity(even, odd)
+
+
+def cut_kernel(near, owners, offsets, laid, lower_out, upper_out, slab):
+    def even():
+        slab[:, 2 * tile :] = near[...]
+
+    def odd():
+        slab[:, :tile] = near[...]
 
     by_scan_parity(even, odd)
     upper = upper_position()
@@ -178,7 +178,7 @@
             last = layer == group - 1
             wave = two_sided(times(wave, pair(windows, layer)), fourier if last else table)
         far_real, far_imag = wave
-        residual = far_real * far_real + far_imag * far_imag - measured[column() // 2]
+        residual = far_real * far_real + far_imag * far_imag - measured[column() & 1]
         adjoint = two_sided((residual * far_real, -(residual * far_imag)), fourier)
         put(adjoint_out, backward(adjoint, waves, windows, updates, table, False))
         share(updates, parts)
@@ -197,41 +197,30 @@
         share(updates, parts)
 
 
-def place_kernel(owners, offsets, own, zero, one, two, three, slab, far):
+def place_kernel(owners, offsets, zero, one, two, three, slab, near, far):
     slab[...] = jnp.zeros_like(slab)
-    local = (role() == 0) | (role() == group - 1)
-    late = two[...] + three[...]
-    early = one[...] + jnp.where(local, own[...], zero[...])
     upper = upper_position()
-    for at, update in ((upper, late), (1 - upper, early)):
+    for at, update in ((upper, two[...] + three[...]), (1 - upper, zero[...] + one[...])):
         rows = pl.ds(start_of(at, owners, offsets), side)
         slab[:, rows, :] = slab[:, rows, :] + update
 
-    def even_scan():
+    def even():
         far[...] = slab[:, :tile]
-
-    def odd_scan():
+        near[...] = slab[:, 2 * tile :]
+
+    def odd():
+        near[...] = slab[:, :tile]
         far[...] = slab[:, 2 * tile :]
 
-    by_scan_parity(even_scan, odd_scan)
-
-
-def near_kernel(slab, near_top, near_bottom):
-    def even_scan():
-        near_top[...] = slab[:, 2 * tile : 2 * tile + side]
-
-    def odd_scan():
-        near_top[...] = slab[:, :side]
-        near_bottom[...] = slab[:, side:tile]
-
-    by_scan_parity(even_scan, odd_scan)
-
-
-def last_kernel(block, slab, near_top, near_bottom, far, out):
-    for half, near in enumerate((near_top, near_bottom)):
-        rows = slice(half * side, (half + 1) * side)
-        mine = slab[:, tile + half * side : tile + (half + 1) * side]
-        out[0, :, rows] = block[0, :, rows] - step_size * (mine + near[...] + far[:, rows])
+    by_scan_parity(even, odd)
+
+
+def step_kernel(far, block, slab, out):
+    out[...] = block[0] - step_size * (slab[:, tile : 2 * tile] + far[...])
+
+
+def last_kernel(near, stepped, out):
+    out[0] = stepped[...] - step_size * near[...]
 
 
 def shards(object_slices, probe_wave, intensities, offsets, owners):
@@ -239,9 +228,8 @@
     depths = lax.axis_size("depth")
     axes = ("scan", "depth")
     step_table, fourier_table = tables()
-    bottom = depths - group
-
-    def call(kernel, name, out_shape, arguments, scratch=(), aliases=(), cost=None):
+
+    def call(kernel, name, out_shape, arguments, scratch=(), aliases=()):
         specs = [in_smem if a.dtype == jnp.int32 else in_vmem for a in arguments]
         return pl.pallas_call(
             kernel,
@@ -251,7 +239,6 @@
             scratch_shapes=[pltpu.VMEM(kind.shape, jnp.float32) for kind in scratch],
             input_output_aliases=dict(aliases),
             compiler_params=params,
-            cost_estimate=cost,
             name=name,
         )(*arguments)
 
@@ -261,52 +248,46 @@
     def ends(pairs):
         return [(b, a) for a, b in pairs]
 
-    targets = [(i, (i & 1) + 2 * q) for i in range(scans) for q in range(2)]
-    gathers = []
-    for turn in range(group):
-        pairs = []
-        for i, x in targets:
-            source = x ^ masks[turn]
-            if turn:
-                pairs.append((at(i, source), at(i, x)))
-                pairs.append((at(i, bottom + source), at(i, bottom + x)))
-            pairs.append((at(i, group + source), at(i ^ 1, x)))
-            pairs.append((at(i, 2 * group + source), at(i ^ 1, bottom + x)))
-        gathers.append(pairs)
+    targets = [(i, 2 * (i & 1) + q) for i in range(scans) for q in range(2)]
+    homes = [
+        [(i, group + x), (i ^ 1, group + x), (i ^ 1, 2 * group + x), (i, 2 * group + x)]
+        for i, x in targets
+    ]
+    gathers = [
+        [
+            (at(i, row * group + (x ^ mask)), at(*home[row]))
+            for (i, x), home in zip(targets, homes)
+            for row in range(group)
+        ]
+        for mask in masks
+    ]
     hops = [
-        [(at(i, x), at(i ^ 1, x)) for i, x in targets],
-        [(at(i ^ 1, x), at(i ^ 1, bottom + x)) for i, x in targets],
-        [(at(i ^ 1, bottom + x), at(i, bottom + x)) for i, x in targets],
+        [(at(*home[row]), at(*home[row + 1])) for home in homes] for row in range(group - 1)
     ]
     on_chip = [(i, i ^ 1) for i in range(scans)]
-    downward = [(i, i + 1) for i in range(0, scans, 2)]
     next_chip = [(i, i + 1) for i in range(1, scans - 1, 2)]
     next_chip = next_chip + ends(next_chip)
 
+    near = lax.ppermute(object_slices[0], "scan", on_chip)
     far = lax.ppermute(object_slices[0], "scan", next_chip)
-    near_top, near_bottom = call(
-        stage_kernel, "stage", [window_type] * 2, (object_slices[0],), cost=long_cost
-    )
-    near_top = lax.ppermute(near_top, "scan", on_chip)
-    near_bottom = lax.ppermute(near_bottom, "scan", downward)
-    lower_window, upper_window = call(
+    slab = call(lay_kernel, "lay", slab_type, (far, object_slices))
+    lower_window, upper_window, slab = call(
         cut_kernel,
         "cut",
-        [window_type] * 2,
-        (owners, offsets, object_slices, near_top, near_bottom, far),
-        [slab_type],
+        [window_type, window_type, slab_type],
+        (near, owners, offsets, slab),
+        aliases=[(3, 2)],
     )
     come = [
         lax.ppermute(upper_window if turn & 2 else lower_window, axes, gathers[turn])
         for turn in range(group)
     ]
-    late, *come = come
 
     wave, waves, windows = call(
         functools.partial(forward_kernel, 0),
         "first",
         [window_type, stack_type, stack_type],
-        (probe_wave, lower_window, *come, step_table),
+        (probe_wave, *come, step_table),
     )
     for mine, name in ((1, "second"), (2, "third")):
         wave = lax.ppermute(wave, axes, hops[mine - 1])
@@ -314,7 +295,7 @@
             functools.partial(forward_kernel, mine),
             name,
             [window_type, stack_type, stack_type],
-            (wave, late, *come, step_table, waves, windows),
+            (wave, *come, step_table, waves, windows),
             aliases=((6, 1), (7, 2)),
         )
     wave = lax.ppermute(wave, axes, hops[2])
@@ -322,7 +303,7 @@
         far_kernel,
         "far",
         [window_type] * (1 + group),
-        (wave, lower_window, *come, intensities, step_table, fourier_table),
+        (wave, *come, intensities, step_table, fourier_table),
         [stack_type] * 3,
     )
     for mine, name in ((2, "back_third"), (1, "back_second"), (0, "back_first")):
@@ -337,23 +318,20 @@
         )
         parts, adjoint = returned[:group], returned[-1]
     landed = [lax.ppermute(parts[turn], axes, ends(gathers[turn])) for turn in range(group)]
-    slab, far = call(
+    slab, near, far = call(
         place_kernel,
         "place",
-        [slab_type, tile_type],
-        (owners, offsets, parts[0], *landed),
-    )
+        [slab_type, tile_type, tile_type],
+        (owners, offsets, *landed),
+    )
+    near = lax.ppermute(near, "scan", on_chip)
     far = lax.ppermute(far, "scan", next_chip)
-    near_top, near_bottom = call(
-        near_kernel, "near", [window_type] * 2, (slab,), cost=long_cost
-    )
-    near_top = lax.ppermute(near_top, "scan", on_chip)
-    near_bottom = lax.ppermute(near_bottom, "scan", ends(downward))
+    stepped = call(step_kernel, "step", tile_type, (far, object_slices, slab))
     return call(
         last_kernel,
         "last",
         jax.ShapeDtypeStruct(object_slices.shape, jnp.float32),
-        (object_slices, slab, near_top, near_bottom, far),
+        (near, stepped),
     )
 
 

time: 85.7 us -> 84.6 us (0.987)
  the two profiles are of different devices: /device:TPU:97 before, /device:TPU:233 now
where the time goes in v5:
time: 84.6 us; the launch traced here: 84.1 us
  starting transfers between devices  40.3 us (48%)
  waiting for transfers between devices  36.8 us (43%)
  Pallas kernels  5.64 us (7%)
  local copies, waits for them, and re-layouts  1.13 us (1%)
    ppermute x3, waiting for transfers between devices, shards(): adjoint = lax.ppermute(adjoint, axes, ends(hops[mine]))  15.6 us
    ppermute x4, starting transfers between devices, shards(): lax.ppermute(parts[turn], axes, ends(gathers[turn]))  11.7 us
    ppermute x4, starting transfers between devices, shards(): lax.ppermute(upper_window if turn & 2 else lower_window, axes, gathers[tu...  10.3 us
    pallas_call x12, Pallas kernels, call(): pl.pallas_call(kernel, out_shape=out_shape, in_specs=specs, out_specs=jax...  5.64 us
    ppermute x2, waiting for transfers between devices, shards(): wave = lax.ppermute(wave, axes, hops[mine - 1])  5.57 us
    ppermute x1, starting transfers between devices, shards(): far = lax.ppermute(object_slices[0], 'scan', next_chip)  5.44 us
    ppermute x4, waiting for transfers between devices, shards(): lax.ppermute(upper_window if turn & 2 else lower_window, axes, gathers[tu...  4.97 us
    ppermute x1, waiting for transfers between devices, shards(): far = lax.ppermute(far, 'scan', next_chip)  4.62 us
  transfers between devices with their start and end apart: 18, of which 9 were waited for; matrix products, arithmetic and copies ran while one was open for 0% of the time, Pallas kernels for 0%

profile of v5, /device:TPU:233, one launch (start us, length us, event | category | flops | bytes accessed | tf_op | source)
XLA Modules:
  0.0 84.1 jit_solution(12422283346740081865)
XLA Ops:
  0.0 0.0 copy-start.6
  0.0 0.0 copy-start.7
  0.0 5.4 %collective-permute-start.1 = (f32[2,256,128]{2,1,0:T(8,128)}, f32[2,256,128]{2,1,0:T(8,128)S(1)}, u32[]{:S(2)}, u32[]{:S(2)}) collective-permute-start(f32[2,256,128]{2,1,0:T(8,128)} %bitcast.1), channel_id=1, source_target_pairs={{16,32},{48,64},{80,96},{112,128},{144,160},{176,192},{208,224},{2... | collective-permute-start | bytes 786440 | tf_op jit(solution)/shard_map/ppermute | solution.py:272
  5.5 1.9 %collective-permute-start = (f32[2,256,128]{2,1,0:T(8,128)}, f32[2,256,128]{2,1,0:T(8,128)S(1)}, u32[]{:S(2)}, u32[]{:S(2)}) collective-permute-start(f32[2,256,128]{2,1,0:T(8,128)} %bitcast.2), channel_id=1, source_target_pairs={{0,16},{16,0},{32,48},{48,32},{64,80},{80,64},{96,112},{112,96},{1... | collective-permute-start | bytes 786440 | tf_op jit(solution)/shard_map/ppermute | solution.py:271
  7.4 2.3 %collective-permute-done.1.far = f32[2,256,128]{2,1,0:T(8,128)S(1)} collective-permute-done((f32[2,256,128]{2,1,0:T(8,128)}, f32[2,256,128]{2,1,0:T(8,128)S(1)}, u32[]{:S(2)}, u32[]{:S(2)}) %collective-permute-start.1) | collective-permute-done | bytes 262176 | tf_op jit(solution)/shard_map/ppermute | solution.py:272
  9.7 0.0 copy-start.1
  9.7 0.9 %copy-done.1 = f32[1,2,256,128]{3,2,1,0:T(8,128)S(1)} copy-done((f32[1,2,256,128]{3,2,1,0:T(8,128)S(1)}, f32[1,2,256,128]{3,2,1,0:T(8,128)}, u32[]{:S(2)}) %copy-start.1) | copy-done | bytes 262168
  10.7 0.0 copy-start
  10.7 0.0 copy-start.3
  10.7 0.0 collective-permute-done.near
  10.7 0.0 copy-done.6
  10.7 0.0 copy-done.7
  10.7 0.6 cut.1
  11.4 3.5 %collective-permute-start.3 = (f32[2,128,128]{2,1,0:T(8,128)S(1)}, f32[2,128,128]{2,1,0:T(8,128)S(1)}, u32[]{:S(2)}, u32[]{:S(2)}) collective-permute-start(f32[2,128,128]{2,1,0:T(8,128)S(1)} %get-tuple-element.38), channel_id=1, source_target_pairs={{2,4},{6,20},{10,24},{14,8},{3,5},{7,21},{11,25},{15,9},{16,22},{2... | collective-permute-start | bytes 393224 | tf_op jit(solution)/shard_map/ppermute | solution.py:282
  14.9 1.3 %collective-permute-start.2 = (f32[2,128,128]{2,1,0:T(8,128)S(1)}, f32[2,128,128]{2,1,0:T(8,128)S(1)}, u32[]{:S(2)}, u32[]{:S(2)}) collective-permute-start(f32[2,128,128]{2,1,0:T(8,128)S(1)} %get-tuple-element.38), channel_id=1, source_target_pairs={{0,4},{4,20},{8,24},{12,8},{1,5},{5,21},{9,25},{13,9},{18,22},{22,... | collective-permute-start | bytes 393224 | tf_op jit(solution)/shard_map/ppermute | solution.py:282
  16.2 4.2 %collective-permute-start.5 = (f32[2,128,128]{2,1,0:T(8,128)S(1)}, f32[2,128,128]{2,1,0:T(8,128)S(1)}, u32[]{:S(2)}, u32[]{:S(2)}) collective-permute-start(f32[2,128,128]{2,1,0:T(8,128)S(1)} %get-tuple-element.39), channel_id=1, source_target_pairs={{3,4},{7,20},{11,24},{15,8},{2,5},{6,21},{10,25},{14,9},{17,22},{2... | collective-permute-start | bytes 393224 | tf_op jit(solution)/shard_map/ppermute | solution.py:282
  20.4 1.3 %collective-permute-start.4 = (f32[2,128,128]{2,1,0:T(8,128)S(1)}, f32[2,128,128]{2,1,0:T(8,128)S(1)}, u32[]{:S(2)}, u32[]{:S(2)}) collective-permute-start(f32[2,128,128]{2,1,0:T(8,128)S(1)} %get-tuple-element.39), channel_id=1, source_target_pairs={{1,4},{5,20},{9,24},{13,8},{0,5},{4,21},{8,25},{12,9},{19,22},{23,... | collective-permute-start | bytes 393224 | tf_op jit(solution)/shard_map/ppermute | solution.py:282
  21.7 0.0 collective-permute-done.3.one
  21.7 0.0 collective-permute-done.2.zero
  21.7 2.0 %collective-permute-done.5.three = f32[2,128,128]{2,1,0:T(8,128)S(1)} collective-permute-done((f32[2,128,128]{2,1,0:T(8,128)S(1)}, f32[2,128,128]{2,1,0:T(8,128)S(1)}, u32[]{:S(2)}, u32[]{:S(2)}) %collective-permute-start.5) | collective-permute-done | bytes 131104 | tf_op jit(solution)/shard_map/ppermute | solution.py:282
  23.7 3.0 %collective-permute-done.4.two = f32[2,128,128]{2,1,0:T(8,128)S(1)} collective-permute-done((f32[2,128,128]{2,1,0:T(8,128)S(1)}, f32[2,128,128]{2,1,0:T(8,128)S(1)}, u32[]{:S(2)}, u32[]{:S(2)}) %collective-permute-start.4) | collective-permute-done | bytes 131104 | tf_op jit(solution)/shard_map/ppermute | solution.py:282
  26.7 0.0 copy-done
  26.7 0.0 copy-done.3
  26.7 1.3 %collective-permute-start.6 = (f32[2,128,128]{2,1,0:T(8,128)S(1)}, f32[2,128,128]{2,1,0:T(8,128)S(1)}, u32[]{:S(2)}, u32[]{:S(2)}) collective-permute-start(f32[2,128,128]{2,1,0:T(8,128)S(1)} %get-tuple-element.40), channel_id=1, source_target_pairs={{4,20},{5,21},{22,6},{23,7},{36,52},{37,53},{54,38},{55,39},{68,84... | collective-permute-start | bytes 393224 | tf_op jit(solution)/shard_map/ppermute | solution.py:293
  28.0 3.6 %collective-permute-done.6.wave_in = f32[2,128,128]{2,1,0:T(8,128)S(1)} collective-permute-done((f32[2,128,128]{2,1,0:T(8,128)S(1)}, f32[2,128,128]{2,1,0:T(8,128)S(1)}, u32[]{:S(2)}, u32[]{:S(2)}) %collective-permute-start.6) | collective-permute-done | bytes 131104 | tf_op jit(solution)/shard_map/ppermute | solution.py:293
  31.6 1.8 %second.1 = (f32[2,128,128]{2,1,0:T(8,128)S(1)}, f32[4,2,128,128]{3,2,1,0:T(8,128)S(1)}, f32[4,2,128,128]{3,2,1,0:T(8,128)S(1)}) custom-call(f32[2,128,128]{2,1,0:T(8,128)S(1)} %collective-permute-done.6.wave_in, f32[2,128,128]{2,1,0:T(8,128)S(1)} %collective-permute-done.2.zero, ...), custom_call_target="tpu_custom_call", output_to_operand_aliasing={{1}: (6, {}), {2}: (7, {})} | custom-call | tf_op jit(solution)/shard_map/second/pallas_call | solution.py:234
  33.4 1.3 %collective-permute-start.7 = (f32[2,128,128]{2,1,0:T(8,128)S(1)}, f32[2,128,128]{2,1,0:T(8,128)S(1)}, u32[]{:S(2)}, u32[]{:S(2)}) collective-permute-start(f32[2,128,128]{2,1,0:T(8,128)S(1)} %get-tuple-element.43), channel_id=1, source_target_pairs={{20,24},{21,25},{6,10},{7,11},{52,56},{53,57},{38,42},{39,43},{84,... | collective-permute-start | bytes 393224 | tf_op jit(solution)/shard_map/ppermute | solution.py:293
  34.7 1.9 %collective-permute-done.7.wave_in = f32[2,128,128]{2,1,0:T(8,128)S(1)} collective-permute-done((f32[2,128,128]{2,1,0:T(8,128)S(1)}, f32[2,128,128]{2,1,0:T(8,128)S(1)}, u32[]{:S(2)}, u32[]{:S(2)}) %collective-permute-start.7) | collective-permute-done | bytes 131104 | tf_op jit(solution)/shard_map/ppermute | solution.py:293
  36.6 0.0 copy-start.4
  36.6 0.0 copy-start.5
  36.6 0.8 collective-permute-start.8
  37.4 0.0 collective-permute-done.8.wave_in
  37.4 0.1 copy-done.4
  37.5 0.1 copy-done.5
  37.6 0.7 collective-permute-start.9
  38.2 0.0 collective-permute-done.9.adjoint_in
  38.3 1.3 %collective-permute-start.10 = (f32[2,128,128]{2,1,0:T(8,128)S(1)}, f32[2,128,128]{2,1,0:T(8,128)S(1)}, u32[]{:S(2)}, u32[]{:S(2)}) collective-permute-start(f32[2,128,128]{2,1,0:T(8,128)S(1)} %get-tuple-element.54), channel_id=1, source_target_pairs={{24,20},{25,21},{10,6},{11,7},{56,52},{57,53},{42,38},{43,39},{88,... | collective-permute-start | bytes 393224 | tf_op jit(solution)/shard_map/ppermute | solution.py:310
  39.6 14.6 %collective-permute-done.10.adjoint_in = f32[2,128,128]{2,1,0:T(8,128)S(1)} collective-permute-done((f32[2,128,128]{2,1,0:T(8,128)S(1)}, f32[2,128,128]{2,1,0:T(8,128)S(1)}, u32[]{:S(2)}, u32[]{:S(2)}) %collective-permute-start.10) | collective-permute-done | bytes 131104 | tf_op jit(solution)/shard_map/ppermute | solution.py:310
  54.2 1.7 %back_second.1 = (f32[2,128,128]{2,1,0:T(8,128)S(1)}, f32[2,128,128]{2,1,0:T(8,128)S(1)}, f32[2,128,128]{2,1,0:T(8,128)S(1)}, f32[2,128,128]{2,1,0:T(8,128)S(1)}, f32[2,128,128]{2,1,0:T(8,128)S(1)}) custom-call(f32[2,128,128]{2,1,0:T(8,128)S(1)} %collective-permute-done.10.adjoint_in, ...), custom_call_target="tpu_custom_call", output_to_operand_aliasing={{0}: (4, {}), {1}: (5, {}), {2}: (6, {}), {3}: (7, {})} | custom-call | tf_op jit(solution)/shard_map/back_second/pallas_call | solution.py:234
  56.0 1.3 %collective-permute-start.11 = (f32[2,128,128]{2,1,0:T(8,128)S(1)}, f32[2,128,128]{2,1,0:T(8,128)S(1)}, u32[]{:S(2)}, u32[]{:S(2)}) collective-permute-start(f32[2,128,128]{2,1,0:T(8,128)S(1)} %get-tuple-element.59), channel_id=1, source_target_pairs={{20,4},{21,5},{6,22},{7,23},{52,36},{53,37},{38,54},{39,55},{84,68... | collective-permute-start | bytes 393224 | tf_op jit(solution)/shard_map/ppermute | solution.py:310
  57.3 1.0 %collective-permute-done.11.adjoint_in = f32[2,128,128]{2,1,0:T(8,128)S(1)} collective-permute-done((f32[2,128,128]{2,1,0:T(8,128)S(1)}, f32[2,128,128]{2,1,0:T(8,128)S(1)}, u32[]{:S(2)}, u32[]{:S(2)}) %collective-permute-start.11) | collective-permute-done | bytes 131104 | tf_op jit(solution)/shard_map/ppermute | solution.py:310
  58.2 3.7 %collective-permute-start.12 = (f32[2,128,128]{2,1,0:T(8,128)S(1)}, f32[2,128,128]{2,1,0:T(8,128)S(1)}, u32[]{:S(2)}, u32[]{:S(2)}) collective-permute-start(f32[2,128,128]{2,1,0:T(8,128)S(1)} %get-tuple-element.64), channel_id=1, source_target_pairs={{4,0},{20,4},{24,8},{8,12},{5,1},{21,5},{25,9},{9,13},{22,18},{6,2... | collective-permute-start | bytes 393224 | tf_op jit(solution)/shard_map/ppermute | solution.py:320
  61.9 2.9 %collective-permute-start.13 = (f32[2,128,128]{2,1,0:T(8,128)S(1)}, f32[2,128,128]{2,1,0:T(8,128)S(1)}, u32[]{:S(2)}, u32[]{:S(2)}) collective-permute-start(f32[2,128,128]{2,1,0:T(8,128)S(1)} %get-tuple-element.65), channel_id=1, source_target_pairs={{4,2},{20,6},{24,10},{8,14},{5,3},{21,7},{25,11},{9,15},{22,16},{6... | collective-permute-start | bytes 393224 | tf_op jit(solution)/shard_map/ppermute | solution.py:320
  64.8 1.3 %collective-permute-start.14 = (f32[2,128,128]{2,1,0:T(8,128)S(1)}, f32[2,128,128]{2,1,0:T(8,128)S(1)}, u32[]{:S(2)}, u32[]{:S(2)}) collective-permute-start(f32[2,128,128]{2,1,0:T(8,128)S(1)} %get-tuple-element.66), channel_id=1, source_target_pairs={{4,1},{20,5},{24,9},{8,13},{5,0},{21,4},{25,8},{9,12},{22,19},{6,2... | collective-permute-start | bytes 393224 | tf_op jit(solution)/shard_map/ppermute | solution.py:320
  66.1 0.0 copy-start.2
  66.1 3.9 %collective-permute-start.15 = (f32[2,128,128]{2,1,0:T(8,128)S(1)}, f32[2,128,128]{2,1,0:T(8,128)S(1)}, u32[]{:S(2)}, u32[]{:S(2)}) collective-permute-start(f32[2,128,128]{2,1,0:T(8,128)S(1)} %get-tuple-element.67), channel_id=1, source_target_pairs={{4,3},{20,7},{24,11},{8,15},{5,2},{21,6},{25,10},{9,14},{22,17},{6... | collective-permute-start | bytes 393224 | tf_op jit(solution)/shard_map/ppermute | solution.py:320
  70.0 0.0 collective-permute-done.12.zero
  70.0 0.0 collective-permute-done.13.one
  70.0 0.0 collective-permute-done.14.two
  70.0 3.7 %collective-permute-done.15.three = f32[2,128,128]{2,1,0:T(8,128)S(1)} collective-permute-done((f32[2,128,128]{2,1,0:T(8,128)S(1)}, f32[2,128,128]{2,1,0:T(8,128)S(1)}, u32[]{:S(2)}, u32[]{:S(2)}) %collective-permute-start.15) | collective-permute-done | bytes 131104 | tf_op jit(solution)/shard_map/ppermute | solution.py:320
  73.8 0.7 place.1
  74.4 2.3 %collective-permute-start.17 = (f32[2,256,128]{2,1,0:T(8,128)S(1)}, f32[2,256,128]{2,1,0:T(8,128)S(1)}, u32[]{:S(2)}, u32[]{:S(2)}) collective-permute-start(f32[2,256,128]{2,1,0:T(8,128)S(1)} %get-tuple-element.69), channel_id=1, source_target_pairs={{16,32},{48,64},{80,96},{112,128},{144,160},{176,192},{208,224},{2... | collective-permute-start | bytes 786440 | tf_op jit(solution)/shard_map/ppermute | solution.py:328
  76.8 1.9 %collective-permute-start.16 = (f32[2,256,128]{2,1,0:T(8,128)S(1)}, f32[2,256,128]{2,1,0:T(8,128)S(1)}, u32[]{:S(2)}, u32[]{:S(2)}) collective-permute-start(f32[2,256,128]{2,1,0:T(8,128)S(1)} %get-tuple-element.68), channel_id=1, source_target_pairs={{0,16},{16,0},{32,48},{48,32},{64,80},{80,64},{96,112},{112,96},{1... | collective-permute-start | bytes 786440 | tf_op jit(solution)/shard_map/ppermute | solution.py:327
  78.7 4.6 %collective-permute-done.17.far = f32[2,256,128]{2,1,0:T(8,128)S(1)} collective-permute-done((f32[2,256,128]{2,1,0:T(8,128)S(1)}, f32[2,256,128]{2,1,0:T(8,128)S(1)}, u32[]{:S(2)}, u32[]{:S(2)}) %collective-permute-start.17) | collective-permute-done | bytes 262176 | tf_op jit(solution)/shard_map/ppermute | solution.py:328
  83.3 0.0 copy-done.2
  83.3 0.1 step.1.stepped
  83.4 0.0 collective-permute-done.16.near
  83.4 0.7 last.1
  (6 shorter events, 0.1 us)
Async XLA Ops:
  0.0 10.7 %copy-start.6 = (s32[2]{0:T(128)S(1)}, s32[2]{0:T(128)}, u32[]{:S(2)}) copy-start(s32[2]{0:T(128)} %owners.3) | copy-start | bytes 28
  0.0 10.7 %copy-start.7 = (s32[2]{0:T(128)S(1)}, s32[2]{0:T(128)}, u32[]{:S(2)}) copy-start(s32[2]{0:T(128)} %offsets.3) | copy-start | bytes 28
  0.0 9.7 %collective-permute-start.1 = (f32[2,256,128]{2,1,0:T(8,128)}, f32[2,256,128]{2,1,0:T(8,128)S(1)}, u32[]{:S(2)}, u32[]{:S(2)}) collective-permute-start(f32[2,256,128]{2,1,0:T(8,128)} %bitcast.1), channel_id=1, source_target_pairs={{16,32},{48,64},{80,96},{112,128},{144,160},{176,192},{208,224},{2... | collective-permute-start | bytes 786440 | tf_op jit(solution)/shard_map/ppermute | solution.py:272
  5.5 5.3 %collective-permute-start = (f32[2,256,128]{2,1,0:T(8,128)}, f32[2,256,128]{2,1,0:T(8,128)S(1)}, u32[]{:S(2)}, u32[]{:S(2)}) collective-permute-start(f32[2,256,128]{2,1,0:T(8,128)} %bitcast.2), channel_id=1, source_target_pairs={{0,16},{16,0},{32,48},{48,32},{64,80},{80,64},{96,112},{112,96},{1... | collective-permute-start | bytes 786440 | tf_op jit(solution)/shard_map/ppermute | solution.py:271
  9.7 1.0 %copy-start.1 = (f32[1,2,256,128]{3,2,1,0:T(8,128)S(1)}, f32[1,2,256,128]{3,2,1,0:T(8,128)}, u32[]{:S(2)}) copy-start(f32[1,2,256,128]{3,2,1,0:T(8,128)} %block.3) | copy-start | bytes 786436
  10.7 16.0 %copy-start = (f32[2,128,128]{2,1,0:T(8,128)S(1)}, f32[2,128,128]{2,1,0:T(8,128)}, u32[]{:S(2)}) copy-start(f32[2,128,128]{2,1,0:T(8,128)} %constant.4.clone.table_ref) | copy-start | bytes 393220
  10.7 16.0 %copy-start.3 = (f32[2,128,128]{2,1,0:T(8,128)S(1)}, f32[2,128,128]{2,1,0:T(8,128)}, u32[]{:S(2)}) copy-start(f32[2,128,128]{2,1,0:T(8,128)} %wave_in.1) | copy-start | bytes 393220
  11.4 10.3 %collective-permute-start.3 = (f32[2,128,128]{2,1,0:T(8,128)S(1)}, f32[2,128,128]{2,1,0:T(8,128)S(1)}, u32[]{:S(2)}, u32[]{:S(2)}) collective-permute-start(f32[2,128,128]{2,1,0:T(8,128)S(1)} %get-tuple-element.38), channel_id=1, source_target_pairs={{2,4},{6,20},{10,24},{14,8},{3,5},{7,21},{11,25},{15,9},{16,22},{2... | collective-permute-start | bytes 393224 | tf_op jit(solution)/shard_map/ppermute | solution.py:282
  14.9 6.8 %collective-permute-start.2 = (f32[2,128,128]{2,1,0:T(8,128)S(1)}, f32[2,128,128]{2,1,0:T(8,128)S(1)}, u32[]{:S(2)}, u32[]{:S(2)}) collective-permute-start(f32[2,128,128]{2,1,0:T(8,128)S(1)} %get-tuple-element.38), channel_id=1, source_target_pairs={{0,4},{4,20},{8,24},{12,8},{1,5},{5,21},{9,25},{13,9},{18,22},{22,... | collective-permute-start | bytes 393224 | tf_op jit(solution)/shard_map/ppermute | solution.py:282
  16.2 7.5 %collective-permute-start.5 = (f32[2,128,128]{2,1,0:T(8,128)S(1)}, f32[2,128,128]{2,1,0:T(8,128)S(1)}, u32[]{:S(2)}, u32[]{:S(2)}) collective-permute-start(f32[2,128,128]{2,1,0:T(8,128)S(1)} %get-tuple-element.39), channel_id=1, source_target_pairs={{3,4},{7,20},{11,24},{15,8},{2,5},{6,21},{10,25},{14,9},{17,22},{2... | collective-permute-start | bytes 393224 | tf_op jit(solution)/shard_map/ppermute | solution.py:282
  20.4 6.3 %collective-permute-start.4 = (f32[2,128,128]{2,1,0:T(8,128)S(1)}, f32[2,128,128]{2,1,0:T(8,128)S(1)}, u32[]{:S(2)}, u32[]{:S(2)}) collective-permute-start(f32[2,128,128]{2,1,0:T(8,128)S(1)} %get-tuple-element.39), channel_id=1, source_target_pairs={{1,4},{5,20},{9,24},{13,8},{0,5},{4,21},{8,25},{12,9},{19,22},{23,... | collective-permute-start | bytes 393224 | tf_op jit(solution)/shard_map/ppermute | solution.py:282
  26.7 4.9 %collective-permute-start.6 = (f32[2,128,128]{2,1,0:T(8,128)S(1)}, f32[2,128,128]{2,1,0:T(8,128)S(1)}, u32[]{:S(2)}, u32[]{:S(2)}) collective-permute-start(f32[2,128,128]{2,1,0:T(8,128)S(1)} %get-tuple-element.40), channel_id=1, source_target_pairs={{4,20},{5,21},{22,6},{23,7},{36,52},{37,53},{54,38},{55,39},{68,84... | collective-permute-start | bytes 393224 | tf_op jit(solution)/shard_map/ppermute | solution.py:293
  33.4 3.2 %collective-permute-start.7 = (f32[2,128,128]{2,1,0:T(8,128)S(1)}, f32[2,128,128]{2,1,0:T(8,128)S(1)}, u32[]{:S(2)}, u32[]{:S(2)}) collective-permute-start(f32[2,128,128]{2,1,0:T(8,128)S(1)} %get-tuple-element.43), channel_id=1, source_target_pairs={{20,24},{21,25},{6,10},{7,11},{52,56},{53,57},{38,42},{39,43},{84,... | collective-permute-start | bytes 393224 | tf_op jit(solution)/shard_map/ppermute | solution.py:293
  36.6 0.9 %copy-start.4 = (f32[2,128,128]{2,1,0:T(8,128)S(1)}, f32[2,128,128]{2,1,0:T(8,128)}, u32[]{:S(2)}) copy-start(f32[2,128,128]{2,1,0:T(8,128)} %measured.1) | copy-start | bytes 393220
  36.6 1.0 %copy-start.5 = (f32[2,128,128]{2,1,0:T(8,128)S(1)}, f32[2,128,128]{2,1,0:T(8,128)}, u32[]{:S(2)}) copy-start(f32[2,128,128]{2,1,0:T(8,128)} %constant.5.clone.fourier_ref) | copy-start | bytes 393220
  36.6 0.8 collective-permute-start.8
  37.6 0.7 collective-permute-start.9
  38.3 15.9 %collective-permute-start.10 = (f32[2,128,128]{2,1,0:T(8,128)S(1)}, f32[2,128,128]{2,1,0:T(8,128)S(1)}, u32[]{:S(2)}, u32[]{:S(2)}) collective-permute-start(f32[2,128,128]{2,1,0:T(8,128)S(1)} %get-tuple-element.54), channel_id=1, source_target_pairs={{24,20},{25,21},{10,6},{11,7},{56,52},{57,53},{42,38},{43,39},{88,... | collective-permute-start | bytes 393224 | tf_op jit(solution)/shard_map/ppermute | solution.py:310
  56.0 2.3 %collective-permute-start.11 = (f32[2,128,128]{2,1,0:T(8,128)S(1)}, f32[2,128,128]{2,1,0:T(8,128)S(1)}, u32[]{:S(2)}, u32[]{:S(2)}) collective-permute-start(f32[2,128,128]{2,1,0:T(8,128)S(1)} %get-tuple-element.59), channel_id=1, source_target_pairs={{20,4},{21,5},{6,22},{7,23},{52,36},{53,37},{38,54},{39,55},{84,68... | collective-permute-start | bytes 393224 | tf_op jit(solution)/shard_map/ppermute | solution.py:310
  58.2 11.8 %collective-permute-start.12 = (f32[2,128,128]{2,1,0:T(8,128)S(1)}, f32[2,128,128]{2,1,0:T(8,128)S(1)}, u32[]{:S(2)}, u32[]{:S(2)}) collective-permute-start(f32[2,128,128]{2,1,0:T(8,128)S(1)} %get-tuple-element.64), channel_id=1, source_target_pairs={{4,0},{20,4},{24,8},{8,12},{5,1},{21,5},{25,9},{9,13},{22,18},{6,2... | collective-permute-start | bytes 393224 | tf_op jit(solution)/shard_map/ppermute | solution.py:320
  61.9 8.1 %collective-permute-start.13 = (f32[2,128,128]{2,1,0:T(8,128)S(1)}, f32[2,128,128]{2,1,0:T(8,128)S(1)}, u32[]{:S(2)}, u32[]{:S(2)}) collective-permute-start(f32[2,128,128]{2,1,0:T(8,128)S(1)} %get-tuple-element.65), channel_id=1, source_target_pairs={{4,2},{20,6},{24,10},{8,14},{5,3},{21,7},{25,11},{9,15},{22,16},{6... | collective-permute-start | bytes 393224 | tf_op jit(solution)/shard_map/ppermute | solution.py:320
  64.8 5.2 %collective-permute-start.14 = (f32[2,128,128]{2,1,0:T(8,128)S(1)}, f32[2,128,128]{2,1,0:T(8,128)S(1)}, u32[]{:S(2)}, u32[]{:S(2)}) collective-permute-start(f32[2,128,128]{2,1,0:T(8,128)S(1)} %get-tuple-element.66), channel_id=1, source_target_pairs={{4,1},{20,5},{24,9},{8,13},{5,0},{21,4},{25,8},{9,12},{22,19},{6,2... | collective-permute-start | bytes 393224 | tf_op jit(solution)/shard_map/ppermute | solution.py:320
  66.1 17.2 %copy-start.2 = (f32[1,2,256,128]{3,2,1,0:T(8,128)S(1)}, f32[1,2,256,128]{3,2,1,0:T(8,128)}, u32[]{:S(2)}) copy-start(f32[1,2,256,128]{3,2,1,0:T(8,128)} %block.3) | copy-start | bytes 786436
  66.1 7.6 %collective-permute-start.15 = (f32[2,128,128]{2,1,0:T(8,128)S(1)}, f32[2,128,128]{2,1,0:T(8,128)S(1)}, u32[]{:S(2)}, u32[]{:S(2)}) collective-permute-start(f32[2,128,128]{2,1,0:T(8,128)S(1)} %get-tuple-element.67), channel_id=1, source_target_pairs={{4,3},{20,7},{24,11},{8,15},{5,2},{21,6},{25,10},{9,14},{22,17},{6... | collective-permute-start | bytes 393224 | tf_op jit(solution)/shard_map/ppermute | solution.py:320
  74.4 8.9 %collective-permute-start.17 = (f32[2,256,128]{2,1,0:T(8,128)S(1)}, f32[2,256,128]{2,1,0:T(8,128)S(1)}, u32[]{:S(2)}, u32[]{:S(2)}) collective-permute-start(f32[2,256,128]{2,1,0:T(8,128)S(1)} %get-tuple-element.69), channel_id=1, source_target_pairs={{16,32},{48,64},{80,96},{112,128},{144,160},{176,192},{208,224},{2... | collective-permute-start | bytes 786440 | tf_op jit(solution)/shard_map/ppermute | solution.py:328
  76.8 6.6 %collective-permute-start.16 = (f32[2,256,128]{2,1,0:T(8,128)S(1)}, f32[2,256,128]{2,1,0:T(8,128)S(1)}, u32[]{:S(2)}, u32[]{:S(2)}) collective-permute-start(f32[2,256,128]{2,1,0:T(8,128)S(1)} %get-tuple-element.68), channel_id=1, source_target_pairs={{0,16},{16,0},{32,48},{48,32},{64,80},{80,64},{96,112},{112,96},{1... | collective-permute-start | bytes 786440 | tf_op jit(solution)/shard_map/ppermute | solution.py:327

commit v6 on v5

--- a/solution.py
+++ b/solution.py
@@ -185,7 +185,7 @@
 
 
 def backward_kernel(mine, adjoint_in, waves, windows, table_ref, *rest):
-    parts, updates = rest[group : 2 * group], rest[-1]
+    rest, updates = rest[group if mine else 0 : -1], rest[-1]
 
     @pl.when(role() == mine)
     def _():
@@ -193,14 +193,16 @@
             pair(adjoint_in), waves, windows, updates, blocks(table_ref), mine == 0
         )
         if mine:
-            put(rest[2 * group], adjoint)
-        share(updates, parts)
-
-
-def place_kernel(owners, offsets, zero, one, two, three, slab, near, far):
+            put(rest[group], adjoint)
+        share(updates, rest[:group])
+
+
+def place_kernel(owners, offsets, *rest):
+    landed, (slab, near, far) = rest[: 2 * group], rest[2 * group :]
     slab[...] = jnp.zeros_like(slab)
+    zero, one, two, three = [landed[r][...] + landed[group + r][...] for r in range(group)]
     upper = upper_position()
-    for at, update in ((upper, two[...] + three[...]), (1 - upper, zero[...] + one[...])):
+    for at, update in ((upper, two + three), (1 - upper, zero + one)):
         rows = pl.ds(start_of(at, owners, offsets), side)
         slab[:, rows, :] = slab[:, rows, :] + update
 
@@ -255,11 +257,14 @@
     ]
     gathers = [
         [
-            (at(i, row * group + (x ^ mask)), at(*home[row]))
-            for (i, x), home in zip(targets, homes)
-            for row in range(group)
+            [
+                (at(i, row * group + (x ^ mask)), at(*home[row]))
+                for (i, x), home in zip(targets, homes)
+                for row in rows
+            ]
+            for mask in masks
         ]
-        for mask in masks
+        for rows in ((0,), range(1, group))
     ]
     hops = [
         [(at(*home[row]), at(*home[row + 1])) for home in homes] for row in range(group - 1)
@@ -278,16 +283,19 @@
         (near, owners, offsets, slab),
         aliases=[(3, 2)],
     )
-    come = [
-        lax.ppermute(upper_window if turn & 2 else lower_window, axes, gathers[turn])
-        for turn in range(group)
+    come_first, come = [
+        [
+            lax.ppermute(upper_window if turn & 2 else lower_window, axes, pairs[turn])
+            for turn in range(group)
+        ]
+        for pairs in gathers
     ]
 
     wave, waves, windows = call(
         functools.partial(forward_kernel, 0),
         "first",
         [window_type, stack_type, stack_type],
-        (probe_wave, *come, step_table),
+        (probe_wave, *come_first, step_table),
     )
     for mine, name in ((1, "second"), (2, "third")):
         wave = lax.ppermute(wave, axes, hops[mine - 1])
@@ -306,18 +314,26 @@
         (wave, *come, intensities, step_table, fourier_table),
         [stack_type] * 3,
     )
-    for mine, name in ((2, "back_third"), (1, "back_second"), (0, "back_first")):
+    for mine, name in ((2, "back_third"), (1, "back_second")):
         adjoint = lax.ppermute(adjoint, axes, ends(hops[mine]))
-        returned = call(
+        *parts, adjoint = call(
             functools.partial(backward_kernel, mine),
             name,
-            [window_type] * (group + min(mine, 1)),
+            [window_type] * (group + 1),
             (adjoint, waves, windows, step_table, *parts),
             [stack_type],
             aliases=[(4 + turn, turn) for turn in range(group)],
         )
-        parts, adjoint = returned[:group], returned[-1]
-    landed = [lax.ppermute(parts[turn], axes, ends(gathers[turn])) for turn in range(group)]
+    adjoint = lax.ppermute(adjoint, axes, ends(hops[0]))
+    landed = [lax.ppermute(parts[turn], axes, ends(gathers[1][turn])) for turn in range(group)]
+    parts = call(
+        functools.partial(backward_kernel, 0),
+        "back_first",
+        [window_type] * group,
+        (adjoint, waves, windows, step_table),
+        [stack_type],
+    )
+    landed += [lax.ppermute(parts[turn], axes, ends(gathers[0][turn])) for turn in range(group)]
     slab, near, far = call(
         place_kernel,
         "place",

time: 84.6 us -> 86.1 us (1.018)
  the two profiles are of different devices: /device:TPU:233 before, /device:TPU:231 now
where the time goes in v6:
time: 86.1 us; the launch traced here: 85.5 us
  starting transfers between devices  41.9 us (49%)
  waiting for transfers between devices  39.7 us (46%)
  Pallas kernels  2.32 us (3%)
  local copies, waits for them, and re-layouts  1.08 us (1%)
    ppermute x4, waiting for transfers between devices, shards(): lax.ppermute(parts[turn], axes, ends(gathers[0][turn]))  35.2 us
    ppermute x1, starting transfers between devices, shards(): far = lax.ppermute(far, 'scan', next_chip)  11.7 us
    ppermute x8, starting transfers between devices, shards(): lax.ppermute(upper_window if turn & 2 else lower_window, axes, pairs[turn])  10 us
    ppermute x1, starting transfers between devices, shards(): far = lax.ppermute(object_slices[0], 'scan', next_chip)  5.44 us
    ppermute x4, starting transfers between devices, shards(): lax.ppermute(parts[turn], axes, ends(gathers[0][turn]))  4.05 us
    ppermute x4, starting transfers between devices, shards(): lax.ppermute(parts[turn], axes, ends(gathers[1][turn]))  2.68 us
    pallas_call x12, Pallas kernels, call(): pl.pallas_call(kernel, out_shape=out_shape, in_specs=specs, out_specs=jax...  2.32 us
    ppermute x1, waiting for transfers between devices, shards(): far = lax.ppermute(object_slices[0], 'scan', next_chip)  2.32 us
  transfers between devices with their start and end apart: 26, of which 4 were waited for; matrix products, arithmetic and copies ran while one was open for 0% of the time, Pallas kernels for 0%

profile of v6, /device:TPU:231, one launch (start us, length us, event | category | flops | bytes accessed | tf_op | source)
XLA Modules:
  0.0 85.5 jit_solution(1462758923393248606)
XLA Ops:
  0.0 5.4 %collective-permute-start.1 = (f32[2,256,128]{2,1,0:T(8,128)}, f32[2,256,128]{2,1,0:T(8,128)S(1)}, u32[]{:S(2)}, u32[]{:S(2)}) collective-permute-start(f32[2,256,128]{2,1,0:T(8,128)} %bitcast.1), channel_id=1, source_target_pairs={{16,32},{48,64},{80,96},{112,128},{144,160},{176,192},{208,224},{2... | collective-permute-start | bytes 786440 | tf_op jit(solution)/shard_map/ppermute | solution.py:277
  5.5 1.9 %collective-permute-start = (f32[2,256,128]{2,1,0:T(8,128)}, f32[2,256,128]{2,1,0:T(8,128)S(1)}, u32[]{:S(2)}, u32[]{:S(2)}) collective-permute-start(f32[2,256,128]{2,1,0:T(8,128)} %bitcast.2), channel_id=1, source_target_pairs={{0,16},{16,0},{32,48},{48,32},{64,80},{80,64},{96,112},{112,96},{1... | collective-permute-start | bytes 786440 | tf_op jit(solution)/shard_map/ppermute | solution.py:276
  7.4 2.3 %collective-permute-done.1.far = f32[2,256,128]{2,1,0:T(8,128)S(1)} collective-permute-done((f32[2,256,128]{2,1,0:T(8,128)}, f32[2,256,128]{2,1,0:T(8,128)S(1)}, u32[]{:S(2)}, u32[]{:S(2)}) %collective-permute-start.1) | collective-permute-done | bytes 262176 | tf_op jit(solution)/shard_map/ppermute | solution.py:277
  9.7 0.9 %copy-done.1 = f32[1,2,256,128]{3,2,1,0:T(8,128)S(1)} copy-done((f32[1,2,256,128]{3,2,1,0:T(8,128)S(1)}, f32[1,2,256,128]{3,2,1,0:T(8,128)}, u32[]{:S(2)}) %copy-start.1) | copy-done | bytes 262168
  10.7 0.0 copy-start
  10.7 0.0 copy-start.3
  10.7 0.0 collective-permute-done.near
  10.7 0.6 cut.1
  11.4 0.7 collective-permute-start.3
  12.0 3.8 %collective-permute-start.2 = (f32[2,128,128]{2,1,0:T(8,128)S(1)}, f32[2,128,128]{2,1,0:T(8,128)S(1)}, u32[]{:S(2)}, u32[]{:S(2)}) collective-permute-start(f32[2,128,128]{2,1,0:T(8,128)S(1)} %get-tuple-element.38), channel_id=1, source_target_pairs={{0,4},{1,5},{18,22},{19,23},{32,36},{33,37},{50,54},{51,55},{64,68... | collective-permute-start | bytes 393224 | tf_op jit(solution)/shard_map/ppermute | solution.py:288
  15.9 0.7 collective-permute-start.5
  16.6 2.2 %collective-permute-start.4 = (f32[2,128,128]{2,1,0:T(8,128)S(1)}, f32[2,128,128]{2,1,0:T(8,128)S(1)}, u32[]{:S(2)}, u32[]{:S(2)}) collective-permute-start(f32[2,128,128]{2,1,0:T(8,128)S(1)} %get-tuple-element.39), channel_id=1, source_target_pairs={{1,4},{0,5},{19,22},{18,23},{33,36},{32,37},{51,54},{50,55},{65,68... | collective-permute-start | bytes 393224 | tf_op jit(solution)/shard_map/ppermute | solution.py:288
  18.7 0.7 collective-permute-start.8
  19.4 0.0 collective-permute-done.3.one
  19.4 0.7 collective-permute-start.7
  20.1 0.0 collective-permute-done.2.zero
  20.1 0.7 collective-permute-start.10
  20.8 0.0 collective-permute-done.5.three
  20.8 0.7 collective-permute-start.9
  21.5 0.0 collective-permute-done.4.two
  21.6 0.7 collective-permute-start.6
  22.2 0.0 collective-permute-done.8.one
  22.2 0.0 collective-permute-done.7.zero
  22.3 0.0 collective-permute-done.10.three
  22.3 0.0 collective-permute-done.9.two
  22.3 0.0 collective-permute-done.6.wave_in
  22.3 0.7 collective-permute-start.11
  23.0 0.0 collective-permute-done.11.wave_in
  23.0 0.0 copy-start.4
  23.0 0.0 copy-start.5
  23.1 0.8 collective-permute-start.12
  23.9 0.0 collective-permute-done.12.wave_in
  23.9 0.0 copy-done.4
  23.9 0.1 copy-done.5
  24.0 0.7 collective-permute-start.13
  24.7 0.0 collective-permute-done.13.adjoint_in
  24.7 0.7 collective-permute-start.14
  25.4 0.0 collective-permute-done.14.adjoint_in
  25.4 0.7 collective-permute-start.19
  26.1 0.7 collective-permute-start.15
  26.8 0.7 collective-permute-start.16
  27.5 0.7 collective-permute-start.17
  28.1 0.7 collective-permute-start.18
  28.8 0.0 collective-permute-done.19.adjoint_in
  28.9 1.3 %collective-permute-start.20 = (f32[2,128,128]{2,1,0:T(8,128)S(1)}, f32[2,128,128]{2,1,0:T(8,128)S(1)}, u32[]{:S(2)}, u32[]{:S(2)}) collective-permute-start(f32[2,128,128]{2,1,0:T(8,128)S(1)} %get-tuple-element.64), channel_id=1, source_target_pairs={{4,0},{5,1},{22,18},{23,19},{36,32},{37,33},{54,50},{55,51},{68,64... | collective-permute-start | bytes 393224 | tf_op jit(solution)/shard_map/ppermute | solution.py:336
  30.2 0.0 collective-permute-done.15.rest_0_
  30.2 0.7 collective-permute-start.21
  30.8 0.0 collective-permute-done.16.rest_1_
  30.9 1.3 %collective-permute-start.22 = (f32[2,128,128]{2,1,0:T(8,128)S(1)}, f32[2,128,128]{2,1,0:T(8,128)S(1)}, u32[]{:S(2)}, u32[]{:S(2)}) collective-permute-start(f32[2,128,128]{2,1,0:T(8,128)S(1)} %get-tuple-element.66), channel_id=1, source_target_pairs={{4,1},{5,0},{22,19},{23,18},{36,33},{37,32},{54,51},{55,50},{68,65... | collective-permute-start | bytes 393224 | tf_op jit(solution)/shard_map/ppermute | solution.py:336
  32.2 0.0 collective-permute-done.17.rest_2_
  32.2 0.0 copy-start.2
  32.2 0.8 collective-permute-start.23
  33.0 0.0 collective-permute-done.18.rest_3_
  33.0 30.2 %collective-permute-done.20.rest_4_ = f32[2,128,128]{2,1,0:T(8,128)S(1)} collective-permute-done((f32[2,128,128]{2,1,0:T(8,128)S(1)}, f32[2,128,128]{2,1,0:T(8,128)S(1)}, u32[]{:S(2)}, u32[]{:S(2)}) %collective-permute-start.20) | collective-permute-done | bytes 131104 | tf_op jit(solution)/shard_map/ppermute | solution.py:336
  63.2 0.0 collective-permute-done.21.rest_5_
  63.2 5.0 %collective-permute-done.22.rest_6_ = f32[2,128,128]{2,1,0:T(8,128)S(1)} collective-permute-done((f32[2,128,128]{2,1,0:T(8,128)S(1)}, f32[2,128,128]{2,1,0:T(8,128)S(1)}, u32[]{:S(2)}, u32[]{:S(2)}) %collective-permute-start.22) | collective-permute-done | bytes 131104 | tf_op jit(solution)/shard_map/ppermute | solution.py:336
  68.2 0.0 collective-permute-done.23.rest_7_
  68.2 0.7 place.1
  68.9 11.7 %collective-permute-start.25 = (f32[2,256,128]{2,1,0:T(8,128)S(1)}, f32[2,256,128]{2,1,0:T(8,128)S(1)}, u32[]{:S(2)}, u32[]{:S(2)}) collective-permute-start(f32[2,256,128]{2,1,0:T(8,128)S(1)} %get-tuple-element.69), channel_id=1, source_target_pairs={{16,32},{48,64},{80,96},{112,128},{144,160},{176,192},{208,224},{2... | collective-permute-start | bytes 786440 | tf_op jit(solution)/shard_map/ppermute | solution.py:344
  80.7 1.9 %collective-permute-start.24 = (f32[2,256,128]{2,1,0:T(8,128)S(1)}, f32[2,256,128]{2,1,0:T(8,128)S(1)}, u32[]{:S(2)}, u32[]{:S(2)}) collective-permute-start(f32[2,256,128]{2,1,0:T(8,128)S(1)} %get-tuple-element.68), channel_id=1, source_target_pairs={{0,16},{16,0},{32,48},{48,32},{64,80},{80,64},{96,112},{112,96},{1... | collective-permute-start | bytes 786440 | tf_op jit(solution)/shard_map/ppermute | solution.py:343
  82.6 2.1 %collective-permute-done.25.far = f32[2,256,128]{2,1,0:T(8,128)S(1)} collective-permute-done((f32[2,256,128]{2,1,0:T(8,128)S(1)}, f32[2,256,128]{2,1,0:T(8,128)S(1)}, u32[]{:S(2)}, u32[]{:S(2)}) %collective-permute-start.25) | collective-permute-done | bytes 262176 | tf_op jit(solution)/shard_map/ppermute | solution.py:344
  84.7 0.1 step.1.stepped
  84.8 0.0 collective-permute-done.24.near
  84.8 0.7 last.1
  (16 shorter events, 0.2 us)
Async XLA Ops:
  0.0 10.7 %copy-start.6 = (s32[2]{0:T(128)S(1)}, s32[2]{0:T(128)}, u32[]{:S(2)}) copy-start(s32[2]{0:T(128)} %owners.3) | copy-start | bytes 28
  0.0 10.7 %copy-start.7 = (s32[2]{0:T(128)S(1)}, s32[2]{0:T(128)}, u32[]{:S(2)}) copy-start(s32[2]{0:T(128)} %offsets.3) | copy-start | bytes 28
  0.0 9.7 %collective-permute-start.1 = (f32[2,256,128]{2,1,0:T(8,128)}, f32[2,256,128]{2,1,0:T(8,128)S(1)}, u32[]{:S(2)}, u32[]{:S(2)}) collective-permute-start(f32[2,256,128]{2,1,0:T(8,128)} %bitcast.1), channel_id=1, source_target_pairs={{16,32},{48,64},{80,96},{112,128},{144,160},{176,192},{208,224},{2... | collective-permute-start | bytes 786440 | tf_op jit(solution)/shard_map/ppermute | solution.py:277
  5.5 5.3 %collective-permute-start = (f32[2,256,128]{2,1,0:T(8,128)}, f32[2,256,128]{2,1,0:T(8,128)S(1)}, u32[]{:S(2)}, u32[]{:S(2)}) collective-permute-start(f32[2,256,128]{2,1,0:T(8,128)} %bitcast.2), channel_id=1, source_target_pairs={{0,16},{16,0},{32,48},{48,32},{64,80},{80,64},{96,112},{112,96},{1... | collective-permute-start | bytes 786440 | tf_op jit(solution)/shard_map/ppermute | solution.py:276
  9.7 1.0 %copy-start.1 = (f32[1,2,256,128]{3,2,1,0:T(8,128)S(1)}, f32[1,2,256,128]{3,2,1,0:T(8,128)}, u32[]{:S(2)}) copy-start(f32[1,2,256,128]{3,2,1,0:T(8,128)} %block.3) | copy-start | bytes 786436
  10.7 10.8 %copy-start = (f32[2,128,128]{2,1,0:T(8,128)S(1)}, f32[2,128,128]{2,1,0:T(8,128)}, u32[]{:S(2)}) copy-start(f32[2,128,128]{2,1,0:T(8,128)} %constant.4.clone.table_ref) | copy-start | bytes 393220
  10.7 10.8 %copy-start.3 = (f32[2,128,128]{2,1,0:T(8,128)S(1)}, f32[2,128,128]{2,1,0:T(8,128)}, u32[]{:S(2)}) copy-start(f32[2,128,128]{2,1,0:T(8,128)} %wave_in.1) | copy-start | bytes 393220
  11.4 8.1 %collective-permute-start.3 = (f32[2,128,128]{2,1,0:T(8,128)S(1)}, f32[2,128,128]{2,1,0:T(8,128)S(1)}, u32[]{:S(2)}, u32[]{:S(2)}) collective-permute-start(f32[2,128,128]{2,1,0:T(8,128)S(1)} %get-tuple-element.38), channel_id=1, source_target_pairs={{2,4},{3,5},{16,22},{17,23},{34,36},{35,37},{48,54},{49,55},{66,68... | collective-permute-start | bytes 393224 | tf_op jit(solution)/shard_map/ppermute | solution.py:288
  12.0 8.1 %collective-permute-start.2 = (f32[2,128,128]{2,1,0:T(8,128)S(1)}, f32[2,128,128]{2,1,0:T(8,128)S(1)}, u32[]{:S(2)}, u32[]{:S(2)}) collective-permute-start(f32[2,128,128]{2,1,0:T(8,128)S(1)} %get-tuple-element.38), channel_id=1, source_target_pairs={{0,4},{1,5},{18,22},{19,23},{32,36},{33,37},{50,54},{51,55},{64,68... | collective-permute-start | bytes 393224 | tf_op jit(solution)/shard_map/ppermute | solution.py:288
  15.9 4.9 %collective-permute-start.5 = (f32[2,128,128]{2,1,0:T(8,128)S(1)}, f32[2,128,128]{2,1,0:T(8,128)S(1)}, u32[]{:S(2)}, u32[]{:S(2)}) collective-permute-start(f32[2,128,128]{2,1,0:T(8,128)S(1)} %get-tuple-element.39), channel_id=1, source_target_pairs={{3,4},{2,5},{17,22},{16,23},{35,36},{34,37},{49,54},{48,55},{67,68... | collective-permute-start | bytes 393224 | tf_op jit(solution)/shard_map/ppermute | solution.py:288
  16.6 4.9 %collective-permute-start.4 = (f32[2,128,128]{2,1,0:T(8,128)S(1)}, f32[2,128,128]{2,1,0:T(8,128)S(1)}, u32[]{:S(2)}, u32[]{:S(2)}) collective-permute-start(f32[2,128,128]{2,1,0:T(8,128)S(1)} %get-tuple-element.39), channel_id=1, source_target_pairs={{1,4},{0,5},{19,22},{18,23},{33,36},{32,37},{51,54},{50,55},{65,68... | collective-permute-start | bytes 393224 | tf_op jit(solution)/shard_map/ppermute | solution.py:288
  18.7 3.5 %collective-permute-start.8 = (f32[2,128,128]{2,1,0:T(8,128)S(1)}, f32[2,128,128]{2,1,0:T(8,128)S(1)}, u32[]{:S(2)}, u32[]{:S(2)}) collective-permute-start(f32[2,128,128]{2,1,0:T(8,128)S(1)} %get-tuple-element.38), channel_id=1, source_target_pairs={{6,20},{10,24},{14,8},{7,21},{11,25},{15,9},{20,6},{24,10},{28,26}... | collective-permute-start | bytes 393224 | tf_op jit(solution)/shard_map/ppermute | solution.py:288
  19.4 2.8 %collective-permute-start.7 = (f32[2,128,128]{2,1,0:T(8,128)S(1)}, f32[2,128,128]{2,1,0:T(8,128)S(1)}, u32[]{:S(2)}, u32[]{:S(2)}) collective-permute-start(f32[2,128,128]{2,1,0:T(8,128)S(1)} %get-tuple-element.38), channel_id=1, source_target_pairs={{4,20},{8,24},{12,8},{5,21},{9,25},{13,9},{22,6},{26,10},{30,26},{... | collective-permute-start | bytes 393224 | tf_op jit(solution)/shard_map/ppermute | solution.py:288
  20.1 2.1 %collective-permute-start.10 = (f32[2,128,128]{2,1,0:T(8,128)S(1)}, f32[2,128,128]{2,1,0:T(8,128)S(1)}, u32[]{:S(2)}, u32[]{:S(2)}) collective-permute-start(f32[2,128,128]{2,1,0:T(8,128)S(1)} %get-tuple-element.39), channel_id=1, source_target_pairs={{7,20},{11,24},{15,8},{6,21},{10,25},{14,9},{21,6},{25,10},{29,26}... | collective-permute-start | bytes 393224 | tf_op jit(solution)/shard_map/ppermute | solution.py:288
  20.8 1.5 %collective-permute-start.9 = (f32[2,128,128]{2,1,0:T(8,128)S(1)}, f32[2,128,128]{2,1,0:T(8,128)S(1)}, u32[]{:S(2)}, u32[]{:S(2)}) collective-permute-start(f32[2,128,128]{2,1,0:T(8,128)S(1)} %get-tuple-element.39), channel_id=1, source_target_pairs={{5,20},{9,24},{13,8},{4,21},{8,25},{12,9},{23,6},{27,10},{31,26},{... | collective-permute-start | bytes 393224 | tf_op jit(solution)/shard_map/ppermute | solution.py:288
  21.6 0.7 collective-permute-start.6
  22.3 0.7 collective-permute-start.11
  23.0 0.9 %copy-start.4 = (f32[2,128,128]{2,1,0:T(8,128)S(1)}, f32[2,128,128]{2,1,0:T(8,128)}, u32[]{:S(2)}) copy-start(f32[2,128,128]{2,1,0:T(8,128)} %measured.1) | copy-start | bytes 393220
  23.0 1.0 %copy-start.5 = (f32[2,128,128]{2,1,0:T(8,128)S(1)}, f32[2,128,128]{2,1,0:T(8,128)}, u32[]{:S(2)}) copy-start(f32[2,128,128]{2,1,0:T(8,128)} %constant.5.clone.fourier_ref) | copy-start | bytes 393220
  23.1 0.8 collective-permute-start.12
  24.0 0.7 collective-permute-start.13
  24.7 0.7 collective-permute-start.14
  25.4 3.4 %collective-permute-start.19 = (f32[2,128,128]{2,1,0:T(8,128)S(1)}, f32[2,128,128]{2,1,0:T(8,128)S(1)}, u32[]{:S(2)}, u32[]{:S(2)}) collective-permute-start(f32[2,128,128]{2,1,0:T(8,128)S(1)} %get-tuple-element.63), channel_id=1, source_target_pairs={{20,4},{21,5},{6,22},{7,23},{52,36},{53,37},{38,54},{39,55},{84,68... | collective-permute-start | bytes 393224 | tf_op jit(solution)/shard_map/ppermute | solution.py:327
  26.1 4.1 %collective-permute-start.15 = (f32[2,128,128]{2,1,0:T(8,128)S(1)}, f32[2,128,128]{2,1,0:T(8,128)S(1)}, u32[]{:S(2)}, u32[]{:S(2)}) collective-permute-start(f32[2,128,128]{2,1,0:T(8,128)S(1)} %get-tuple-element.59), channel_id=1, source_target_pairs={{20,4},{24,8},{8,12},{21,5},{25,9},{9,13},{6,22},{10,26},{26,30},{... | collective-permute-start | bytes 393224 | tf_op jit(solution)/shard_map/ppermute | solution.py:328
  26.8 4.1 %collective-permute-start.16 = (f32[2,128,128]{2,1,0:T(8,128)S(1)}, f32[2,128,128]{2,1,0:T(8,128)S(1)}, u32[]{:S(2)}, u32[]{:S(2)}) collective-permute-start(f32[2,128,128]{2,1,0:T(8,128)S(1)} %get-tuple-element.60), channel_id=1, source_target_pairs={{20,6},{24,10},{8,14},{21,7},{25,11},{9,15},{6,20},{10,24},{26,28}... | collective-permute-start | bytes 393224 | tf_op jit(solution)/shard_map/ppermute | solution.py:328
  27.5 4.7 %collective-permute-start.17 = (f32[2,128,128]{2,1,0:T(8,128)S(1)}, f32[2,128,128]{2,1,0:T(8,128)S(1)}, u32[]{:S(2)}, u32[]{:S(2)}) collective-permute-start(f32[2,128,128]{2,1,0:T(8,128)S(1)} %get-tuple-element.61), channel_id=1, source_target_pairs={{20,5},{24,9},{8,13},{21,4},{25,8},{9,12},{6,23},{10,27},{26,31},{... | collective-permute-start | bytes 393224 | tf_op jit(solution)/shard_map/ppermute | solution.py:328
  28.1 4.9 %collective-permute-start.18 = (f32[2,128,128]{2,1,0:T(8,128)S(1)}, f32[2,128,128]{2,1,0:T(8,128)S(1)}, u32[]{:S(2)}, u32[]{:S(2)}) collective-permute-start(f32[2,128,128]{2,1,0:T(8,128)S(1)} %get-tuple-element.62), channel_id=1, source_target_pairs={{20,7},{24,11},{8,15},{21,6},{25,10},{9,14},{6,21},{10,25},{26,29}... | collective-permute-start | bytes 393224 | tf_op jit(solution)/shard_map/ppermute | solution.py:328
  28.9 34.4 %collective-permute-start.20 = (f32[2,128,128]{2,1,0:T(8,128)S(1)}, f32[2,128,128]{2,1,0:T(8,128)S(1)}, u32[]{:S(2)}, u32[]{:S(2)}) collective-permute-start(f32[2,128,128]{2,1,0:T(8,128)S(1)} %get-tuple-element.64), channel_id=1, source_target_pairs={{4,0},{5,1},{22,18},{23,19},{36,32},{37,33},{54,50},{55,51},{68,64... | collective-permute-start | bytes 393224 | tf_op jit(solution)/shard_map/ppermute | solution.py:336
  30.2 33.0 %collective-permute-start.21 = (f32[2,128,128]{2,1,0:T(8,128)S(1)}, f32[2,128,128]{2,1,0:T(8,128)S(1)}, u32[]{:S(2)}, u32[]{:S(2)}) collective-permute-start(f32[2,128,128]{2,1,0:T(8,128)S(1)} %get-tuple-element.65), channel_id=1, source_target_pairs={{4,2},{5,3},{22,16},{23,17},{36,34},{37,35},{54,48},{55,49},{68,66... | collective-permute-start | bytes 393224 | tf_op jit(solution)/shard_map/ppermute | solution.py:336
  30.9 37.4 %collective-permute-start.22 = (f32[2,128,128]{2,1,0:T(8,128)S(1)}, f32[2,128,128]{2,1,0:T(8,128)S(1)}, u32[]{:S(2)}, u32[]{:S(2)}) collective-permute-start(f32[2,128,128]{2,1,0:T(8,128)S(1)} %get-tuple-element.66), channel_id=1, source_target_pairs={{4,1},{5,0},{22,19},{23,18},{36,33},{37,32},{54,51},{55,50},{68,65... | collective-permute-start | bytes 393224 | tf_op jit(solution)/shard_map/ppermute | solution.py:336
  32.2 52.5 %copy-start.2 = (f32[1,2,256,128]{3,2,1,0:T(8,128)S(1)}, f32[1,2,256,128]{3,2,1,0:T(8,128)}, u32[]{:S(2)}) copy-start(f32[1,2,256,128]{3,2,1,0:T(8,128)} %block.3) | copy-start | bytes 786436
  32.2 36.0 %collective-permute-start.23 = (f32[2,128,128]{2,1,0:T(8,128)S(1)}, f32[2,128,128]{2,1,0:T(8,128)S(1)}, u32[]{:S(2)}, u32[]{:S(2)}) collective-permute-start(f32[2,128,128]{2,1,0:T(8,128)S(1)} %get-tuple-element.67), channel_id=1, source_target_pairs={{4,3},{5,2},{22,17},{23,16},{36,35},{37,34},{54,49},{55,48},{68,67... | collective-permute-start | bytes 393224 | tf_op jit(solution)/shard_map/ppermute | solution.py:336
  68.9 15.8 %collective-permute-start.25 = (f32[2,256,128]{2,1,0:T(8,128)S(1)}, f32[2,256,128]{2,1,0:T(8,128)S(1)}, u32[]{:S(2)}, u32[]{:S(2)}) collective-permute-start(f32[2,256,128]{2,1,0:T(8,128)S(1)} %get-tuple-element.69), channel_id=1, source_target_pairs={{16,32},{48,64},{80,96},{112,128},{144,160},{176,192},{208,224},{2... | collective-permute-start | bytes 786440 | tf_op jit(solution)/shard_map/ppermute | solution.py:344
  80.7 4.1 %collective-permute-start.24 = (f32[2,256,128]{2,1,0:T(8,128)S(1)}, f32[2,256,128]{2,1,0:T(8,128)S(1)}, u32[]{:S(2)}, u32[]{:S(2)}) collective-permute-start(f32[2,256,128]{2,1,0:T(8,128)S(1)} %get-tuple-element.68), channel_id=1, source_target_pairs={{0,16},{16,0},{32,48},{48,32},{64,80},{80,64},{96,112},{112,96},{1... | collective-permute-start | bytes 786440 | tf_op jit(solution)/shard_map/ppermute | solution.py:343

commit v7 on v5

--- a/solution.py
+++ b/solution.py
@@ -13,6 +13,7 @@
 tile = 256
 group = 4
 masks = (0, 2, 1, 3)
+back_masks = (1, 2, 3, 0)
 params = pltpu.CompilerParams(vmem_limit_bytes=48 * 2**20)
 in_vmem = pl.BlockSpec(memory_space=pltpu.VMEM)
 in_smem = pl.BlockSpec(memory_space=pltpu.SMEM)
@@ -82,8 +83,8 @@
 def role():
     depth, scan = lax.axis_index("depth"), lax.axis_index("scan")
     row, home = depth // group, (depth % group) // 2 == (scan & 1)
-    second, third = row == 1, row == 2
-    return jnp.where(second, jnp.where(home, 0, 1), jnp.where(third, jnp.where(home, 3, 2), -1))
+    top, bottom = row == 0, row == group - 1
+    return jnp.where(top, jnp.where(home, 0, 1), jnp.where(bottom, jnp.where(home, 3, 2), -1))
 
 
 def column():
@@ -105,9 +106,11 @@
     pl.when(jnp.logical_not(even_scan))(odd)
 
 
-def lay_kernel(far, block, slab):
+def stage_kernel(block, slab):
     slab[:, tile : 2 * tile] = block[0]
 
+
+def lay_kernel(far, staged, slab):
     def even():
         slab[:, :tile] = far[...]
 
@@ -117,7 +120,7 @@
     by_scan_parity(even, odd)
 
 
-def cut_kernel(near, owners, offsets, laid, lower_out, upper_out, slab):
+def cut_kernel(near, owners, offsets, laid, lower_out, upper_out, own, slab):
     def even():
         slab[:, 2 * tile :] = near[...]
 
@@ -128,6 +131,7 @@
     upper = upper_position()
     for at, out in ((upper, upper_out), (1 - upper, lower_out)):
         out[...] = slab[:, pl.ds(start_of(at, owners, offsets), side), :]
+    own[...] = lower_out[...]
 
 
 def collect(arrived, windows):
@@ -162,7 +166,7 @@
 def share(updates, parts):
     me = column()
     for turn in range(group):
-        parts[turn][...] = updates[me ^ masks[turn]]
+        parts[turn][...] = updates[me ^ back_masks[turn]]
 
 
 def far_kernel(wave_in, zero, one, two, three, measured, table_ref, fourier_ref, *rest):
@@ -185,7 +189,7 @@
 
 
 def backward_kernel(mine, adjoint_in, waves, windows, table_ref, *rest):
-    parts, updates = rest[group : 2 * group], rest[-1]
+    rest, updates = rest[group:-1], rest[-1]
 
     @pl.when(role() == mine)
     def _():
@@ -193,14 +197,17 @@
             pair(adjoint_in), waves, windows, updates, blocks(table_ref), mine == 0
         )
         if mine:
-            put(rest[2 * group], adjoint)
-        share(updates, parts)
-
-
-def place_kernel(owners, offsets, zero, one, two, three, slab, near, far):
+            put(rest[group], adjoint)
+        share(updates, rest[:group])
+
+
+def place_kernel(owners, offsets, own, one, two, three, zero, slab, near, far):
     slab[...] = jnp.zeros_like(slab)
+    local = (role() == 0) | (role() == group - 1)
+    late = one[...] + three[...]
+    early = two[...] + jnp.where(local, own[...], zero[...])
     upper = upper_position()
-    for at, update in ((upper, two[...] + three[...]), (1 - upper, zero[...] + one[...])):
+    for at, update in ((upper, late), (1 - upper, early)):
         rows = pl.ds(start_of(at, owners, offsets), side)
         slab[:, rows, :] = slab[:, rows, :] + update
 
@@ -249,18 +256,17 @@
         return [(b, a) for a, b in pairs]
 
     targets = [(i, 2 * (i & 1) + q) for i in range(scans) for q in range(2)]
-    homes = [
-        [(i, group + x), (i ^ 1, group + x), (i ^ 1, 2 * group + x), (i, 2 * group + x)]
-        for i, x in targets
-    ]
-    gathers = [
-        [
+    bottom = depths - group
+    homes = [[(i, x), (i ^ 1, x), (i ^ 1, bottom + x), (i, bottom + x)] for i, x in targets]
+
+    def sends(mask):
+        pairs = [
             (at(i, row * group + (x ^ mask)), at(*home[row]))
             for (i, x), home in zip(targets, homes)
             for row in range(group)
         ]
-        for mask in masks
-    ]
+        return [(a, b) for a, b in pairs if a != b]
+
     hops = [
         [(at(*home[row]), at(*home[row + 1])) for home in homes] for row in range(group - 1)
     ]
@@ -270,24 +276,25 @@
 
     near = lax.ppermute(object_slices[0], "scan", on_chip)
     far = lax.ppermute(object_slices[0], "scan", next_chip)
-    slab = call(lay_kernel, "lay", slab_type, (far, object_slices))
-    lower_window, upper_window, slab = call(
+    slab = call(stage_kernel, "stage", slab_type, (object_slices,))
+    slab = call(lay_kernel, "lay", slab_type, (far, slab), aliases=[(1, 0)])
+    lower_window, upper_window, own, slab = call(
         cut_kernel,
         "cut",
-        [window_type, window_type, slab_type],
+        [window_type] * 3 + [slab_type],
         (near, owners, offsets, slab),
-        aliases=[(3, 2)],
+        aliases=[(3, 3)],
     )
     come = [
-        lax.ppermute(upper_window if turn & 2 else lower_window, axes, gathers[turn])
-        for turn in range(group)
+        lax.ppermute(upper_window if mask & 1 else lower_window, axes, sends(mask))
+        for mask in masks
     ]
 
     wave, waves, windows = call(
         functools.partial(forward_kernel, 0),
         "first",
         [window_type, stack_type, stack_type],
-        (probe_wave, *come, step_table),
+        (probe_wave, own, *come[1:], step_table),
     )
     for mine, name in ((1, "second"), (2, "third")):
         wave = lax.ppermute(wave, axes, hops[mine - 1])
@@ -303,7 +310,7 @@
         far_kernel,
         "far",
         [window_type] * (1 + group),
-        (wave, *come, intensities, step_table, fourier_table),
+        (wave, own, *come[1:], intensities, step_table, fourier_table),
         [stack_type] * 3,
     )
     for mine, name in ((2, "back_third"), (1, "back_second"), (0, "back_first")):
@@ -317,12 +324,14 @@
             aliases=[(4 + turn, turn) for turn in range(group)],
         )
         parts, adjoint = returned[:group], returned[-1]
-    landed = [lax.ppermute(parts[turn], axes, ends(gathers[turn])) for turn in range(group)]
+    landed = [
+        lax.ppermute(part, axes, ends(sends(mask))) for mask, part in zip(back_masks, parts)
+    ]
     slab, near, far = call(
         place_kernel,
         "place",
         [slab_type, tile_type, tile_type],
-        (owners, offsets, *landed),
+        (owners, offsets, parts[-1], *landed),
     )
     near = lax.ppermute(near, "scan", on_chip)
     far = lax.ppermute(far, "scan", next_chip)

time: 84.6 us -> 79.9 us (0.944)
  the two profiles are of different devices: /device:TPU:233 before, /device:TPU:97 now
where the time goes in v7:
time: 79.9 us; the launch traced here: 79.4 us
  waiting for transfers between devices  38.2 us (48%)
  starting transfers between devices  34 us (43%)
  Pallas kernels  5.65 us (7%)
  local copies, waits for them, and re-layouts  1.14 us (1%)
    ppermute x3, waiting for transfers between devices, shards(): adjoint = lax.ppermute(adjoint, axes, ends(hops[mine]))  16.8 us
    ppermute x4, starting transfers between devices, shards(): lax.ppermute(upper_window if mask & 1 else lower_window, axes, sends(mask))  9.16 us
    ppermute x4, starting transfers between devices, shards(): lax.ppermute(part, axes, ends(sends(mask)))  6.56 us
    ppermute x4, waiting for transfers between devices, shards(): lax.ppermute(part, axes, ends(sends(mask)))  6.5 us
    pallas_call x13, Pallas kernels, call(): pl.pallas_call(kernel, out_shape=out_shape, in_specs=specs, out_specs=jax...  5.65 us
    ppermute x4, waiting for transfers between devices, shards(): lax.ppermute(upper_window if mask & 1 else lower_window, axes, sends(mask))  5.37 us
    ppermute x1, starting transfers between devices, shards(): far = lax.ppermute(object_slices[0], 'scan', next_chip)  5.31 us
    ppermute x1, waiting for transfers between devices, shards(): far = lax.ppermute(far, 'scan', next_chip)  4.4 us
  transfers between devices with their start and end apart: 18, of which 10 were waited for; matrix products, arithmetic and copies ran while one was open for 0% of the time, Pallas kernels for 0%

profile of v7, /device:TPU:97, one launch (start us, length us, event | category | flops | bytes accessed | tf_op | source)
XLA Modules:
  0.0 79.4 jit_solution(11940370766178910923)
XLA Ops:
  0.0 5.3 %collective-permute-start.1 = (f32[2,256,128]{2,1,0:T(8,128)}, f32[2,256,128]{2,1,0:T(8,128)S(1)}, u32[]{:S(2)}, u32[]{:S(2)}) collective-permute-start(f32[2,256,128]{2,1,0:T(8,128)} %bitcast.1), channel_id=1, source_target_pairs={{16,32},{48,64},{80,96},{112,128},{144,160},{176,192},{208,224},{2... | collective-permute-start | bytes 786440 | tf_op jit(solution)/shard_map/ppermute | solution.py:278
  5.3 1.9 %collective-permute-start = (f32[2,256,128]{2,1,0:T(8,128)}, f32[2,256,128]{2,1,0:T(8,128)S(1)}, u32[]{:S(2)}, u32[]{:S(2)}) collective-permute-start(f32[2,256,128]{2,1,0:T(8,128)} %bitcast.2), channel_id=1, source_target_pairs={{0,16},{16,0},{32,48},{48,32},{64,80},{80,64},{96,112},{112,96},{1... | collective-permute-start | bytes 786440 | tf_op jit(solution)/shard_map/ppermute | solution.py:277
  7.2 0.0 copy-start.1
  7.3 0.9 %copy-done.1 = f32[1,2,256,128]{3,2,1,0:T(8,128)S(1)} copy-done((f32[1,2,256,128]{3,2,1,0:T(8,128)S(1)}, f32[1,2,256,128]{3,2,1,0:T(8,128)}, u32[]{:S(2)}) %copy-start.1) | copy-done | bytes 262168
  8.2 0.0 copy-start.6
  8.2 0.0 copy-start.7
  8.2 1.3 %collective-permute-done.1.far = f32[2,256,128]{2,1,0:T(8,128)S(1)} collective-permute-done((f32[2,256,128]{2,1,0:T(8,128)}, f32[2,256,128]{2,1,0:T(8,128)S(1)}, u32[]{:S(2)}, u32[]{:S(2)}) %collective-permute-start.1) | collective-permute-done | bytes 262176 | tf_op jit(solution)/shard_map/ppermute | solution.py:278
  9.6 0.0 copy-start
  9.6 0.0 copy-start.3
  9.6 0.0 collective-permute-done.near
  9.6 0.0 copy-done.6
  9.6 0.0 copy-done.7
  9.6 0.6 cut.1
  10.3 4.7 %collective-permute-start.2 = (f32[2,128,128]{2,1,0:T(8,128)S(1)}, f32[2,128,128]{2,1,0:T(8,128)S(1)}, u32[]{:S(2)}, u32[]{:S(2)}) collective-permute-start(f32[2,128,128]{2,1,0:T(8,128)S(1)} %get-tuple-element.40), channel_id=1, source_target_pairs={{2,0},{6,16},{10,28},{14,12},{3,1},{7,17},{11,29},{15,13},{16,18},... | collective-permute-start | bytes 393224 | tf_op jit(solution)/shard_map/ppermute | solution.py:289
  14.9 1.9 %collective-permute-start.4 = (f32[2,128,128]{2,1,0:T(8,128)S(1)}, f32[2,128,128]{2,1,0:T(8,128)S(1)}, u32[]{:S(2)}, u32[]{:S(2)}) collective-permute-start(f32[2,128,128]{2,1,0:T(8,128)S(1)} %get-tuple-element.41), channel_id=1, source_target_pairs={{3,0},{7,16},{11,28},{15,12},{2,1},{6,17},{10,29},{14,13},{17,18},... | collective-permute-start | bytes 393224 | tf_op jit(solution)/shard_map/ppermute | solution.py:289
  16.9 1.3 %collective-permute-start.3 = (f32[2,128,128]{2,1,0:T(8,128)S(1)}, f32[2,128,128]{2,1,0:T(8,128)S(1)}, u32[]{:S(2)}, u32[]{:S(2)}) collective-permute-start(f32[2,128,128]{2,1,0:T(8,128)S(1)} %get-tuple-element.41), channel_id=1, source_target_pairs={{1,0},{5,16},{9,28},{13,12},{0,1},{4,17},{8,29},{12,13},{19,18},{2... | collective-permute-start | bytes 393224 | tf_op jit(solution)/shard_map/ppermute | solution.py:289
  18.2 1.3 %collective-permute-start.6 = (f32[2,128,128]{2,1,0:T(8,128)S(1)}, f32[2,128,128]{2,1,0:T(8,128)S(1)}, u32[]{:S(2)}, u32[]{:S(2)}) collective-permute-start(f32[2,128,128]{2,1,0:T(8,128)S(1)} %get-tuple-element.40), channel_id=1, source_target_pairs={{4,16},{8,28},{5,17},{9,29},{22,2},{26,14},{23,3},{27,15},{36,48},... | collective-permute-start | bytes 393224 | tf_op jit(solution)/shard_map/ppermute | solution.py:289
  19.5 0.0 collective-permute-done.2.one
  19.5 4.6 %collective-permute-done.4.three = f32[2,128,128]{2,1,0:T(8,128)S(1)} collective-permute-done((f32[2,128,128]{2,1,0:T(8,128)S(1)}, f32[2,128,128]{2,1,0:T(8,128)S(1)}, u32[]{:S(2)}, u32[]{:S(2)}) %collective-permute-start.4) | collective-permute-done | bytes 131104 | tf_op jit(solution)/shard_map/ppermute | solution.py:289
  24.1 0.7 collective-permute-done.3.two
  24.8 0.0 copy-done
  24.8 0.0 copy-done.3
  24.8 1.3 %collective-permute-start.5 = (f32[2,128,128]{2,1,0:T(8,128)S(1)}, f32[2,128,128]{2,1,0:T(8,128)S(1)}, u32[]{:S(2)}, u32[]{:S(2)}) collective-permute-start(f32[2,128,128]{2,1,0:T(8,128)S(1)} %get-tuple-element.42), channel_id=1, source_target_pairs={{0,16},{1,17},{18,2},{19,3},{32,48},{33,49},{50,34},{51,35},{64,80... | collective-permute-start | bytes 393224 | tf_op jit(solution)/shard_map/ppermute | solution.py:300
  26.1 0.0 collective-permute-done.6.zero
  26.1 1.9 %collective-permute-done.5.wave_in = f32[2,128,128]{2,1,0:T(8,128)S(1)} collective-permute-done((f32[2,128,128]{2,1,0:T(8,128)S(1)}, f32[2,128,128]{2,1,0:T(8,128)S(1)}, u32[]{:S(2)}, u32[]{:S(2)}) %collective-permute-start.5) | collective-permute-done | bytes 131104 | tf_op jit(solution)/shard_map/ppermute | solution.py:300
  28.1 1.8 %second.1 = (f32[2,128,128]{2,1,0:T(8,128)S(1)}, f32[4,2,128,128]{3,2,1,0:T(8,128)S(1)}, f32[4,2,128,128]{3,2,1,0:T(8,128)S(1)}) custom-call(f32[2,128,128]{2,1,0:T(8,128)S(1)} %collective-permute-done.5.wave_in, f32[2,128,128]{2,1,0:T(8,128)S(1)} %collective-permute-done.6.zero, ...), custom_call_target="tpu_custom_call", output_to_operand_aliasing={{1}: (6, {}), {2}: (7, {})} | custom-call | tf_op jit(solution)/shard_map/second/pallas_call | solution.py:241
  29.8 1.3 %collective-permute-start.7 = (f32[2,128,128]{2,1,0:T(8,128)S(1)}, f32[2,128,128]{2,1,0:T(8,128)S(1)}, u32[]{:S(2)}, u32[]{:S(2)}) collective-permute-start(f32[2,128,128]{2,1,0:T(8,128)S(1)} %get-tuple-element.45), channel_id=1, source_target_pairs={{16,28},{17,29},{2,14},{3,15},{48,60},{49,61},{34,46},{35,47},{80,... | collective-permute-start | bytes 393224 | tf_op jit(solution)/shard_map/ppermute | solution.py:300
  31.1 1.9 %collective-permute-done.7.wave_in = f32[2,128,128]{2,1,0:T(8,128)S(1)} collective-permute-done((f32[2,128,128]{2,1,0:T(8,128)S(1)}, f32[2,128,128]{2,1,0:T(8,128)S(1)}, u32[]{:S(2)}, u32[]{:S(2)}) %collective-permute-start.7) | collective-permute-done | bytes 131104 | tf_op jit(solution)/shard_map/ppermute | solution.py:300
  33.1 0.0 copy-start.4
  33.1 0.0 copy-start.5
  33.1 0.8 collective-permute-start.8
  33.9 0.0 collective-permute-done.8.wave_in
  33.9 0.1 copy-done.4
  34.0 0.1 copy-done.5
  34.0 0.7 collective-permute-start.9
  34.7 0.0 collective-permute-done.9.adjoint_in
  34.8 1.3 %collective-permute-start.10 = (f32[2,128,128]{2,1,0:T(8,128)S(1)}, f32[2,128,128]{2,1,0:T(8,128)S(1)}, u32[]{:S(2)}, u32[]{:S(2)}) collective-permute-start(f32[2,128,128]{2,1,0:T(8,128)S(1)} %get-tuple-element.56), channel_id=1, source_target_pairs={{28,16},{29,17},{14,2},{15,3},{60,48},{61,49},{46,34},{47,35},{92,... | collective-permute-start | bytes 393224 | tf_op jit(solution)/shard_map/ppermute | solution.py:317
  36.1 15.8 %collective-permute-done.10.adjoint_in = f32[2,128,128]{2,1,0:T(8,128)S(1)} collective-permute-done((f32[2,128,128]{2,1,0:T(8,128)S(1)}, f32[2,128,128]{2,1,0:T(8,128)S(1)}, u32[]{:S(2)}, u32[]{:S(2)}) %collective-permute-start.10) | collective-permute-done | bytes 131104 | tf_op jit(solution)/shard_map/ppermute | solution.py:317
  51.9 1.7 %back_second.1 = (f32[2,128,128]{2,1,0:T(8,128)S(1)}, f32[2,128,128]{2,1,0:T(8,128)S(1)}, f32[2,128,128]{2,1,0:T(8,128)S(1)}, f32[2,128,128]{2,1,0:T(8,128)S(1)}, f32[2,128,128]{2,1,0:T(8,128)S(1)}) custom-call(f32[2,128,128]{2,1,0:T(8,128)S(1)} %collective-permute-done.10.adjoint_in, ...), custom_call_target="tpu_custom_call", output_to_operand_aliasing={{0}: (4, {}), {1}: (5, {}), {2}: (6, {}), {3}: (7, {})} | custom-call | tf_op jit(solution)/shard_map/back_second/pallas_call | solution.py:241
  53.6 1.3 %collective-permute-start.11 = (f32[2,128,128]{2,1,0:T(8,128)S(1)}, f32[2,128,128]{2,1,0:T(8,128)S(1)}, u32[]{:S(2)}, u32[]{:S(2)}) collective-permute-start(f32[2,128,128]{2,1,0:T(8,128)S(1)} %get-tuple-element.61), channel_id=1, source_target_pairs={{16,0},{17,1},{2,18},{3,19},{48,32},{49,33},{34,50},{35,51},{80,64... | collective-permute-start | bytes 393224 | tf_op jit(solution)/shard_map/ppermute | solution.py:317
  54.9 1.0 %collective-permute-done.11.adjoint_in = f32[2,128,128]{2,1,0:T(8,128)S(1)} collective-permute-done((f32[2,128,128]{2,1,0:T(8,128)S(1)}, f32[2,128,128]{2,1,0:T(8,128)S(1)}, u32[]{:S(2)}, u32[]{:S(2)}) %collective-permute-start.11) | collective-permute-done | bytes 131104 | tf_op jit(solution)/shard_map/ppermute | solution.py:317
  55.9 1.3 %collective-permute-start.12 = (f32[2,128,128]{2,1,0:T(8,128)S(1)}, f32[2,128,128]{2,1,0:T(8,128)S(1)}, u32[]{:S(2)}, u32[]{:S(2)}) collective-permute-start(f32[2,128,128]{2,1,0:T(8,128)S(1)} %get-tuple-element.67), channel_id=1, source_target_pairs={{0,1},{16,5},{28,9},{12,13},{1,0},{17,4},{29,8},{13,12},{18,19},{2... | collective-permute-start | bytes 393224 | tf_op jit(solution)/shard_map/ppermute | solution.py:328
  57.2 1.9 %collective-permute-start.13 = (f32[2,128,128]{2,1,0:T(8,128)S(1)}, f32[2,128,128]{2,1,0:T(8,128)S(1)}, u32[]{:S(2)}, u32[]{:S(2)}) collective-permute-start(f32[2,128,128]{2,1,0:T(8,128)S(1)} %get-tuple-element.68), channel_id=1, source_target_pairs={{0,2},{16,6},{28,10},{12,14},{1,3},{17,7},{29,11},{13,15},{18,16},... | collective-permute-start | bytes 393224 | tf_op jit(solution)/shard_map/ppermute | solution.py:328
  59.1 1.9 %collective-permute-start.14 = (f32[2,128,128]{2,1,0:T(8,128)S(1)}, f32[2,128,128]{2,1,0:T(8,128)S(1)}, u32[]{:S(2)}, u32[]{:S(2)}) collective-permute-start(f32[2,128,128]{2,1,0:T(8,128)S(1)} %get-tuple-element.69), channel_id=1, source_target_pairs={{0,3},{16,7},{28,11},{12,15},{1,2},{17,6},{29,10},{13,14},{18,17},... | collective-permute-start | bytes 393224 | tf_op jit(solution)/shard_map/ppermute | solution.py:328
  61.0 0.0 copy-start.2
  61.1 1.4 %collective-permute-start.15 = (f32[2,128,128]{2,1,0:T(8,128)S(1)}, f32[2,128,128]{2,1,0:T(8,128)S(1)}, u32[]{:S(2)}, u32[]{:S(2)}) collective-permute-start(f32[2,128,128]{2,1,0:T(8,128)S(1)} %get-tuple-element.66.own), channel_id=1, source_target_pairs={{16,4},{28,8},{17,5},{29,9},{2,22},{14,26},{3,23},{15,27},{48,36},... | collective-permute-start | bytes 393224 | tf_op jit(solution)/shard_map/ppermute | solution.py:328
  62.5 0.0 collective-permute-done.12.one
  62.5 4.2 %collective-permute-done.13.two = f32[2,128,128]{2,1,0:T(8,128)S(1)} collective-permute-done((f32[2,128,128]{2,1,0:T(8,128)S(1)}, f32[2,128,128]{2,1,0:T(8,128)S(1)}, u32[]{:S(2)}, u32[]{:S(2)}) %collective-permute-start.13) | collective-permute-done | bytes 131104 | tf_op jit(solution)/shard_map/ppermute | solution.py:328
  66.7 2.3 %collective-permute-done.14.three = f32[2,128,128]{2,1,0:T(8,128)S(1)} collective-permute-done((f32[2,128,128]{2,1,0:T(8,128)S(1)}, f32[2,128,128]{2,1,0:T(8,128)S(1)}, u32[]{:S(2)}, u32[]{:S(2)}) %collective-permute-start.14) | collective-permute-done | bytes 131104 | tf_op jit(solution)/shard_map/ppermute | solution.py:328
  69.0 0.0 collective-permute-done.15.zero
  69.0 0.7 place.1
  69.7 2.6 %collective-permute-start.17 = (f32[2,256,128]{2,1,0:T(8,128)S(1)}, f32[2,256,128]{2,1,0:T(8,128)S(1)}, u32[]{:S(2)}, u32[]{:S(2)}) collective-permute-start(f32[2,256,128]{2,1,0:T(8,128)S(1)} %get-tuple-element.71), channel_id=1, source_target_pairs={{16,32},{48,64},{80,96},{112,128},{144,160},{176,192},{208,224},{2... | collective-permute-start | bytes 786440 | tf_op jit(solution)/shard_map/ppermute | solution.py:337
  72.2 1.9 %collective-permute-start.16 = (f32[2,256,128]{2,1,0:T(8,128)S(1)}, f32[2,256,128]{2,1,0:T(8,128)S(1)}, u32[]{:S(2)}, u32[]{:S(2)}) collective-permute-start(f32[2,256,128]{2,1,0:T(8,128)S(1)} %get-tuple-element.70), channel_id=1, source_target_pairs={{0,16},{16,0},{32,48},{48,32},{64,80},{80,64},{96,112},{112,96},{1... | collective-permute-start | bytes 786440 | tf_op jit(solution)/shard_map/ppermute | solution.py:336
  74.2 4.4 %collective-permute-done.17.far = f32[2,256,128]{2,1,0:T(8,128)S(1)} collective-permute-done((f32[2,256,128]{2,1,0:T(8,128)S(1)}, f32[2,256,128]{2,1,0:T(8,128)S(1)}, u32[]{:S(2)}, u32[]{:S(2)}) %collective-permute-start.17) | collective-permute-done | bytes 262176 | tf_op jit(solution)/shard_map/ppermute | solution.py:337
  78.6 0.0 copy-done.2
  78.6 0.1 step.1.stepped
  78.6 0.0 collective-permute-done.16.near
  78.6 0.7 last.1
  (7 shorter events, 0.1 us)
Async XLA Ops:
  0.0 9.6 %collective-permute-start.1 = (f32[2,256,128]{2,1,0:T(8,128)}, f32[2,256,128]{2,1,0:T(8,128)S(1)}, u32[]{:S(2)}, u32[]{:S(2)}) collective-permute-start(f32[2,256,128]{2,1,0:T(8,128)} %bitcast.1), channel_id=1, source_target_pairs={{16,32},{48,64},{80,96},{112,128},{144,160},{176,192},{208,224},{2... | collective-permute-start | bytes 786440 | tf_op jit(solution)/shard_map/ppermute | solution.py:278
  5.3 4.3 %collective-permute-start = (f32[2,256,128]{2,1,0:T(8,128)}, f32[2,256,128]{2,1,0:T(8,128)S(1)}, u32[]{:S(2)}, u32[]{:S(2)}) collective-permute-start(f32[2,256,128]{2,1,0:T(8,128)} %bitcast.2), channel_id=1, source_target_pairs={{0,16},{16,0},{32,48},{48,32},{64,80},{80,64},{96,112},{112,96},{1... | collective-permute-start | bytes 786440 | tf_op jit(solution)/shard_map/ppermute | solution.py:277
  7.2 1.0 %copy-start.1 = (f32[1,2,256,128]{3,2,1,0:T(8,128)S(1)}, f32[1,2,256,128]{3,2,1,0:T(8,128)}, u32[]{:S(2)}) copy-start(f32[1,2,256,128]{3,2,1,0:T(8,128)} %block.3) | copy-start | bytes 786436
  8.2 1.4 %copy-start.6 = (s32[2]{0:T(128)S(1)}, s32[2]{0:T(128)}, u32[]{:S(2)}) copy-start(s32[2]{0:T(128)} %owners.3) | copy-start | bytes 28
  8.2 1.4 %copy-start.7 = (s32[2]{0:T(128)S(1)}, s32[2]{0:T(128)}, u32[]{:S(2)}) copy-start(s32[2]{0:T(128)} %offsets.3) | copy-start | bytes 28
  9.6 15.2 %copy-start = (f32[2,128,128]{2,1,0:T(8,128)S(1)}, f32[2,128,128]{2,1,0:T(8,128)}, u32[]{:S(2)}) copy-start(f32[2,128,128]{2,1,0:T(8,128)} %constant.4.clone.table_ref) | copy-start | bytes 393220
  9.6 15.2 %copy-start.3 = (f32[2,128,128]{2,1,0:T(8,128)S(1)}, f32[2,128,128]{2,1,0:T(8,128)}, u32[]{:S(2)}) copy-start(f32[2,128,128]{2,1,0:T(8,128)} %wave_in.1) | copy-start | bytes 393220
  10.3 9.2 %collective-permute-start.2 = (f32[2,128,128]{2,1,0:T(8,128)S(1)}, f32[2,128,128]{2,1,0:T(8,128)S(1)}, u32[]{:S(2)}, u32[]{:S(2)}) collective-permute-start(f32[2,128,128]{2,1,0:T(8,128)S(1)} %get-tuple-element.40), channel_id=1, source_target_pairs={{2,0},{6,16},{10,28},{14,12},{3,1},{7,17},{11,29},{15,13},{16,18},... | collective-permute-start | bytes 393224 | tf_op jit(solution)/shard_map/ppermute | solution.py:289
  14.9 9.2 %collective-permute-start.4 = (f32[2,128,128]{2,1,0:T(8,128)S(1)}, f32[2,128,128]{2,1,0:T(8,128)S(1)}, u32[]{:S(2)}, u32[]{:S(2)}) collective-permute-start(f32[2,128,128]{2,1,0:T(8,128)S(1)} %get-tuple-element.41), channel_id=1, source_target_pairs={{3,0},{7,16},{11,28},{15,12},{2,1},{6,17},{10,29},{14,13},{17,18},... | collective-permute-start | bytes 393224 | tf_op jit(solution)/shard_map/ppermute | solution.py:289
  16.9 8.0 %collective-permute-start.3 = (f32[2,128,128]{2,1,0:T(8,128)S(1)}, f32[2,128,128]{2,1,0:T(8,128)S(1)}, u32[]{:S(2)}, u32[]{:S(2)}) collective-permute-start(f32[2,128,128]{2,1,0:T(8,128)S(1)} %get-tuple-element.41), channel_id=1, source_target_pairs={{1,0},{5,16},{9,28},{13,12},{0,1},{4,17},{8,29},{12,13},{19,18},{2... | collective-permute-start | bytes 393224 | tf_op jit(solution)/shard_map/ppermute | solution.py:289
  18.2 8.0 %collective-permute-start.6 = (f32[2,128,128]{2,1,0:T(8,128)S(1)}, f32[2,128,128]{2,1,0:T(8,128)S(1)}, u32[]{:S(2)}, u32[]{:S(2)}) collective-permute-start(f32[2,128,128]{2,1,0:T(8,128)S(1)} %get-tuple-element.40), channel_id=1, source_target_pairs={{4,16},{8,28},{5,17},{9,29},{22,2},{26,14},{23,3},{27,15},{36,48},... | collective-permute-start | bytes 393224 | tf_op jit(solution)/shard_map/ppermute | solution.py:289
  24.8 3.2 %collective-permute-start.5 = (f32[2,128,128]{2,1,0:T(8,128)S(1)}, f32[2,128,128]{2,1,0:T(8,128)S(1)}, u32[]{:S(2)}, u32[]{:S(2)}) collective-permute-start(f32[2,128,128]{2,1,0:T(8,128)S(1)} %get-tuple-element.42), channel_id=1, source_target_pairs={{0,16},{1,17},{18,2},{19,3},{32,48},{33,49},{50,34},{51,35},{64,80... | collective-permute-start | bytes 393224 | tf_op jit(solution)/shard_map/ppermute | solution.py:300
  29.8 3.2 %collective-permute-start.7 = (f32[2,128,128]{2,1,0:T(8,128)S(1)}, f32[2,128,128]{2,1,0:T(8,128)S(1)}, u32[]{:S(2)}, u32[]{:S(2)}) collective-permute-start(f32[2,128,128]{2,1,0:T(8,128)S(1)} %get-tuple-element.45), channel_id=1, source_target_pairs={{16,28},{17,29},{2,14},{3,15},{48,60},{49,61},{34,46},{35,47},{80,... | collective-permute-start | bytes 393224 | tf_op jit(solution)/shard_map/ppermute | solution.py:300
  33.1 0.9 %copy-start.4 = (f32[2,128,128]{2,1,0:T(8,128)S(1)}, f32[2,128,128]{2,1,0:T(8,128)}, u32[]{:S(2)}) copy-start(f32[2,128,128]{2,1,0:T(8,128)} %measured.1) | copy-start | bytes 393220
  33.1 1.0 %copy-start.5 = (f32[2,128,128]{2,1,0:T(8,128)S(1)}, f32[2,128,128]{2,1,0:T(8,128)}, u32[]{:S(2)}) copy-start(f32[2,128,128]{2,1,0:T(8,128)} %constant.5.clone.fourier_ref) | copy-start | bytes 393220
  33.1 0.8 %collective-permute-start.8 = (f32[2,128,128]{2,1,0:T(8,128)S(1)}, f32[2,128,128]{2,1,0:T(8,128)S(1)}, u32[]{:S(2)}, u32[]{:S(2)}) collective-permute-start(f32[2,128,128]{2,1,0:T(8,128)S(1)} %get-tuple-element.48), channel_id=1, source_target_pairs={{28,12},{29,13},{14,30},{15,31},{60,44},{61,45},{46,62},{47,63},{9... | collective-permute-start | bytes 393224 | tf_op jit(solution)/shard_map/ppermute | solution.py:308
  34.0 0.7 collective-permute-start.9
  34.8 17.1 %collective-permute-start.10 = (f32[2,128,128]{2,1,0:T(8,128)S(1)}, f32[2,128,128]{2,1,0:T(8,128)S(1)}, u32[]{:S(2)}, u32[]{:S(2)}) collective-permute-start(f32[2,128,128]{2,1,0:T(8,128)S(1)} %get-tuple-element.56), channel_id=1, source_target_pairs={{28,16},{29,17},{14,2},{15,3},{60,48},{61,49},{46,34},{47,35},{92,... | collective-permute-start | bytes 393224 | tf_op jit(solution)/shard_map/ppermute | solution.py:317
  53.6 2.3 %collective-permute-start.11 = (f32[2,128,128]{2,1,0:T(8,128)S(1)}, f32[2,128,128]{2,1,0:T(8,128)S(1)}, u32[]{:S(2)}, u32[]{:S(2)}) collective-permute-start(f32[2,128,128]{2,1,0:T(8,128)S(1)} %get-tuple-element.61), channel_id=1, source_target_pairs={{16,0},{17,1},{2,18},{3,19},{48,32},{49,33},{34,50},{35,51},{80,64... | collective-permute-start | bytes 393224 | tf_op jit(solution)/shard_map/ppermute | solution.py:317
  55.9 6.6 %collective-permute-start.12 = (f32[2,128,128]{2,1,0:T(8,128)S(1)}, f32[2,128,128]{2,1,0:T(8,128)S(1)}, u32[]{:S(2)}, u32[]{:S(2)}) collective-permute-start(f32[2,128,128]{2,1,0:T(8,128)S(1)} %get-tuple-element.67), channel_id=1, source_target_pairs={{0,1},{16,5},{28,9},{12,13},{1,0},{17,4},{29,8},{13,12},{18,19},{2... | collective-permute-start | bytes 393224 | tf_op jit(solution)/shard_map/ppermute | solution.py:328
  57.2 9.5 %collective-permute-start.13 = (f32[2,128,128]{2,1,0:T(8,128)S(1)}, f32[2,128,128]{2,1,0:T(8,128)S(1)}, u32[]{:S(2)}, u32[]{:S(2)}) collective-permute-start(f32[2,128,128]{2,1,0:T(8,128)S(1)} %get-tuple-element.68), channel_id=1, source_target_pairs={{0,2},{16,6},{28,10},{12,14},{1,3},{17,7},{29,11},{13,15},{18,16},... | collective-permute-start | bytes 393224 | tf_op jit(solution)/shard_map/ppermute | solution.py:328
  59.1 9.9 %collective-permute-start.14 = (f32[2,128,128]{2,1,0:T(8,128)S(1)}, f32[2,128,128]{2,1,0:T(8,128)S(1)}, u32[]{:S(2)}, u32[]{:S(2)}) collective-permute-start(f32[2,128,128]{2,1,0:T(8,128)S(1)} %get-tuple-element.69), channel_id=1, source_target_pairs={{0,3},{16,7},{28,11},{12,15},{1,2},{17,6},{29,10},{13,14},{18,17},... | collective-permute-start | bytes 393224 | tf_op jit(solution)/shard_map/ppermute | solution.py:328
  61.0 17.5 %copy-start.2 = (f32[1,2,256,128]{3,2,1,0:T(8,128)S(1)}, f32[1,2,256,128]{3,2,1,0:T(8,128)}, u32[]{:S(2)}) copy-start(f32[1,2,256,128]{3,2,1,0:T(8,128)} %block.3) | copy-start | bytes 786436
  61.1 7.9 %collective-permute-start.15 = (f32[2,128,128]{2,1,0:T(8,128)S(1)}, f32[2,128,128]{2,1,0:T(8,128)S(1)}, u32[]{:S(2)}, u32[]{:S(2)}) collective-permute-start(f32[2,128,128]{2,1,0:T(8,128)S(1)} %get-tuple-element.66.own), channel_id=1, source_target_pairs={{16,4},{28,8},{17,5},{29,9},{2,22},{14,26},{3,23},{15,27},{48,36},... | collective-permute-start | bytes 393224 | tf_op jit(solution)/shard_map/ppermute | solution.py:328
  69.7 8.9 %collective-permute-start.17 = (f32[2,256,128]{2,1,0:T(8,128)S(1)}, f32[2,256,128]{2,1,0:T(8,128)S(1)}, u32[]{:S(2)}, u32[]{:S(2)}) collective-permute-start(f32[2,256,128]{2,1,0:T(8,128)S(1)} %get-tuple-element.71), channel_id=1, source_target_pairs={{16,32},{48,64},{80,96},{112,128},{144,160},{176,192},{208,224},{2... | collective-permute-start | bytes 786440 | tf_op jit(solution)/shard_map/ppermute | solution.py:337
  72.2 6.4 %collective-permute-start.16 = (f32[2,256,128]{2,1,0:T(8,128)S(1)}, f32[2,256,128]{2,1,0:T(8,128)S(1)}, u32[]{:S(2)}, u32[]{:S(2)}) collective-permute-start(f32[2,256,128]{2,1,0:T(8,128)S(1)} %get-tuple-element.70), channel_id=1, source_target_pairs={{0,16},{16,0},{32,48},{48,32},{64,80},{80,64},{96,112},{112,96},{1... | collective-permute-start | bytes 786440 | tf_op jit(solution)/shard_map/ppermute | solution.py:336

commit v8 on v7

--- a/solution.py
+++ b/solution.py
@@ -12,14 +12,13 @@
 side = 128
 tile = 256
 group = 4
-masks = (0, 2, 1, 3)
-back_masks = (1, 2, 3, 0)
 params = pltpu.CompilerParams(vmem_limit_bytes=48 * 2**20)
 in_vmem = pl.BlockSpec(memory_space=pltpu.VMEM)
 in_smem = pl.BlockSpec(memory_space=pltpu.SMEM)
 window_type = jax.ShapeDtypeStruct((2, side, side), jnp.float32)
 tile_type = jax.ShapeDtypeStruct((2, tile, side), jnp.float32)
 slab_type = jax.ShapeDtypeStruct((2, 3 * tile, side), jnp.float32)
+double_type = jax.ShapeDtypeStruct((2 * group, 2, side, side), jnp.float32)
 stack_type = jax.ShapeDtypeStruct((group, 2, side, side), jnp.float32)
 
 
@@ -84,7 +83,7 @@
     depth, scan = lax.axis_index("depth"), lax.axis_index("scan")
     row, home = depth // group, (depth % group) // 2 == (scan & 1)
     top, bottom = row == 0, row == group - 1
-    return jnp.where(top, jnp.where(home, 0, 1), jnp.where(bottom, jnp.where(home, 3, 2), -1))
+    return jnp.where(top, jnp.where(home, 0, 1), jnp.where(bottom & home, 2, -1))
 
 
 def column():
@@ -134,10 +133,10 @@
     own[...] = lower_out[...]
 
 
-def collect(arrived, windows):
+def collect(arrived, windows, base=0):
     me = column()
-    for turn in range(group):
-        windows[me ^ masks[turn]] = arrived[turn][...]
+    for mask, window in enumerate(arrived):
+        windows[base + (me ^ mask)] = window[...]
 
 
 def forward_kernel(mine, wave_in, zero, one, two, three, table_ref, *rest):
@@ -155,7 +154,7 @@
 
 
 def backward(adjoint, waves, windows, updates, table, last):
-    for layer in reversed(range(group)):
+    for layer in reversed(range(updates.shape[0])):
         real, imag = times(pair(waves, layer), adjoint)
         put(updates, (real, -imag), layer)
         if layer or not last:
@@ -163,33 +162,42 @@
     return adjoint
 
 
-def share(updates, parts):
+def share(updates, parts, base=0):
     me = column()
-    for turn in range(group):
-        parts[turn][...] = updates[me ^ back_masks[turn]]
-
-
-def far_kernel(wave_in, zero, one, two, three, measured, table_ref, fourier_ref, *rest):
-    adjoint_out, parts, (waves, windows, updates) = rest[0], rest[1 : 1 + group], rest[1 + group :]
-
-    @pl.when(role() == group - 1)
+    for mask, part in enumerate(parts):
+        part[...] = updates[base + (me ^ mask)]
+
+
+def far_kernel(wave_in, *rest):
+    third, fourth, (measured, table_ref, fourier_ref), rest = (
+        rest[:group],
+        rest[group : 2 * group],
+        rest[2 * group : 2 * group + 3],
+        rest[2 * group + 3 :],
+    )
+    adjoint_out, third_parts, fourth_parts = rest[0], rest[1 : 1 + group], rest[1 + group : -3]
+    waves, windows, updates = rest[-3:]
+
+    @pl.when(role() == 2)
     def _():
-        collect((zero, one, two, three), windows)
+        collect(third, windows)
+        collect(fourth, windows, group)
         table, fourier = blocks(table_ref), blocks(fourier_ref)
         wave = pair(wave_in)
-        for layer in range(group):
+        for layer in range(2 * group):
             put(waves, wave, layer)
-            last = layer == group - 1
+            last = layer == 2 * group - 1
             wave = two_sided(times(wave, pair(windows, layer)), fourier if last else table)
         far_real, far_imag = wave
         residual = far_real * far_real + far_imag * far_imag - measured[column() & 1]
         adjoint = two_sided((residual * far_real, -(residual * far_imag)), fourier)
         put(adjoint_out, backward(adjoint, waves, windows, updates, table, False))
-        share(updates, parts)
-
-
-def backward_kernel(mine, adjoint_in, waves, windows, table_ref, *rest):
-    rest, updates = rest[group:-1], rest[-1]
+        share(updates, third_parts)
+        share(updates, fourth_parts, group)
+
+
+def backward_kernel(mine, extra, adjoint_in, waves, windows, table_ref, *rest):
+    rest, updates = rest[group + extra : -1], rest[-1]
 
     @pl.when(role() == mine)
     def _():
@@ -201,11 +209,13 @@
         share(updates, rest[:group])
 
 
-def place_kernel(owners, offsets, own, one, two, three, zero, slab, near, far):
+def place_kernel(owners, offsets, first_own, fourth_own, *rest):
+    (zero, one, two, three), fourth, (slab, near, far) = rest[:group], rest[group:-3], rest[-3:]
     slab[...] = jnp.zeros_like(slab)
-    local = (role() == 0) | (role() == group - 1)
-    late = one[...] + three[...]
-    early = two[...] + jnp.where(local, own[...], zero[...])
+    mine = role()
+    own = jnp.where(mine == 0, first_own[...], jnp.where(mine == 2, fourth_own[...], zero[...]))
+    late = (one[...] + three[...]) + (fourth[0][...] + fourth[2][...])
+    early = (two[...] + fourth[1][...]) + own
     upper = upper_position()
     for at, update in ((upper, late), (1 - upper, early)):
         rows = pl.ds(start_of(at, owners, offsets), side)
@@ -236,8 +246,9 @@
     axes = ("scan", "depth")
     step_table, fourier_table = tables()
 
-    def call(kernel, name, out_shape, arguments, scratch=(), aliases=()):
+    def call(kernel, name, out_shape, arguments, scratch=(), aliases=(), after=()):
         specs = [in_smem if a.dtype == jnp.int32 else in_vmem for a in arguments]
+        specs += [pl.BlockSpec(memory_space=pl.ANY)] * len(after)
         return pl.pallas_call(
             kernel,
             out_shape=out_shape,
@@ -247,7 +258,7 @@
             input_output_aliases=dict(aliases),
             compiler_params=params,
             name=name,
-        )(*arguments)
+        )(*arguments, *after)
 
     def at(scan, depth):
         return scan * depths + depth
@@ -257,19 +268,17 @@
 
     targets = [(i, 2 * (i & 1) + q) for i in range(scans) for q in range(2)]
     bottom = depths - group
-    homes = [[(i, x), (i ^ 1, x), (i ^ 1, bottom + x), (i, bottom + x)] for i, x in targets]
-
-    def sends(mask):
+    homes = [[(i, x), (i ^ 1, x), (i, bottom + x), (i, bottom + x)] for i, x in targets]
+
+    def sends(mask, *groups):
         pairs = [
             (at(i, row * group + (x ^ mask)), at(*home[row]))
             for (i, x), home in zip(targets, homes)
-            for row in range(group)
+            for row in groups
         ]
         return [(a, b) for a, b in pairs if a != b]
 
-    hops = [
-        [(at(*home[row]), at(*home[row + 1])) for home in homes] for row in range(group - 1)
-    ]
+    hops = [[(at(*home[row]), at(*home[row + 1])) for home in homes] for row in range(2)]
     on_chip = [(i, i ^ 1) for i in range(scans)]
     next_chip = [(i, i + 1) for i in range(1, scans - 1, 2)]
     next_chip = next_chip + ends(next_chip)
@@ -285,53 +294,66 @@
         (near, owners, offsets, slab),
         aliases=[(3, 3)],
     )
-    come = [
-        lax.ppermute(upper_window if mask & 1 else lower_window, axes, sends(mask))
-        for mask in masks
-    ]
+    def gather(mask, *groups):
+        return lax.ppermute(upper_window if mask & 1 else lower_window, axes, sends(mask, *groups))
+
+    two, three = gather(2, 0, 1, 2), gather(3, 0, 1, 2)
+    mate = gather(1, 0, 3)
+    zero, one = gather(0, 1, 2), gather(1, 1, 2)
+    fourth_two, fourth_three = gather(2, 3), gather(3, 3)
 
     wave, waves, windows = call(
         functools.partial(forward_kernel, 0),
         "first",
         [window_type, stack_type, stack_type],
-        (probe_wave, own, *come[1:], step_table),
-    )
-    for mine, name in ((1, "second"), (2, "third")):
-        wave = lax.ppermute(wave, axes, hops[mine - 1])
-        wave, waves, windows = call(
-            functools.partial(forward_kernel, mine),
-            name,
-            [window_type, stack_type, stack_type],
-            (wave, *come, step_table, waves, windows),
-            aliases=((6, 1), (7, 2)),
-        )
-    wave = lax.ppermute(wave, axes, hops[2])
+        (probe_wave, own, mate, two, three, step_table),
+    )
+    wave = lax.ppermute(wave, axes, hops[0])
+    wave, waves, windows = call(
+        functools.partial(forward_kernel, 1),
+        "second",
+        [window_type, stack_type, stack_type],
+        (wave, zero, one, two, three, step_table, waves, windows),
+        aliases=((6, 1), (7, 2)),
+    )
+    wave = lax.ppermute(wave, axes, hops[1])
+    third, fourth = (zero, one, two, three), (own, mate, fourth_two, fourth_three)
     adjoint, *parts = call(
         far_kernel,
         "far",
-        [window_type] * (1 + group),
-        (wave, own, *come[1:], intensities, step_table, fourier_table),
-        [stack_type] * 3,
-    )
-    for mine, name in ((2, "back_third"), (1, "back_second"), (0, "back_first")):
+        [window_type] * (1 + 2 * group),
+        (wave, *third, *fourth, intensities, step_table, fourier_table),
+        [double_type] * 3,
+    )
+    parts, (fourth_own, *fourth_parts) = parts[:group], parts[group:]
+
+    def scatter(part, mask, *groups):
+        return lax.ppermute(part, axes, ends(sends(mask, *groups)))
+
+    for mine, name in ((1, "back_second"), (0, "back_first")):
         adjoint = lax.ppermute(adjoint, axes, ends(hops[mine]))
+        early = ()
+        if mine:
+            landed = early = [scatter(part, 1 + turn, 3) for turn, part in enumerate(fourth_parts)]
         returned = call(
-            functools.partial(backward_kernel, mine),
+            functools.partial(backward_kernel, mine, len(early)),
             name,
-            [window_type] * (group + min(mine, 1)),
+            [window_type] * (group + mine),
             (adjoint, waves, windows, step_table, *parts),
             [stack_type],
-            aliases=[(4 + turn, turn) for turn in range(group)],
+            aliases=[(4 + mask, mask) for mask in range(group)],
+            after=early,
         )
         parts, adjoint = returned[:group], returned[-1]
     landed = [
-        lax.ppermute(part, axes, ends(sends(mask))) for mask, part in zip(back_masks, parts)
-    ]
+        scatter(part, mask, *((1, 2) if mask == 0 else (0, 1, 2)))
+        for mask, part in enumerate(parts)
+    ] + landed
     slab, near, far = call(
         place_kernel,
         "place",
         [slab_type, tile_type, tile_type],
-        (owners, offsets, parts[-1], *landed),
+        (owners, offsets, parts[0], fourth_own, *landed),
     )
     near = lax.ppermute(near, "scan", on_chip)
     far = lax.ppermute(far, "scan", next_chip)

time: 79.9 us -> 73.7 us (0.922)
  the two profiles are of different devices: /device:TPU:97 before, /device:TPU:225 now
where the time goes in v8:
time: 73.7 us; the launch traced here: 73.1 us
  starting transfers between devices  37.2 us (50%)
  waiting for transfers between devices  28.8 us (39%)
  Pallas kernels  5.73 us (8%)
  local copies, waits for them, and re-layouts  0.98 us (1%)
    ppermute x2, waiting for transfers between devices, shards(): adjoint = lax.ppermute(adjoint, axes, ends(hops[mine]))  12.3 us
    ppermute x7, starting transfers between devices, gather(): lax.ppermute(upper_window if mask & 1 else lower_window, axes, sends(mask...  11.2 us
    ppermute x7, starting transfers between devices, scatter(): return lax.ppermute(part, axes, ends(sends(mask, *groups)))  8.43 us
    ppermute x7, waiting for transfers between devices, scatter(): return lax.ppermute(part, axes, ends(sends(mask, *groups)))  5.77 us
    pallas_call x11, Pallas kernels, call(): pl.pallas_call(kernel, out_shape=out_shape, in_specs=specs, out_specs=jax...  5.73 us
    ppermute x1, starting transfers between devices, shards(): far = lax.ppermute(object_slices[0], 'scan', next_chip)  5.31 us
    ppermute x1, waiting for transfers between devices, shards(): far = lax.ppermute(far, 'scan', next_chip)  3.67 us
    ppermute x1, starting transfers between devices, shards(): far = lax.ppermute(far, 'scan', next_chip)  3.3 us
  transfers between devices with their start and end apart: 22, of which 9 were waited for; matrix products, arithmetic and copies ran while one was open for 0% of the time, Pallas kernels for 3%

profile of v8, /device:TPU:225, one launch (start us, length us, event | category | flops | bytes accessed | tf_op | source)
XLA Modules:
  0.0 73.1 jit_solution(11156548484939803663)
XLA Ops:
  0.0 5.3 %collective-permute-start.1 = (f32[2,256,128]{2,1,0:T(8,128)}, f32[2,256,128]{2,1,0:T(8,128)S(1)}, u32[]{:S(2)}, u32[]{:S(2)}) collective-permute-start(f32[2,256,128]{2,1,0:T(8,128)} %bitcast.1), channel_id=1, source_target_pairs={{16,32},{48,64},{80,96},{112,128},{144,160},{176,192},{208,224},{2... | collective-permute-start | bytes 786440 | tf_op jit(solution)/shard_map/ppermute | solution.py:287
  5.3 1.9 %collective-permute-start = (f32[2,256,128]{2,1,0:T(8,128)}, f32[2,256,128]{2,1,0:T(8,128)S(1)}, u32[]{:S(2)}, u32[]{:S(2)}) collective-permute-start(f32[2,256,128]{2,1,0:T(8,128)} %bitcast.2), channel_id=1, source_target_pairs={{0,16},{16,0},{32,48},{48,32},{64,80},{80,64},{96,112},{112,96},{1... | collective-permute-start | bytes 786440 | tf_op jit(solution)/shard_map/ppermute | solution.py:286
  7.2 0.0 copy-start.1
  7.3 0.9 %copy-done.1 = f32[1,2,256,128]{3,2,1,0:T(8,128)S(1)} copy-done((f32[1,2,256,128]{3,2,1,0:T(8,128)S(1)}, f32[1,2,256,128]{3,2,1,0:T(8,128)}, u32[]{:S(2)}) %copy-start.1) | copy-done | bytes 262168
  8.2 0.0 copy-start.6
  8.2 0.0 copy-start.7
  8.2 1.3 %collective-permute-done.1.far = f32[2,256,128]{2,1,0:T(8,128)S(1)} collective-permute-done((f32[2,256,128]{2,1,0:T(8,128)}, f32[2,256,128]{2,1,0:T(8,128)S(1)}, u32[]{:S(2)}, u32[]{:S(2)}) %collective-permute-start.1) | collective-permute-done | bytes 262176 | tf_op jit(solution)/shard_map/ppermute | solution.py:287
  9.6 0.0 copy-start
  9.6 0.0 copy-start.5
  9.6 0.0 collective-permute-done.near
  9.6 0.0 copy-done.6
  9.6 0.0 copy-done.7
  9.6 0.6 cut.1
  10.3 4.7 %collective-permute-start.3 = (f32[2,128,128]{2,1,0:T(8,128)S(1)}, f32[2,128,128]{2,1,0:T(8,128)S(1)}, u32[]{:S(2)}, u32[]{:S(2)}) collective-permute-start(f32[2,128,128]{2,1,0:T(8,128)S(1)} %get-tuple-element.37), channel_id=1, source_target_pairs={{2,0},{6,16},{10,12},{3,1},{7,17},{11,13},{16,18},{20,2},{24,30},{... | collective-permute-start | bytes 393224 | tf_op jit(solution)/shard_map/ppermute | solution.py:298
  14.9 1.9 %collective-permute-start.4 = (f32[2,128,128]{2,1,0:T(8,128)S(1)}, f32[2,128,128]{2,1,0:T(8,128)S(1)}, u32[]{:S(2)}, u32[]{:S(2)}) collective-permute-start(f32[2,128,128]{2,1,0:T(8,128)S(1)} %get-tuple-element.36), channel_id=1, source_target_pairs={{3,0},{7,16},{11,12},{2,1},{6,17},{10,13},{17,18},{21,2},{25,30},{... | collective-permute-start | bytes 393224 | tf_op jit(solution)/shard_map/ppermute | solution.py:298
  16.9 0.7 collective-permute-start.2
  17.5 1.3 %collective-permute-start.6 = (f32[2,128,128]{2,1,0:T(8,128)S(1)}, f32[2,128,128]{2,1,0:T(8,128)S(1)}, u32[]{:S(2)}, u32[]{:S(2)}) collective-permute-start(f32[2,128,128]{2,1,0:T(8,128)S(1)} %get-tuple-element.37), channel_id=1, source_target_pairs={{4,16},{8,12},{5,17},{9,13},{22,2},{26,30},{23,3},{27,31},{36,48},... | collective-permute-start | bytes 393224 | tf_op jit(solution)/shard_map/ppermute | solution.py:298
  18.8 1.3 %collective-permute-start.7 = (f32[2,128,128]{2,1,0:T(8,128)S(1)}, f32[2,128,128]{2,1,0:T(8,128)S(1)}, u32[]{:S(2)}, u32[]{:S(2)}) collective-permute-start(f32[2,128,128]{2,1,0:T(8,128)S(1)} %get-tuple-element.36), channel_id=1, source_target_pairs={{5,16},{9,12},{4,17},{8,13},{23,2},{27,30},{22,3},{26,31},{37,48},... | collective-permute-start | bytes 393224 | tf_op jit(solution)/shard_map/ppermute | solution.py:298
  20.1 0.0 collective-permute-done.3.two.rest_2_
  20.1 3.3 %collective-permute-done.4.three.rest_3_ = f32[2,128,128]{2,1,0:T(8,128)S(1)} collective-permute-done((f32[2,128,128]{2,1,0:T(8,128)S(1)}, f32[2,128,128]{2,1,0:T(8,128)S(1)}, u32[]{:S(2)}, u32[]{:S(2)}) %collective-permute-start.4) | collective-permute-done | bytes 131104 | tf_op jit(solution)/shard_map/ppermute | solution.py:298
  23.4 0.0 collective-permute-done.2.one.rest_5_
  23.4 0.0 copy-done
  23.4 0.0 copy-done.5
  23.5 1.3 %collective-permute-start.5 = (f32[2,128,128]{2,1,0:T(8,128)S(1)}, f32[2,128,128]{2,1,0:T(8,128)S(1)}, u32[]{:S(2)}, u32[]{:S(2)}) collective-permute-start(f32[2,128,128]{2,1,0:T(8,128)S(1)} %get-tuple-element.38), channel_id=1, source_target_pairs={{0,16},{1,17},{18,2},{19,3},{32,48},{33,49},{50,34},{51,35},{64,80... | collective-permute-start | bytes 393224 | tf_op jit(solution)/shard_map/ppermute | solution.py:311
  24.8 0.7 collective-permute-start.9
  25.5 0.7 collective-permute-start.10
  26.1 0.0 collective-permute-done.6.zero.rest_0_
  26.1 0.0 collective-permute-done.7.one.rest_1_
  26.2 0.6 collective-permute-done.5.wave_in
  26.7 0.0 copy-start.4
  26.7 1.8 %second.1 = (f32[2,128,128]{2,1,0:T(8,128)S(1)}, f32[4,2,128,128]{3,2,1,0:T(8,128)S(1)}, f32[4,2,128,128]{3,2,1,0:T(8,128)S(1)}) custom-call(f32[2,128,128]{2,1,0:T(8,128)S(1)} %collective-permute-done.5.wave_in, f32[2,128,128]{2,1,0:T(8,128)S(1)} %collective-permute-done.6.zero.rest_0_, ...), custom_call_target="tpu_custom_call", output_to_operand_aliasing={{1}: (6, {}), {2}: (7, {})} | custom-call | tf_op jit(solution)/shard_map/second/pallas_call | solution.py:252
  28.5 1.3 %collective-permute-start.8 = (f32[2,128,128]{2,1,0:T(8,128)S(1)}, f32[2,128,128]{2,1,0:T(8,128)S(1)}, u32[]{:S(2)}, u32[]{:S(2)}) collective-permute-start(f32[2,128,128]{2,1,0:T(8,128)S(1)} %get-tuple-element.41), channel_id=1, source_target_pairs={{16,12},{17,13},{2,30},{3,31},{48,44},{49,45},{34,62},{35,63},{80,... | collective-permute-start | bytes 393224 | tf_op jit(solution)/shard_map/ppermute | solution.py:319
  29.8 0.0 collective-permute-done.9.rest_6_
  29.8 0.0 collective-permute-done.10.rest_7_
  29.8 1.9 %collective-permute-done.8.wave_in = f32[2,128,128]{2,1,0:T(8,128)S(1)} collective-permute-done((f32[2,128,128]{2,1,0:T(8,128)S(1)}, f32[2,128,128]{2,1,0:T(8,128)S(1)}, u32[]{:S(2)}, u32[]{:S(2)}) %collective-permute-start.8) | collective-permute-done | bytes 131104 | tf_op jit(solution)/shard_map/ppermute | solution.py:319
  31.7 0.0 copy-done.3
  31.7 0.0 copy-done.4
  31.7 1.3 %collective-permute-start.11 = (f32[2,128,128]{2,1,0:T(8,128)S(1)}, f32[2,128,128]{2,1,0:T(8,128)S(1)}, u32[]{:S(2)}, u32[]{:S(2)}) collective-permute-start(f32[2,128,128]{2,1,0:T(8,128)S(1)} %get-tuple-element.42), channel_id=1, source_target_pairs={{12,16},{13,17},{30,2},{31,3},{44,48},{45,49},{62,34},{63,35},{76,... | collective-permute-start | bytes 393224 | tf_op jit(solution)/shard_map/ppermute | solution.py:334
  33.0 0.7 collective-permute-start.12
  33.7 0.7 collective-permute-start.13
  34.4 0.7 collective-permute-start.14
  35.0 11.4 %collective-permute-done.11.adjoint_in = f32[2,128,128]{2,1,0:T(8,128)S(1)} collective-permute-done((f32[2,128,128]{2,1,0:T(8,128)S(1)}, f32[2,128,128]{2,1,0:T(8,128)S(1)}, u32[]{:S(2)}, u32[]{:S(2)}) %collective-permute-start.11) | collective-permute-done | bytes 131104 | tf_op jit(solution)/shard_map/ppermute | solution.py:334
  46.4 0.0 collective-permute-done.12.rest_4_
  46.4 0.0 collective-permute-done.13.rest_5_
  46.4 0.0 collective-permute-done.14.rest_6_
  46.4 1.8 %back_second.1 = (f32[2,128,128]{2,1,0:T(8,128)S(1)}, f32[2,128,128]{2,1,0:T(8,128)S(1)}, f32[2,128,128]{2,1,0:T(8,128)S(1)}, f32[2,128,128]{2,1,0:T(8,128)S(1)}, f32[2,128,128]{2,1,0:T(8,128)S(1)}) custom-call(f32[2,128,128]{2,1,0:T(8,128)S(1)} %collective-permute-done.11.adjoint_in, ...), custom_call_target="tpu_custom_call", output_to_operand_aliasing={{0}: (4, {}), {1}: (5, {}), {2}: (6, {}), {3}: (7, {})} | custom-call | tf_op jit(solution)/shard_map/back_second/pallas_call | solution.py:252
  48.2 1.3 %collective-permute-start.15 = (f32[2,128,128]{2,1,0:T(8,128)S(1)}, f32[2,128,128]{2,1,0:T(8,128)S(1)}, u32[]{:S(2)}, u32[]{:S(2)}) collective-permute-start(f32[2,128,128]{2,1,0:T(8,128)S(1)} %get-tuple-element.52), channel_id=1, source_target_pairs={{16,0},{17,1},{2,18},{3,19},{48,32},{49,33},{34,50},{35,51},{80,64... | collective-permute-start | bytes 393224 | tf_op jit(solution)/shard_map/ppermute | solution.py:334
  49.5 1.0 %collective-permute-done.15.adjoint_in = f32[2,128,128]{2,1,0:T(8,128)S(1)} collective-permute-done((f32[2,128,128]{2,1,0:T(8,128)S(1)}, f32[2,128,128]{2,1,0:T(8,128)S(1)}, u32[]{:S(2)}, u32[]{:S(2)}) %collective-permute-start.15) | collective-permute-done | bytes 131104 | tf_op jit(solution)/shard_map/ppermute | solution.py:334
  50.5 1.3 %collective-permute-start.17 = (f32[2,128,128]{2,1,0:T(8,128)S(1)}, f32[2,128,128]{2,1,0:T(8,128)S(1)}, u32[]{:S(2)}, u32[]{:S(2)}) collective-permute-start(f32[2,128,128]{2,1,0:T(8,128)S(1)} %get-tuple-element.59), channel_id=1, source_target_pairs={{0,1},{16,5},{12,9},{1,0},{17,4},{13,8},{18,19},{2,23},{30,27},{19... | collective-permute-start | bytes 393224 | tf_op jit(solution)/shard_map/ppermute | solution.py:331
  51.8 1.9 %collective-permute-start.18 = (f32[2,128,128]{2,1,0:T(8,128)S(1)}, f32[2,128,128]{2,1,0:T(8,128)S(1)}, u32[]{:S(2)}, u32[]{:S(2)}) collective-permute-start(f32[2,128,128]{2,1,0:T(8,128)S(1)} %get-tuple-element.60), channel_id=1, source_target_pairs={{0,2},{16,6},{12,10},{1,3},{17,7},{13,11},{18,16},{2,20},{30,24},{... | collective-permute-start | bytes 393224 | tf_op jit(solution)/shard_map/ppermute | solution.py:331
  53.7 1.9 %collective-permute-start.19 = (f32[2,128,128]{2,1,0:T(8,128)S(1)}, f32[2,128,128]{2,1,0:T(8,128)S(1)}, u32[]{:S(2)}, u32[]{:S(2)}) collective-permute-start(f32[2,128,128]{2,1,0:T(8,128)S(1)} %get-tuple-element.61), channel_id=1, source_target_pairs={{0,3},{16,7},{12,11},{1,2},{17,6},{13,10},{18,17},{2,21},{30,25},{... | collective-permute-start | bytes 393224 | tf_op jit(solution)/shard_map/ppermute | solution.py:331
  55.6 1.3 %collective-permute-start.16 = (f32[2,128,128]{2,1,0:T(8,128)S(1)}, f32[2,128,128]{2,1,0:T(8,128)S(1)}, u32[]{:S(2)}, u32[]{:S(2)}) collective-permute-start(f32[2,128,128]{2,1,0:T(8,128)S(1)} %get-tuple-element.57.first_own), channel_id=1, source_target_pairs={{16,4},{12,8},{17,5},{13,9},{2,22},{30,26},{3,23},{31,27},{48,36},... | collective-permute-start | bytes 393224 | tf_op jit(solution)/shard_map/ppermute | solution.py:331
  56.9 0.0 collective-permute-done.17.rest_1_
  56.9 4.0 %collective-permute-done.18.rest_2_ = f32[2,128,128]{2,1,0:T(8,128)S(1)} collective-permute-done((f32[2,128,128]{2,1,0:T(8,128)S(1)}, f32[2,128,128]{2,1,0:T(8,128)S(1)}, u32[]{:S(2)}, u32[]{:S(2)}) %collective-permute-start.18) | collective-permute-done | bytes 131104 | tf_op jit(solution)/shard_map/ppermute | solution.py:331
  60.9 1.8 %collective-permute-done.19.rest_3_ = f32[2,128,128]{2,1,0:T(8,128)S(1)} collective-permute-done((f32[2,128,128]{2,1,0:T(8,128)S(1)}, f32[2,128,128]{2,1,0:T(8,128)S(1)}, u32[]{:S(2)}, u32[]{:S(2)}) %collective-permute-start.19) | collective-permute-done | bytes 131104 | tf_op jit(solution)/shard_map/ppermute | solution.py:331
  62.7 0.0 collective-permute-done.16.rest_0_
  62.7 0.7 place.1
  63.4 3.3 %collective-permute-start.21 = (f32[2,256,128]{2,1,0:T(8,128)S(1)}, f32[2,256,128]{2,1,0:T(8,128)S(1)}, u32[]{:S(2)}, u32[]{:S(2)}) collective-permute-start(f32[2,256,128]{2,1,0:T(8,128)S(1)} %get-tuple-element.63), channel_id=1, source_target_pairs={{16,32},{48,64},{80,96},{112,128},{144,160},{176,192},{208,224},{2... | collective-permute-start | bytes 786440 | tf_op jit(solution)/shard_map/ppermute | solution.py:359
  66.7 1.9 %collective-permute-start.20 = (f32[2,256,128]{2,1,0:T(8,128)S(1)}, f32[2,256,128]{2,1,0:T(8,128)S(1)}, u32[]{:S(2)}, u32[]{:S(2)}) collective-permute-start(f32[2,256,128]{2,1,0:T(8,128)S(1)} %get-tuple-element.62), channel_id=1, source_target_pairs={{0,16},{16,0},{32,48},{48,32},{64,80},{80,64},{96,112},{112,96},{1... | collective-permute-start | bytes 786440 | tf_op jit(solution)/shard_map/ppermute | solution.py:358
  68.7 3.7 %collective-permute-done.21.far = f32[2,256,128]{2,1,0:T(8,128)S(1)} collective-permute-done((f32[2,256,128]{2,1,0:T(8,128)S(1)}, f32[2,256,128]{2,1,0:T(8,128)S(1)}, u32[]{:S(2)}, u32[]{:S(2)}) %collective-permute-start.21) | collective-permute-done | bytes 262176 | tf_op jit(solution)/shard_map/ppermute | solution.py:359
  72.3 0.0 copy-done.2
  72.3 0.1 step.1.stepped
  72.4 0.0 collective-permute-done.20.near
  72.4 0.7 %last.1 = f32[1,2,256,128]{3,2,1,0:T(8,128)} custom-call(f32[2,256,128]{2,1,0:T(8,128)S(1)} %collective-permute-done.20.near, f32[2,256,128]{2,1,0:T(8,128)S(1)} %step.1.stepped), custom_call_target="tpu_custom_call" | custom-call | tf_op jit(solution)/shard_map/last/pallas_call | solution.py:252
  (7 shorter events, 0.1 us)
Async XLA Ops:
  0.0 9.6 %collective-permute-start.1 = (f32[2,256,128]{2,1,0:T(8,128)}, f32[2,256,128]{2,1,0:T(8,128)S(1)}, u32[]{:S(2)}, u32[]{:S(2)}) collective-permute-start(f32[2,256,128]{2,1,0:T(8,128)} %bitcast.1), channel_id=1, source_target_pairs={{16,32},{48,64},{80,96},{112,128},{144,160},{176,192},{208,224},{2... | collective-permute-start | bytes 786440 | tf_op jit(solution)/shard_map/ppermute | solution.py:287
  5.3 4.3 %collective-permute-start = (f32[2,256,128]{2,1,0:T(8,128)}, f32[2,256,128]{2,1,0:T(8,128)S(1)}, u32[]{:S(2)}, u32[]{:S(2)}) collective-permute-start(f32[2,256,128]{2,1,0:T(8,128)} %bitcast.2), channel_id=1, source_target_pairs={{0,16},{16,0},{32,48},{48,32},{64,80},{80,64},{96,112},{112,96},{1... | collective-permute-start | bytes 786440 | tf_op jit(solution)/shard_map/ppermute | solution.py:286
  7.2 1.0 %copy-start.1 = (f32[1,2,256,128]{3,2,1,0:T(8,128)S(1)}, f32[1,2,256,128]{3,2,1,0:T(8,128)}, u32[]{:S(2)}) copy-start(f32[1,2,256,128]{3,2,1,0:T(8,128)} %block.3) | copy-start | bytes 786436
  8.2 1.4 %copy-start.6 = (s32[2]{0:T(128)S(1)}, s32[2]{0:T(128)}, u32[]{:S(2)}) copy-start(s32[2]{0:T(128)} %owners.3) | copy-start | bytes 28
  8.2 1.4 %copy-start.7 = (s32[2]{0:T(128)S(1)}, s32[2]{0:T(128)}, u32[]{:S(2)}) copy-start(s32[2]{0:T(128)} %offsets.3) | copy-start | bytes 28
  9.6 13.8 %copy-start = (f32[2,128,128]{2,1,0:T(8,128)S(1)}, f32[2,128,128]{2,1,0:T(8,128)}, u32[]{:S(2)}) copy-start(f32[2,128,128]{2,1,0:T(8,128)} %constant.4.clone.table_ref.rest_9_) | copy-start | bytes 393220
  9.6 13.8 %copy-start.5 = (f32[2,128,128]{2,1,0:T(8,128)S(1)}, f32[2,128,128]{2,1,0:T(8,128)}, u32[]{:S(2)}) copy-start(f32[2,128,128]{2,1,0:T(8,128)} %wave_in.1) | copy-start | bytes 393220
  10.3 9.9 %collective-permute-start.3 = (f32[2,128,128]{2,1,0:T(8,128)S(1)}, f32[2,128,128]{2,1,0:T(8,128)S(1)}, u32[]{:S(2)}, u32[]{:S(2)}) collective-permute-start(f32[2,128,128]{2,1,0:T(8,128)S(1)} %get-tuple-element.37), channel_id=1, source_target_pairs={{2,0},{6,16},{10,12},{3,1},{7,17},{11,13},{16,18},{20,2},{24,30},{... | collective-permute-start | bytes 393224 | tf_op jit(solution)/shard_map/ppermute | solution.py:298
  14.9 8.5 %collective-permute-start.4 = (f32[2,128,128]{2,1,0:T(8,128)S(1)}, f32[2,128,128]{2,1,0:T(8,128)S(1)}, u32[]{:S(2)}, u32[]{:S(2)}) collective-permute-start(f32[2,128,128]{2,1,0:T(8,128)S(1)} %get-tuple-element.36), channel_id=1, source_target_pairs={{3,0},{7,16},{11,12},{2,1},{6,17},{10,13},{17,18},{21,2},{25,30},{... | collective-permute-start | bytes 393224 | tf_op jit(solution)/shard_map/ppermute | solution.py:298
  16.9 6.6 %collective-permute-start.2 = (f32[2,128,128]{2,1,0:T(8,128)S(1)}, f32[2,128,128]{2,1,0:T(8,128)S(1)}, u32[]{:S(2)}, u32[]{:S(2)}) collective-permute-start(f32[2,128,128]{2,1,0:T(8,128)S(1)} %get-tuple-element.36), channel_id=1, source_target_pairs={{1,0},{13,12},{0,1},{12,13},{19,18},{31,30},{18,19},{30,31},{33,32... | collective-permute-start | bytes 393224 | tf_op jit(solution)/shard_map/ppermute | solution.py:298
  17.5 8.6 %collective-permute-start.6 = (f32[2,128,128]{2,1,0:T(8,128)S(1)}, f32[2,128,128]{2,1,0:T(8,128)S(1)}, u32[]{:S(2)}, u32[]{:S(2)}) collective-permute-start(f32[2,128,128]{2,1,0:T(8,128)S(1)} %get-tuple-element.37), channel_id=1, source_target_pairs={{4,16},{8,12},{5,17},{9,13},{22,2},{26,30},{23,3},{27,31},{36,48},... | collective-permute-start | bytes 393224 | tf_op jit(solution)/shard_map/ppermute | solution.py:298
  18.8 7.3 %collective-permute-start.7 = (f32[2,128,128]{2,1,0:T(8,128)S(1)}, f32[2,128,128]{2,1,0:T(8,128)S(1)}, u32[]{:S(2)}, u32[]{:S(2)}) collective-permute-start(f32[2,128,128]{2,1,0:T(8,128)S(1)} %get-tuple-element.36), channel_id=1, source_target_pairs={{5,16},{9,12},{4,17},{8,13},{23,2},{27,30},{22,3},{26,31},{37,48},... | collective-permute-start | bytes 393224 | tf_op jit(solution)/shard_map/ppermute | solution.py:298
  23.5 3.2 %collective-permute-start.5 = (f32[2,128,128]{2,1,0:T(8,128)S(1)}, f32[2,128,128]{2,1,0:T(8,128)S(1)}, u32[]{:S(2)}, u32[]{:S(2)}) collective-permute-start(f32[2,128,128]{2,1,0:T(8,128)S(1)} %get-tuple-element.38), channel_id=1, source_target_pairs={{0,16},{1,17},{18,2},{19,3},{32,48},{33,49},{50,34},{51,35},{64,80... | collective-permute-start | bytes 393224 | tf_op jit(solution)/shard_map/ppermute | solution.py:311
  24.8 5.0 %collective-permute-start.9 = (f32[2,128,128]{2,1,0:T(8,128)S(1)}, f32[2,128,128]{2,1,0:T(8,128)S(1)}, u32[]{:S(2)}, u32[]{:S(2)}) collective-permute-start(f32[2,128,128]{2,1,0:T(8,128)S(1)} %get-tuple-element.37), channel_id=1, source_target_pairs={{14,12},{15,13},{28,30},{29,31},{46,44},{47,45},{60,62},{61,63},{7... | collective-permute-start | bytes 393224 | tf_op jit(solution)/shard_map/ppermute | solution.py:298
  25.5 4.4 %collective-permute-start.10 = (f32[2,128,128]{2,1,0:T(8,128)S(1)}, f32[2,128,128]{2,1,0:T(8,128)S(1)}, u32[]{:S(2)}, u32[]{:S(2)}) collective-permute-start(f32[2,128,128]{2,1,0:T(8,128)S(1)} %get-tuple-element.36), channel_id=1, source_target_pairs={{15,12},{14,13},{29,30},{28,31},{47,44},{46,45},{61,62},{60,63},{7... | collective-permute-start | bytes 393224 | tf_op jit(solution)/shard_map/ppermute | solution.py:298
  26.7 5.0 %copy-start.3 = (f32[2,128,128]{2,1,0:T(8,128)S(1)}, f32[2,128,128]{2,1,0:T(8,128)}, u32[]{:S(2)}) copy-start(f32[2,128,128]{2,1,0:T(8,128)} %rest_8_.1) | copy-start | bytes 393220
  26.7 5.0 %copy-start.4 = (f32[2,128,128]{2,1,0:T(8,128)S(1)}, f32[2,128,128]{2,1,0:T(8,128)}, u32[]{:S(2)}) copy-start(f32[2,128,128]{2,1,0:T(8,128)} %constant.5.clone.rest_10_) | copy-start | bytes 393220
  28.5 3.2 %collective-permute-start.8 = (f32[2,128,128]{2,1,0:T(8,128)S(1)}, f32[2,128,128]{2,1,0:T(8,128)S(1)}, u32[]{:S(2)}, u32[]{:S(2)}) collective-permute-start(f32[2,128,128]{2,1,0:T(8,128)S(1)} %get-tuple-element.41), channel_id=1, source_target_pairs={{16,12},{17,13},{2,30},{3,31},{48,44},{49,45},{34,62},{35,63},{80,... | collective-permute-start | bytes 393224 | tf_op jit(solution)/shard_map/ppermute | solution.py:319
  31.7 14.7 %collective-permute-start.11 = (f32[2,128,128]{2,1,0:T(8,128)S(1)}, f32[2,128,128]{2,1,0:T(8,128)S(1)}, u32[]{:S(2)}, u32[]{:S(2)}) collective-permute-start(f32[2,128,128]{2,1,0:T(8,128)S(1)} %get-tuple-element.42), channel_id=1, source_target_pairs={{12,16},{13,17},{30,2},{31,3},{44,48},{45,49},{62,34},{63,35},{76,... | collective-permute-start | bytes 393224 | tf_op jit(solution)/shard_map/ppermute | solution.py:334
  33.0 13.4 %collective-permute-start.12 = (f32[2,128,128]{2,1,0:T(8,128)S(1)}, f32[2,128,128]{2,1,0:T(8,128)S(1)}, u32[]{:S(2)}, u32[]{:S(2)}) collective-permute-start(f32[2,128,128]{2,1,0:T(8,128)S(1)} %get-tuple-element.49), channel_id=1, source_target_pairs={{12,13},{13,12},{30,31},{31,30},{44,45},{45,44},{62,63},{63,62},{7... | collective-permute-start | bytes 393224 | tf_op jit(solution)/shard_map/ppermute | solution.py:331
  33.7 12.7 %collective-permute-start.13 = (f32[2,128,128]{2,1,0:T(8,128)S(1)}, f32[2,128,128]{2,1,0:T(8,128)S(1)}, u32[]{:S(2)}, u32[]{:S(2)}) collective-permute-start(f32[2,128,128]{2,1,0:T(8,128)S(1)} %get-tuple-element.50), channel_id=1, source_target_pairs={{12,14},{13,15},{30,28},{31,29},{44,46},{45,47},{62,60},{63,61},{7... | collective-permute-start | bytes 393224 | tf_op jit(solution)/shard_map/ppermute | solution.py:331
  34.4 12.0 %collective-permute-start.14 = (f32[2,128,128]{2,1,0:T(8,128)S(1)}, f32[2,128,128]{2,1,0:T(8,128)S(1)}, u32[]{:S(2)}, u32[]{:S(2)}) collective-permute-start(f32[2,128,128]{2,1,0:T(8,128)S(1)} %get-tuple-element.51), channel_id=1, source_target_pairs={{12,15},{13,14},{30,29},{31,28},{44,47},{45,46},{62,61},{63,60},{7... | collective-permute-start | bytes 393224 | tf_op jit(solution)/shard_map/ppermute | solution.py:331
  48.2 2.3 %collective-permute-start.15 = (f32[2,128,128]{2,1,0:T(8,128)S(1)}, f32[2,128,128]{2,1,0:T(8,128)S(1)}, u32[]{:S(2)}, u32[]{:S(2)}) collective-permute-start(f32[2,128,128]{2,1,0:T(8,128)S(1)} %get-tuple-element.52), channel_id=1, source_target_pairs={{16,0},{17,1},{2,18},{3,19},{48,32},{49,33},{34,50},{35,51},{80,64... | collective-permute-start | bytes 393224 | tf_op jit(solution)/shard_map/ppermute | solution.py:334
  50.5 6.5 %collective-permute-start.17 = (f32[2,128,128]{2,1,0:T(8,128)S(1)}, f32[2,128,128]{2,1,0:T(8,128)S(1)}, u32[]{:S(2)}, u32[]{:S(2)}) collective-permute-start(f32[2,128,128]{2,1,0:T(8,128)S(1)} %get-tuple-element.59), channel_id=1, source_target_pairs={{0,1},{16,5},{12,9},{1,0},{17,4},{13,8},{18,19},{2,23},{30,27},{19... | collective-permute-start | bytes 393224 | tf_op jit(solution)/shard_map/ppermute | solution.py:331
  51.8 9.1 %collective-permute-start.18 = (f32[2,128,128]{2,1,0:T(8,128)S(1)}, f32[2,128,128]{2,1,0:T(8,128)S(1)}, u32[]{:S(2)}, u32[]{:S(2)}) collective-permute-start(f32[2,128,128]{2,1,0:T(8,128)S(1)} %get-tuple-element.60), channel_id=1, source_target_pairs={{0,2},{16,6},{12,10},{1,3},{17,7},{13,11},{18,16},{2,20},{30,24},{... | collective-permute-start | bytes 393224 | tf_op jit(solution)/shard_map/ppermute | solution.py:331
  53.7 9.0 %collective-permute-start.19 = (f32[2,128,128]{2,1,0:T(8,128)S(1)}, f32[2,128,128]{2,1,0:T(8,128)S(1)}, u32[]{:S(2)}, u32[]{:S(2)}) collective-permute-start(f32[2,128,128]{2,1,0:T(8,128)S(1)} %get-tuple-element.61), channel_id=1, source_target_pairs={{0,3},{16,7},{12,11},{1,2},{17,6},{13,10},{18,17},{2,21},{30,25},{... | collective-permute-start | bytes 393224 | tf_op jit(solution)/shard_map/ppermute | solution.py:331
  55.6 7.1 %collective-permute-start.16 = (f32[2,128,128]{2,1,0:T(8,128)S(1)}, f32[2,128,128]{2,1,0:T(8,128)S(1)}, u32[]{:S(2)}, u32[]{:S(2)}) collective-permute-start(f32[2,128,128]{2,1,0:T(8,128)S(1)} %get-tuple-element.57.first_own), channel_id=1, source_target_pairs={{16,4},{12,8},{17,5},{13,9},{2,22},{30,26},{3,23},{31,27},{48,36},... | collective-permute-start | bytes 393224 | tf_op jit(solution)/shard_map/ppermute | solution.py:331
  62.7 9.6 %copy-start.2 = (f32[1,2,256,128]{3,2,1,0:T(8,128)S(1)}, f32[1,2,256,128]{3,2,1,0:T(8,128)}, u32[]{:S(2)}) copy-start(f32[1,2,256,128]{3,2,1,0:T(8,128)} %block.3) | copy-start | bytes 786436
  63.4 8.9 %collective-permute-start.21 = (f32[2,256,128]{2,1,0:T(8,128)S(1)}, f32[2,256,128]{2,1,0:T(8,128)S(1)}, u32[]{:S(2)}, u32[]{:S(2)}) collective-permute-start(f32[2,256,128]{2,1,0:T(8,128)S(1)} %get-tuple-element.63), channel_id=1, source_target_pairs={{16,32},{48,64},{80,96},{112,128},{144,160},{176,192},{208,224},{2... | collective-permute-start | bytes 786440 | tf_op jit(solution)/shard_map/ppermute | solution.py:359
  66.7 5.7 %collective-permute-start.20 = (f32[2,256,128]{2,1,0:T(8,128)S(1)}, f32[2,256,128]{2,1,0:T(8,128)S(1)}, u32[]{:S(2)}, u32[]{:S(2)}) collective-permute-start(f32[2,256,128]{2,1,0:T(8,128)S(1)} %get-tuple-element.62), channel_id=1, source_target_pairs={{0,16},{16,0},{32,48},{48,32},{64,80},{80,64},{96,112},{112,96},{1... | collective-permute-start | bytes 786440 | tf_op jit(solution)/shard_map/ppermute | solution.py:358

commit v9 on v8

--- a/solution.py
+++ b/solution.py
@@ -14,7 +14,6 @@
 group = 4
 params = pltpu.CompilerParams(vmem_limit_bytes=48 * 2**20)
 in_vmem = pl.BlockSpec(memory_space=pltpu.VMEM)
-in_smem = pl.BlockSpec(memory_space=pltpu.SMEM)
 window_type = jax.ShapeDtypeStruct((2, side, side), jnp.float32)
 tile_type = jax.ShapeDtypeStruct((2, tile, side), jnp.float32)
 slab_type = jax.ShapeDtypeStruct((2, 3 * tile, side), jnp.float32)
@@ -94,8 +93,9 @@
     return 1 - (column() & 1)
 
 
-def start_of(at, owners, offsets):
-    start = (owners[at] - lax.axis_index("scan") + 1) * tile + offsets[at]
+def start_of(at, starts):
+    chosen = lax.broadcasted_iota(jnp.int32, starts.shape, 1) == at
+    start = jnp.sum(jnp.where(chosen, starts[...], 0.0)).astype(jnp.int32)
     return jnp.clip(start, 0, 2 * tile)
 
 
@@ -105,7 +105,9 @@
     pl.when(jnp.logical_not(even_scan))(odd)
 
 
-def stage_kernel(block, slab):
+def stage_kernel(owners, offsets, block, starts, slab):
+    tiles = owners[...] - (lax.axis_index("scan") - 1)
+    starts[...] = (tiles * tile + offsets[...]).astype(jnp.float32)
     slab[:, tile : 2 * tile] = block[0]
 
 
@@ -119,7 +121,7 @@
     by_scan_parity(even, odd)
 
 
-def cut_kernel(near, owners, offsets, laid, lower_out, upper_out, own, slab):
+def cut_kernel(near, starts, laid, lower_out, upper_out, own, slab):
     def even():
         slab[:, 2 * tile :] = near[...]
 
@@ -129,7 +131,7 @@
     by_scan_parity(even, odd)
     upper = upper_position()
     for at, out in ((upper, upper_out), (1 - upper, lower_out)):
-        out[...] = slab[:, pl.ds(start_of(at, owners, offsets), side), :]
+        out[...] = slab[:, pl.ds(start_of(at, starts), side), :]
     own[...] = lower_out[...]
 
 
@@ -209,7 +211,7 @@
         share(updates, rest[:group])
 
 
-def place_kernel(owners, offsets, first_own, fourth_own, *rest):
+def place_kernel(starts, first_own, fourth_own, *rest):
     (zero, one, two, three), fourth, (slab, near, far) = rest[:group], rest[group:-3], rest[-3:]
     slab[...] = jnp.zeros_like(slab)
     mine = role()
@@ -218,7 +220,7 @@
     early = (two[...] + fourth[1][...]) + own
     upper = upper_position()
     for at, update in ((upper, late), (1 - upper, early)):
-        rows = pl.ds(start_of(at, owners, offsets), side)
+        rows = pl.ds(start_of(at, starts), side)
         slab[:, rows, :] = slab[:, rows, :] + update
 
     def even():
@@ -247,7 +249,7 @@
     step_table, fourier_table = tables()
 
     def call(kernel, name, out_shape, arguments, scratch=(), aliases=(), after=()):
-        specs = [in_smem if a.dtype == jnp.int32 else in_vmem for a in arguments]
+        specs = [in_vmem] * len(arguments)
         specs += [pl.BlockSpec(memory_space=pl.ANY)] * len(after)
         return pl.pallas_call(
             kernel,
@@ -285,14 +287,20 @@
 
     near = lax.ppermute(object_slices[0], "scan", on_chip)
     far = lax.ppermute(object_slices[0], "scan", next_chip)
-    slab = call(stage_kernel, "stage", slab_type, (object_slices,))
+    starts_type = jax.ShapeDtypeStruct((1, offsets.shape[0]), jnp.float32)
+    starts, slab = call(
+        stage_kernel,
+        "stage",
+        [starts_type, slab_type],
+        (owners[None], offsets[None], object_slices),
+    )
     slab = call(lay_kernel, "lay", slab_type, (far, slab), aliases=[(1, 0)])
     lower_window, upper_window, own, slab = call(
         cut_kernel,
         "cut",
         [window_type] * 3 + [slab_type],
-        (near, owners, offsets, slab),
-        aliases=[(3, 3)],
+        (near, starts, slab),
+        aliases=[(2, 3)],
     )
     def gather(mask, *groups):
         return lax.ppermute(upper_window if mask & 1 else lower_window, axes, sends(mask, *groups))
@@ -353,7 +361,7 @@
         place_kernel,
         "place",
         [slab_type, tile_type, tile_type],
-        (owners, offsets, parts[0], fourth_own, *landed),
+        (starts, parts[0], fourth_own, *landed),
     )
     near = lax.ppermute(near, "scan", on_chip)
     far = lax.ppermute(far, "scan", next_chip)

time: 73.7 us -> 72.7 us (0.986)
  the two profiles are of different devices: /device:TPU:225 before, /device:TPU:97 now
where the time goes in v9:
time: 72.7 us; the launch traced here: 72.2 us
  starting transfers between devices  37.3 us (51%)
  waiting for transfers between devices  28.1 us (39%)
  Pallas kernels  4.81 us (7%)
  local copies, waits for them, and re-layouts  1.63 us (2%)
    ppermute x2, waiting for transfers between devices, shards(): adjoint = lax.ppermute(adjoint, axes, ends(hops[mine]))  12.3 us
    ppermute x7, starting transfers between devices, gather(): lax.ppermute(upper_window if mask & 1 else lower_window, axes, sends(mask...  11.2 us
    ppermute x7, starting transfers between devices, scatter(): return lax.ppermute(part, axes, ends(sends(mask, *groups)))  8.43 us
    ppermute x7, waiting for transfers between devices, scatter(): return lax.ppermute(part, axes, ends(sends(mask, *groups)))  5.66 us
    ppermute x1, starting transfers between devices, shards(): far = lax.ppermute(object_slices[0], 'scan', next_chip)  5.31 us
    pallas_call x11, Pallas kernels, call(): pl.pallas_call(kernel, out_shape=out_shape, in_specs=specs, out_specs=jax...  4.81 us
    ppermute x1, waiting for transfers between devices, shards(): far = lax.ppermute(far, 'scan', next_chip)  3.67 us
    ppermute x7, waiting for transfers between devices, gather(): lax.ppermute(upper_window if mask & 1 else lower_window, axes, sends(mask...  3.3 us
  transfers between devices with their start and end apart: 22, of which 9 were waited for; matrix products, arithmetic and copies ran while one was open for 0% of the time, Pallas kernels for 3%

profile of v9, /device:TPU:97, one launch (start us, length us, event | category | flops | bytes accessed | tf_op | source)
XLA Modules:
  0.0 72.2 jit_solution(3242009501358934355)
XLA Ops:
  0.0 5.3 %collective-permute-start.1 = (f32[2,256,128]{2,1,0:T(8,128)}, f32[2,256,128]{2,1,0:T(8,128)S(1)}, u32[]{:S(2)}, u32[]{:S(2)}) collective-permute-start(f32[2,256,128]{2,1,0:T(8,128)} %bitcast.3), channel_id=1, source_target_pairs={{16,32},{48,64},{80,96},{112,128},{144,160},{176,192},{208,224},{2... | collective-permute-start | bytes 786440 | tf_op jit(solution)/shard_map/ppermute | solution.py:289
  5.3 1.9 %collective-permute-start = (f32[2,256,128]{2,1,0:T(8,128)}, f32[2,256,128]{2,1,0:T(8,128)S(1)}, u32[]{:S(2)}, u32[]{:S(2)}) collective-permute-start(f32[2,256,128]{2,1,0:T(8,128)} %bitcast.4), channel_id=1, source_target_pairs={{0,16},{16,0},{32,48},{48,32},{64,80},{80,64},{96,112},{112,96},{1... | collective-permute-start | bytes 786440 | tf_op jit(solution)/shard_map/ppermute | solution.py:288
  7.2 0.0 copy-start.6
  7.3 0.0 copy-start.7
  7.3 0.6 copy-done.6
  7.9 0.0 copy-done.7
  7.9 0.0 copy-start.1
  7.9 0.9 %copy-done.1 = f32[1,2,256,128]{3,2,1,0:T(8,128)S(1)} copy-done((f32[1,2,256,128]{3,2,1,0:T(8,128)S(1)}, f32[1,2,256,128]{3,2,1,0:T(8,128)}, u32[]{:S(2)}) %copy-start.1) | copy-done | bytes 262168
  8.9 0.7 collective-permute-done.1.far
  9.6 0.0 collective-permute-done.near
  9.6 0.0 copy-start
  9.6 0.0 copy-start.5
  9.6 0.2 cut.1
  9.8 4.7 %collective-permute-start.3 = (f32[2,128,128]{2,1,0:T(8,128)S(1)}, f32[2,128,128]{2,1,0:T(8,128)S(1)}, u32[]{:S(2)}, u32[]{:S(2)}) collective-permute-start(f32[2,128,128]{2,1,0:T(8,128)S(1)} %get-tuple-element.41), channel_id=1, source_target_pairs={{2,0},{6,16},{10,12},{3,1},{7,17},{11,13},{16,18},{20,2},{24,30},{... | collective-permute-start | bytes 393224 | tf_op jit(solution)/shard_map/ppermute | solution.py:306
  14.5 1.9 %collective-permute-start.4 = (f32[2,128,128]{2,1,0:T(8,128)S(1)}, f32[2,128,128]{2,1,0:T(8,128)S(1)}, u32[]{:S(2)}, u32[]{:S(2)}) collective-permute-start(f32[2,128,128]{2,1,0:T(8,128)S(1)} %get-tuple-element.40), channel_id=1, source_target_pairs={{3,0},{7,16},{11,12},{2,1},{6,17},{10,13},{17,18},{21,2},{25,30},{... | collective-permute-start | bytes 393224 | tf_op jit(solution)/shard_map/ppermute | solution.py:306
  16.4 0.7 collective-permute-start.2
  17.1 1.3 %collective-permute-start.6 = (f32[2,128,128]{2,1,0:T(8,128)S(1)}, f32[2,128,128]{2,1,0:T(8,128)S(1)}, u32[]{:S(2)}, u32[]{:S(2)}) collective-permute-start(f32[2,128,128]{2,1,0:T(8,128)S(1)} %get-tuple-element.41), channel_id=1, source_target_pairs={{4,16},{8,12},{5,17},{9,13},{22,2},{26,30},{23,3},{27,31},{36,48},... | collective-permute-start | bytes 393224 | tf_op jit(solution)/shard_map/ppermute | solution.py:306
  18.4 1.3 %collective-permute-start.7 = (f32[2,128,128]{2,1,0:T(8,128)S(1)}, f32[2,128,128]{2,1,0:T(8,128)S(1)}, u32[]{:S(2)}, u32[]{:S(2)}) collective-permute-start(f32[2,128,128]{2,1,0:T(8,128)S(1)} %get-tuple-element.40), channel_id=1, source_target_pairs={{5,16},{9,12},{4,17},{8,13},{23,2},{27,30},{22,3},{26,31},{37,48},... | collective-permute-start | bytes 393224 | tf_op jit(solution)/shard_map/ppermute | solution.py:306
  19.7 0.0 collective-permute-done.3.two.rest_2_
  19.7 3.3 %collective-permute-done.4.three.rest_3_ = f32[2,128,128]{2,1,0:T(8,128)S(1)} collective-permute-done((f32[2,128,128]{2,1,0:T(8,128)S(1)}, f32[2,128,128]{2,1,0:T(8,128)S(1)}, u32[]{:S(2)}, u32[]{:S(2)}) %collective-permute-start.4) | collective-permute-done | bytes 131104 | tf_op jit(solution)/shard_map/ppermute | solution.py:306
  23.0 0.0 collective-permute-done.2.one.rest_5_
  23.0 0.0 copy-done
  23.0 0.0 copy-done.5
  23.0 1.3 %collective-permute-start.5 = (f32[2,128,128]{2,1,0:T(8,128)S(1)}, f32[2,128,128]{2,1,0:T(8,128)S(1)}, u32[]{:S(2)}, u32[]{:S(2)}) collective-permute-start(f32[2,128,128]{2,1,0:T(8,128)S(1)} %get-tuple-element.42), channel_id=1, source_target_pairs={{0,16},{1,17},{18,2},{19,3},{32,48},{33,49},{50,34},{51,35},{64,80... | collective-permute-start | bytes 393224 | tf_op jit(solution)/shard_map/ppermute | solution.py:319
  24.3 0.7 collective-permute-start.9
  25.0 0.7 collective-permute-start.10
  25.7 0.0 collective-permute-done.6.zero.rest_0_
  25.7 0.0 collective-permute-done.7.one.rest_1_
  25.7 0.6 collective-permute-done.5.wave_in
  26.3 0.0 copy-start.3
  26.3 1.8 %second.1 = (f32[2,128,128]{2,1,0:T(8,128)S(1)}, f32[4,2,128,128]{3,2,1,0:T(8,128)S(1)}, f32[4,2,128,128]{3,2,1,0:T(8,128)S(1)}) custom-call(f32[2,128,128]{2,1,0:T(8,128)S(1)} %collective-permute-done.5.wave_in, f32[2,128,128]{2,1,0:T(8,128)S(1)} %collective-permute-done.6.zero.rest_0_, ...), custom_call_target="tpu_custom_call", output_to_operand_aliasing={{1}: (6, {}), {2}: (7, {})} | custom-call | tf_op jit(solution)/shard_map/second/pallas_call | solution.py:254
  28.0 1.4 %collective-permute-start.8 = (f32[2,128,128]{2,1,0:T(8,128)S(1)}, f32[2,128,128]{2,1,0:T(8,128)S(1)}, u32[]{:S(2)}, u32[]{:S(2)}) collective-permute-start(f32[2,128,128]{2,1,0:T(8,128)S(1)} %get-tuple-element.45), channel_id=1, source_target_pairs={{16,12},{17,13},{2,30},{3,31},{48,44},{49,45},{34,62},{35,63},{80,... | collective-permute-start | bytes 393224 | tf_op jit(solution)/shard_map/ppermute | solution.py:327
  29.5 0.0 collective-permute-done.9.rest_6_
  29.5 0.0 collective-permute-done.10.rest_7_
  29.5 1.9 %collective-permute-done.8.wave_in = f32[2,128,128]{2,1,0:T(8,128)S(1)} collective-permute-done((f32[2,128,128]{2,1,0:T(8,128)S(1)}, f32[2,128,128]{2,1,0:T(8,128)S(1)}, u32[]{:S(2)}, u32[]{:S(2)}) %collective-permute-start.8) | collective-permute-done | bytes 131104 | tf_op jit(solution)/shard_map/ppermute | solution.py:327
  31.4 0.0 copy-done.3
  31.4 0.0 copy-done.4
  31.4 1.3 %collective-permute-start.11 = (f32[2,128,128]{2,1,0:T(8,128)S(1)}, f32[2,128,128]{2,1,0:T(8,128)S(1)}, u32[]{:S(2)}, u32[]{:S(2)}) collective-permute-start(f32[2,128,128]{2,1,0:T(8,128)S(1)} %get-tuple-element.46), channel_id=1, source_target_pairs={{12,16},{13,17},{30,2},{31,3},{44,48},{45,49},{62,34},{63,35},{76,... | collective-permute-start | bytes 393224 | tf_op jit(solution)/shard_map/ppermute | solution.py:342
  32.7 0.7 collective-permute-start.12
  33.4 0.7 collective-permute-start.13
  34.0 0.7 collective-permute-start.14
  34.7 11.4 %collective-permute-done.11.adjoint_in = f32[2,128,128]{2,1,0:T(8,128)S(1)} collective-permute-done((f32[2,128,128]{2,1,0:T(8,128)S(1)}, f32[2,128,128]{2,1,0:T(8,128)S(1)}, u32[]{:S(2)}, u32[]{:S(2)}) %collective-permute-start.11) | collective-permute-done | bytes 131104 | tf_op jit(solution)/shard_map/ppermute | solution.py:342
  46.1 0.0 collective-permute-done.12.rest_4_
  46.1 0.0 collective-permute-done.13.rest_5_
  46.1 0.0 collective-permute-done.14.rest_6_
  46.1 1.8 %back_second.1 = (f32[2,128,128]{2,1,0:T(8,128)S(1)}, f32[2,128,128]{2,1,0:T(8,128)S(1)}, f32[2,128,128]{2,1,0:T(8,128)S(1)}, f32[2,128,128]{2,1,0:T(8,128)S(1)}, f32[2,128,128]{2,1,0:T(8,128)S(1)}) custom-call(f32[2,128,128]{2,1,0:T(8,128)S(1)} %collective-permute-done.11.adjoint_in, ...), custom_call_target="tpu_custom_call", output_to_operand_aliasing={{0}: (4, {}), {1}: (5, {}), {2}: (6, {}), {3}: (7, {})} | custom-call | tf_op jit(solution)/shard_map/back_second/pallas_call | solution.py:254
  47.9 1.3 %collective-permute-start.15 = (f32[2,128,128]{2,1,0:T(8,128)S(1)}, f32[2,128,128]{2,1,0:T(8,128)S(1)}, u32[]{:S(2)}, u32[]{:S(2)}) collective-permute-start(f32[2,128,128]{2,1,0:T(8,128)S(1)} %get-tuple-element.56), channel_id=1, source_target_pairs={{16,0},{17,1},{2,18},{3,19},{48,32},{49,33},{34,50},{35,51},{80,64... | collective-permute-start | bytes 393224 | tf_op jit(solution)/shard_map/ppermute | solution.py:342
  49.2 1.0 %collective-permute-done.15.adjoint_in = f32[2,128,128]{2,1,0:T(8,128)S(1)} collective-permute-done((f32[2,128,128]{2,1,0:T(8,128)S(1)}, f32[2,128,128]{2,1,0:T(8,128)S(1)}, u32[]{:S(2)}, u32[]{:S(2)}) %collective-permute-start.15) | collective-permute-done | bytes 131104 | tf_op jit(solution)/shard_map/ppermute | solution.py:342
  50.1 1.3 %collective-permute-start.17 = (f32[2,128,128]{2,1,0:T(8,128)S(1)}, f32[2,128,128]{2,1,0:T(8,128)S(1)}, u32[]{:S(2)}, u32[]{:S(2)}) collective-permute-start(f32[2,128,128]{2,1,0:T(8,128)S(1)} %get-tuple-element.63), channel_id=1, source_target_pairs={{0,1},{16,5},{12,9},{1,0},{17,4},{13,8},{18,19},{2,23},{30,27},{19... | collective-permute-start | bytes 393224 | tf_op jit(solution)/shard_map/ppermute | solution.py:339
  51.4 1.9 %collective-permute-start.18 = (f32[2,128,128]{2,1,0:T(8,128)S(1)}, f32[2,128,128]{2,1,0:T(8,128)S(1)}, u32[]{:S(2)}, u32[]{:S(2)}) collective-permute-start(f32[2,128,128]{2,1,0:T(8,128)S(1)} %get-tuple-element.64), channel_id=1, source_target_pairs={{0,2},{16,6},{12,10},{1,3},{17,7},{13,11},{18,16},{2,20},{30,24},{... | collective-permute-start | bytes 393224 | tf_op jit(solution)/shard_map/ppermute | solution.py:339
  53.4 1.9 %collective-permute-start.19 = (f32[2,128,128]{2,1,0:T(8,128)S(1)}, f32[2,128,128]{2,1,0:T(8,128)S(1)}, u32[]{:S(2)}, u32[]{:S(2)}) collective-permute-start(f32[2,128,128]{2,1,0:T(8,128)S(1)} %get-tuple-element.65), channel_id=1, source_target_pairs={{0,3},{16,7},{12,11},{1,2},{17,6},{13,10},{18,17},{2,21},{30,25},{... | collective-permute-start | bytes 393224 | tf_op jit(solution)/shard_map/ppermute | solution.py:339
  55.3 1.3 %collective-permute-start.16 = (f32[2,128,128]{2,1,0:T(8,128)S(1)}, f32[2,128,128]{2,1,0:T(8,128)S(1)}, u32[]{:S(2)}, u32[]{:S(2)}) collective-permute-start(f32[2,128,128]{2,1,0:T(8,128)S(1)} %get-tuple-element.61.first_own), channel_id=1, source_target_pairs={{16,4},{12,8},{17,5},{13,9},{2,22},{30,26},{3,23},{31,27},{48,36},... | collective-permute-start | bytes 393224 | tf_op jit(solution)/shard_map/ppermute | solution.py:339
  56.6 0.0 collective-permute-done.17.rest_1_
  56.6 3.8 %collective-permute-done.18.rest_2_ = f32[2,128,128]{2,1,0:T(8,128)S(1)} collective-permute-done((f32[2,128,128]{2,1,0:T(8,128)S(1)}, f32[2,128,128]{2,1,0:T(8,128)S(1)}, u32[]{:S(2)}, u32[]{:S(2)}) %collective-permute-start.18) | collective-permute-done | bytes 131104 | tf_op jit(solution)/shard_map/ppermute | solution.py:339
  60.5 1.8 %collective-permute-done.19.rest_3_ = f32[2,128,128]{2,1,0:T(8,128)S(1)} collective-permute-done((f32[2,128,128]{2,1,0:T(8,128)S(1)}, f32[2,128,128]{2,1,0:T(8,128)S(1)}, u32[]{:S(2)}, u32[]{:S(2)}) %collective-permute-start.19) | collective-permute-done | bytes 131104 | tf_op jit(solution)/shard_map/ppermute | solution.py:339
  62.2 0.0 collective-permute-done.16.rest_0_
  62.3 0.2 place.1
  62.5 3.3 %collective-permute-start.21 = (f32[2,256,128]{2,1,0:T(8,128)S(1)}, f32[2,256,128]{2,1,0:T(8,128)S(1)}, u32[]{:S(2)}, u32[]{:S(2)}) collective-permute-start(f32[2,256,128]{2,1,0:T(8,128)S(1)} %get-tuple-element.67), channel_id=1, source_target_pairs={{16,32},{48,64},{80,96},{112,128},{144,160},{176,192},{208,224},{2... | collective-permute-start | bytes 786440 | tf_op jit(solution)/shard_map/ppermute | solution.py:367
  65.8 1.9 %collective-permute-start.20 = (f32[2,256,128]{2,1,0:T(8,128)S(1)}, f32[2,256,128]{2,1,0:T(8,128)S(1)}, u32[]{:S(2)}, u32[]{:S(2)}) collective-permute-start(f32[2,256,128]{2,1,0:T(8,128)S(1)} %get-tuple-element.66), channel_id=1, source_target_pairs={{0,16},{16,0},{32,48},{48,32},{64,80},{80,64},{96,112},{112,96},{1... | collective-permute-start | bytes 786440 | tf_op jit(solution)/shard_map/ppermute | solution.py:366
  67.7 3.7 %collective-permute-done.21.far = f32[2,256,128]{2,1,0:T(8,128)S(1)} collective-permute-done((f32[2,256,128]{2,1,0:T(8,128)S(1)}, f32[2,256,128]{2,1,0:T(8,128)S(1)}, u32[]{:S(2)}, u32[]{:S(2)}) %collective-permute-start.21) | collective-permute-done | bytes 262176 | tf_op jit(solution)/shard_map/ppermute | solution.py:367
  71.4 0.0 copy-done.2
  71.4 0.1 step.1.stepped
  71.4 0.0 collective-permute-done.20.near
  71.5 0.7 %last.1 = f32[1,2,256,128]{3,2,1,0:T(8,128)} custom-call(f32[2,256,128]{2,1,0:T(8,128)S(1)} %collective-permute-done.20.near, f32[2,256,128]{2,1,0:T(8,128)S(1)} %step.1.stepped), custom_call_target="tpu_custom_call" | custom-call | tf_op jit(solution)/shard_map/last/pallas_call | solution.py:254
  (7 shorter events, 0.1 us)
Async XLA Ops:
  0.0 9.6 %collective-permute-start.1 = (f32[2,256,128]{2,1,0:T(8,128)}, f32[2,256,128]{2,1,0:T(8,128)S(1)}, u32[]{:S(2)}, u32[]{:S(2)}) collective-permute-start(f32[2,256,128]{2,1,0:T(8,128)} %bitcast.3), channel_id=1, source_target_pairs={{16,32},{48,64},{80,96},{112,128},{144,160},{176,192},{208,224},{2... | collective-permute-start | bytes 786440 | tf_op jit(solution)/shard_map/ppermute | solution.py:289
  5.3 4.3 %collective-permute-start = (f32[2,256,128]{2,1,0:T(8,128)}, f32[2,256,128]{2,1,0:T(8,128)S(1)}, u32[]{:S(2)}, u32[]{:S(2)}) collective-permute-start(f32[2,256,128]{2,1,0:T(8,128)} %bitcast.4), channel_id=1, source_target_pairs={{0,16},{16,0},{32,48},{48,32},{64,80},{80,64},{96,112},{112,96},{1... | collective-permute-start | bytes 786440 | tf_op jit(solution)/shard_map/ppermute | solution.py:288
  7.2 0.7 copy-start.6
  7.3 0.7 copy-start.7
  7.9 0.9 %copy-start.1 = (f32[1,2,256,128]{3,2,1,0:T(8,128)S(1)}, f32[1,2,256,128]{3,2,1,0:T(8,128)}, u32[]{:S(2)}) copy-start(f32[1,2,256,128]{3,2,1,0:T(8,128)} %block.3) | copy-start | bytes 786436
  9.6 13.4 %copy-start = (f32[2,128,128]{2,1,0:T(8,128)S(1)}, f32[2,128,128]{2,1,0:T(8,128)}, u32[]{:S(2)}) copy-start(f32[2,128,128]{2,1,0:T(8,128)} %constant.4.clone.table_ref.rest_9_) | copy-start | bytes 393220
  9.6 13.4 %copy-start.5 = (f32[2,128,128]{2,1,0:T(8,128)S(1)}, f32[2,128,128]{2,1,0:T(8,128)}, u32[]{:S(2)}) copy-start(f32[2,128,128]{2,1,0:T(8,128)} %wave_in.1) | copy-start | bytes 393220
  9.8 9.9 %collective-permute-start.3 = (f32[2,128,128]{2,1,0:T(8,128)S(1)}, f32[2,128,128]{2,1,0:T(8,128)S(1)}, u32[]{:S(2)}, u32[]{:S(2)}) collective-permute-start(f32[2,128,128]{2,1,0:T(8,128)S(1)} %get-tuple-element.41), channel_id=1, source_target_pairs={{2,0},{6,16},{10,12},{3,1},{7,17},{11,13},{16,18},{20,2},{24,30},{... | collective-permute-start | bytes 393224 | tf_op jit(solution)/shard_map/ppermute | solution.py:306
  14.5 8.5 %collective-permute-start.4 = (f32[2,128,128]{2,1,0:T(8,128)S(1)}, f32[2,128,128]{2,1,0:T(8,128)S(1)}, u32[]{:S(2)}, u32[]{:S(2)}) collective-permute-start(f32[2,128,128]{2,1,0:T(8,128)S(1)} %get-tuple-element.40), channel_id=1, source_target_pairs={{3,0},{7,16},{11,12},{2,1},{6,17},{10,13},{17,18},{21,2},{25,30},{... | collective-permute-start | bytes 393224 | tf_op jit(solution)/shard_map/ppermute | solution.py:306
  16.4 6.6 %collective-permute-start.2 = (f32[2,128,128]{2,1,0:T(8,128)S(1)}, f32[2,128,128]{2,1,0:T(8,128)S(1)}, u32[]{:S(2)}, u32[]{:S(2)}) collective-permute-start(f32[2,128,128]{2,1,0:T(8,128)S(1)} %get-tuple-element.40), channel_id=1, source_target_pairs={{1,0},{13,12},{0,1},{12,13},{19,18},{31,30},{18,19},{30,31},{33,32... | collective-permute-start | bytes 393224 | tf_op jit(solution)/shard_map/ppermute | solution.py:306
  17.1 8.6 %collective-permute-start.6 = (f32[2,128,128]{2,1,0:T(8,128)S(1)}, f32[2,128,128]{2,1,0:T(8,128)S(1)}, u32[]{:S(2)}, u32[]{:S(2)}) collective-permute-start(f32[2,128,128]{2,1,0:T(8,128)S(1)} %get-tuple-element.41), channel_id=1, source_target_pairs={{4,16},{8,12},{5,17},{9,13},{22,2},{26,30},{23,3},{27,31},{36,48},... | collective-permute-start | bytes 393224 | tf_op jit(solution)/shard_map/ppermute | solution.py:306
  18.4 7.3 %collective-permute-start.7 = (f32[2,128,128]{2,1,0:T(8,128)S(1)}, f32[2,128,128]{2,1,0:T(8,128)S(1)}, u32[]{:S(2)}, u32[]{:S(2)}) collective-permute-start(f32[2,128,128]{2,1,0:T(8,128)S(1)} %get-tuple-element.40), channel_id=1, source_target_pairs={{5,16},{9,12},{4,17},{8,13},{23,2},{27,30},{22,3},{26,31},{37,48},... | collective-permute-start | bytes 393224 | tf_op jit(solution)/shard_map/ppermute | solution.py:306
  23.0 3.2 %collective-permute-start.5 = (f32[2,128,128]{2,1,0:T(8,128)S(1)}, f32[2,128,128]{2,1,0:T(8,128)S(1)}, u32[]{:S(2)}, u32[]{:S(2)}) collective-permute-start(f32[2,128,128]{2,1,0:T(8,128)S(1)} %get-tuple-element.42), channel_id=1, source_target_pairs={{0,16},{1,17},{18,2},{19,3},{32,48},{33,49},{50,34},{51,35},{64,80... | collective-permute-start | bytes 393224 | tf_op jit(solution)/shard_map/ppermute | solution.py:319
  24.3 5.1 %collective-permute-start.9 = (f32[2,128,128]{2,1,0:T(8,128)S(1)}, f32[2,128,128]{2,1,0:T(8,128)S(1)}, u32[]{:S(2)}, u32[]{:S(2)}) collective-permute-start(f32[2,128,128]{2,1,0:T(8,128)S(1)} %get-tuple-element.41), channel_id=1, source_target_pairs={{14,12},{15,13},{28,30},{29,31},{46,44},{47,45},{60,62},{61,63},{7... | collective-permute-start | bytes 393224 | tf_op jit(solution)/shard_map/ppermute | solution.py:306
  25.0 4.5 %collective-permute-start.10 = (f32[2,128,128]{2,1,0:T(8,128)S(1)}, f32[2,128,128]{2,1,0:T(8,128)S(1)}, u32[]{:S(2)}, u32[]{:S(2)}) collective-permute-start(f32[2,128,128]{2,1,0:T(8,128)S(1)} %get-tuple-element.40), channel_id=1, source_target_pairs={{15,12},{14,13},{29,30},{28,31},{47,44},{46,45},{61,62},{60,63},{7... | collective-permute-start | bytes 393224 | tf_op jit(solution)/shard_map/ppermute | solution.py:306
  26.3 5.1 %copy-start.3 = (f32[2,128,128]{2,1,0:T(8,128)S(1)}, f32[2,128,128]{2,1,0:T(8,128)}, u32[]{:S(2)}) copy-start(f32[2,128,128]{2,1,0:T(8,128)} %rest_8_.1) | copy-start | bytes 393220
  26.3 5.1 %copy-start.4 = (f32[2,128,128]{2,1,0:T(8,128)S(1)}, f32[2,128,128]{2,1,0:T(8,128)}, u32[]{:S(2)}) copy-start(f32[2,128,128]{2,1,0:T(8,128)} %constant.5.clone.rest_10_) | copy-start | bytes 393220
  28.0 3.3 %collective-permute-start.8 = (f32[2,128,128]{2,1,0:T(8,128)S(1)}, f32[2,128,128]{2,1,0:T(8,128)S(1)}, u32[]{:S(2)}, u32[]{:S(2)}) collective-permute-start(f32[2,128,128]{2,1,0:T(8,128)S(1)} %get-tuple-element.45), channel_id=1, source_target_pairs={{16,12},{17,13},{2,30},{3,31},{48,44},{49,45},{34,62},{35,63},{80,... | collective-permute-start | bytes 393224 | tf_op jit(solution)/shard_map/ppermute | solution.py:327
  31.4 14.7 %collective-permute-start.11 = (f32[2,128,128]{2,1,0:T(8,128)S(1)}, f32[2,128,128]{2,1,0:T(8,128)S(1)}, u32[]{:S(2)}, u32[]{:S(2)}) collective-permute-start(f32[2,128,128]{2,1,0:T(8,128)S(1)} %get-tuple-element.46), channel_id=1, source_target_pairs={{12,16},{13,17},{30,2},{31,3},{44,48},{45,49},{62,34},{63,35},{76,... | collective-permute-start | bytes 393224 | tf_op jit(solution)/shard_map/ppermute | solution.py:342
  32.7 13.4 %collective-permute-start.12 = (f32[2,128,128]{2,1,0:T(8,128)S(1)}, f32[2,128,128]{2,1,0:T(8,128)S(1)}, u32[]{:S(2)}, u32[]{:S(2)}) collective-permute-start(f32[2,128,128]{2,1,0:T(8,128)S(1)} %get-tuple-element.53), channel_id=1, source_target_pairs={{12,13},{13,12},{30,31},{31,30},{44,45},{45,44},{62,63},{63,62},{7... | collective-permute-start | bytes 393224 | tf_op jit(solution)/shard_map/ppermute | solution.py:339
  33.4 12.7 %collective-permute-start.13 = (f32[2,128,128]{2,1,0:T(8,128)S(1)}, f32[2,128,128]{2,1,0:T(8,128)S(1)}, u32[]{:S(2)}, u32[]{:S(2)}) collective-permute-start(f32[2,128,128]{2,1,0:T(8,128)S(1)} %get-tuple-element.54), channel_id=1, source_target_pairs={{12,14},{13,15},{30,28},{31,29},{44,46},{45,47},{62,60},{63,61},{7... | collective-permute-start | bytes 393224 | tf_op jit(solution)/shard_map/ppermute | solution.py:339
  34.0 12.0 %collective-permute-start.14 = (f32[2,128,128]{2,1,0:T(8,128)S(1)}, f32[2,128,128]{2,1,0:T(8,128)S(1)}, u32[]{:S(2)}, u32[]{:S(2)}) collective-permute-start(f32[2,128,128]{2,1,0:T(8,128)S(1)} %get-tuple-element.55), channel_id=1, source_target_pairs={{12,15},{13,14},{30,29},{31,28},{44,47},{45,46},{62,61},{63,60},{7... | collective-permute-start | bytes 393224 | tf_op jit(solution)/shard_map/ppermute | solution.py:339
  47.9 2.3 %collective-permute-start.15 = (f32[2,128,128]{2,1,0:T(8,128)S(1)}, f32[2,128,128]{2,1,0:T(8,128)S(1)}, u32[]{:S(2)}, u32[]{:S(2)}) collective-permute-start(f32[2,128,128]{2,1,0:T(8,128)S(1)} %get-tuple-element.56), channel_id=1, source_target_pairs={{16,0},{17,1},{2,18},{3,19},{48,32},{49,33},{34,50},{35,51},{80,64... | collective-permute-start | bytes 393224 | tf_op jit(solution)/shard_map/ppermute | solution.py:342
  50.1 6.5 %collective-permute-start.17 = (f32[2,128,128]{2,1,0:T(8,128)S(1)}, f32[2,128,128]{2,1,0:T(8,128)S(1)}, u32[]{:S(2)}, u32[]{:S(2)}) collective-permute-start(f32[2,128,128]{2,1,0:T(8,128)S(1)} %get-tuple-element.63), channel_id=1, source_target_pairs={{0,1},{16,5},{12,9},{1,0},{17,4},{13,8},{18,19},{2,23},{30,27},{19... | collective-permute-start | bytes 393224 | tf_op jit(solution)/shard_map/ppermute | solution.py:339
  51.4 9.0 %collective-permute-start.18 = (f32[2,128,128]{2,1,0:T(8,128)S(1)}, f32[2,128,128]{2,1,0:T(8,128)S(1)}, u32[]{:S(2)}, u32[]{:S(2)}) collective-permute-start(f32[2,128,128]{2,1,0:T(8,128)S(1)} %get-tuple-element.64), channel_id=1, source_target_pairs={{0,2},{16,6},{12,10},{1,3},{17,7},{13,11},{18,16},{2,20},{30,24},{... | collective-permute-start | bytes 393224 | tf_op jit(solution)/shard_map/ppermute | solution.py:339
  53.4 8.9 %collective-permute-start.19 = (f32[2,128,128]{2,1,0:T(8,128)S(1)}, f32[2,128,128]{2,1,0:T(8,128)S(1)}, u32[]{:S(2)}, u32[]{:S(2)}) collective-permute-start(f32[2,128,128]{2,1,0:T(8,128)S(1)} %get-tuple-element.65), channel_id=1, source_target_pairs={{0,3},{16,7},{12,11},{1,2},{17,6},{13,10},{18,17},{2,21},{30,25},{... | collective-permute-start | bytes 393224 | tf_op jit(solution)/shard_map/ppermute | solution.py:339
  55.3 7.0 %collective-permute-start.16 = (f32[2,128,128]{2,1,0:T(8,128)S(1)}, f32[2,128,128]{2,1,0:T(8,128)S(1)}, u32[]{:S(2)}, u32[]{:S(2)}) collective-permute-start(f32[2,128,128]{2,1,0:T(8,128)S(1)} %get-tuple-element.61.first_own), channel_id=1, source_target_pairs={{16,4},{12,8},{17,5},{13,9},{2,22},{30,26},{3,23},{31,27},{48,36},... | collective-permute-start | bytes 393224 | tf_op jit(solution)/shard_map/ppermute | solution.py:339
  62.3 9.1 %copy-start.2 = (f32[1,2,256,128]{3,2,1,0:T(8,128)S(1)}, f32[1,2,256,128]{3,2,1,0:T(8,128)}, u32[]{:S(2)}) copy-start(f32[1,2,256,128]{3,2,1,0:T(8,128)} %block.3) | copy-start | bytes 786436
  62.5 8.9 %collective-permute-start.21 = (f32[2,256,128]{2,1,0:T(8,128)S(1)}, f32[2,256,128]{2,1,0:T(8,128)S(1)}, u32[]{:S(2)}, u32[]{:S(2)}) collective-permute-start(f32[2,256,128]{2,1,0:T(8,128)S(1)} %get-tuple-element.67), channel_id=1, source_target_pairs={{16,32},{48,64},{80,96},{112,128},{144,160},{176,192},{208,224},{2... | collective-permute-start | bytes 786440 | tf_op jit(solution)/shard_map/ppermute | solution.py:367
  65.8 5.7 %collective-permute-start.20 = (f32[2,256,128]{2,1,0:T(8,128)S(1)}, f32[2,256,128]{2,1,0:T(8,128)S(1)}, u32[]{:S(2)}, u32[]{:S(2)}) collective-permute-start(f32[2,256,128]{2,1,0:T(8,128)S(1)} %get-tuple-element.66), channel_id=1, source_target_pairs={{0,16},{16,0},{32,48},{48,32},{64,80},{80,64},{96,112},{112,96},{1... | collective-permute-start | bytes 786440 | tf_op jit(solution)/shard_map/ppermute | solution.py:366
